TPU v7x, 128 devices: a whole 4x4x4 slice. The times are simulated.
128 devices in a mesh: facet: 16 (over x, y), sub: 8 (over z, core).
Axes of the slice: x: 4, y: 4, z: 4, core: 2. Of those that a mesh axis runs over, the one named last changes fastest.
Arguments:
- facet_spec: bfloat16 [16, 2, 1216, 704], P('facet'), may hold values from -3 to 3
- worker_of_subgrid: int32 [128], replicated, may hold values from 0 to 127, each once
- vis_count: int32 [128], P(('facet', 'sub')), may hold values from 512 to 8192, as said below
- bin_offsets: int32 [128, 2, 8192], P(('facet', 'sub')), may hold values from 0 to 248
- bin_fractions: float32 [128, 2, 8192], P(('facet', 'sub')), may hold values from 0 to 1
- observed: float32 [128, 2, 8192], P(('facet', 'sub')), may hold values from -6 to 6
Outputs:
- residual_vis: float32 [128, 2, 8192], P(('facet', 'sub'))
- facet_update: float32 [16, 2, 1216, 704], P('facet', None, 'sub')
Inputs may be any that keep to these rules, and one draw needn't show every extreme that they name: `worker_of_subgrid`: a permutation of the subgrids. `vis_count`: some device row has all 8192 slots live in every draw.
All inputs are finite; a program needn't handle non-finite values.
Results may differ from a plain program's by a relative error of at most 0.014.
Values may be sent and summed in bfloat16 or wider, within the bound.
No kernel may reach another device: no remote copies, remote signals or barrier semaphores. Data moves between devices by JAX's collectives and lax.ppermute only.
A program may use at most 128 MiB of HBM per device.

v0:
```python
import math

import jax
import jax.numpy as jnp
from jax import lax
from jax.sharding import PartitionSpec as P

SUB = 256
MC = 256
STEP = 64
KS = 8
VB = 512


TWO_PI = 2.0 * math.pi


def cut_along(shard, dim, count):
    before, after = (shard.shape[:dim], shard.shape[dim + 1 :])
    return jnp.moveaxis(shard.reshape(*before, count, -1, *after), dim, 0)


def cut_rows(length, count):
    step = length // count
    if step >= 8:
        step -= step % 8
    return [step * k for k in range(1, count)]


def in_order(blocks, dim):
    dims = list(blocks.shape[1:])
    dims[dim] *= blocks.shape[0]
    return jnp.moveaxis(blocks, 0, dim).reshape(dims)


def exchange_in_pieces(shard, axis, pieces, split_dim, concat_dim):
    blocks = cut_along(shard, split_dim, lax.axis_size(axis))
    split_at = max(range(1, max(2, blocks.ndim - 1)), key=lambda d: blocks.shape[d])
    finished = []
    for piece in jnp.split(blocks, cut_rows(blocks.shape[split_at], pieces), axis=split_at):
        if piece.size:
            finished.append(lax.all_to_all(piece, axis, split_axis=0, concat_axis=0, tiled=True))
    return in_order(jnp.concatenate(finished, axis=split_at), concat_dim)


def phase_table(offset, facets, swapped, conj_sign):
    sub_index = jnp.arange(SUB, dtype=jnp.int32) - SUB // 2
    win_index = jnp.arange(MC, dtype=jnp.int32) - MC // 2
    if swapped:
        sub_part = sub_index[None, :]
        win_part = win_index[:, None]
    else:
        sub_part = sub_index[:, None]
        win_part = win_index[None, :]
    modulus = SUB * facets
    residue = jnp.mod(sub_part * win_part * facets + sub_part * offset, modulus)
    angles = residue.astype(jnp.float32) * (TWO_PI / modulus)
    factor = MC ** (-0.5)
    return jnp.stack([jnp.cos(angles) * factor, conj_sign * jnp.sin(angles) * factor]).astype(
        jnp.bfloat16
    )


def pair_dot(first_pair, second_pair):
    real_real = jnp.dot(first_pair[0], second_pair[0], preferred_element_type=jnp.float32)
    imag_imag = jnp.dot(first_pair[1], second_pair[1], preferred_element_type=jnp.float32)
    real_imag = jnp.dot(first_pair[0], second_pair[1], preferred_element_type=jnp.float32)
    imag_real = jnp.dot(first_pair[1], second_pair[0], preferred_element_type=jnp.float32)
    return jnp.stack([real_real - imag_imag, real_imag + imag_real])


def kernel_rows(offsets, fractions):
    cells = jnp.arange(SUB, dtype=jnp.int32)[None, :] - offsets[:, None]
    distance = cells.astype(jnp.float32) - fractions[:, None] - (0.5 * KS - 1.0)
    inside = (cells >= 0) & (cells < KS)
    weights = jnp.where(inside, 0.5 * jnp.exp(-jnp.square(distance * (9.0 / KS))), 0.0)
    return weights.astype(jnp.bfloat16)


def subgrid_holder(worker):
    total_rows = worker.shape[0]
    slot_ids = jnp.arange(total_rows, dtype=jnp.int32)
    matches = (worker[None, :] == slot_ids[:, None]).astype(jnp.int32)
    return jnp.sum(matches * slot_ids[None, :], axis=1)


def corner_of(subgrid, pos_v):
    top_row = subgrid // pos_v * STEP
    left_col = subgrid % pos_v * STEP
    return (top_row, left_col)


def window_of(spectrum, subgrid, pos_v):
    top_row, left_col = corner_of(subgrid, pos_v)
    return lax.dynamic_slice(spectrum, (jnp.int32(0), top_row, left_col), (2, MC, MC))


def add_window(plane, window, subgrid, pos_v):
    top_row, left_col = corner_of(subgrid, pos_v)
    anchor = jnp.int32(0)
    current = lax.dynamic_slice(plane, (anchor, top_row, left_col), (2, MC, MC))
    return lax.dynamic_update_slice(
        plane, current + window.astype(jnp.float32), (anchor, top_row, left_col)
    )


def grid_from(incoming, facets):

    def add_facet(running, member):
        contribution, facet_id = member
        left_table = phase_table(facet_id, facets, False, 1.0)
        right_table = phase_table(jnp.mod(5 * facet_id + 3, facets), facets, True, 1.0)
        partial_value = pair_dot(left_table, contribution).astype(jnp.bfloat16)
        return (running + pair_dot(partial_value, right_table), None)

    starting = jnp.zeros((2, SUB, SUB), jnp.float32)
    running, _ = lax.scan(add_facet, starting, (incoming, jnp.arange(facets, dtype=jnp.int32)))
    return running


def adjoint_window(resid_grid, facet_id, facets):
    left_table = phase_table(facet_id, facets, True, -1.0)
    right_table = phase_table(jnp.mod(5 * facet_id + 3, facets), facets, False, -1.0)
    partial_value = pair_dot(left_table, resid_grid).astype(jnp.bfloat16)
    return pair_dot(partial_value, right_table).astype(jnp.bfloat16)


def degrid_rows(grid_cat, offsets, fractions, observed_rows, live_count):
    slot_total = offsets.shape[1]
    blocks = (live_count + VB - 1) // VB

    def block_step(block_id, carried):
        residual, gridded = carried
        first_slot = (block_id * VB).astype(jnp.int32)
        block_offsets = lax.dynamic_slice_in_dim(offsets, first_slot, VB, 1)
        block_fractions = lax.dynamic_slice_in_dim(fractions, first_slot, VB, 1)
        block_observed = lax.dynamic_slice_in_dim(observed_rows, first_slot, VB, 1)
        u_weights = kernel_rows(block_offsets[0], block_fractions[0])
        v_weights = kernel_rows(block_offsets[1], block_fractions[1])
        product = jnp.dot(u_weights, grid_cat, preferred_element_type=jnp.float32)
        v_float = v_weights.astype(jnp.float32)
        model_real = jnp.sum(product[:, :SUB] * v_float, axis=1)
        model_imag = jnp.sum(product[:, SUB:] * v_float, axis=1)
        live_mask = first_slot + jnp.arange(VB, dtype=jnp.int32) < live_count
        real_part = jnp.where(live_mask, block_observed[0] - model_real, 0.0)
        imag_part = jnp.where(live_mask, block_observed[1] - model_imag, 0.0)
        residual = lax.dynamic_update_slice_in_dim(
            residual, jnp.stack([real_part, imag_part]), first_slot, 1
        )
        weighted = jnp.concatenate(
            [real_part[:, None] * v_float, imag_part[:, None] * v_float], axis=1
        ).astype(jnp.bfloat16)
        gridded = gridded + lax.dot_general(
            u_weights, weighted, (((0,), (0,)), ((), ())), preferred_element_type=jnp.float32
        )
        return (residual, gridded)

    starting = (jnp.zeros((2, slot_total), jnp.float32), jnp.zeros((SUB, 2 * SUB), jnp.float32))
    return lax.fori_loop(0, blocks, block_step, starting)


def on_device(facet_spec, worker_of_subgrid, vis_count, bin_offsets, bin_fractions, observed):
    sub_rank = lax.axis_index("sub")
    pos_u = lax.axis_size("facet")
    pos_v = lax.axis_size("sub")
    holder = subgrid_holder(worker_of_subgrid)
    targets = holder[jnp.arange(pos_u, dtype=jnp.int32) * pos_v + sub_rank]
    own_facet = facet_spec[0]

    def own_window(subgrid):
        return window_of(own_facet, subgrid, pos_v)

    outgoing = jax.vmap(own_window)(targets)
    incoming = exchange_in_pieces(outgoing, "facet", 2, 0, 0)
    grid_sum = grid_from(incoming, pos_u)
    grid_half = grid_sum.astype(jnp.bfloat16)
    grid_cat = jnp.concatenate([grid_half[0], grid_half[1]], axis=1)
    residual, gridded = degrid_rows(
        grid_cat, bin_offsets[0], bin_fractions[0], observed[0], vis_count[0]
    )
    residual = residual[None]
    resid_grid = jnp.stack([gridded[:, :SUB], gridded[:, SUB:]]).astype(jnp.bfloat16)

    def one_window(facet_id):
        return adjoint_window(resid_grid, facet_id, pos_u)

    windows = lax.map(one_window, jnp.arange(pos_u, dtype=jnp.int32))
    returned = lax.all_to_all(windows, "facet", split_axis=0, concat_axis=0, tiled=True)
    plane_rows = facet_spec.shape[2]
    plane_cols = facet_spec.shape[3]
    plane = jnp.zeros((2, plane_rows, plane_cols), jnp.float32)

    def place_one(source, state):
        return add_window(state, returned[source], targets[source], pos_v)

    plane = lax.fori_loop(0, pos_u, place_one, plane)
    update = lax.psum_scatter(plane, "sub", scatter_dimension=1, tiled=True)
    return (residual, update[None])


def solution(mesh):
    placed = (
        P("facet", None, None, None),
        P(),
        P(("facet", "sub")),
        P(("facet", "sub"), None, None),
        P(("facet", "sub"), None, None),
        P(("facet", "sub"), None, None),
    )
    return jax.shard_map(
        on_device,
        mesh=mesh,
        in_specs=placed,
        out_specs=(P(("facet", "sub"), None, None), P("facet", None, "sub", None)),
        check_vma=False,
    )
```

profile of v0, /device:TPU:24, one launch (start us, length us, event | category | flops | bytes accessed | tf_op | source)
XLA Modules:
  0.0 966.5 jit_solution(1981416925247066654)
XLA Ops:
  8.6 6.1 copy.11
  14.8 2.4 broadcast.1506.clone
  17.2 59.3 %while.61 = (s32[]{:T(128)}, bf16[2,1216,704]{2,1,0:T(8,128)(2,1)}, s32[16,3]{0,1:T(4,128)S(1)}, bf16[16,2,256,256]{3,2,1,0:T(8,128)(2,1)}, s32[]{:T(128)}) while((s32[]{:T(128)}, bf16[2,1216,704]{2,1,0:T(8,128)(2,1)}, s32[16,3]{0,1:T(4,128)S(1)}, bf16[16,2,256,256]{3,2,1,0:T(8,128)(2,1)}, s32[]{:T(128)}) %tuple.178), condition=%wide.while_cond, body=%wide.while_body.sunk | while | flops 2 | bytes 525429 | solution.py:95
  17.8 3.1 bitcast_dynamic-update-slice_fusion.2
  21.5 3.1 bitcast_dynamic-update-slice_fusion.2
  25.2 3.1 bitcast_dynamic-update-slice_fusion.2
  28.9 3.1 bitcast_dynamic-update-slice_fusion.2
  32.6 3.1 bitcast_dynamic-update-slice_fusion.2
  36.3 3.1 bitcast_dynamic-update-slice_fusion.2
  40.0 3.1 bitcast_dynamic-update-slice_fusion.2
  43.7 3.1 bitcast_dynamic-update-slice_fusion.2
  47.4 3.1 bitcast_dynamic-update-slice_fusion.2
  51.1 3.1 bitcast_dynamic-update-slice_fusion.2
  54.8 3.1 bitcast_dynamic-update-slice_fusion.2
  58.5 3.1 bitcast_dynamic-update-slice_fusion.2
  62.2 3.1 bitcast_dynamic-update-slice_fusion.2
  65.9 3.1 bitcast_dynamic-update-slice_fusion.2
  69.6 3.1 bitcast_dynamic-update-slice_fusion.2
  73.4 3.1 bitcast_dynamic-update-slice_fusion.2
  76.4 4.1 fusion.194
  80.5 33.0 %all_to_all.15 = bf16[16,1,2,128,256]{4,3,2,1,0:T(8,128)(2,1)S(1)} all-to-all(bf16[16,1,2,128,256]{4,3,2,1,0:T(8,128)(2,1)S(1)} %get-tuple-element.515), channel_id=1, replica_groups=mesh['facet'=16,'sub'=8] {'facet'}, dimensions={0} | all-to-all | bytes 4194304 | tf_op jit(solution)/shard_map/all_to_all | solution.py:42
  113.5 6.5 all-to-all-start.1
  120.7 24.7 %all-to-all-done.1 = bf16[16,1,2,128,256]{4,3,2,1,0:T(8,128)(2,1)} async-done(((bf16[16,1,2,128,256]{4,3,2,1,0:T(8,128)(2,1)}), bf16[16,1,2,128,256]{4,3,2,1,0:T(8,128)(2,1)}, u32[]{:S(2)}, u32[]{:S(2)}) %all-to-all-start.1) | async-done | bytes 2097184 | tf_op jit(solution)/shard_map/all_to_all | solution.py:42
  145.4 3.9 maximum_bitcast_fusion
  149.3 242.0 %while.62 = (s32[]{:T(128)}, f32[2,256,256]{2,1,0:T(8,128)S(1)}, s32[16]{0:T(128)S(1)}, bf16[16,2,256,256]{3,2,1,0:T(8,128)(2,1)}, s32[]{:T(128)}, /*index=5*/s3...) while((s32[]{:T(128)}, f32[2,256,256]{2,1,0:T(8,128)S(1)}, ...), condition=%wide.region_2.3_spmd.clone, body=%wide.region_1.2_spmd.clone.sunk | while | flops 278660096 | bytes 5528892 | solution.py:117
  153.0 2.1 fusion.308
  157.2 2.1 fusion.304
  168.2 2.1 fusion.308
  172.3 2.1 fusion.304
  183.3 2.1 fusion.308
  187.5 2.1 fusion.304
  198.4 2.1 fusion.308
  202.6 2.1 fusion.304
  213.5 2.1 fusion.308
  217.7 2.1 fusion.304
  228.7 2.1 fusion.308
  232.8 2.1 fusion.304
  243.8 2.1 fusion.308
  248.0 2.1 fusion.304
  369.0 2.1 fusion.304
  391.4 86.6 %while.58 = (s32[]{:T(128)}, f32[2,8192]{1,0:T(2,128)S(1)}, f32[256,512]{1,0:T(8,128)S(1)}, s32[]{:T(128)}, s32[]{:T(128)}, /*index=5*/f32[2,8192]{1,0:T(2,128)}...) while((s32[]{:T(128)}, f32[2,8192]{1,0:T(2,128)S(1)}, ...), condition=%wide.region_6.7_spmd, body=%wide.region_3.6_spmd.sunk | while | flops 277747712 | bytes 4534507 | solution.py:159
  478.2 2.4 broadcast.1506
  480.6 196.5 %while.59 = (s32[]{:T(128)}, bf16[16,2,256,256]{3,2,1,0:T(8,128)(2,1)}, s32[16]{0:T(128)S(1)}, bf16[2,256,256]{2,1,0:T(8,128)(2,1)S(1)}, s32[]{:T(128)}, /*index...) while((s32[]{:T(128)}, bf16[16,2,256,256]{3,2,1,0:T(8,128)(2,1)}, s32[16]{0:T(128)S(1)}, ...), condition=%wide.region_8.9_spmd, body=%wide.region_7.8_spmd.sunk | while | flops 278922240 | bytes 4218122 | solution.py:187
  677.1 6.0 all-to-all-start.2
  683.1 50.1 %all-to-all-done.2 = bf16[16,2,256,256]{3,2,1,0:T(8,128)(2,1)} async-done(((bf16[16,2,256,256]{3,2,1,0:T(8,128)(2,1)}), bf16[16,2,256,256]{3,2,1,0:T(8,128)(2,1)}, u32[]{:S(2)}, u32[]{:S(2)}) %all-to-all-start.2) | async-done | bytes 4194336 | tf_op jit(solution)/shard_map/all_to_all | solution.py:188
  733.2 3.5 broadcast_in_dim.61
  736.7 169.1 %while.60 = (s32[]{:T(128)}, f32[2,1216,704]{2,1,0:T(8,128)}, s32[16]{0:T(128)S(1)}, bf16[16,2,256,256]{3,2,1,0:T(8,128)(2,1)}, s32[]{:T(128)}, /*index=5*/s32[]...) while((s32[]{:T(128)}, f32[2,1216,704]{2,1,0:T(8,128)}, ...), condition=%wide.region_10.11_spmd, body=%wide.region_9.10_spmd.sunk | while | flops 262173 | bytes 2359736 | solution.py:196
  741.0 6.8 dynamic_update_slice.32
  752.0 5.5 dynamic_update_slice.32
  761.8 6.7 dynamic_update_slice.32
  772.8 5.9 dynamic_update_slice.32
  783.0 6.0 dynamic_update_slice.32
  793.3 6.0 dynamic_update_slice.32
  803.6 5.9 dynamic_update_slice.32
  813.8 6.7 dynamic_update_slice.32
  824.8 6.7 dynamic_update_slice.32
  835.8 5.9 dynamic_update_slice.32
  846.1 6.8 dynamic_update_slice.32
  857.2 5.9 dynamic_update_slice.32
  867.4 6.7 dynamic_update_slice.32
  878.4 6.8 dynamic_update_slice.32
  889.4 5.5 dynamic_update_slice.32
  899.2 6.5 dynamic_update_slice.32
  905.7 53.9 %reduce-scatter.2.cloned.1.call-done = f32[2,152,704]{2,1,0:T(8,128)} async-done(((f32[2,1216,704]{2,1,0:T(8,128)}), f32[2,152,704]{2,1,0:T(8,128)}) %reduce-scatter.2.cloned.1.call-update) | async-done | bytes 856080 | tf_op jit(solution)/shard_map/reduce_scatter | solution.py:197
  (599 shorter events, 513.8 us)
Async XLA Ops:
  113.5 31.8 %all-to-all-start.1 = ((bf16[16,1,2,128,256]{4,3,2,1,0:T(8,128)(2,1)}), bf16[16,1,2,128,256]{4,3,2,1,0:T(8,128)(2,1)}, u32[]{:S(2)}, u32[]{:S(2)}) async-start(bf16[16,1,2,128,256]{4,3,2,1,0:T(8,128)(2,1)} %get-tuple-element.516), calls=%async_computation.1 | async-start | bytes 4194304 | tf_op jit(solution)/shard_map/all_to_all | solution.py:42
  478.0 2.6 copy-start
  677.1 56.1 %all-to-all-start.2 = ((bf16[16,2,256,256]{3,2,1,0:T(8,128)(2,1)}), bf16[16,2,256,256]{3,2,1,0:T(8,128)(2,1)}, u32[]{:S(2)}, u32[]{:S(2)}) async-start(bf16[16,2,256,256]{3,2,1,0:T(8,128)(2,1)} %get-tuple-element.418), calls=%async_computation.2 | async-start | bytes 8388608 | tf_op jit(solution)/shard_map/all_to_all | solution.py:188
  683.0 276.6 %reduce-scatter.2.cloned.1.call-start = ((), (), s32[]{:S(2)}) async-start(), calls=%async_computation.4 | async-start | bytes 8404992 | tf_op jit(solution)/shard_map/reduce_scatter | solution.py:197
Sparse Core Ops, SparseCore 0:
  905.9 53.7 reduce-scatter.1
where the time goes:
time: 975 us; the launch traced here: 966 us
  matrix products  379 us (39%)
  local copies, waits for them, and re-layouts  233 us (24%)
  waiting for transfers between devices  129 us (13%)
  other arithmetic  105 us (11%)
  loops' own time  59.6 us (6%)
  blocking collectives  33 us (3%)
  between operations  14.8 us (2%)
  starting transfers between devices  12.4 us (1%)
    dynamic_update_slice x16, local copies, waits for them, and re-layouts, add_window(): lax.dynamic_update_slice(plane, current + window.astype(jnp.float32), (an...  100 us
    dot_general x64, matrix products, pair_dot(): jnp.dot(first_pair[1], second_pair[1], preferred_element_type=jnp.float32)  91.7 us
    dot_general x64, matrix products, pair_dot(): jnp.dot(first_pair[1], second_pair[0], preferred_element_type=jnp.float32)  91.5 us
    dot_general x64, matrix products, pair_dot(): jnp.dot(first_pair[0], second_pair[1], preferred_element_type=jnp.float32)  91 us
    dot_general x64, matrix products, pair_dot(): jnp.dot(first_pair[0], second_pair[0], preferred_element_type=jnp.float32)  90.9 us
    gather x48, local copies, waits for them, and re-layouts  59.2 us
    reduce_scatter x1, waiting for transfers between devices, on_device(): update = lax.psum_scatter(plane, 'sub', scatter_dimension=1, tiled=True)  53.9 us
    all_to_all x1, waiting for transfers between devices, on_device(): lax.all_to_all(windows, 'facet', split_axis=0, concat_axis=0, tiled=True)  50.1 us
  transfers between devices with their start and end apart: 3, of which 3 were waited for; matrix products, arithmetic and copies ran while one was open for 0% of the time, Pallas kernels for 0%

commit v1 on v0

v1 whole, which is shorter than its diff:
```python
import math

import jax
import jax.numpy as jnp
import numpy as np
from jax import lax
from jax.experimental import pallas as pl
from jax.experimental.pallas import tpu as pltpu
from jax.sharding import PartitionSpec as P

SUB = 256
MC = 256
STEP = 64
KS = 8
BLOCK = 1024
LANES = 128
MIB = 1 << 20


def phase_tables(facets):
    sub_part = (np.arange(SUB) - SUB // 2)[:, None]
    win_part = (np.arange(MC) - MC // 2)[None, :]
    modulus = SUB * facets
    tables = []
    for offset in range(facets):
        residue = np.mod(sub_part * win_part * facets + sub_part * offset, modulus)
        angles = residue.astype(np.float32).astype(np.float64) * (2.0 * math.pi / modulus)
        factor = MC ** (-0.5)
        tables.append(np.stack([np.cos(angles) * factor, np.sin(angles) * factor]))
    return np.stack(tables).astype(jnp.bfloat16)


def side_by_side(first, second):
    return jnp.concatenate([first, second], axis=1)


def stacked(first, second):
    return jnp.concatenate([first, second], axis=0)


def f32_dot(left, right):
    return jnp.dot(left, right, preferred_element_type=jnp.float32)


def contribution_kernel(place, spec, left, right, out, shifted_spec, left_mat, right_mat):
    step = pl.program_id(0)
    reach = shifted_spec.shape[2]

    @pl.when(step == 0)
    def _():
        for part in range(2):
            shifted_spec[part] = spec[0, part, :, STEP : STEP + reach]
        a_re, a_im = left[0, 0], left[0, 1]
        left_mat[...] = stacked(side_by_side(a_re, -a_im), side_by_side(a_im, a_re))
        b_re, b_im = right[0, 0], right[0, 1]
        right_mat[...] = stacked(side_by_side(b_re, b_im), side_by_side(-b_im, b_re))

    top = pl.multiple_of(place[2 + 2 * step], STEP)
    left_step = place[3 + 2 * step]
    col = pl.multiple_of(left_step // 2 * LANES, LANES)

    def finish(window):
        half = f32_dot(left_mat[...], window).astype(jnp.bfloat16)
        whole = f32_dot(side_by_side(half[:SUB], half[SUB:]), right_mat[...])
        out[0, :SUB] = whole[:, :SUB].astype(jnp.bfloat16)
        out[0, SUB:] = whole[:, SUB:].astype(jnp.bfloat16)

    @pl.when(left_step % 2 == 0)
    def _():
        finish(
            stacked(
                spec[0, 0, pl.ds(top, MC), pl.ds(col, MC)],
                spec[0, 1, pl.ds(top, MC), pl.ds(col, MC)],
            )
        )

    @pl.when(left_step % 2 == 1)
    def _():
        finish(
            stacked(
                shifted_spec[0, pl.ds(top, MC), pl.ds(col, MC)],
                shifted_spec[1, pl.ds(top, MC), pl.ds(col, MC)],
            )
        )


def contributions(place, spec, tables, tables_t):
    facets = tables.shape[0]
    rows, cols = spec.shape[2:]
    flops = facets * 2 * 2 * 512 * 512 * 256
    return pl.pallas_call(
        contribution_kernel,
        out_shape=jax.ShapeDtypeStruct((facets, 2 * SUB, SUB), jnp.bfloat16),
        grid_spec=pltpu.PrefetchScalarGridSpec(
            num_scalar_prefetch=1,
            grid=(facets,),
            in_specs=[
                pl.BlockSpec((1, 2, rows, cols), lambda t, place: (0, 0, 0, 0)),
                pl.BlockSpec((1, 2, SUB, MC), lambda t, place: (place[0], 0, 0, 0)),
                pl.BlockSpec((1, 2, MC, SUB), lambda t, place: (place[1], 0, 0, 0)),
            ],
            out_specs=pl.BlockSpec((1, 2 * SUB, SUB), lambda t, place: (t, 0, 0)),
            scratch_shapes=[
                pltpu.VMEM((2, rows, cols - STEP), jnp.bfloat16),
                pltpu.VMEM((2 * SUB, 2 * MC), jnp.bfloat16),
                pltpu.VMEM((2 * MC, 2 * SUB), jnp.bfloat16),
            ],
        ),
        compiler_params=pltpu.CompilerParams(vmem_limit_bytes=32 * MIB),
        cost_estimate=pl.CostEstimate(
            flops=flops, bytes_accessed=8 * MIB, transcendentals=0
        ),
        name="facet_contributions",
    )(place, spec, tables, tables_t)


def weights_kernel(offsets, fractions, u_out, v_out):
    cells = lax.broadcasted_iota(jnp.int32, (SUB, BLOCK), 0).astype(jnp.float32)
    scale = -((9.0 / KS) ** 2) / math.log(2.0)
    for axis, out in enumerate((u_out, v_out)):
        first = offsets[0, axis : axis + 1, :].astype(jnp.float32)
        inside = jnp.abs(cells - (first + 0.5 * (KS - 1))) < 0.5 * KS
        distance = cells - (first + (fractions[0, axis : axis + 1, :] + (0.5 * KS - 1.0)))
        weights = jnp.exp2(distance * distance * scale - 1.0)
        out[...] = jnp.where(inside, weights, 0.0).astype(jnp.bfloat16)


def kernel_weights(offsets, fractions):
    slots = offsets.shape[2]
    block_in = pl.BlockSpec((1, 2, BLOCK), lambda b: (0, 0, b))
    block_out = pl.BlockSpec((SUB, BLOCK), lambda b: (0, b))
    shape = jax.ShapeDtypeStruct((SUB, slots), jnp.bfloat16)
    return pl.pallas_call(
        weights_kernel,
        out_shape=(shape, shape),
        grid=(slots // BLOCK,),
        in_specs=[block_in, block_in],
        out_specs=(block_out, block_out),
        compiler_params=pltpu.CompilerParams(vmem_limit_bytes=32 * MIB),
        cost_estimate=pl.CostEstimate(
            flops=20 * SUB * slots, bytes_accessed=4 * SUB * slots, transcendentals=2 * SUB * slots
        ),
        name="kernel_weights",
    )(offsets, fractions)


def residual_kernel(count, grid_in, u_in, v_in, observed, resid_out, grid_out, total):
    step = pl.program_id(0)

    @pl.when(step == 0)
    def _():
        total[...] = jnp.zeros_like(total)

    u_half = u_in[...]
    v_half = v_in[...]
    product = f32_dot(grid_in[0], v_half)
    u_wide = u_half.astype(jnp.float32)
    v_wide = v_half.astype(jnp.float32)
    slot = step * BLOCK + lax.broadcasted_iota(jnp.int32, (1, BLOCK), 1)
    live = slot < count[0]
    for part in range(2):
        model = jnp.sum(product[part * SUB : (part + 1) * SUB] * u_wide, axis=0, keepdims=True)
        resid = jnp.where(live, observed[0, part : part + 1, :] - model, 0.0)
        resid_out[0, part : part + 1, :] = resid
        weighted = (resid * v_wide).astype(jnp.bfloat16)
        total[part * SUB : (part + 1) * SUB] += lax.dot_general(
            u_half, weighted, (((1,), (1,)), ((), ())), preferred_element_type=jnp.float32
        )

    @pl.when(step == pl.num_programs(0) - 1)
    def _():
        grid_out[...] = total[...].astype(jnp.bfloat16)


def residuals(count, grid, u_weights, v_weights, observed):
    slots = observed.shape[2]
    vis_block = pl.BlockSpec((1, 2, BLOCK), lambda b, count: (0, 0, b))
    weight_block = pl.BlockSpec((SUB, BLOCK), lambda b, count: (0, b))
    return pl.pallas_call(
        residual_kernel,
        out_shape=(
            jax.ShapeDtypeStruct(observed.shape, jnp.float32),
            jax.ShapeDtypeStruct((2 * SUB, SUB), jnp.bfloat16),
        ),
        grid_spec=pltpu.PrefetchScalarGridSpec(
            num_scalar_prefetch=1,
            grid=(slots // BLOCK,),
            in_specs=[
                pl.BlockSpec((1, 2 * SUB, SUB), lambda b, count: (0, 0, 0)),
                weight_block,
                weight_block,
                vis_block,
            ],
            out_specs=(vis_block, pl.BlockSpec((2 * SUB, SUB), lambda b, count: (0, 0))),
            scratch_shapes=[pltpu.VMEM((2 * SUB, SUB), jnp.float32)],
        ),
        compiler_params=pltpu.CompilerParams(vmem_limit_bytes=32 * MIB),
        cost_estimate=pl.CostEstimate(
            flops=4 * 512 * 256 * slots, bytes_accessed=4 * SUB * slots, transcendentals=0
        ),
        name="residuals",
    )(count, grid, u_weights, v_weights, observed)


def adjoint_kernel(place, grids, left, right, out, plane, left_mat, right_mat):
    step = pl.program_id(0)
    bands, _, band_rows, cols = out.shape

    @pl.when(step == 0)
    def _():
        plane[...] = jnp.zeros_like(plane)
        a_re, a_im = left[0, 0], left[0, 1]
        left_mat[...] = stacked(side_by_side(a_re, a_im), side_by_side(-a_im, a_re))
        b_re, b_im = right[0, 0], right[0, 1]
        right_mat[...] = stacked(side_by_side(b_re, -b_im), side_by_side(b_im, b_re))

    top = pl.multiple_of(place[2 + 2 * step], STEP)
    left_step = place[3 + 2 * step]
    col = pl.multiple_of(left_step // 2 * LANES, LANES)
    half = f32_dot(left_mat[...], grids[0]).astype(jnp.bfloat16)
    whole = f32_dot(side_by_side(half[:MC], half[MC:]), right_mat[...])

    @pl.when(left_step % 2 == 0)
    def _():
        for part in range(2):
            plane[part, pl.ds(top, MC), pl.ds(col, MC)] += whole[:, part * MC : (part + 1) * MC]

    @pl.when(left_step % 2 == 1)
    def _():
        edge = jnp.zeros((MC, STEP), jnp.float32)
        for part in range(2):
            plane[part, pl.ds(top, MC), pl.ds(col, MC + LANES)] += jnp.concatenate(
                [edge, whole[:, part * MC : (part + 1) * MC], edge], axis=1
            )

    @pl.when(step == pl.num_programs(0) - 1)
    def _():
        for band in range(bands):
            for part in range(2):
                out[band, part] = plane[
                    part, band * band_rows : (band + 1) * band_rows, :cols
                ].astype(jnp.bfloat16)


def adjoint_plane(place, grids, tables, tables_t, bands, rows, cols):
    facets = tables.shape[0]
    flops = facets * 2 * 2 * 512 * 512 * 256
    wide = (cols + LANES - 1) // LANES * LANES
    return pl.pallas_call(
        adjoint_kernel,
        out_shape=jax.ShapeDtypeStruct((bands, 2, rows // bands, cols), jnp.bfloat16),
        grid_spec=pltpu.PrefetchScalarGridSpec(
            num_scalar_prefetch=1,
            grid=(facets,),
            in_specs=[
                pl.BlockSpec((1, 2 * SUB, SUB), lambda t, place: (t, 0, 0)),
                pl.BlockSpec((1, 2, MC, SUB), lambda t, place: (place[0], 0, 0, 0)),
                pl.BlockSpec((1, 2, SUB, MC), lambda t, place: (place[1], 0, 0, 0)),
            ],
            out_specs=pl.BlockSpec((bands, 2, rows // bands, cols), lambda t, place: (0, 0, 0, 0)),
            scratch_shapes=[
                pltpu.VMEM((2, rows, wide), jnp.float32),
                pltpu.VMEM((2 * MC, 2 * SUB), jnp.bfloat16),
                pltpu.VMEM((2 * SUB, 2 * MC), jnp.bfloat16),
            ],
        ),
        compiler_params=pltpu.CompilerParams(vmem_limit_bytes=40 * MIB),
        cost_estimate=pl.CostEstimate(
            flops=flops, bytes_accessed=8 * MIB, transcendentals=0
        ),
        name="adjoint_plane",
    )(place, grids, tables_t, tables)


def places(worker, facets, subs):
    facet = lax.axis_index("facet")
    rows = jnp.arange(facets, dtype=jnp.int32) * subs + lax.axis_index("sub")
    ids = jnp.arange(worker.shape[0], dtype=jnp.int32)
    held = jnp.sum(jnp.where(worker[None, :] == rows[:, None], ids[None, :], 0), axis=1)
    head = jnp.stack([facet, jnp.mod(5 * facet + 3, facets)]).astype(jnp.int32)
    corners = jnp.stack([held // subs * STEP, held % subs], axis=1)
    return jnp.concatenate([head, corners.reshape(-1)])


def on_device(facet_spec, worker_of_subgrid, vis_count, bin_offsets, bin_fractions, observed):
    facets = lax.axis_size("facet")
    subs = lax.axis_size("sub")
    rows, cols = facet_spec.shape[2:]
    table = phase_tables(facets)
    tables = jnp.asarray(table)
    tables_t = jnp.asarray(np.ascontiguousarray(table.transpose(0, 1, 3, 2)))
    place = places(worker_of_subgrid, facets, subs)
    parts = contributions(place, facet_spec, tables, tables_t)
    u_weights, v_weights = kernel_weights(bin_offsets, bin_fractions)
    grid = lax.psum_scatter(parts, "facet", scatter_dimension=0, tiled=True)
    residual, resid_grid = residuals(vis_count, grid, u_weights, v_weights, observed)
    grids = lax.all_gather(resid_grid, "facet", axis=0, tiled=False)
    plane = adjoint_plane(place, grids, tables, tables_t, subs, rows, cols)
    update = lax.psum_scatter(plane, "sub", scatter_dimension=0, tiled=True)
    return (residual, update.astype(jnp.float32))


def solution(mesh):
    placed = (
        P("facet", None, None, None),
        P(),
        P(("facet", "sub")),
        P(("facet", "sub"), None, None),
        P(("facet", "sub"), None, None),
        P(("facet", "sub"), None, None),
    )
    return jax.shard_map(
        on_device,
        mesh=mesh,
        in_specs=placed,
        out_specs=(P(("facet", "sub"), None, None), P("facet", None, "sub", None)),
        check_vma=False,
    )
```

time: 975 us -> 249 us (0.26)
  matrix products: 379 us -> 0 us
  local copies, waits for them, and re-layouts: 233 us -> 30.2 us
  other arithmetic: 105 us -> 2.95 us
  loops' own time: 59.6 us -> 0 us
  Pallas kernels: 0 us -> 43.8 us
  blocking collectives: 33 us -> 0 us
  waiting for transfers between devices: 129 us -> 157 us
  starting transfers between devices: 12.4 us -> 0.12 us
    dot_general x288 -> x0, matrix products: 379 us -> none  [the longest x64 91.7 us: pair_dot(): jnp.dot(first_pair[1], second_pair[1], preferred_element_type=jnp.float32)]
    dynamic_update_slice x16 -> x0, local copies, waits for them, and re-layouts: 100 us -> none  [add_window(): lax.dynamic_update_slice(plane, current + window.astype(jnp.float32), (an...]
    all_to_all x2 -> x0, waiting for transfers between devices: 74.8 us -> none  [the longest x1 50.1 us: on_device(): lax.all_to_all(windows, 'facet', split_axis=0, concat_axis=0, tiled=True)]
    unnamed x1 -> x4, waiting for transfers between devices: 0.02 us -> 68.8 us
    gather x49 -> x0, local copies, waits for them, and re-layouts: 59.9 us -> none
    another operation x5 -> x0, loops' own time: 59.6 us -> none  [the longest x1 36.9 us: on_device(): plane = lax.fori_loop(0, pos_u, place_one, plane)]
    all_gather x0 -> x1, waiting for transfers between devices: none -> 51.2 us  [on_device(): grids = lax.all_gather(resid_grid, 'facet', axis=0, tiled=False)]
    pallas_call x0 -> x4, Pallas kernels: none -> 43.8 us  [the longest x1 16 us: adjoint_plane(): pl.pallas_call(adjoint_kernel, out_shape=jax.ShapeDtypeStruct((bands, 2,...]
  transfers between devices with their start and end apart: 3 -> 3, of which waited for: 3 -> 3; matrix products, arithmetic and copies ran while one was open for 0% -> 0% of each run, Pallas kernels for 0% -> 2%
where the time goes in v1:
time: 249 us; the launch traced here: 248 us
  waiting for transfers between devices  157 us (63%)
  Pallas kernels  43.8 us (18%)
  local copies, waits for them, and re-layouts  30.2 us (12%)
  between operations  14.5 us (6%)
  other arithmetic  2.95 us (1%)
    unnamed x4, waiting for transfers between devices  68.8 us
    all_gather x1, waiting for transfers between devices, on_device(): grids = lax.all_gather(resid_grid, 'facet', axis=0, tiled=False)  51.2 us
    reduce_scatter x1, waiting for transfers between devices, on_device(): update = lax.psum_scatter(plane, 'sub', scatter_dimension=0, tiled=True)  36.7 us
    unnamed x31, local copies, waits for them, and re-layouts  30.1 us
    pallas_call x1, Pallas kernels, adjoint_plane(): pl.pallas_call(adjoint_kernel, out_shape=jax.ShapeDtypeStruct((bands, 2,...  16 us
    pallas_call x1, Pallas kernels, contributions(): pl.pallas_call(contribution_kernel, out_shape=jax.ShapeDtypeStruct((facet...  12.9 us
    pallas_call x1, Pallas kernels, residuals(): pl.pallas_call(residual_kernel, out_shape=(jax.ShapeDtypeStruct(observed....  8.99 us
    pallas_call x1, Pallas kernels, kernel_weights(): pl.pallas_call(weights_kernel, out_shape=(shape, shape), grid=(slots // B...  5.86 us
  transfers between devices with their start and end apart: 3, of which 3 were waited for; matrix products, arithmetic and copies ran while one was open for 0% of the time, Pallas kernels for 2%

profile of v1, /device:TPU:24, one launch (start us, length us, event | category | flops | bytes accessed | tf_op | source)
XLA Modules:
  0.0 248.3 jit_solution(3932566661916256886)
XLA Ops:
  7.2 0.0 reduce-scatter.7.cloned.1.call-start
  7.2 0.8 select_reduce_fusion
  8.1 0.1 copy.16
  8.2 0.1 reshape.88
  8.3 6.1 %copy.17.spec = bf16[1,2,1216,704]{3,2,1,0:T(8,128)(2,1)} copy(bf16[1,2,1216,704]{2,3,1,0:T(8,128)(2,1)} %param.8) | data formatting | bytes 6848512 | tf_op args[0]
  14.4 0.1 pad_add_fusion.1.place
  14.5 0.0 copy-start
  14.5 2.2 copy-done
  16.7 0.0 copy-start.2
  16.7 2.2 copy-done.2
  18.9 0.0 copy-start.4
  18.9 2.1 copy-done.4
  20.9 12.9 %facet_contributions.1 = bf16[16,512,256]{2,1,0:T(8,128)(2,1)S(1)} custom-call(s32[34]{0:T(128)S(1)} %pad_add_fusion.1.place, bf16[1,2,1216,704]{3,2,1,0:T(8,128)(2,1)S(1)} %copy-done.4, bf16[16,2,256,256]{3,2,1,0:T(8,128)(2,1)S(1)} %copy-done.2, bf16[16,2,256,256]{3,2,1,0:T(8,128)(2,1)S(1)} %copy-done), custom_call_target="tpu_custom_call" | custom-call | flops 4294967296 | bytes 8388608 | tf_op jit(solution)/shard_map/facet_contributions/pallas_call | solution.py:91
  33.9 0.0 copy-start.3
  33.9 1.9 copy-done.3
  35.8 0.0 copy-start.8
  35.8 0.0 copy-start.9
  35.8 0.0 reduce-scatter.7.cloned.1.call-update
  35.8 0.0 copy-start.10
  35.9 0.0 all-gather.3.cloned.1.call-start
  36.6 0.1 copy-done.8
  36.7 0.0 copy-done.9
  36.7 5.9 %kernel_weights.1 = (bf16[256,8192]{1,0:T(8,128)(2,1)S(1)}, bf16[256,8192]{1,0:T(8,128)(2,1)S(1)}) custom-call(s32[1,2,8192]{2,1,0:T(2,128)S(1)} %copy-done.8, f32[1,2,8192]{2,1,0:T(2,128)S(1)} %copy-done.9), custom_call_target="tpu_custom_call" | custom-call | flops 41943040 | bytes 8388608 | tf_op jit(solution)/shard_map/kernel_weights/pallas_call | solution.py:133
  42.6 0.0 copy-start.11
  42.6 2.0 copy-done.11
  44.5 0.0 copy-start.13
  44.5 2.0 copy-done.13
  46.5 68.8 %reduce-scatter.7.cloned.1.call-done.grid_in = bf16[1,512,256]{2,1,0:T(8,128)(2,1)} async-done(((bf16[16,512,256]{2,1,0:T(8,128)(2,1)}), bf16[1,512,256]{2,1,0:T(8,128)(2,1)}) %reduce-scatter.7.cloned.1.call-update) | async-done | bytes 262160
  115.3 0.0 copy-done.10
  115.3 0.0 copy-start.7
  115.3 0.9 copy-done.7
  116.2 0.0 copy-start.12
  116.2 2.2 copy-done.12
  118.4 0.0 copy-start.14
  118.4 2.2 copy-done.14
  120.6 9.0 %residuals.1 = (f32[1,2,8192]{2,1,0:T(2,128)}, bf16[512,256]{1,0:T(8,128)(2,1)}) custom-call(s32[1]{0:T(128)S(6)} %copy.18.count, bf16[1,512,256]{2,1,0:T(8,128)(2,1)S(1)} %copy-done.7, bf16[256,8192]{1,0:T(8,128)(2,1)S(1)} %copy-done.12, bf16[256,8192]{1,0:T(8,128)(2,1)S(1)} %copy-done.14, f32[1,2,8192]{2,1,0:T(2,128)S(1)} %copy-done.10), custom_call_target="tpu_custom_call" | custom-call | flops 4294967296 | bytes 8388608 | tf_op jit(solution)/shard_map/residuals/pallas_call | solution.py:179
  129.6 0.0 all-gather.3.cloned.1.call-update
  129.6 0.0 reduce-scatter.5.cloned.1.call-start
  129.7 51.2 %all-gather.3.cloned.1.call-done = bf16[8192,256]{1,0:T(8,128)(2,1)} async-done(((bf16[512,256]{1,0:T(8,128)(2,1)}), bf16[8192,256]{1,0:T(8,128)(2,1)}) %all-gather.3.cloned.1.call-update) | async-done | bytes 4194320 | tf_op jit(solution)/shard_map/all_gather | solution.py:297
  180.8 0.0 copy-start.1
  180.9 2.2 copy-done.1
  183.0 0.0 copy-start.6
  183.0 2.2 copy-done.6
  185.2 16.0 %adjoint_plane.1 = bf16[8,2,152,704]{3,2,1,0:T(8,128)(2,1)S(1)} custom-call(s32[34]{0:T(128)S(1)} %pad_add_fusion.1.place, bf16[16,512,256]{2,1,0:T(8,128)(2,1)S(1)} %bitcast.21, bf16[16,2,256,256]{3,2,1,0:T(8,128)(2,1)S(1)} %copy-done.1, bf16[16,2,256,256]{3,2,1,0:T(8,128)(2,1)} %constant.60.clone.left.right), custom_call_target="tpu_custom_call" | custom-call | flops 4294967296 | bytes 8388608 | tf_op jit(solution)/shard_map/adjoint_plane/pallas_call | solution.py:249
  201.2 0.0 copy-start.5
  201.3 1.8 copy-done.5
  203.1 0.0 reduce-scatter.5.cloned.1.call-update
  203.1 36.7 %reduce-scatter.5.cloned.1.call-done = bf16[1,2,152,704]{3,2,1,0:T(8,128)(2,1)} async-done(((bf16[8,2,152,704]{3,2,1,0:T(8,128)(2,1)}), bf16[1,2,152,704]{3,2,1,0:T(8,128)(2,1)}) %reduce-scatter.5.cloned.1.call-update) | async-done | bytes 428048 | tf_op jit(solution)/shard_map/reduce_scatter | solution.py:299
  239.7 2.0 convert_element_type.3
  (3 shorter events, 0.0 us)
Async XLA Ops:
  7.2 108.1 %reduce-scatter.7.cloned.1.call-start = ((), (), s32[]{:S(2)}) async-start(), calls=%async_computation.4 | async-start | bytes 4456448
  14.5 2.2 copy-start
  16.7 2.2 copy-start.2
  18.9 2.1 copy-start.4
  33.9 2.0 copy-start.3
  35.8 0.8 copy-start.8
  35.8 0.9 copy-start.9
  35.8 79.4 %copy-start.10 = (f32[1,2,8192]{2,1,0:T(2,128)S(1)}, f32[1,2,8192]{2,1,0:T(2,128)}, u32[]{:S(2)}) copy-start(f32[1,2,8192]{2,1,0:T(2,128)} %observed.1) | copy-start | bytes 196612
  35.9 145.0 %all-gather.3.cloned.1.call-start = ((), (), s32[]{:S(2)}) async-start(), calls=%async_computation.3 | async-start | bytes 4456448 | tf_op jit(solution)/shard_map/all_gather | solution.py:297
  42.6 2.0 copy-start.11
  44.5 2.0 copy-start.13
  115.3 1.0 copy-start.7
  116.2 2.2 copy-start.12
  118.4 2.2 copy-start.14
  129.6 110.1 %reduce-scatter.5.cloned.1.call-start = ((), (), s32[]{:S(2)}) async-start(), calls=%async_computation.2 | async-start | bytes 4202496 | tf_op jit(solution)/shard_map/reduce_scatter | solution.py:299
  180.8 2.2 copy-start.1
  183.0 2.2 copy-start.6
  201.2 1.8 copy-start.5
Sparse Core Ops, SparseCore 0:
  36.0 79.2 reduce-scatter.6
  129.7 51.0 all-gather.2
  203.2 36.4 reduce-scatter.4

commit v2 on v1

v2 whole, which is shorter than its diff:
```python
import math

import jax
import jax.numpy as jnp
import numpy as np
from jax import lax
from jax.experimental import pallas as pl
from jax.experimental.pallas import tpu as pltpu
from jax.sharding import PartitionSpec as P

SUB = 256
MC = 256
STEP = 64
KS = 8
BLOCK = 1024
LANES = 128
HALF = SUB // 2
RING = 4
NEAR = (0, 1, RING - 1, 2)
MIB = 1 << 20
VMEM_LIMIT = 58 * MIB


def phase_tables(facets):
    sub_part = (np.arange(SUB) - SUB // 2)[:, None]
    win_part = (np.arange(MC) - MC // 2)[None, :]
    modulus = SUB * facets
    tables = []
    for offset in range(facets):
        residue = np.mod(sub_part * win_part * facets + sub_part * offset, modulus)
        angles = residue.astype(np.float32).astype(np.float64) * (2.0 * math.pi / modulus)
        factor = MC ** (-0.5)
        tables.append(np.stack([np.cos(angles) * factor, np.sin(angles) * factor]))
    return np.stack(tables).astype(jnp.bfloat16)


def side_by_side(*blocks):
    return jnp.concatenate(blocks, axis=1)


def stacked(*blocks):
    return jnp.concatenate(blocks, axis=0)


def f32_dot(left, right):
    return jnp.dot(left, right, preferred_element_type=jnp.float32)


def contribution_kernel(place, spec, left, right, *rest):
    a_own, a_up, a_down, a_far_up, a_far_down = rest[:5]
    b_own, b_up, b_down, b_far_up, b_far_down = rest[5:10]
    windows, left_mat, right_mat = rest[10:]
    step = pl.program_id(0)
    reach = windows.shape[3]

    @pl.when(step == 0)
    def _():
        for part in range(2):
            windows[0, part] = spec[0, part, :, :reach]
            windows[1, part] = spec[0, part, :, STEP : STEP + reach]
        a_re, a_im = left[0, 0], left[0, 1]
        right_mat[...] = stacked(side_by_side(a_re, a_im), side_by_side(-a_im, a_re))
        b_re, b_im = right[0, 0], right[0, 1]
        left_mat[...] = stacked(side_by_side(b_re, -b_im), side_by_side(b_im, b_re))

    results = []
    for other in range(RING):
        target = step * RING + other
        row_step = place[2 + 2 * target]
        first_col = pl.multiple_of(place[3 + 2 * target], STEP)
        odd = row_step % 2
        first_row = pl.multiple_of(row_step // 2 * LANES, LANES)
        window = side_by_side(
            windows[odd, 0, pl.ds(first_col, MC), pl.ds(first_row, MC)],
            windows[odd, 1, pl.ds(first_col, MC), pl.ds(first_row, MC)],
        )
        half = f32_dot(window, right_mat[...]).astype(jnp.bfloat16)
        whole = f32_dot(left_mat[...], stacked(half[:, :SUB], half[:, SUB:]))
        results.append(whole.astype(jnp.bfloat16))

    for near, out in ((0, a_own), (1, a_up), (2, a_down)):

        @pl.when(step == near)
        def _():
            for other in range(RING):
                out[other] = results[other][:SUB]

    @pl.when(step == 3)
    def _():
        for other in range(RING):
            a_far_up[other] = results[other][:HALF]
            a_far_down[other] = results[other][HALF:SUB]

    b_own[0] = results[0][SUB:]
    b_up[0] = results[1][SUB:]
    b_down[0] = results[2][SUB:]
    b_far_up[0] = results[3][SUB : SUB + HALF]
    b_far_down[0] = results[3][SUB + HALF :]


def contributions(place, spec, tables, tables_t):
    facets = tables.shape[0]
    cols, rows = spec.shape[2:]
    flops = facets * 2 * 2 * 512 * 512 * 256
    full = jax.ShapeDtypeStruct((RING, SUB, SUB), jnp.bfloat16)
    part = jax.ShapeDtypeStruct((RING, HALF, SUB), jnp.bfloat16)
    shapes = (full, full, full, part, part)
    whole = tuple(pl.BlockSpec(s.shape, lambda t, place: (0, 0, 0)) for s in shapes)
    stepped = tuple(pl.BlockSpec((1,) + s.shape[1:], lambda t, place: (t, 0, 0)) for s in shapes)
    return pl.pallas_call(
        contribution_kernel,
        out_shape=shapes + shapes,
        grid_spec=pltpu.PrefetchScalarGridSpec(
            num_scalar_prefetch=1,
            grid=(RING,),
            in_specs=[
                pl.BlockSpec((1, 2, cols, rows), lambda t, place: (0, 0, 0, 0)),
                pl.BlockSpec((1, 2, MC, SUB), lambda t, place: (place[0], 0, 0, 0)),
                pl.BlockSpec((1, 2, SUB, MC), lambda t, place: (place[1], 0, 0, 0)),
            ],
            out_specs=whole + stepped,
            scratch_shapes=[
                pltpu.VMEM((2, 2, cols, rows - STEP), jnp.bfloat16),
                pltpu.VMEM((2 * MC, 2 * SUB), jnp.bfloat16),
                pltpu.VMEM((2 * SUB, 2 * MC), jnp.bfloat16),
            ],
        ),
        compiler_params=pltpu.CompilerParams(vmem_limit_bytes=VMEM_LIMIT),
        cost_estimate=pl.CostEstimate(flops=flops, bytes_accessed=8 * MIB, transcendentals=0),
        name="facet_contributions",
    )(place, spec, tables_t, tables)


def weights_kernel(offsets, fractions, u_out, v_out):
    cells = lax.broadcasted_iota(jnp.int32, (SUB, BLOCK), 0).astype(jnp.float32)
    scale = -((9.0 / KS) ** 2) / math.log(2.0)
    for axis, out in enumerate((u_out, v_out)):
        first = offsets[0, axis : axis + 1, :].astype(jnp.float32)
        inside = jnp.abs(cells - (first + 0.5 * (KS - 1))) < 0.5 * KS
        distance = cells - (first + (fractions[0, axis : axis + 1, :] + (0.5 * KS - 1.0)))
        weights = jnp.exp2(distance * distance * scale - 1.0)
        out[...] = jnp.where(inside, weights, 0.0).astype(jnp.bfloat16)


def kernel_weights(offsets, fractions):
    slots = offsets.shape[2]
    block_in = pl.BlockSpec((1, 2, BLOCK), lambda b: (0, 0, b))
    block_out = pl.BlockSpec((SUB, BLOCK), lambda b: (0, b))
    shape = jax.ShapeDtypeStruct((SUB, slots), jnp.bfloat16)
    return pl.pallas_call(
        weights_kernel,
        out_shape=(shape, shape),
        grid=(slots // BLOCK,),
        in_specs=[block_in, block_in],
        out_specs=(block_out, block_out),
        compiler_params=pltpu.CompilerParams(vmem_limit_bytes=VMEM_LIMIT),
        cost_estimate=pl.CostEstimate(
            flops=20 * SUB * slots, bytes_accessed=4 * SUB * slots, transcendentals=2 * SUB * slots
        ),
        name="kernel_weights",
    )(offsets, fractions)


def residual_kernel(count, *refs):
    grid_parts = refs[:6]
    u_in, v_in, observed, resid_out, re_out, im_out, grid, total = refs[6:]
    step = pl.program_id(0)

    @pl.when(step == 0)
    def _():
        total[...] = jnp.zeros_like(total)
        for part in range(2):
            own, low, high = (ref[0].astype(jnp.float32) for ref in grid_parts[3 * part : 3 * part + 3])
            grid[part * SUB : (part + 1) * SUB] = (own + low + high).astype(jnp.bfloat16)

    u_half = u_in[...]
    v_wide = v_in[...].astype(jnp.float32)
    product = f32_dot(grid[...], u_half)
    slot = step * BLOCK + lax.broadcasted_iota(jnp.int32, (1, BLOCK), 1)
    live = slot < count[0]
    for part in range(2):
        model = jnp.sum(product[part * SUB : (part + 1) * SUB] * v_wide, axis=0, keepdims=True)
        resid = jnp.where(live, observed[0, part : part + 1, :] - model, 0.0)
        resid_out[0, part : part + 1, :] = resid
        weighted = (resid * v_wide).astype(jnp.bfloat16)
        total[part * SUB : (part + 1) * SUB] += lax.dot_general(
            u_half, weighted, (((1,), (1,)), ((), ())), preferred_element_type=jnp.float32
        )

    @pl.when(step == pl.num_programs(0) - 1)
    def _():
        re_out[0] = total[:SUB].astype(jnp.bfloat16)
        im_out[0] = total[SUB:].astype(jnp.bfloat16)


def residuals(count, grid_parts, u_weights, v_weights, observed):
    slots = observed.shape[2]
    vis_block = pl.BlockSpec((1, 2, BLOCK), lambda b, count: (0, 0, b))
    weight_block = pl.BlockSpec((SUB, BLOCK), lambda b, count: (0, b))
    whole = pl.BlockSpec((1, SUB, SUB), lambda b, count: (0, 0, 0))
    half = jax.ShapeDtypeStruct((1, SUB, SUB), jnp.bfloat16)
    return pl.pallas_call(
        residual_kernel,
        out_shape=(jax.ShapeDtypeStruct(observed.shape, jnp.float32), half, half),
        grid_spec=pltpu.PrefetchScalarGridSpec(
            num_scalar_prefetch=1,
            grid=(slots // BLOCK,),
            in_specs=[whole] * 6 + [weight_block, weight_block, vis_block],
            out_specs=(vis_block, whole, whole),
            scratch_shapes=[
                pltpu.VMEM((2 * SUB, SUB), jnp.bfloat16),
                pltpu.VMEM((2 * SUB, SUB), jnp.float32),
            ],
        ),
        compiler_params=pltpu.CompilerParams(vmem_limit_bytes=VMEM_LIMIT),
        cost_estimate=pl.CostEstimate(
            flops=4 * 512 * 256 * slots, bytes_accessed=4 * SUB * slots, transcendentals=0
        ),
        name="residuals",
    )(count, *grid_parts, u_weights, v_weights, observed)


def adjoint_kernel(place, *refs):
    re_own, re_high, re_low, re_far_low, re_far_high = refs[:5]
    im_own, im_high, im_low, im_far_low, im_far_high = refs[5:10]
    left, right, kept, given, plane, im_all, left_mat, right_mat = refs[10:]
    step = pl.program_id(0)
    band_rows, cols = kept.shape[2:]

    @pl.when(step == 0)
    def _():
        plane[...] = jnp.zeros_like(plane)
        im_all[0] = im_own[...]
        im_all[1] = im_high[...]
        im_all[2] = im_low[...]
        im_all[3, :, :HALF] = im_far_low[...]
        im_all[3, :, HALF:] = im_far_high[...]
        a_re, a_im = left[0, 0], left[0, 1]
        left_mat[...] = stacked(side_by_side(a_re, a_im), side_by_side(-a_im, a_re))
        b_re, b_im = right[0, 0], right[0, 1]
        right_mat[...] = stacked(side_by_side(b_re, -b_im), side_by_side(b_im, b_re))

    re_blocks = (re_own[0], re_high[0], re_low[0], stacked(re_far_low[0], re_far_high[0]))
    edge = jnp.zeros((MC, LANES), jnp.float32)
    for other in range(RING):
        source = step * RING + other
        top = pl.multiple_of(place[2 + 2 * source] * STEP, STEP)
        left_col = place[3 + 2 * source]
        odd = left_col // STEP % 2
        col = pl.multiple_of(left_col // LANES * LANES, LANES)
        grid = stacked(re_blocks[other], im_all[step, other])
        half = f32_dot(left_mat[...], grid).astype(jnp.bfloat16)
        whole = f32_dot(side_by_side(half[:MC], half[MC:]), right_mat[...])
        for part in range(2):
            wide = side_by_side(whole[:, part * MC : (part + 1) * MC], edge)
            plane[part, pl.ds(top, MC), pl.ds(col, MC + LANES)] += pltpu.roll(wide, odd * STEP, 1)

    @pl.when(step == RING - 1)
    def _():
        for group, out in enumerate((kept, given)):
            for near in range(RING):
                band = place[2 + 2 * RING * RING + RING * group + near]
                first = pl.multiple_of(band * band_rows, 8)
                for part in range(2):
                    rows = plane[part, pl.ds(first, band_rows), :]
                    out[near, part] = rows[:, :cols].astype(jnp.bfloat16)


def adjoint_plane(place, re_parts, im_parts, tables, tables_t, bands, rows, cols):
    facets = tables.shape[0]
    flops = facets * 2 * 2 * 512 * 512 * 256
    wide = (cols + LANES - 1) // LANES * LANES
    band_shape = (RING, 2, rows // bands, cols)
    stepped = [pl.BlockSpec((1,) + x.shape[1:], lambda t, place: (t, 0, 0)) for x in re_parts]
    whole = [pl.BlockSpec(x.shape, lambda t, place: (0, 0, 0)) for x in im_parts]
    return pl.pallas_call(
        adjoint_kernel,
        out_shape=(jax.ShapeDtypeStruct(band_shape, jnp.bfloat16),) * 2,
        grid_spec=pltpu.PrefetchScalarGridSpec(
            num_scalar_prefetch=1,
            grid=(RING,),
            in_specs=stepped
            + whole
            + [
                pl.BlockSpec((1, 2, MC, SUB), lambda t, place: (place[0], 0, 0, 0)),
                pl.BlockSpec((1, 2, SUB, MC), lambda t, place: (place[1], 0, 0, 0)),
            ],
            out_specs=(pl.BlockSpec(band_shape, lambda t, place: (0, 0, 0, 0)),) * 2,
            scratch_shapes=[
                pltpu.VMEM((2, rows, wide), jnp.float32),
                pltpu.VMEM((RING, RING, SUB, SUB), jnp.bfloat16),
                pltpu.VMEM((2 * MC, 2 * SUB), jnp.bfloat16),
                pltpu.VMEM((2 * SUB, 2 * MC), jnp.bfloat16),
            ],
        ),
        compiler_params=pltpu.CompilerParams(vmem_limit_bytes=VMEM_LIMIT),
        cost_estimate=pl.CostEstimate(flops=flops, bytes_accessed=8 * MIB, transcendentals=0),
        name="adjoint_plane",
    )(place, *re_parts, *im_parts, tables_t, tables)


def along_x(shift):
    return "facet", [(i, (i // RING + shift) % RING * RING + i % RING) for i in range(RING * RING)]


def along_y(shift):
    return "facet", [(i, i // RING * RING + (i % RING + shift) % RING) for i in range(RING * RING)]


def along_z(shift):
    return "sub", [(i, (i // 2 + shift) % RING * 2 + i % 2) for i in range(2 * RING)]


def move(value, route):
    return lax.ppermute(value, *route)


def places(worker):
    facet = lax.axis_index("facet")
    sub = lax.axis_index("sub")
    subs = lax.axis_size("sub")
    near = jnp.asarray(NEAR, jnp.int32)
    x_near = (facet // RING + near) % RING
    y_near = (facet % RING + near) % RING
    rows = (x_near[:, None] * RING + y_near[None, :]).reshape(-1) * subs + sub
    ids = jnp.arange(worker.shape[0], dtype=jnp.int32)
    held = jnp.sum(jnp.where(worker[None, :] == rows[:, None], ids[None, :], 0), axis=1)
    head = jnp.stack([facet, jnp.mod(5 * facet + 3, RING * RING)]).astype(jnp.int32)
    corners = jnp.stack([held // subs, held % subs * STEP], axis=1).reshape(-1)
    z_near = (sub // 2 + near) % RING * 2
    bands = jnp.concatenate([z_near + sub % 2, z_near + 1 - sub % 2])
    return jnp.concatenate([head, corners, bands]).astype(jnp.int32)


def add_rows(block, first, second):
    upper, lower = block[:, :HALF], block[:, HALF:]
    if first is not None:
        upper = upper + first
    if second is not None:
        lower = lower + second
    return jnp.concatenate([upper, lower], axis=1)


def reduce_rings(pieces, routes):
    firsts = []
    for (_, _, _, far_up, far_down), route in zip(pieces, routes):
        firsts.append((move(far_up, route(1)), move(far_down, route(-1))))
    firsts = lax.optimization_barrier(firsts)
    seconds = []
    for (_, up, down, _, _), route, (low, high) in zip(pieces, routes, firsts):
        seconds.append((add_rows(up, low, None), add_rows(down, None, high)))
    arrived = [(move(up, route(1)), move(down, route(-1))) for (up, down), route in zip(seconds, routes)]
    arrived = lax.optimization_barrier(arrived)
    return [(piece[0],) + pair for piece, pair in zip(pieces, arrived)]


def gather_rings(blocks, routes):
    near = [(move(block, route(-1)), move(block, route(1))) for block, route in zip(blocks, routes)]
    near = lax.optimization_barrier(near)
    far = [
        (move(low[:, :HALF], route(1)), move(high[:, HALF:], route(-1)))
        for (high, low), route in zip(near, routes)
    ]
    far = lax.optimization_barrier(far)
    return [(block,) + pair + ends for block, pair, ends in zip(blocks, near, far)]


def in_one(parts):
    own, high, low, far_low, far_high = parts
    return jnp.concatenate([own, high, low, jnp.concatenate([far_low, far_high], axis=1)], axis=0)


def sum_rings(kept, given):
    swapped = lax.ppermute(given, "sub", [(i, i ^ 1) for i in range(2 * RING)])
    far = (kept[3] + swapped[3])
    low = move(far[0], along_z(1))
    high = move(far[1], along_z(-1))
    low, high = lax.optimization_barrier((low, high))
    up = jnp.stack([kept[1, 0] + swapped[1, 0] + low, kept[1, 1] + swapped[1, 1]])
    down = jnp.stack([kept[2, 0] + swapped[2, 0], kept[2, 1] + swapped[2, 1] + high])
    low, high = move(up, along_z(1)), move(down, along_z(-1))
    wide = [x.astype(jnp.float32) for x in (kept[0], swapped[0], low, high)]
    return wide[0] + wide[1] + wide[2] + wide[3]


def on_device(facet_spec, worker_of_subgrid, vis_count, bin_offsets, bin_fractions, observed):
    subs = lax.axis_size("sub")
    rows, cols = facet_spec.shape[2:]
    table = phase_tables(lax.axis_size("facet"))
    tables = jnp.asarray(table)
    tables_t = jnp.asarray(np.ascontiguousarray(table.transpose(0, 1, 3, 2)))
    routes = (along_x, along_y)
    place = places(worker_of_subgrid)
    outs = contributions(place, jnp.swapaxes(facet_spec, 2, 3), tables, tables_t)
    u_weights, v_weights = kernel_weights(bin_offsets, bin_fractions)
    sums = reduce_rings((outs[:5], outs[5:]), routes)
    again = []
    for own, low, high in sums:
        total = own.astype(jnp.float32) + low.astype(jnp.float32) + high.astype(jnp.float32)
        total = total.astype(jnp.bfloat16)
        again.append(
            (total[:1], total[1:2], total[2:3], total[3:4, :HALF], total[3:4, HALF:])
        )
    sums = reduce_rings(again, routes[::-1])
    residual, re_part, im_part = residuals(
        vis_count, sums[0] + sums[1], u_weights, v_weights, observed
    )
    gathered = gather_rings((re_part, im_part), routes)
    gathered = gather_rings([in_one(parts) for parts in gathered], routes[::-1])
    kept, given = adjoint_plane(
        place, gathered[0], gathered[1], tables, tables_t, subs, rows, cols
    )
    update = sum_rings(kept, given)
    return (residual, update[None])


def solution(mesh):
    placed = (
        P("facet", None, None, None),
        P(),
        P(("facet", "sub")),
        P(("facet", "sub"), None, None),
        P(("facet", "sub"), None, None),
        P(("facet", "sub"), None, None),
    )
    return jax.shard_map(
        on_device,
        mesh=mesh,
        in_specs=placed,
        out_specs=(P(("facet", "sub"), None, None), P("facet", None, "sub", None)),
        check_vma=False,
    )
```

time: 249 us -> 181 us (0.73)
  waiting for transfers between devices: 157 us -> 69.7 us
  starting transfers between devices: 0.12 us -> 53.1 us
  local copies, waits for them, and re-layouts: 30.2 us -> 4.26 us
  between operations: 14.5 us -> 1.76 us
  other arithmetic: 2.95 us -> 7.81 us
    ppermute x0 -> x37, waiting for transfers between devices: none -> 69.7 us  [the longest x36 65.7 us: move(): return lax.ppermute(value, *route)]
    unnamed x4 -> x0, waiting for transfers between devices: 68.8 us -> none
    ppermute x0 -> x37, starting transfers between devices: none -> 53.1 us  [the longest x36 53 us: move(): return lax.ppermute(value, *route)]
    all_gather x1 -> x0, waiting for transfers between devices: 51.2 us -> none  [on_device(): grids = lax.all_gather(resid_grid, 'facet', axis=0, tiled=False)]
    reduce_scatter x1 -> x0, waiting for transfers between devices: 36.7 us -> none  [on_device(): update = lax.psum_scatter(plane, 'sub', scatter_dimension=0, tiled=True)]
    unnamed x31 -> x40, local copies, waits for them, and re-layouts: 30.1 us -> 1.95 us
    pallas_call x2, Pallas kernels: 28.9 us -> 24.8 us  [the longest x1 12.7 us: contributions(): pl.pallas_call(contribution_kernel, out_shape=shapes + shapes, grid_spec=...]
  transfers between devices with their start and end apart: 3 -> 37, of which waited for: 3 -> 23; matrix products, arithmetic and copies ran while one was open for 0% -> 1% of each run, Pallas kernels for 2% -> 4%
where the time goes in v2:
time: 181 us; the launch traced here: 180 us
  waiting for transfers between devices  69.7 us (39%)
  starting transfers between devices  53.1 us (29%)
  Pallas kernels  43.3 us (24%)
  other arithmetic  7.81 us (4%)
  local copies, waits for them, and re-layouts  4.26 us (2%)
    ppermute x36, waiting for transfers between devices, move(): return lax.ppermute(value, *route)  65.7 us
    ppermute x36, starting transfers between devices, move(): return lax.ppermute(value, *route)  53 us
    pallas_call x1, Pallas kernels, contributions(): pl.pallas_call(contribution_kernel, out_shape=shapes + shapes, grid_spec=...  12.7 us
    pallas_call x1, Pallas kernels, adjoint_plane(): pl.pallas_call(adjoint_kernel, out_shape=(jax.ShapeDtypeStruct(band_shape...  12.1 us
    pallas_call x1, Pallas kernels, residuals(): pl.pallas_call(residual_kernel, out_shape=(jax.ShapeDtypeStruct(observed....  10.9 us
    pallas_call x1, Pallas kernels, kernel_weights(): pl.pallas_call(weights_kernel, out_shape=(shape, shape), grid=(slots // B...  7.5 us
    ppermute x1, waiting for transfers between devices, sum_rings(): swapped = lax.ppermute(given, 'sub', [(i, i ^ 1) for i in range(2 * RING)])  4.03 us
  transfers between devices with their start and end apart: 37, of which 23 were waited for; matrix products, arithmetic and copies ran while one was open for 1% of the time, Pallas kernels for 4%

profile of v2, /device:TPU:24, one launch (start us, length us, event | category | flops | bytes accessed | tf_op | source)
XLA Modules:
  0.0 179.9 jit_solution(7132178612285917384)
XLA Ops:
  0.7 0.7 add_subtract_fusion
  1.5 0.8 select_reduce_fusion
  2.6 0.6 concatenate.39.place
  3.1 12.7 %facet_contributions.1 = (bf16[4,256,256]{2,1,0:T(8,128)(2,1)}, bf16[4,256,256]{2,1,0:T(8,128)(2,1)}, bf16[4,256,256]{2,1,0:T(8,128)(2,1)}, bf16[4,128,256]{2,1,...) custom-call(s32[42]{0:T(128)} %concatenate.39.place, ...), custom_call_target="tpu_custom_call" | custom-call | flops 4294967296 | bytes 8388608 | tf_op jit(solution)/shard_map/facet_contributions/pallas_call | solution.py:110
  15.8 1.6 collective-permute-start
  17.4 1.7 collective-permute-start.1
  19.3 1.9 %collective-permute-start.3 = (bf16[4,128,256]{2,1,0:T(8,128)(2,1)}, bf16[4,128,256]{2,1,0:T(8,128)(2,1)S(1)}, u32[]{:S(2)}, u32[]{:S(2)}) collective-permute-start(bf16[4,128,256]{2,1,0:T(8,128)(2,1)} %get-tuple-element.58), channel_id=1, source_target_pairs={{0,24},{8,0},{16,8},{24,16},{32,56},{40,32},{48,40},{56,48},{64,88... | collective-permute-start | bytes 786440 | tf_op jit(solution)/shard_map/ppermute | solution.py:315
  21.2 4.2 %collective-permute-done = bf16[4,128,256]{2,1,0:T(8,128)(2,1)S(1)} collective-permute-done((bf16[4,128,256]{2,1,0:T(8,128)(2,1)}, bf16[4,128,256]{2,1,0:T(8,128)(2,1)S(1)}, u32[]{:S(2)}, u32[]{:S(2)}) %collective-permute-start) | collective-permute-done | bytes 262176 | tf_op jit(solution)/shard_map/ppermute | solution.py:315
  25.3 1.5 collective-permute-done.2
  26.8 1.2 collective-permute-done.3
  28.0 1.1 fusion.21
  29.1 0.6 collective-permute-start.7
  29.8 2.8 %collective-permute-start.6 = (bf16[4,256,256]{2,1,0:T(8,128)(2,1)S(1)}, bf16[4,256,256]{2,1,0:T(8,128)(2,1)S(1)}, u32[]{:S(2)}, u32[]{:S(2)}) collective-permute-start(bf16[4,256,256]{2,1,0:T(8,128)(2,1)S(1)} %pad_maximum_fusion.2), channel_id=1, source_target_pairs={{0,8},{8,16},{16,24},{24,0},{32,40},{40,48},{48,56},{56,32},{64,72... | collective-permute-start | bytes 1572872 | tf_op jit(solution)/shard_map/ppermute | solution.py:315
  32.7 1.6 collective-permute-start.5
  34.4 0.5 collective-permute-start.4
  35.0 7.4 %collective-permute-done.7 = bf16[4,256,256]{2,1,0:T(8,128)(2,1)S(1)} collective-permute-done((bf16[4,256,256]{2,1,0:T(8,128)(2,1)S(1)}, bf16[4,256,256]{2,1,0:T(8,128)(2,1)S(1)}, u32[]{:S(2)}, u32[]{:S(2)}) %collective-permute-start.7) | collective-permute-done | bytes 524320 | tf_op jit(solution)/shard_map/ppermute | solution.py:315
  42.4 1.8 %collective-permute-done.5 = bf16[4,256,256]{2,1,0:T(8,128)(2,1)S(1)} collective-permute-done((bf16[4,256,256]{2,1,0:T(8,128)(2,1)S(1)}, bf16[4,256,256]{2,1,0:T(8,128)(2,1)S(1)}, u32[]{:S(2)}, u32[]{:S(2)}) %collective-permute-start.5) | collective-permute-done | bytes 524320 | tf_op jit(solution)/shard_map/ppermute | solution.py:315
  44.2 2.6 %collective-permute-done.4 = bf16[4,256,256]{2,1,0:T(8,128)(2,1)S(1)} collective-permute-done((bf16[4,256,256]{2,1,0:T(8,128)(2,1)S(1)}, bf16[4,256,256]{2,1,0:T(8,128)(2,1)S(1)}, u32[]{:S(2)}, u32[]{:S(2)}) %collective-permute-start.4) | collective-permute-done | bytes 524320 | tf_op jit(solution)/shard_map/ppermute | solution.py:315
  46.8 0.4 add_convert_fusion
  47.4 1.9 %collective-permute-start.10 = (bf16[1,128,256]{2,1,0:T(8,128)(2,1)S(1)}, bf16[1,128,256]{2,1,0:T(8,128)(2,1)S(1)}, u32[]{:S(2)}, u32[]{:S(2)}) collective-permute-start(bf16[1,128,256]{2,1,0:T(8,128)(2,1)S(1)} %get-tuple-element.119), channel_id=1, source_target_pairs={{0,32},{8,40},{16,48},{24,56},{32,64},{40,72},{48,80},{56,88},{64,... | collective-permute-start | bytes 196616 | tf_op jit(solution)/shard_map/ppermute | solution.py:315
  49.4 3.2 %collective-permute-start.8 = (bf16[1,128,256]{2,1,0:T(8,128)(2,1)S(1)}, bf16[1,128,256]{2,1,0:T(8,128)(2,1)S(1)}, u32[]{:S(2)}, u32[]{:S(2)}) collective-permute-start(bf16[1,128,256]{2,1,0:T(8,128)(2,1)S(1)} %get-tuple-element.121), channel_id=1, source_target_pairs={{0,8},{8,16},{16,24},{24,0},{32,40},{40,48},{48,56},{56,32},{64,72... | collective-permute-start | bytes 196616 | tf_op jit(solution)/shard_map/ppermute | solution.py:315
  52.7 0.3 collective-permute-done.10
  52.9 2.0 %collective-permute-done.9 = bf16[1,128,256]{2,1,0:T(8,128)(2,1)S(1)} collective-permute-done((bf16[1,128,256]{2,1,0:T(8,128)(2,1)S(1)}, bf16[1,128,256]{2,1,0:T(8,128)(2,1)S(1)}, u32[]{:S(2)}, u32[]{:S(2)}) %collective-permute-start.9) | collective-permute-done | bytes 65568 | tf_op jit(solution)/shard_map/ppermute | solution.py:315
  55.3 3.8 %collective-permute-start.12 = (bf16[1,256,256]{2,1,0:T(8,128)(2,1)S(1)}, bf16[1,256,256]{2,1,0:T(8,128)(2,1)S(1)}, u32[]{:S(2)}, u32[]{:S(2)}) collective-permute-start(bf16[1,256,256]{2,1,0:T(8,128)(2,1)S(1)} %pad_maximum_fusion.6), channel_id=1, source_target_pairs={{0,8},{8,16},{16,24},{24,0},{32,40},{40,48},{48,56},{56,32},{64,72... | collective-permute-start | bytes 393224 | tf_op jit(solution)/shard_map/ppermute | solution.py:315
  59.2 3.3 %collective-permute-start.15 = (bf16[1,256,256]{2,1,0:T(8,128)(2,1)S(1)}, bf16[1,256,256]{2,1,0:T(8,128)(2,1)S(1)}, u32[]{:S(2)}, u32[]{:S(2)}) collective-permute-start(bf16[1,256,256]{2,1,0:T(8,128)(2,1)S(1)} %pad_maximum_fusion.9), channel_id=1, source_target_pairs={{0,96},{8,104},{16,112},{24,120},{32,0},{40,8},{48,16},{56,24},{64... | collective-permute-start | bytes 393224 | tf_op jit(solution)/shard_map/ppermute | solution.py:315
  63.1 7.5 %kernel_weights.1 = (bf16[256,8192]{1,0:T(8,128)(2,1)}, bf16[256,8192]{1,0:T(8,128)(2,1)}) custom-call(s32[1,2,8192]{2,1,0:T(2,128)} %offsets.1, f32[1,2,8192]{2,1,0:T(2,128)} %fractions.1), custom_call_target="tpu_custom_call" | custom-call | flops 41943040 | bytes 8388608 | tf_op jit(solution)/shard_map/kernel_weights/pallas_call | solution.py:150
  70.6 0.7 slice.203.refs_3_
  71.3 0.7 slice.190.refs_0_
  72.0 0.6 copy-done.16
  72.7 10.9 %residuals.1 = (f32[1,2,8192]{2,1,0:T(2,128)}, bf16[1,256,256]{2,1,0:T(8,128)(2,1)}, bf16[1,256,256]{2,1,0:T(8,128)(2,1)}) custom-call(s32[1]{0:T(128)S(6)} %copy.14.count, bf16[1,256,256]{2,1,0:T(8,128)(2,1)} %slice.190.refs_0_, bf16[1,256,256]{2,1,0:T(8,128)(2,1)} %copy-done.17, bf16[1,256,256]{2,1,0:T(8,128)(2,1)} %copy-done.18, ...), custom_call_target="tpu_custom_call" | custom-call | flops 4294967296 | bytes 8388608 | tf_op jit(solution)/shard_map/residuals/pallas_call | solution.py:202
  83.9 3.2 %collective-permute-start.16 = (bf16[1,256,256]{2,1,0:T(8,128)(2,1)}, bf16[1,256,256]{2,1,0:T(8,128)(2,1)S(1)}, u32[]{:S(2)}, u32[]{:S(2)}) collective-permute-start(bf16[1,256,256]{2,1,0:T(8,128)(2,1)} %get-tuple-element.82), channel_id=1, source_target_pairs={{0,96},{8,104},{16,112},{24,120},{32,0},{40,8},{48,16},{56,24},{64... | collective-permute-start | bytes 393224 | tf_op jit(solution)/shard_map/ppermute | solution.py:315
  87.1 3.2 %collective-permute-start.19 = (bf16[1,256,256]{2,1,0:T(8,128)(2,1)}, bf16[1,256,256]{2,1,0:T(8,128)(2,1)S(1)}, u32[]{:S(2)}, u32[]{:S(2)}) collective-permute-start(bf16[1,256,256]{2,1,0:T(8,128)(2,1)} %get-tuple-element.83), channel_id=1, source_target_pairs={{0,8},{8,16},{16,24},{24,0},{32,40},{40,48},{48,56},{56,32},{64,72... | collective-permute-start | bytes 393224 | tf_op jit(solution)/shard_map/ppermute | solution.py:315
  90.4 2.8 %collective-permute-done.19 = bf16[1,256,256]{2,1,0:T(8,128)(2,1)S(1)} collective-permute-done((bf16[1,256,256]{2,1,0:T(8,128)(2,1)}, bf16[1,256,256]{2,1,0:T(8,128)(2,1)S(1)}, u32[]{:S(2)}, u32[]{:S(2)}) %collective-permute-start.19) | collective-permute-done | bytes 131104 | tf_op jit(solution)/shard_map/ppermute | solution.py:315
  93.2 3.6 %collective-permute-done.18 = bf16[1,256,256]{2,1,0:T(8,128)(2,1)S(1)} collective-permute-done((bf16[1,256,256]{2,1,0:T(8,128)(2,1)}, bf16[1,256,256]{2,1,0:T(8,128)(2,1)S(1)}, u32[]{:S(2)}, u32[]{:S(2)}) %collective-permute-start.18) | collective-permute-done | bytes 131104 | tf_op jit(solution)/shard_map/ppermute | solution.py:315
  96.9 3.2 %collective-permute-start.22 = (bf16[1,128,256]{2,1,0:T(8,128)(2,1)S(1)}, bf16[1,128,256]{2,1,0:T(8,128)(2,1)S(1)}, u32[]{:S(2)}, u32[]{:S(2)}) collective-permute-start(bf16[1,128,256]{2,1,0:T(8,128)(2,1)S(1)} %slice.170), channel_id=1, source_target_pairs={{0,8},{8,16},{16,24},{24,0},{32,40},{40,48},{48,56},{56,32},{64,72... | collective-permute-start | bytes 196616 | tf_op jit(solution)/shard_map/ppermute | solution.py:315
  100.1 3.2 %collective-permute-start.21 = (bf16[1,128,256]{2,1,0:T(8,128)(2,1)S(1)}, bf16[1,128,256]{2,1,0:T(8,128)(2,1)S(1)}, u32[]{:S(2)}, u32[]{:S(2)}) collective-permute-start(bf16[1,128,256]{2,1,0:T(8,128)(2,1)S(1)} %slice.169), channel_id=1, source_target_pairs={{0,96},{8,104},{16,112},{24,120},{32,0},{40,8},{48,16},{56,24},{64... | collective-permute-start | bytes 196616 | tf_op jit(solution)/shard_map/ppermute | solution.py:315
  103.4 2.5 %collective-permute-done.20 = bf16[1,128,256]{2,1,0:T(8,128)(2,1)S(1)} collective-permute-done((bf16[1,128,256]{2,1,0:T(8,128)(2,1)S(1)}, bf16[1,128,256]{2,1,0:T(8,128)(2,1)S(1)}, u32[]{:S(2)}, u32[]{:S(2)}) %collective-permute-start.20) | collective-permute-done | bytes 65568 | tf_op jit(solution)/shard_map/ppermute | solution.py:315
  105.9 0.9 maximum_maximum_fusion.1.refs_5_
  106.9 3.2 %collective-permute-start.26 = (bf16[4,256,256]{2,1,0:T(8,128)(2,1)S(1)}, bf16[4,256,256]{2,1,0:T(8,128)(2,1)S(1)}, u32[]{:S(2)}, u32[]{:S(2)}) collective-permute-start(bf16[4,256,256]{2,1,0:T(8,128)(2,1)S(1)} %maximum_maximum_fusion.1.refs_5_), channel_id=1, source_target_pairs={{0,96},{8,104},{16,112},{24,120},{32,0},{40,8},{48,16},{56,24},{64... | collective-permute-start | bytes 1572872 | tf_op jit(solution)/shard_map/ppermute | solution.py:315
  110.1 0.9 maximum_maximum_fusion.refs_0_
  111.1 0.5 collective-permute-start.25
  111.6 1.6 collective-permute-start.24
  113.2 6.9 %collective-permute-done.27.refs_7_ = bf16[4,256,256]{2,1,0:T(8,128)(2,1)S(1)} collective-permute-done((bf16[4,256,256]{2,1,0:T(8,128)(2,1)S(1)}, bf16[4,256,256]{2,1,0:T(8,128)(2,1)S(1)}, u32[]{:S(2)}, u32[]{:S(2)}) %collective-permute-start.27) | collective-permute-done | bytes 524320 | tf_op jit(solution)/shard_map/ppermute | solution.py:315
  120.1 1.4 collective-permute-done.25.refs_2_
  121.5 1.8 %collective-permute-done.24.refs_1_ = bf16[4,256,256]{2,1,0:T(8,128)(2,1)S(1)} collective-permute-done((bf16[4,256,256]{2,1,0:T(8,128)(2,1)S(1)}, bf16[4,256,256]{2,1,0:T(8,128)(2,1)S(1)}, u32[]{:S(2)}, u32[]{:S(2)}) %collective-permute-start.24) | collective-permute-done | bytes 524320 | tf_op jit(solution)/shard_map/ppermute | solution.py:315
  123.4 2.6 %collective-permute-start.31 = (bf16[4,128,256]{2,1,0:T(8,128)(2,1)S(1)}, bf16[4,128,256]{2,1,0:T(8,128)(2,1)S(1)}, u32[]{:S(2)}, u32[]{:S(2)}) collective-permute-start(bf16[4,128,256]{2,1,0:T(8,128)(2,1)S(1)} %slice.175), channel_id=1, source_target_pairs={{0,96},{8,104},{16,112},{24,120},{32,0},{40,8},{48,16},{56,24},{64... | collective-permute-start | bytes 786440 | tf_op jit(solution)/shard_map/ppermute | solution.py:315
  126.0 0.3 collective-permute-start.28
  126.3 1.7 collective-permute-start.29
  128.0 1.9 %collective-permute-done.31.refs_9_ = bf16[4,128,256]{2,1,0:T(8,128)(2,1)S(1)} collective-permute-done((bf16[4,128,256]{2,1,0:T(8,128)(2,1)S(1)}, bf16[4,128,256]{2,1,0:T(8,128)(2,1)S(1)}, u32[]{:S(2)}, u32[]{:S(2)}) %collective-permute-start.31) | collective-permute-done | bytes 262176 | tf_op jit(solution)/shard_map/ppermute | solution.py:315
  129.9 3.7 %collective-permute-done.30.refs_8_ = bf16[4,128,256]{2,1,0:T(8,128)(2,1)S(1)} collective-permute-done((bf16[4,128,256]{2,1,0:T(8,128)(2,1)S(1)}, bf16[4,128,256]{2,1,0:T(8,128)(2,1)S(1)}, u32[]{:S(2)}, u32[]{:S(2)}) %collective-permute-start.30) | collective-permute-done | bytes 262176 | tf_op jit(solution)/shard_map/ppermute | solution.py:315
  133.6 0.3 collective-permute-done.29.refs_4_
  133.9 0.4 copy-done.13
  134.4 0.7 copy-done.15
  135.1 12.1 %adjoint_plane.1 = (bf16[4,2,152,704]{3,2,1,0:T(8,128)(2,1)}, bf16[4,2,152,704]{3,2,1,0:T(8,128)(2,1)}) custom-call(s32[42]{0:T(128)} %concatenate.39.place, bf16[4,256,256]{2,1,0:T(8,128)(2,1)} %copy-done.3, bf16[4,256,256]{2,1,0:T(8,128)(2,1)} %copy-done.11, bf16[4,256,256]{2,1,0:T(8,128)(2,1)} %copy-done.10, bf16[4,128,256]{2,1,0:T(8,128)(2,1)} %copy-done.14, ...), custom_call_target="tpu_custom_call" | custom-call | flops 4294967296 | bytes 8388608 | tf_op jit(solution)/shard_map/adjoint_plane/pallas_call | solution.py:276
  147.3 4.0 %collective-permute-done.32 = bf16[4,2,152,704]{3,2,1,0:T(8,128)(2,1)S(1)} collective-permute-done((bf16[4,2,152,704]{3,2,1,0:T(8,128)(2,1)}, bf16[4,2,152,704]{3,2,1,0:T(8,128)(2,1)S(1)}, u32[]{:S(2)}, u32[]{:S(2)}) %collective-permute-start.32) | collective-permute-done | bytes 1712160 | tf_op jit(solution)/shard_map/ppermute | solution.py:374
  151.4 1.1 slice_add_fusion
  152.5 4.2 %collective-permute-start.34 = (bf16[152,704]{1,0:T(8,128)(2,1)S(1)}, bf16[152,704]{1,0:T(8,128)(2,1)S(1)}, u32[]{:S(2)}, u32[]{:S(2)}) collective-permute-start(bf16[152,704]{1,0:T(8,128)(2,1)S(1)} %get-tuple-element.130), channel_id=1, source_target_pairs={{0,6},{1,7},{2,0},{3,1},{4,2},{5,3},{6,4},{7,5},{8,14},{9,15},{10,... | collective-permute-start | bytes 642056 | tf_op jit(solution)/shard_map/ppermute | solution.py:315
  156.7 5.2 %collective-permute-done.34 = bf16[152,704]{1,0:T(8,128)(2,1)S(1)} collective-permute-done((bf16[152,704]{1,0:T(8,128)(2,1)S(1)}, bf16[152,704]{1,0:T(8,128)(2,1)S(1)}, u32[]{:S(2)}, u32[]{:S(2)}) %collective-permute-start.34) | collective-permute-done | bytes 214048 | tf_op jit(solution)/shard_map/ppermute | solution.py:315
  161.9 3.4 %collective-permute-done.33 = bf16[152,704]{1,0:T(8,128)(2,1)S(1)} collective-permute-done((bf16[152,704]{1,0:T(8,128)(2,1)S(1)}, bf16[152,704]{1,0:T(8,128)(2,1)S(1)}, u32[]{:S(2)}, u32[]{:S(2)}) %collective-permute-start.33) | collective-permute-done | bytes 214048 | tf_op jit(solution)/shard_map/ppermute | solution.py:315
  165.4 0.4 collective-permute-start.36
  165.8 1.8 %collective-permute-start.35 = (bf16[2,152,704]{2,1,0:T(8,128)(2,1)S(1)}, bf16[2,152,704]{2,1,0:T(8,128)(2,1)S(1)}, u32[]{:S(2)}, u32[]{:S(2)}) collective-permute-start(bf16[2,152,704]{2,1,0:T(8,128)(2,1)S(1)} %pad_maximum_fusion.4), channel_id=1, source_target_pairs={{0,2},{1,3},{2,4},{3,5},{4,6},{5,7},{6,0},{7,1},{8,10},{9,11},{10,... | collective-permute-start | bytes 1284104 | tf_op jit(solution)/shard_map/ppermute | solution.py:315
  167.6 9.4 %collective-permute-done.36 = bf16[2,152,704]{2,1,0:T(8,128)(2,1)S(1)} collective-permute-done((bf16[2,152,704]{2,1,0:T(8,128)(2,1)S(1)}, bf16[2,152,704]{2,1,0:T(8,128)(2,1)S(1)}, u32[]{:S(2)}, u32[]{:S(2)}) %collective-permute-start.36) | collective-permute-done | bytes 428064 | tf_op jit(solution)/shard_map/ppermute | solution.py:315
  177.1 1.7 collective-permute-done.35
  178.7 1.1 fusion.1
  (100 shorter events, 2.7 us)
Async XLA Ops:
  15.8 13.9 %copy-start.5 = (bf16[4,256,256]{2,1,0:T(8,128)(2,1)S(1)}, bf16[4,256,256]{2,1,0:T(8,128)(2,1)}, u32[]{:S(2)}) copy-start(bf16[4,256,256]{2,1,0:T(8,128)(2,1)} %get-tuple-element.62) | copy-start | bytes 1572868
  15.8 9.5 %collective-permute-start = (bf16[4,128,256]{2,1,0:T(8,128)(2,1)}, bf16[4,128,256]{2,1,0:T(8,128)(2,1)S(1)}, u32[]{:S(2)}, u32[]{:S(2)}) collective-permute-start(bf16[4,128,256]{2,1,0:T(8,128)(2,1)} %get-tuple-element.55), channel_id=1, source_target_pairs={{0,32},{8,40},{16,48},{24,56},{32,64},{40,72},{48,80},{56,88},{64,... | collective-permute-start | bytes 786440 | tf_op jit(solution)/shard_map/ppermute | solution.py:315
  17.4 7.9 %collective-permute-start.1 = (bf16[4,128,256]{2,1,0:T(8,128)(2,1)}, bf16[4,128,256]{2,1,0:T(8,128)(2,1)S(1)}, u32[]{:S(2)}, u32[]{:S(2)}) collective-permute-start(bf16[4,128,256]{2,1,0:T(8,128)(2,1)} %get-tuple-element.56), channel_id=1, source_target_pairs={{0,96},{8,104},{16,112},{24,120},{32,0},{40,8},{48,16},{56,24},{64... | collective-permute-start | bytes 786440 | tf_op jit(solution)/shard_map/ppermute | solution.py:315
  19.1 7.7 %collective-permute-start.2 = (bf16[4,128,256]{2,1,0:T(8,128)(2,1)}, bf16[4,128,256]{2,1,0:T(8,128)(2,1)S(1)}, u32[]{:S(2)}, u32[]{:S(2)}) collective-permute-start(bf16[4,128,256]{2,1,0:T(8,128)(2,1)} %get-tuple-element.57), channel_id=1, source_target_pairs={{0,8},{8,16},{16,24},{24,0},{32,40},{40,48},{48,56},{56,32},{64,72... | collective-permute-start | bytes 786440 | tf_op jit(solution)/shard_map/ppermute | solution.py:315
  19.3 8.7 %collective-permute-start.3 = (bf16[4,128,256]{2,1,0:T(8,128)(2,1)}, bf16[4,128,256]{2,1,0:T(8,128)(2,1)S(1)}, u32[]{:S(2)}, u32[]{:S(2)}) collective-permute-start(bf16[4,128,256]{2,1,0:T(8,128)(2,1)} %get-tuple-element.58), channel_id=1, source_target_pairs={{0,24},{8,0},{16,8},{24,16},{32,56},{40,32},{48,40},{56,48},{64,88... | collective-permute-start | bytes 786440 | tf_op jit(solution)/shard_map/ppermute | solution.py:315
  29.1 3.5 %copy-start.4 = (bf16[4,256,256]{2,1,0:T(8,128)(2,1)S(1)}, bf16[4,256,256]{2,1,0:T(8,128)(2,1)}, u32[]{:S(2)}) copy-start(bf16[4,256,256]{2,1,0:T(8,128)(2,1)} %get-tuple-element.60) | copy-start | bytes 1572868
  29.1 13.3 %collective-permute-start.7 = (bf16[4,256,256]{2,1,0:T(8,128)(2,1)S(1)}, bf16[4,256,256]{2,1,0:T(8,128)(2,1)S(1)}, u32[]{:S(2)}, u32[]{:S(2)}) collective-permute-start(bf16[4,256,256]{2,1,0:T(8,128)(2,1)S(1)} %pad_maximum_fusion.3), channel_id=1, source_target_pairs={{0,24},{8,0},{16,8},{24,16},{32,56},{40,32},{48,40},{56,48},{64,88... | collective-permute-start | bytes 1572872 | tf_op jit(solution)/shard_map/ppermute | solution.py:315
  29.8 4.6 %copy-start.2 = (bf16[4,256,256]{2,1,0:T(8,128)(2,1)S(1)}, bf16[4,256,256]{2,1,0:T(8,128)(2,1)}, u32[]{:S(2)}) copy-start(bf16[4,256,256]{2,1,0:T(8,128)(2,1)} %get-tuple-element.54) | copy-start | bytes 1572868
  29.8 12.6 %collective-permute-start.6 = (bf16[4,256,256]{2,1,0:T(8,128)(2,1)S(1)}, bf16[4,256,256]{2,1,0:T(8,128)(2,1)S(1)}, u32[]{:S(2)}, u32[]{:S(2)}) collective-permute-start(bf16[4,256,256]{2,1,0:T(8,128)(2,1)S(1)} %pad_maximum_fusion.2), channel_id=1, source_target_pairs={{0,8},{8,16},{16,24},{24,0},{32,40},{40,48},{48,56},{56,32},{64,72... | collective-permute-start | bytes 1572872 | tf_op jit(solution)/shard_map/ppermute | solution.py:315
  32.7 14.1 %copy-start.6 = (bf16[4,256,256]{2,1,0:T(8,128)(2,1)S(1)}, bf16[4,256,256]{2,1,0:T(8,128)(2,1)}, u32[]{:S(2)}) copy-start(bf16[4,256,256]{2,1,0:T(8,128)(2,1)} %get-tuple-element.53) | copy-start | bytes 1572868
  32.7 14.1 %copy-start.7 = (bf16[4,256,256]{2,1,0:T(8,128)(2,1)S(1)}, bf16[4,256,256]{2,1,0:T(8,128)(2,1)}, u32[]{:S(2)}) copy-start(bf16[4,256,256]{2,1,0:T(8,128)(2,1)} %get-tuple-element.68) | copy-start | bytes 1572868
  32.7 11.5 %collective-permute-start.5 = (bf16[4,256,256]{2,1,0:T(8,128)(2,1)S(1)}, bf16[4,256,256]{2,1,0:T(8,128)(2,1)S(1)}, u32[]{:S(2)}, u32[]{:S(2)}) collective-permute-start(bf16[4,256,256]{2,1,0:T(8,128)(2,1)S(1)} %pad_maximum_fusion.1), channel_id=1, source_target_pairs={{0,96},{8,104},{16,112},{24,120},{32,0},{40,8},{48,16},{56,24},{64... | collective-permute-start | bytes 1572872 | tf_op jit(solution)/shard_map/ppermute | solution.py:315
  34.4 12.3 %collective-permute-start.4 = (bf16[4,256,256]{2,1,0:T(8,128)(2,1)S(1)}, bf16[4,256,256]{2,1,0:T(8,128)(2,1)S(1)}, u32[]{:S(2)}, u32[]{:S(2)}) collective-permute-start(bf16[4,256,256]{2,1,0:T(8,128)(2,1)S(1)} %pad_maximum_fusion), channel_id=1, source_target_pairs={{0,32},{8,40},{16,48},{24,56},{32,64},{40,72},{48,80},{56,88},{64,... | collective-permute-start | bytes 1572872 | tf_op jit(solution)/shard_map/ppermute | solution.py:315
  47.2 5.4 %collective-permute-start.11 = (bf16[1,128,256]{2,1,0:T(8,128)(2,1)S(1)}, bf16[1,128,256]{2,1,0:T(8,128)(2,1)S(1)}, u32[]{:S(2)}, u32[]{:S(2)}) collective-permute-start(bf16[1,128,256]{2,1,0:T(8,128)(2,1)S(1)} %get-tuple-element.118), channel_id=1, source_target_pairs={{0,96},{8,104},{16,112},{24,120},{32,0},{40,8},{48,16},{56,24},{64... | collective-permute-start | bytes 196616 | tf_op jit(solution)/shard_map/ppermute | solution.py:315
  47.4 5.5 %collective-permute-start.10 = (bf16[1,128,256]{2,1,0:T(8,128)(2,1)S(1)}, bf16[1,128,256]{2,1,0:T(8,128)(2,1)S(1)}, u32[]{:S(2)}, u32[]{:S(2)}) collective-permute-start(bf16[1,128,256]{2,1,0:T(8,128)(2,1)S(1)} %get-tuple-element.119), channel_id=1, source_target_pairs={{0,32},{8,40},{16,48},{24,56},{32,64},{40,72},{48,80},{56,88},{64,... | collective-permute-start | bytes 196616 | tf_op jit(solution)/shard_map/ppermute | solution.py:315
  49.4 5.5 %collective-permute-start.9 = (bf16[1,128,256]{2,1,0:T(8,128)(2,1)S(1)}, bf16[1,128,256]{2,1,0:T(8,128)(2,1)S(1)}, u32[]{:S(2)}, u32[]{:S(2)}) collective-permute-start(bf16[1,128,256]{2,1,0:T(8,128)(2,1)S(1)} %get-tuple-element.120), channel_id=1, source_target_pairs={{0,24},{8,0},{16,8},{24,16},{32,56},{40,32},{48,40},{56,48},{64,88... | collective-permute-start | bytes 196616 | tf_op jit(solution)/shard_map/ppermute | solution.py:315
  49.4 5.7 %collective-permute-start.8 = (bf16[1,128,256]{2,1,0:T(8,128)(2,1)S(1)}, bf16[1,128,256]{2,1,0:T(8,128)(2,1)S(1)}, u32[]{:S(2)}, u32[]{:S(2)}) collective-permute-start(bf16[1,128,256]{2,1,0:T(8,128)(2,1)S(1)} %get-tuple-element.121), channel_id=1, source_target_pairs={{0,8},{8,16},{16,24},{24,0},{32,40},{40,48},{48,56},{56,32},{64,72... | collective-permute-start | bytes 196616 | tf_op jit(solution)/shard_map/ppermute | solution.py:315
  55.1 16.8 %collective-permute-start.14 = (bf16[1,256,256]{2,1,0:T(8,128)(2,1)S(1)}, bf16[1,256,256]{2,1,0:T(8,128)(2,1)S(1)}, u32[]{:S(2)}, u32[]{:S(2)}) collective-permute-start(bf16[1,256,256]{2,1,0:T(8,128)(2,1)S(1)} %pad_maximum_fusion.8), channel_id=1, source_target_pairs={{0,32},{8,40},{16,48},{24,56},{32,64},{40,72},{48,80},{56,88},{64,... | collective-permute-start | bytes 393224 | tf_op jit(solution)/shard_map/ppermute | solution.py:315
  55.3 16.7 %collective-permute-start.12 = (bf16[1,256,256]{2,1,0:T(8,128)(2,1)S(1)}, bf16[1,256,256]{2,1,0:T(8,128)(2,1)S(1)}, u32[]{:S(2)}, u32[]{:S(2)}) collective-permute-start(bf16[1,256,256]{2,1,0:T(8,128)(2,1)S(1)} %pad_maximum_fusion.6), channel_id=1, source_target_pairs={{0,8},{8,16},{16,24},{24,0},{32,40},{40,48},{48,56},{56,32},{64,72... | collective-permute-start | bytes 393224 | tf_op jit(solution)/shard_map/ppermute | solution.py:315
  59.0 12.9 %collective-permute-start.13 = (bf16[1,256,256]{2,1,0:T(8,128)(2,1)S(1)}, bf16[1,256,256]{2,1,0:T(8,128)(2,1)S(1)}, u32[]{:S(2)}, u32[]{:S(2)}) collective-permute-start(bf16[1,256,256]{2,1,0:T(8,128)(2,1)S(1)} %pad_maximum_fusion.7), channel_id=1, source_target_pairs={{0,24},{8,0},{16,8},{24,16},{32,56},{40,32},{48,40},{56,48},{64,88... | collective-permute-start | bytes 393224 | tf_op jit(solution)/shard_map/ppermute | solution.py:315
  59.2 12.8 %collective-permute-start.15 = (bf16[1,256,256]{2,1,0:T(8,128)(2,1)S(1)}, bf16[1,256,256]{2,1,0:T(8,128)(2,1)S(1)}, u32[]{:S(2)}, u32[]{:S(2)}) collective-permute-start(bf16[1,256,256]{2,1,0:T(8,128)(2,1)S(1)} %pad_maximum_fusion.9), channel_id=1, source_target_pairs={{0,96},{8,104},{16,112},{24,120},{32,0},{40,8},{48,16},{56,24},{64... | collective-permute-start | bytes 393224 | tf_op jit(solution)/shard_map/ppermute | solution.py:315
  71.9 0.6 copy-start.16
  71.9 0.7 copy-start.17
  72.0 0.7 copy-start.18
  72.0 0.7 copy-start.19
  83.7 6.7 %collective-permute-start.17 = (bf16[1,256,256]{2,1,0:T(8,128)(2,1)}, bf16[1,256,256]{2,1,0:T(8,128)(2,1)S(1)}, u32[]{:S(2)}, u32[]{:S(2)}) collective-permute-start(bf16[1,256,256]{2,1,0:T(8,128)(2,1)} %get-tuple-element.82), channel_id=1, source_target_pairs={{0,32},{8,40},{16,48},{24,56},{32,64},{40,72},{48,80},{56,88},{64,... | collective-permute-start | bytes 393224 | tf_op jit(solution)/shard_map/ppermute | solution.py:315
  83.9 6.5 %collective-permute-start.16 = (bf16[1,256,256]{2,1,0:T(8,128)(2,1)}, bf16[1,256,256]{2,1,0:T(8,128)(2,1)S(1)}, u32[]{:S(2)}, u32[]{:S(2)}) collective-permute-start(bf16[1,256,256]{2,1,0:T(8,128)(2,1)} %get-tuple-element.82), channel_id=1, source_target_pairs={{0,96},{8,104},{16,112},{24,120},{32,0},{40,8},{48,16},{56,24},{64... | collective-permute-start | bytes 393224 | tf_op jit(solution)/shard_map/ppermute | solution.py:315
  87.1 6.1 %collective-permute-start.19 = (bf16[1,256,256]{2,1,0:T(8,128)(2,1)}, bf16[1,256,256]{2,1,0:T(8,128)(2,1)S(1)}, u32[]{:S(2)}, u32[]{:S(2)}) collective-permute-start(bf16[1,256,256]{2,1,0:T(8,128)(2,1)} %get-tuple-element.83), channel_id=1, source_target_pairs={{0,8},{8,16},{16,24},{24,0},{32,40},{40,48},{48,56},{56,32},{64,72... | collective-permute-start | bytes 393224 | tf_op jit(solution)/shard_map/ppermute | solution.py:315
  90.4 6.4 %collective-permute-start.18 = (bf16[1,256,256]{2,1,0:T(8,128)(2,1)}, bf16[1,256,256]{2,1,0:T(8,128)(2,1)S(1)}, u32[]{:S(2)}, u32[]{:S(2)}) collective-permute-start(bf16[1,256,256]{2,1,0:T(8,128)(2,1)} %get-tuple-element.83), channel_id=1, source_target_pairs={{0,24},{8,0},{16,8},{24,16},{32,56},{40,32},{48,40},{56,48},{64,88... | collective-permute-start | bytes 393224 | tf_op jit(solution)/shard_map/ppermute | solution.py:315
  96.8 6.5 %collective-permute-start.23 = (bf16[1,128,256]{2,1,0:T(8,128)(2,1)S(1)}, bf16[1,128,256]{2,1,0:T(8,128)(2,1)S(1)}, u32[]{:S(2)}, u32[]{:S(2)}) collective-permute-start(bf16[1,128,256]{2,1,0:T(8,128)(2,1)S(1)} %slice.171), channel_id=1, source_target_pairs={{0,24},{8,0},{16,8},{24,16},{32,56},{40,32},{48,40},{56,48},{64,88... | collective-permute-start | bytes 196616 | tf_op jit(solution)/shard_map/ppermute | solution.py:315
  96.9 6.5 %collective-permute-start.22 = (bf16[1,128,256]{2,1,0:T(8,128)(2,1)S(1)}, bf16[1,128,256]{2,1,0:T(8,128)(2,1)S(1)}, u32[]{:S(2)}, u32[]{:S(2)}) collective-permute-start(bf16[1,128,256]{2,1,0:T(8,128)(2,1)S(1)} %slice.170), channel_id=1, source_target_pairs={{0,8},{8,16},{16,24},{24,0},{32,40},{40,48},{48,56},{56,32},{64,72... | collective-permute-start | bytes 196616 | tf_op jit(solution)/shard_map/ppermute | solution.py:315
  100.1 5.8 %collective-permute-start.20 = (bf16[1,128,256]{2,1,0:T(8,128)(2,1)S(1)}, bf16[1,128,256]{2,1,0:T(8,128)(2,1)S(1)}, u32[]{:S(2)}, u32[]{:S(2)}) collective-permute-start(bf16[1,128,256]{2,1,0:T(8,128)(2,1)S(1)} %slice.168), channel_id=1, source_target_pairs={{0,32},{8,40},{16,48},{24,56},{32,64},{40,72},{48,80},{56,88},{64,... | collective-permute-start | bytes 196616 | tf_op jit(solution)/shard_map/ppermute | solution.py:315
  100.1 5.8 %collective-permute-start.21 = (bf16[1,128,256]{2,1,0:T(8,128)(2,1)S(1)}, bf16[1,128,256]{2,1,0:T(8,128)(2,1)S(1)}, u32[]{:S(2)}, u32[]{:S(2)}) collective-permute-start(bf16[1,128,256]{2,1,0:T(8,128)(2,1)S(1)} %slice.169), channel_id=1, source_target_pairs={{0,96},{8,104},{16,112},{24,120},{32,0},{40,8},{48,16},{56,24},{64... | collective-permute-start | bytes 196616 | tf_op jit(solution)/shard_map/ppermute | solution.py:315
  106.8 27.1 %copy-start.1 = (bf16[4,256,256]{2,1,0:T(8,128)(2,1)}, bf16[4,256,256]{2,1,0:T(8,128)(2,1)S(1)}, u32[]{:S(2)}) copy-start(bf16[4,256,256]{2,1,0:T(8,128)(2,1)S(1)} %maximum_maximum_fusion.1.refs_5_) | copy-start | bytes 1572868
  106.8 13.3 %collective-permute-start.27 = (bf16[4,256,256]{2,1,0:T(8,128)(2,1)S(1)}, bf16[4,256,256]{2,1,0:T(8,128)(2,1)S(1)}, u32[]{:S(2)}, u32[]{:S(2)}) collective-permute-start(bf16[4,256,256]{2,1,0:T(8,128)(2,1)S(1)} %maximum_maximum_fusion.1.refs_5_), channel_id=1, source_target_pairs={{0,32},{8,40},{16,48},{24,56},{32,64},{40,72},{48,80},{56,88},{64,... | collective-permute-start | bytes 1572872 | tf_op jit(solution)/shard_map/ppermute | solution.py:315
  106.9 13.2 %collective-permute-start.26 = (bf16[4,256,256]{2,1,0:T(8,128)(2,1)S(1)}, bf16[4,256,256]{2,1,0:T(8,128)(2,1)S(1)}, u32[]{:S(2)}, u32[]{:S(2)}) collective-permute-start(bf16[4,256,256]{2,1,0:T(8,128)(2,1)S(1)} %maximum_maximum_fusion.1.refs_5_), channel_id=1, source_target_pairs={{0,96},{8,104},{16,112},{24,120},{32,0},{40,8},{48,16},{56,24},{64... | collective-permute-start | bytes 1572872 | tf_op jit(solution)/shard_map/ppermute | solution.py:315
  111.1 22.8 %copy-start.3 = (bf16[4,256,256]{2,1,0:T(8,128)(2,1)}, bf16[4,256,256]{2,1,0:T(8,128)(2,1)S(1)}, u32[]{:S(2)}) copy-start(bf16[4,256,256]{2,1,0:T(8,128)(2,1)S(1)} %maximum_maximum_fusion.refs_0_) | copy-start | bytes 1572868
  111.1 10.4 %collective-permute-start.25 = (bf16[4,256,256]{2,1,0:T(8,128)(2,1)S(1)}, bf16[4,256,256]{2,1,0:T(8,128)(2,1)S(1)}, u32[]{:S(2)}, u32[]{:S(2)}) collective-permute-start(bf16[4,256,256]{2,1,0:T(8,128)(2,1)S(1)} %maximum_maximum_fusion.refs_0_), channel_id=1, source_target_pairs={{0,8},{8,16},{16,24},{24,0},{32,40},{40,48},{48,56},{56,32},{64,72... | collective-permute-start | bytes 1572872 | tf_op jit(solution)/shard_map/ppermute | solution.py:315
  111.6 11.7 %collective-permute-start.24 = (bf16[4,256,256]{2,1,0:T(8,128)(2,1)S(1)}, bf16[4,256,256]{2,1,0:T(8,128)(2,1)S(1)}, u32[]{:S(2)}, u32[]{:S(2)}) collective-permute-start(bf16[4,256,256]{2,1,0:T(8,128)(2,1)S(1)} %maximum_maximum_fusion.refs_0_), channel_id=1, source_target_pairs={{0,24},{8,0},{16,8},{24,16},{32,56},{40,32},{48,40},{56,48},{64,88... | collective-permute-start | bytes 1572872 | tf_op jit(solution)/shard_map/ppermute | solution.py:315
  120.1 13.8 %copy-start.8 = (bf16[4,256,256]{2,1,0:T(8,128)(2,1)}, bf16[4,256,256]{2,1,0:T(8,128)(2,1)S(1)}, u32[]{:S(2)}) copy-start(bf16[4,256,256]{2,1,0:T(8,128)(2,1)S(1)} %collective-permute-done.27.refs_7_) | copy-start | bytes 1572868
  120.1 13.8 %copy-start.9 = (bf16[4,256,256]{2,1,0:T(8,128)(2,1)}, bf16[4,256,256]{2,1,0:T(8,128)(2,1)S(1)}, u32[]{:S(2)}) copy-start(bf16[4,256,256]{2,1,0:T(8,128)(2,1)S(1)} %collective-permute-done.26.refs_6_) | copy-start | bytes 1572868
  121.5 12.4 %copy-start.10 = (bf16[4,256,256]{2,1,0:T(8,128)(2,1)}, bf16[4,256,256]{2,1,0:T(8,128)(2,1)S(1)}, u32[]{:S(2)}) copy-start(bf16[4,256,256]{2,1,0:T(8,128)(2,1)S(1)} %collective-permute-done.25.refs_2_) | copy-start | bytes 1572868
  123.3 10.6 %copy-start.11 = (bf16[4,256,256]{2,1,0:T(8,128)(2,1)}, bf16[4,256,256]{2,1,0:T(8,128)(2,1)S(1)}, u32[]{:S(2)}) copy-start(bf16[4,256,256]{2,1,0:T(8,128)(2,1)S(1)} %collective-permute-done.24.refs_1_) | copy-start | bytes 1572868
  123.4 6.5 %collective-permute-start.31 = (bf16[4,128,256]{2,1,0:T(8,128)(2,1)S(1)}, bf16[4,128,256]{2,1,0:T(8,128)(2,1)S(1)}, u32[]{:S(2)}, u32[]{:S(2)}) collective-permute-start(bf16[4,128,256]{2,1,0:T(8,128)(2,1)S(1)} %slice.175), channel_id=1, source_target_pairs={{0,96},{8,104},{16,112},{24,120},{32,0},{40,8},{48,16},{56,24},{64... | collective-permute-start | bytes 786440 | tf_op jit(solution)/shard_map/ppermute | solution.py:315
  126.0 7.6 %collective-permute-start.30 = (bf16[4,128,256]{2,1,0:T(8,128)(2,1)S(1)}, bf16[4,128,256]{2,1,0:T(8,128)(2,1)S(1)}, u32[]{:S(2)}, u32[]{:S(2)}) collective-permute-start(bf16[4,128,256]{2,1,0:T(8,128)(2,1)S(1)} %slice.174), channel_id=1, source_target_pairs={{0,32},{8,40},{16,48},{24,56},{32,64},{40,72},{48,80},{56,88},{64,... | collective-permute-start | bytes 786440 | tf_op jit(solution)/shard_map/ppermute | solution.py:315
  126.0 7.6 %collective-permute-start.28 = (bf16[4,128,256]{2,1,0:T(8,128)(2,1)S(1)}, bf16[4,128,256]{2,1,0:T(8,128)(2,1)S(1)}, u32[]{:S(2)}, u32[]{:S(2)}) collective-permute-start(bf16[4,128,256]{2,1,0:T(8,128)(2,1)S(1)} %slice.172), channel_id=1, source_target_pairs={{0,8},{8,16},{16,24},{24,0},{32,40},{40,48},{48,56},{56,32},{64,72... | collective-permute-start | bytes 786440 | tf_op jit(solution)/shard_map/ppermute | solution.py:315
  126.3 7.6 %collective-permute-start.29 = (bf16[4,128,256]{2,1,0:T(8,128)(2,1)S(1)}, bf16[4,128,256]{2,1,0:T(8,128)(2,1)S(1)}, u32[]{:S(2)}, u32[]{:S(2)}) collective-permute-start(bf16[4,128,256]{2,1,0:T(8,128)(2,1)S(1)} %slice.173), channel_id=1, source_target_pairs={{0,24},{8,0},{16,8},{24,16},{32,56},{40,32},{48,40},{56,48},{64,88... | collective-permute-start | bytes 786440 | tf_op jit(solution)/shard_map/ppermute | solution.py:315
  129.9 4.0 %copy-start.12 = (bf16[4,128,256]{2,1,0:T(8,128)(2,1)}, bf16[4,128,256]{2,1,0:T(8,128)(2,1)S(1)}, u32[]{:S(2)}) copy-start(bf16[4,128,256]{2,1,0:T(8,128)(2,1)S(1)} %collective-permute-done.31.refs_9_) | copy-start | bytes 786436
  133.6 0.7 copy-start.13
  133.6 0.8 copy-start.14
  134.4 0.7 copy-start.15
  147.2 9.4 %copy-start = (bf16[4,2,152,704]{3,2,1,0:T(8,128)(2,1)S(1)}, bf16[4,2,152,704]{3,2,1,0:T(8,128)(2,1)}, u32[]{:S(2)}) copy-start(bf16[4,2,152,704]{3,2,1,0:T(8,128)(2,1)} %get-tuple-element.100) | copy-start | bytes 5136388
  147.2 4.1 %collective-permute-start.32 = (bf16[4,2,152,704]{3,2,1,0:T(8,128)(2,1)}, bf16[4,2,152,704]{3,2,1,0:T(8,128)(2,1)S(1)}, u32[]{:S(2)}, u32[]{:S(2)}) collective-permute-start(bf16[4,2,152,704]{3,2,1,0:T(8,128)(2,1)} %get-tuple-element.101), channel_id=1, source_target_pairs={{0,1},{1,0},{2,3},{3,2},{4,5},{5,4},{6,7},{7,6},{8,9},{9,8},{10,11... | collective-permute-start | bytes 5136392 | tf_op jit(solution)/shard_map/ppermute | solution.py:374
  152.5 9.4 %collective-permute-start.34 = (bf16[152,704]{1,0:T(8,128)(2,1)S(1)}, bf16[152,704]{1,0:T(8,128)(2,1)S(1)}, u32[]{:S(2)}, u32[]{:S(2)}) collective-permute-start(bf16[152,704]{1,0:T(8,128)(2,1)S(1)} %get-tuple-element.130), channel_id=1, source_target_pairs={{0,6},{1,7},{2,0},{3,1},{4,2},{5,3},{6,4},{7,5},{8,14},{9,15},{10,... | collective-permute-start | bytes 642056 | tf_op jit(solution)/shard_map/ppermute | solution.py:315
  156.6 8.7 %collective-permute-start.33 = (bf16[152,704]{1,0:T(8,128)(2,1)S(1)}, bf16[152,704]{1,0:T(8,128)(2,1)S(1)}, u32[]{:S(2)}, u32[]{:S(2)}) collective-permute-start(bf16[152,704]{1,0:T(8,128)(2,1)S(1)} %get-tuple-element.131), channel_id=1, source_target_pairs={{0,2},{1,3},{2,4},{3,5},{4,6},{5,7},{6,0},{7,1},{8,10},{9,11},{10,... | collective-permute-start | bytes 642056 | tf_op jit(solution)/shard_map/ppermute | solution.py:315
  165.4 11.7 %collective-permute-start.36 = (bf16[2,152,704]{2,1,0:T(8,128)(2,1)S(1)}, bf16[2,152,704]{2,1,0:T(8,128)(2,1)S(1)}, u32[]{:S(2)}, u32[]{:S(2)}) collective-permute-start(bf16[2,152,704]{2,1,0:T(8,128)(2,1)S(1)} %pad_maximum_fusion.5), channel_id=1, source_target_pairs={{0,6},{1,7},{2,0},{3,1},{4,2},{5,3},{6,4},{7,5},{8,14},{9,15},{10,... | collective-permute-start | bytes 1284104 | tf_op jit(solution)/shard_map/ppermute | solution.py:315
  165.8 12.9 %collective-permute-start.35 = (bf16[2,152,704]{2,1,0:T(8,128)(2,1)S(1)}, bf16[2,152,704]{2,1,0:T(8,128)(2,1)S(1)}, u32[]{:S(2)}, u32[]{:S(2)}) collective-permute-start(bf16[2,152,704]{2,1,0:T(8,128)(2,1)S(1)} %pad_maximum_fusion.4), channel_id=1, source_target_pairs={{0,2},{1,3},{2,4},{3,5},{4,6},{5,7},{6,0},{7,1},{8,10},{9,11},{10,... | collective-permute-start | bytes 1284104 | tf_op jit(solution)/shard_map/ppermute | solution.py:315

commit v3 on v2

--- a/solution.py
+++ b/solution.py
@@ -12,13 +12,14 @@
 MC = 256
 STEP = 64
 KS = 8
-BLOCK = 1024
+BLOCK = 2048
 LANES = 128
 HALF = SUB // 2
 RING = 4
 NEAR = (0, 1, RING - 1, 2)
 MIB = 1 << 20
 VMEM_LIMIT = 58 * MIB
+SMALL_LIMIT = 30 * MIB
 
 
 def phase_tables(facets):
@@ -63,18 +64,23 @@
         b_re, b_im = right[0, 0], right[0, 1]
         left_mat[...] = stacked(side_by_side(b_re, -b_im), side_by_side(b_im, b_re))
 
-    results = []
+    views = []
     for other in range(RING):
         target = step * RING + other
         row_step = place[2 + 2 * target]
         first_col = pl.multiple_of(place[3 + 2 * target], STEP)
         odd = row_step % 2
         first_row = pl.multiple_of(row_step // 2 * LANES, LANES)
-        window = side_by_side(
-            windows[odd, 0, pl.ds(first_col, MC), pl.ds(first_row, MC)],
-            windows[odd, 1, pl.ds(first_col, MC), pl.ds(first_row, MC)],
+        views.append(
+            side_by_side(
+                windows[odd, 0, pl.ds(first_col, MC), pl.ds(first_row, MC)],
+                windows[odd, 1, pl.ds(first_col, MC), pl.ds(first_row, MC)],
+            )
         )
-        half = f32_dot(window, right_mat[...]).astype(jnp.bfloat16)
+    halves = f32_dot(stacked(*views), right_mat[...]).astype(jnp.bfloat16)
+    results = []
+    for other in range(RING):
+        half = halves[other * MC : (other + 1) * MC]
         whole = f32_dot(left_mat[...], stacked(half[:, :SUB], half[:, SUB:]))
         results.append(whole.astype(jnp.bfloat16))
 
@@ -153,7 +159,7 @@
         grid=(slots // BLOCK,),
         in_specs=[block_in, block_in],
         out_specs=(block_out, block_out),
-        compiler_params=pltpu.CompilerParams(vmem_limit_bytes=VMEM_LIMIT),
+        compiler_params=pltpu.CompilerParams(vmem_limit_bytes=SMALL_LIMIT),
         cost_estimate=pl.CostEstimate(
             flops=20 * SUB * slots, bytes_accessed=4 * SUB * slots, transcendentals=2 * SUB * slots
         ),
@@ -162,16 +168,16 @@
 
 
 def residual_kernel(count, *refs):
-    grid_parts = refs[:6]
-    u_in, v_in, observed, resid_out, re_out, im_out, grid, total = refs[6:]
+    grid_parts = refs[:8]
+    u_in, v_in, observed, resid_out, re_out, im_out, grid, total = refs[8:]
     step = pl.program_id(0)
 
     @pl.when(step == 0)
     def _():
         total[...] = jnp.zeros_like(total)
         for part in range(2):
-            own, low, high = (ref[0].astype(jnp.float32) for ref in grid_parts[3 * part : 3 * part + 3])
-            grid[part * SUB : (part + 1) * SUB] = (own + low + high).astype(jnp.bfloat16)
+            own, *others = (ref[0].astype(jnp.float32) for ref in grid_parts[4 * part : 4 * part + 4])
+            grid[part * SUB : (part + 1) * SUB] = sum(others, own).astype(jnp.bfloat16)
 
     u_half = u_in[...]
     v_wide = v_in[...].astype(jnp.float32)
@@ -205,14 +211,14 @@
         grid_spec=pltpu.PrefetchScalarGridSpec(
             num_scalar_prefetch=1,
             grid=(slots // BLOCK,),
-            in_specs=[whole] * 6 + [weight_block, weight_block, vis_block],
+            in_specs=[whole] * 8 + [weight_block, weight_block, vis_block],
             out_specs=(vis_block, whole, whole),
             scratch_shapes=[
                 pltpu.VMEM((2 * SUB, SUB), jnp.bfloat16),
                 pltpu.VMEM((2 * SUB, SUB), jnp.float32),
             ],
         ),
-        compiler_params=pltpu.CompilerParams(vmem_limit_bytes=VMEM_LIMIT),
+        compiler_params=pltpu.CompilerParams(vmem_limit_bytes=SMALL_LIMIT),
         cost_estimate=pl.CostEstimate(
             flops=4 * 512 * 256 * slots, bytes_accessed=4 * SUB * slots, transcendentals=0
         ),
@@ -242,18 +248,22 @@
 
     re_blocks = (re_own[0], re_high[0], re_low[0], stacked(re_far_low[0], re_far_high[0]))
     edge = jnp.zeros((MC, LANES), jnp.float32)
+    halves = []
+    for other in range(RING):
+        grid = stacked(re_blocks[other], im_all[step, other])
+        half = f32_dot(left_mat[...], grid).astype(jnp.bfloat16)
+        halves.append(side_by_side(half[:MC], half[MC:]))
+    wholes = f32_dot(stacked(*halves), right_mat[...])
     for other in range(RING):
         source = step * RING + other
         top = pl.multiple_of(place[2 + 2 * source] * STEP, STEP)
         left_col = place[3 + 2 * source]
         odd = left_col // STEP % 2
         col = pl.multiple_of(left_col // LANES * LANES, LANES)
-        grid = stacked(re_blocks[other], im_all[step, other])
-        half = f32_dot(left_mat[...], grid).astype(jnp.bfloat16)
-        whole = f32_dot(side_by_side(half[:MC], half[MC:]), right_mat[...])
         for part in range(2):
-            wide = side_by_side(whole[:, part * MC : (part + 1) * MC], edge)
-            plane[part, pl.ds(top, MC), pl.ds(col, MC + LANES)] += pltpu.roll(wide, odd * STEP, 1)
+            whole = wholes[other * MC : (other + 1) * MC, part * MC : (part + 1) * MC]
+            wide = pltpu.roll(side_by_side(whole, edge), odd * STEP, 1)
+            plane[part, pl.ds(top, MC), pl.ds(col, MC + LANES)] += wide
 
     @pl.when(step == RING - 1)
     def _():
@@ -293,7 +303,7 @@
                 pltpu.VMEM((2 * SUB, 2 * MC), jnp.bfloat16),
             ],
         ),
-        compiler_params=pltpu.CompilerParams(vmem_limit_bytes=VMEM_LIMIT),
+        compiler_params=pltpu.CompilerParams(vmem_limit_bytes=SMALL_LIMIT),
         cost_estimate=pl.CostEstimate(flops=flops, bytes_accessed=8 * MIB, transcendentals=0),
         name="adjoint_plane",
     )(place, *re_parts, *im_parts, tables_t, tables)
@@ -313,56 +323,63 @@
 
 def move(value, route):
     return lax.ppermute(value, *route)
+
+
+def near_shift(index):
+    return index ^ (index >> 1)
 
 
 def places(worker):
     facet = lax.axis_index("facet")
     sub = lax.axis_index("sub")
     subs = lax.axis_size("sub")
-    near = jnp.asarray(NEAR, jnp.int32)
-    x_near = (facet // RING + near) % RING
-    y_near = (facet % RING + near) % RING
-    rows = (x_near[:, None] * RING + y_near[None, :]).reshape(-1) * subs + sub
+    facets = RING * RING
+    entry = jnp.arange(2 + 2 * facets + 2 * RING, dtype=jnp.int32)
+    target = ((entry - 2) >> 1) & (facets - 1)
+    x_at = ((facet >> 2) + near_shift(target >> 2)) & (RING - 1)
+    y_at = (facet + near_shift(target & (RING - 1))) & (RING - 1)
+    row = (x_at * RING + y_at) * subs + sub
     ids = jnp.arange(worker.shape[0], dtype=jnp.int32)
-    held = jnp.sum(jnp.where(worker[None, :] == rows[:, None], ids[None, :], 0), axis=1)
-    head = jnp.stack([facet, jnp.mod(5 * facet + 3, RING * RING)]).astype(jnp.int32)
-    corners = jnp.stack([held // subs, held % subs * STEP], axis=1).reshape(-1)
-    z_near = (sub // 2 + near) % RING * 2
-    bands = jnp.concatenate([z_near + sub % 2, z_near + 1 - sub % 2])
-    return jnp.concatenate([head, corners, bands]).astype(jnp.int32)
-
-
-def add_rows(block, first, second):
-    upper, lower = block[:, :HALF], block[:, HALF:]
-    if first is not None:
-        upper = upper + first
-    if second is not None:
-        lower = lower + second
-    return jnp.concatenate([upper, lower], axis=1)
-
-
-def reduce_rings(pieces, routes):
-    firsts = []
-    for (_, _, _, far_up, far_down), route in zip(pieces, routes):
-        firsts.append((move(far_up, route(1)), move(far_down, route(-1))))
-    firsts = lax.optimization_barrier(firsts)
-    seconds = []
-    for (_, up, down, _, _), route, (low, high) in zip(pieces, routes, firsts):
-        seconds.append((add_rows(up, low, None), add_rows(down, None, high)))
-    arrived = [(move(up, route(1)), move(down, route(-1))) for (up, down), route in zip(seconds, routes)]
-    arrived = lax.optimization_barrier(arrived)
-    return [(piece[0],) + pair for piece, pair in zip(pieces, arrived)]
+    held = jnp.sum(jnp.where(worker[None, :] == row[:, None], ids[None, :], 0), axis=1)
+    corner = jnp.where(entry & 1 == 0, held >> 3, (held & (subs - 1)) * STEP)
+    table = jnp.where(entry == 0, facet, (5 * facet + 3) & (facets - 1))
+    band = entry - 2 - 2 * facets
+    z_at = ((sub >> 1) + near_shift(band & (RING - 1))) & (RING - 1)
+    band = z_at * 2 + ((sub & 1) ^ (band >> 2 & 1))
+    return jnp.where(entry < 2, table, jnp.where(entry < 2 + 2 * facets, corner, band)).astype(jnp.int32)
+
+
+def with_rows(block, rows, first):
+    space = [(0, 0, 0)] * block.ndim
+    space[-2] = (first, block.shape[-2] - rows.shape[-2] - first, 0)
+    return block + lax.pad(rows, jnp.zeros((), rows.dtype), space)
+
+
+def reduce_large(pieces, routes):
+    sums = []
+    for (own, up, down, far_up, far_down), route in zip(pieces, routes):
+        low, high = move(far_up, route(1)), move(far_down, route(-1))
+        up = with_rows(up, low, 0)
+        down = with_rows(down, high, HALF)
+        sums.append((own, move(up, route(1)), move(down, route(-1))))
+    return sums
+
+
+def reduce_small(blocks, routes):
+    return [
+        (block[:1],)
+        + tuple(move(block[k : k + 1], route(NEAR[k])) for k in range(1, RING))
+        for block, route in zip(blocks, routes)
+    ]
 
 
 def gather_rings(blocks, routes):
-    near = [(move(block, route(-1)), move(block, route(1))) for block, route in zip(blocks, routes)]
-    near = lax.optimization_barrier(near)
-    far = [
-        (move(low[:, :HALF], route(1)), move(high[:, HALF:], route(-1)))
-        for (high, low), route in zip(near, routes)
-    ]
-    far = lax.optimization_barrier(far)
-    return [(block,) + pair + ends for block, pair, ends in zip(blocks, near, far)]
+    parts = []
+    for block, route in zip(blocks, routes):
+        low, high = move(block, route(1)), move(block, route(-1))
+        far = (move(low[:, :HALF], route(1)), move(high[:, HALF:], route(-1)))
+        parts.append((block, high, low) + far)
+    return parts
 
 
 def in_one(parts):
@@ -376,8 +393,9 @@
     low = move(far[0], along_z(1))
     high = move(far[1], along_z(-1))
     low, high = lax.optimization_barrier((low, high))
-    up = jnp.stack([kept[1, 0] + swapped[1, 0] + low, kept[1, 1] + swapped[1, 1]])
-    down = jnp.stack([kept[2, 0] + swapped[2, 0], kept[2, 1] + swapped[2, 1] + high])
+    nothing = jnp.zeros_like(low)
+    up = kept[1] + swapped[1] + jnp.stack([low, nothing])
+    down = kept[2] + swapped[2] + jnp.stack([nothing, high])
     low, high = move(up, along_z(1)), move(down, along_z(-1))
     wide = [x.astype(jnp.float32) for x in (kept[0], swapped[0], low, high)]
     return wide[0] + wide[1] + wide[2] + wide[3]
@@ -392,18 +410,14 @@
     routes = (along_x, along_y)
     place = places(worker_of_subgrid)
     outs = contributions(place, jnp.swapaxes(facet_spec, 2, 3), tables, tables_t)
-    u_weights, v_weights = kernel_weights(bin_offsets, bin_fractions)
-    sums = reduce_rings((outs[:5], outs[5:]), routes)
-    again = []
-    for own, low, high in sums:
-        total = own.astype(jnp.float32) + low.astype(jnp.float32) + high.astype(jnp.float32)
-        total = total.astype(jnp.bfloat16)
-        again.append(
-            (total[:1], total[1:2], total[2:3], total[3:4, :HALF], total[3:4, HALF:])
-        )
-    sums = reduce_rings(again, routes[::-1])
+    first, bin_offsets = lax.optimization_barrier((outs[0], bin_offsets))
+    weights = kernel_weights(bin_offsets, bin_fractions)
+    first, weights = lax.optimization_barrier((first, weights))
+    sums = reduce_large(((first,) + tuple(outs[1:5]), outs[5:]), routes)
+    wide = [sum(x.astype(jnp.float32) for x in parts) for parts in sums]
+    sums = reduce_small([x.astype(jnp.bfloat16) for x in wide], routes[::-1])
     residual, re_part, im_part = residuals(
-        vis_count, sums[0] + sums[1], u_weights, v_weights, observed
+        vis_count, sums[0] + sums[1], *weights, observed
     )
     gathered = gather_rings((re_part, im_part), routes)
     gathered = gather_rings([in_one(parts) for parts in gathered], routes[::-1])

time: 181 us -> 146 us (0.81)
  waiting for transfers between devices: 69.7 us -> 54.8 us
  Pallas kernels: 43.3 us -> 31.7 us
  local copies, waits for them, and re-layouts: 4.26 us -> 0.26 us
  other arithmetic: 7.81 us -> 5.73 us
    ppermute x36 -> x34, waiting for transfers between devices: 65.7 us -> 51 us  [move(): return lax.ppermute(value, *route)]
    pallas_call x1, Pallas kernels: 10.9 us -> 6.63 us  [residuals(): pl.pallas_call(residual_kernel, out_shape=(jax.ShapeDtypeStruct(observed....]
    pallas_call x1, Pallas kernels: 12.1 us -> 8.16 us  [adjoint_plane(): pl.pallas_call(adjoint_kernel, out_shape=(jax.ShapeDtypeStruct(band_shape...]
    add x5 -> x6, other arithmetic: 0.21 us -> 2.63 us  [the longest x4 2.46 us: with_rows(): return block + lax.pad(rows, jnp.zeros((), rows.dtype), space)]
    unnamed x40 -> x22, local copies, waits for them, and re-layouts: 1.95 us -> 0.05 us
    ppermute x36 -> x34, starting transfers between devices: 53 us -> 51.4 us  [move(): return lax.ppermute(value, *route)]
  transfers between devices with their start and end apart: 37 -> 35, of which waited for: 23 -> 15; matrix products, arithmetic and copies ran while one was open for 1% -> 2% of each run, Pallas kernels for 4% -> 4%
where the time goes in v3:
time: 146 us
  waiting for transfers between devices  54.8 us (38%)
  starting transfers between devices  51.5 us (35%)
  Pallas kernels  31.7 us (22%)
  other arithmetic  5.73 us (4%)
  between operations  1.62 us (1%)
    ppermute x34, starting transfers between devices, move(): return lax.ppermute(value, *route)  51.4 us
    ppermute x34, waiting for transfers between devices, move(): return lax.ppermute(value, *route)  51 us
    pallas_call x1, Pallas kernels, contributions(): pl.pallas_call(contribution_kernel, out_shape=shapes + shapes, grid_spec=...  11.1 us
    pallas_call x1, Pallas kernels, adjoint_plane(): pl.pallas_call(adjoint_kernel, out_shape=(jax.ShapeDtypeStruct(band_shape...  8.16 us
    pallas_call x1, Pallas kernels, residuals(): pl.pallas_call(residual_kernel, out_shape=(jax.ShapeDtypeStruct(observed....  6.63 us
    pallas_call x1, Pallas kernels, kernel_weights(): pl.pallas_call(weights_kernel, out_shape=(shape, shape), grid=(slots // B...  5.78 us
    ppermute x1, waiting for transfers between devices, sum_rings(): swapped = lax.ppermute(given, 'sub', [(i, i ^ 1) for i in range(2 * RING)])  3.82 us
  transfers between devices with their start and end apart: 35, of which 15 were waited for; matrix products, arithmetic and copies ran while one was open for 2% of the time, Pallas kernels for 4%

profile of v3, /device:TPU:24, one launch (start us, length us, event | category | flops | bytes accessed | tf_op | source)
XLA Modules:
  0.0 145.6 jit_solution(10868256759589887342)
XLA Ops:
  0.7 0.8 select_reduce_fusion
  1.5 0.6 compare_select_fusion.3.place
  2.1 11.1 %facet_contributions.1 = (bf16[4,256,256]{2,1,0:T(8,128)(2,1)}, bf16[4,256,256]{2,1,0:T(8,128)(2,1)}, bf16[4,256,256]{2,1,0:T(8,128)(2,1)}, bf16[4,128,256]{2,1,...) custom-call(s32[42]{0:T(128)} %compare_select_fusion.3.place, ...), custom_call_target="tpu_custom_call" | custom-call | flops 4294967296 | bytes 8388608 | tf_op jit(solution)/shard_map/facet_contributions/pallas_call | solution.py:116
  13.1 0.8 collective-permute-start.9
  13.9 2.5 %collective-permute-start.7 = (bf16[4,128,256]{2,1,0:T(8,128)(2,1)}, bf16[4,128,256]{2,1,0:T(8,128)(2,1)S(1)}, u32[]{:S(2)}, u32[]{:S(2)}) collective-permute-start(bf16[4,128,256]{2,1,0:T(8,128)(2,1)} %get-tuple-element.38), channel_id=1, source_target_pairs={{0,8},{8,16},{16,24},{24,0},{32,40},{40,48},{48,56},{56,32},{64,72... | collective-permute-start | bytes 786440 | tf_op jit(solution)/shard_map/ppermute | solution.py:325
  16.4 2.8 %collective-permute-start.2 = (bf16[4,128,256]{2,1,0:T(8,128)(2,1)}, bf16[4,128,256]{2,1,0:T(8,128)(2,1)S(1)}, u32[]{:S(2)}, u32[]{:S(2)}) collective-permute-start(bf16[4,128,256]{2,1,0:T(8,128)(2,1)} %get-tuple-element.35), channel_id=1, source_target_pairs={{0,96},{8,104},{16,112},{24,120},{32,0},{40,8},{48,16},{56,24},{64... | collective-permute-start | bytes 786440 | tf_op jit(solution)/shard_map/ppermute | solution.py:325
  19.2 3.5 %collective-permute-done.9 = bf16[4,128,256]{2,1,0:T(8,128)(2,1)S(1)} collective-permute-done((bf16[4,128,256]{2,1,0:T(8,128)(2,1)}, bf16[4,128,256]{2,1,0:T(8,128)(2,1)S(1)}, u32[]{:S(2)}, u32[]{:S(2)}) %collective-permute-start.9) | collective-permute-done | bytes 262176 | tf_op jit(solution)/shard_map/ppermute | solution.py:325
  22.7 1.2 pad_add_fusion
  23.9 0.1 collective-permute-start.10
  24.0 1.1 pad_add_fusion.1
  25.1 3.3 %collective-permute-start.8 = (bf16[4,256,256]{2,1,0:T(8,128)(2,1)S(1)}, bf16[4,256,256]{2,1,0:T(8,128)(2,1)S(1)}, u32[]{:S(2)}, u32[]{:S(2)}) collective-permute-start(bf16[4,256,256]{2,1,0:T(8,128)(2,1)S(1)} %pad_add_fusion.1), channel_id=1, source_target_pairs={{0,8},{8,16},{16,24},{24,0},{32,40},{40,48},{48,56},{56,32},{64,72... | collective-permute-start | bytes 1572872 | tf_op jit(solution)/shard_map/ppermute | solution.py:325
  28.4 1.5 %collective-permute-start = (bf16[4,128,256]{2,1,0:T(8,128)(2,1)S(1)}, bf16[4,128,256]{2,1,0:T(8,128)(2,1)S(1)}, u32[]{:S(2)}, u32[]{:S(2)}) collective-permute-start(bf16[4,128,256]{2,1,0:T(8,128)(2,1)S(1)} %copy-done.10), channel_id=1, source_target_pairs={{0,32},{8,40},{16,48},{24,56},{32,64},{40,72},{48,80},{56,88},{64,... | collective-permute-start | bytes 786440 | tf_op jit(solution)/shard_map/ppermute | solution.py:325
  29.9 0.1 pad_add_fusion.2
  30.0 1.8 %collective-permute-start.3 = (bf16[4,256,256]{2,1,0:T(8,128)(2,1)S(1)}, bf16[4,256,256]{2,1,0:T(8,128)(2,1)S(1)}, u32[]{:S(2)}, u32[]{:S(2)}) collective-permute-start(bf16[4,256,256]{2,1,0:T(8,128)(2,1)S(1)} %pad_add_fusion.2), channel_id=1, source_target_pairs={{0,96},{8,104},{16,112},{24,120},{32,0},{40,8},{48,16},{56,24},{64... | collective-permute-start | bytes 1572872 | tf_op jit(solution)/shard_map/ppermute | solution.py:325
  31.8 4.4 %collective-permute-done = bf16[4,128,256]{2,1,0:T(8,128)(2,1)S(1)} collective-permute-done((bf16[4,128,256]{2,1,0:T(8,128)(2,1)S(1)}, bf16[4,128,256]{2,1,0:T(8,128)(2,1)S(1)}, u32[]{:S(2)}, u32[]{:S(2)}) %collective-permute-start) | collective-permute-done | bytes 262176 | tf_op jit(solution)/shard_map/ppermute | solution.py:325
  36.2 0.1 pad_add_fusion.3
  36.3 0.3 collective-permute-start.1
  36.6 5.8 %kernel_weights.1 = (bf16[256,8192]{1,0:T(8,128)(2,1)S(1)}, bf16[256,8192]{1,0:T(8,128)(2,1)S(1)}) custom-call(s32[1,2,8192]{2,1,0:T(2,128)S(1)} %copy-done.1, f32[1,2,8192]{2,1,0:T(2,128)S(1)} %copy-done.2), custom_call_target="tpu_custom_call" | custom-call | flops 41943040 | bytes 8388608 | tf_op jit(solution)/shard_map/kernel_weights/pallas_call | solution.py:156
  42.5 0.2 add_convert_fusion
  42.7 2.8 %collective-permute-start.13 = (bf16[1,256,256]{2,1,0:T(8,128)(2,1)S(1)}, bf16[1,256,256]{2,1,0:T(8,128)(2,1)S(1)}, u32[]{:S(2)}, u32[]{:S(2)}) collective-permute-start(bf16[1,256,256]{2,1,0:T(8,128)(2,1)S(1)} %get-tuple-element.52), channel_id=1, source_target_pairs={{0,64},{8,72},{16,80},{24,88},{32,96},{40,104},{48,112},{56,120},{... | collective-permute-start | bytes 393224 | tf_op jit(solution)/shard_map/ppermute | solution.py:325
  45.5 1.5 %collective-permute-start.12 = (bf16[1,256,256]{2,1,0:T(8,128)(2,1)S(1)}, bf16[1,256,256]{2,1,0:T(8,128)(2,1)S(1)}, u32[]{:S(2)}, u32[]{:S(2)}) collective-permute-start(bf16[1,256,256]{2,1,0:T(8,128)(2,1)S(1)} %get-tuple-element.53), channel_id=1, source_target_pairs={{0,96},{8,104},{16,112},{24,120},{32,0},{40,8},{48,16},{56,24},{64... | collective-permute-start | bytes 393224 | tf_op jit(solution)/shard_map/ppermute | solution.py:325
  47.0 0.6 collective-permute-start.11
  47.6 5.5 %collective-permute-done.1 = bf16[4,256,256]{2,1,0:T(8,128)(2,1)S(1)} collective-permute-done((bf16[4,256,256]{2,1,0:T(8,128)(2,1)S(1)}, bf16[4,256,256]{2,1,0:T(8,128)(2,1)S(1)}, u32[]{:S(2)}, u32[]{:S(2)}) %collective-permute-start.1) | collective-permute-done | bytes 524320 | tf_op jit(solution)/shard_map/ppermute | solution.py:325
  53.1 0.2 add_convert_fusion.1
  53.3 0.1 collective-permute-start.6
  53.4 1.5 %collective-permute-start.5 = (bf16[1,256,256]{2,1,0:T(8,128)(2,1)S(1)}, bf16[1,256,256]{2,1,0:T(8,128)(2,1)S(1)}, u32[]{:S(2)}, u32[]{:S(2)}) collective-permute-start(bf16[1,256,256]{2,1,0:T(8,128)(2,1)S(1)} %get-tuple-element.57), channel_id=1, source_target_pairs={{0,24},{8,0},{16,8},{24,16},{32,56},{40,32},{48,40},{56,48},{64,88... | collective-permute-start | bytes 393224 | tf_op jit(solution)/shard_map/ppermute | solution.py:325
  54.9 1.8 %collective-permute-start.4 = (bf16[1,256,256]{2,1,0:T(8,128)(2,1)S(1)}, bf16[1,256,256]{2,1,0:T(8,128)(2,1)S(1)}, u32[]{:S(2)}, u32[]{:S(2)}) collective-permute-start(bf16[1,256,256]{2,1,0:T(8,128)(2,1)S(1)} %get-tuple-element.58), channel_id=1, source_target_pairs={{0,8},{8,16},{16,24},{24,0},{32,40},{40,48},{48,56},{56,32},{64,72... | collective-permute-start | bytes 393224 | tf_op jit(solution)/shard_map/ppermute | solution.py:325
  57.4 2.6 %collective-permute-done.6.refs_3_ = bf16[1,256,256]{2,1,0:T(8,128)(2,1)S(1)} collective-permute-done((bf16[1,256,256]{2,1,0:T(8,128)(2,1)S(1)}, bf16[1,256,256]{2,1,0:T(8,128)(2,1)S(1)}, u32[]{:S(2)}, u32[]{:S(2)}) %collective-permute-start.6) | collective-permute-done | bytes 131104 | tf_op jit(solution)/shard_map/ppermute | solution.py:325
  60.0 1.1 collective-permute-done.5.refs_2_
  61.1 6.6 %residuals.1 = (f32[1,2,8192]{2,1,0:T(2,128)}, bf16[1,256,256]{2,1,0:T(8,128)(2,1)S(1)}, bf16[1,256,256]{2,1,0:T(8,128)(2,1)S(1)}) custom-call(s32[1]{0:T(128)S(6)} %copy.10.count, bf16[1,256,256]{2,1,0:T(8,128)(2,1)S(1)} %get-tuple-element.59.refs_0_, bf16[1,256,256]{2,1,0:T(8,128)(2,1)S(1)} %collective-permute-done.4.refs_1_, ...), custom_call_target="tpu_custom_call" | custom-call | flops 4294967296 | bytes 8388608 | tf_op jit(solution)/shard_map/residuals/pallas_call | solution.py:208
  67.7 1.8 %collective-permute-start.23 = (bf16[1,256,256]{2,1,0:T(8,128)(2,1)S(1)}, bf16[1,256,256]{2,1,0:T(8,128)(2,1)S(1)}, u32[]{:S(2)}, u32[]{:S(2)}) collective-permute-start(bf16[1,256,256]{2,1,0:T(8,128)(2,1)S(1)} %get-tuple-element.45), channel_id=1, source_target_pairs={{0,8},{8,16},{16,24},{24,0},{32,40},{40,48},{48,56},{56,32},{64,72... | collective-permute-start | bytes 393224 | tf_op jit(solution)/shard_map/ppermute | solution.py:325
  69.6 0.2 collective-permute-start.22
  69.8 3.2 %collective-permute-start.14 = (bf16[1,256,256]{2,1,0:T(8,128)(2,1)S(1)}, bf16[1,256,256]{2,1,0:T(8,128)(2,1)S(1)}, u32[]{:S(2)}, u32[]{:S(2)}) collective-permute-start(bf16[1,256,256]{2,1,0:T(8,128)(2,1)S(1)} %get-tuple-element.44), channel_id=1, source_target_pairs={{0,96},{8,104},{16,112},{24,120},{32,0},{40,8},{48,16},{56,24},{64... | collective-permute-start | bytes 393224 | tf_op jit(solution)/shard_map/ppermute | solution.py:325
  73.0 3.1 %collective-permute-start.24 = (bf16[1,128,256]{2,1,0:T(8,128)(2,1)S(1)}, bf16[1,128,256]{2,1,0:T(8,128)(2,1)S(1)}, u32[]{:S(2)}, u32[]{:S(2)}) collective-permute-start(bf16[1,128,256]{2,1,0:T(8,128)(2,1)S(1)} %slice.118), channel_id=1, source_target_pairs={{0,8},{8,16},{16,24},{24,0},{32,40},{40,48},{48,56},{56,32},{64,72... | collective-permute-start | bytes 196616 | tf_op jit(solution)/shard_map/ppermute | solution.py:325
  76.1 0.1 collective-permute-start.25
  76.2 1.1 collective-permute-done.15
  77.4 0.0 copy-start.4
  77.4 3.3 %collective-permute-start.17 = (bf16[1,128,256]{2,1,0:T(8,128)(2,1)S(1)}, bf16[1,128,256]{2,1,0:T(8,128)(2,1)S(1)}, u32[]{:S(2)}, u32[]{:S(2)}) collective-permute-start(bf16[1,128,256]{2,1,0:T(8,128)(2,1)S(1)} %slice.115), channel_id=1, source_target_pairs={{0,96},{8,104},{16,112},{24,120},{32,0},{40,8},{48,16},{56,24},{64... | collective-permute-start | bytes 196616 | tf_op jit(solution)/shard_map/ppermute | solution.py:325
  80.7 1.8 %collective-permute-done.25 = bf16[1,128,256]{2,1,0:T(8,128)(2,1)S(1)} collective-permute-done((bf16[1,128,256]{2,1,0:T(8,128)(2,1)S(1)}, bf16[1,128,256]{2,1,0:T(8,128)(2,1)S(1)}, u32[]{:S(2)}, u32[]{:S(2)}) %collective-permute-start.25) | collective-permute-done | bytes 65568 | tf_op jit(solution)/shard_map/ppermute | solution.py:325
  82.5 0.1 collective-permute-start.27
  82.6 3.2 %collective-permute-start.26 = (bf16[4,256,256]{2,1,0:T(8,128)(2,1)S(1)}, bf16[4,256,256]{2,1,0:T(8,128)(2,1)S(1)}, u32[]{:S(2)}, u32[]{:S(2)}) collective-permute-start(bf16[4,256,256]{2,1,0:T(8,128)(2,1)S(1)} %maximum_maximum_fusion.1.refs_5_), channel_id=1, source_target_pairs={{0,96},{8,104},{16,112},{24,120},{32,0},{40,8},{48,16},{56,24},{64... | collective-permute-start | bytes 1572872 | tf_op jit(solution)/shard_map/ppermute | solution.py:325
  85.8 0.1 maximum_maximum_fusion.refs_0_
  85.8 1.4 collective-permute-start.19
  87.3 0.7 collective-permute-start.18
  87.9 6.0 %collective-permute-done.27.refs_7_ = bf16[4,256,256]{2,1,0:T(8,128)(2,1)S(1)} collective-permute-done((bf16[4,256,256]{2,1,0:T(8,128)(2,1)S(1)}, bf16[4,256,256]{2,1,0:T(8,128)(2,1)S(1)}, u32[]{:S(2)}, u32[]{:S(2)}) %collective-permute-start.27) | collective-permute-done | bytes 524320 | tf_op jit(solution)/shard_map/ppermute | solution.py:325
  94.0 0.1 collective-permute-start.28
  94.1 3.3 %collective-permute-start.29 = (bf16[4,128,256]{2,1,0:T(8,128)(2,1)S(1)}, bf16[4,128,256]{2,1,0:T(8,128)(2,1)S(1)}, u32[]{:S(2)}, u32[]{:S(2)}) collective-permute-start(bf16[4,128,256]{2,1,0:T(8,128)(2,1)S(1)} %slice.121), channel_id=1, source_target_pairs={{0,96},{8,104},{16,112},{24,120},{32,0},{40,8},{48,16},{56,24},{64... | collective-permute-start | bytes 786440 | tf_op jit(solution)/shard_map/ppermute | solution.py:325
  97.4 1.3 collective-permute-start.20
  98.7 0.9 collective-permute-start.21
  99.6 2.0 %collective-permute-done.28.refs_8_ = bf16[4,128,256]{2,1,0:T(8,128)(2,1)S(1)} collective-permute-done((bf16[4,128,256]{2,1,0:T(8,128)(2,1)S(1)}, bf16[4,128,256]{2,1,0:T(8,128)(2,1)S(1)}, u32[]{:S(2)}, u32[]{:S(2)}) %collective-permute-start.28) | collective-permute-done | bytes 262176 | tf_op jit(solution)/shard_map/ppermute | solution.py:325
  101.6 2.2 %collective-permute-done.20.refs_3_ = bf16[4,128,256]{2,1,0:T(8,128)(2,1)S(1)} collective-permute-done((bf16[4,128,256]{2,1,0:T(8,128)(2,1)S(1)}, bf16[4,128,256]{2,1,0:T(8,128)(2,1)S(1)}, u32[]{:S(2)}, u32[]{:S(2)}) %collective-permute-start.20) | collective-permute-done | bytes 262176 | tf_op jit(solution)/shard_map/ppermute | solution.py:325
  103.8 2.5 %collective-permute-done.21.refs_4_ = bf16[4,128,256]{2,1,0:T(8,128)(2,1)S(1)} collective-permute-done((bf16[4,128,256]{2,1,0:T(8,128)(2,1)S(1)}, bf16[4,128,256]{2,1,0:T(8,128)(2,1)S(1)}, u32[]{:S(2)}, u32[]{:S(2)}) %collective-permute-start.21) | collective-permute-done | bytes 262176 | tf_op jit(solution)/shard_map/ppermute | solution.py:325
  106.3 8.2 %adjoint_plane.1 = (bf16[4,2,152,704]{3,2,1,0:T(8,128)(2,1)S(1)}, bf16[4,2,152,704]{3,2,1,0:T(8,128)(2,1)S(1)}) custom-call(s32[42]{0:T(128)S(1)} %copy-done, bf16[4,256,256]{2,1,0:T(8,128)(2,1)S(1)} %maximum_maximum_fusion.refs_0_, bf16[4,256,256]{2,1,0:T(8,128)(2,1)S(1)} %collective-permute-done.18.refs_1_, ...), custom_call_target="tpu_custom_call" | custom-call | flops 4294967296 | bytes 8388608 | tf_op jit(solution)/shard_map/adjoint_plane/pallas_call | solution.py:286
  114.5 0.1 collective-permute-start.30
  114.6 3.8 %collective-permute-done.30 = bf16[4,2,152,704]{3,2,1,0:T(8,128)(2,1)S(1)} collective-permute-done((bf16[4,2,152,704]{3,2,1,0:T(8,128)(2,1)S(1)}, bf16[4,2,152,704]{3,2,1,0:T(8,128)(2,1)S(1)}, u32[]{:S(2)}, u32[]{:S(2)}) %collective-permute-start.30) | collective-permute-done | bytes 1712160 | tf_op jit(solution)/shard_map/ppermute | solution.py:391
  118.4 0.1 slice_add_fusion.1
  118.5 4.2 %collective-permute-start.32 = (bf16[152,704]{1,0:T(8,128)(2,1)S(1)}, bf16[152,704]{1,0:T(8,128)(2,1)S(1)}, u32[]{:S(2)}, u32[]{:S(2)}) collective-permute-start(bf16[152,704]{1,0:T(8,128)(2,1)S(1)} %get-tuple-element.60), channel_id=1, source_target_pairs={{0,6},{1,7},{2,0},{3,1},{4,2},{5,3},{6,4},{7,5},{8,14},{9,15},{10,... | collective-permute-start | bytes 642056 | tf_op jit(solution)/shard_map/ppermute | solution.py:325
  122.7 5.2 %collective-permute-done.32 = bf16[152,704]{1,0:T(8,128)(2,1)S(1)} collective-permute-done((bf16[152,704]{1,0:T(8,128)(2,1)S(1)}, bf16[152,704]{1,0:T(8,128)(2,1)S(1)}, u32[]{:S(2)}, u32[]{:S(2)}) %collective-permute-start.32) | collective-permute-done | bytes 214048 | tf_op jit(solution)/shard_map/ppermute | solution.py:325
  127.9 3.4 %collective-permute-done.31 = bf16[152,704]{1,0:T(8,128)(2,1)S(1)} collective-permute-done((bf16[152,704]{1,0:T(8,128)(2,1)S(1)}, bf16[152,704]{1,0:T(8,128)(2,1)S(1)}, u32[]{:S(2)}, u32[]{:S(2)}) %collective-permute-start.31) | collective-permute-done | bytes 214048 | tf_op jit(solution)/shard_map/ppermute | solution.py:325
  131.4 0.2 fusion.5
  131.5 0.1 collective-permute-start.33
  131.6 3.2 %collective-permute-start.34 = (bf16[2,152,704]{2,1,0:T(8,128)(2,1)S(1)}, bf16[2,152,704]{2,1,0:T(8,128)(2,1)S(1)}, u32[]{:S(2)}, u32[]{:S(2)}) collective-permute-start(bf16[2,152,704]{2,1,0:T(8,128)(2,1)S(1)} %get-tuple-element.51), channel_id=1, source_target_pairs={{0,6},{1,7},{2,0},{3,1},{4,2},{5,3},{6,4},{7,5},{8,14},{9,15},{10,... | collective-permute-start | bytes 1284104 | tf_op jit(solution)/shard_map/ppermute | solution.py:325
  134.8 9.6 %collective-permute-done.33 = bf16[2,152,704]{2,1,0:T(8,128)(2,1)S(1)} collective-permute-done((bf16[2,152,704]{2,1,0:T(8,128)(2,1)S(1)}, bf16[2,152,704]{2,1,0:T(8,128)(2,1)S(1)}, u32[]{:S(2)}, u32[]{:S(2)}) %collective-permute-start.33) | collective-permute-done | bytes 428064 | tf_op jit(solution)/shard_map/ppermute | solution.py:325
  144.4 1.2 fusion.1
  (57 shorter events, 0.4 us)
Async XLA Ops:
  13.1 15.3 %copy-start.10 = (bf16[4,128,256]{2,1,0:T(8,128)(2,1)S(1)}, bf16[4,128,256]{2,1,0:T(8,128)(2,1)}, u32[]{:S(2)}) copy-start(bf16[4,128,256]{2,1,0:T(8,128)(2,1)} %get-tuple-element.33) | copy-start | bytes 786436
  13.1 16.7 %copy-start.7 = (bf16[4,256,256]{2,1,0:T(8,128)(2,1)S(1)}, bf16[4,256,256]{2,1,0:T(8,128)(2,1)}, u32[]{:S(2)}) copy-start(bf16[4,256,256]{2,1,0:T(8,128)(2,1)} %get-tuple-element.34) | copy-start | bytes 1572868
  13.1 9.5 %collective-permute-start.9 = (bf16[4,128,256]{2,1,0:T(8,128)(2,1)}, bf16[4,128,256]{2,1,0:T(8,128)(2,1)S(1)}, u32[]{:S(2)}, u32[]{:S(2)}) collective-permute-start(bf16[4,128,256]{2,1,0:T(8,128)(2,1)} %get-tuple-element.40), channel_id=1, source_target_pairs={{0,24},{8,0},{16,8},{24,16},{32,56},{40,32},{48,40},{56,48},{64,88... | collective-permute-start | bytes 786440 | tf_op jit(solution)/shard_map/ppermute | solution.py:325
  13.9 10.0 %collective-permute-start.7 = (bf16[4,128,256]{2,1,0:T(8,128)(2,1)}, bf16[4,128,256]{2,1,0:T(8,128)(2,1)S(1)}, u32[]{:S(2)}, u32[]{:S(2)}) collective-permute-start(bf16[4,128,256]{2,1,0:T(8,128)(2,1)} %get-tuple-element.38), channel_id=1, source_target_pairs={{0,8},{8,16},{16,24},{24,0},{32,40},{40,48},{48,56},{56,32},{64,72... | collective-permute-start | bytes 786440 | tf_op jit(solution)/shard_map/ppermute | solution.py:325
  16.4 13.4 %collective-permute-start.2 = (bf16[4,128,256]{2,1,0:T(8,128)(2,1)}, bf16[4,128,256]{2,1,0:T(8,128)(2,1)S(1)}, u32[]{:S(2)}, u32[]{:S(2)}) collective-permute-start(bf16[4,128,256]{2,1,0:T(8,128)(2,1)} %get-tuple-element.35), channel_id=1, source_target_pairs={{0,96},{8,104},{16,112},{24,120},{32,0},{40,8},{48,16},{56,24},{64... | collective-permute-start | bytes 786440 | tf_op jit(solution)/shard_map/ppermute | solution.py:325
  22.7 13.5 %copy-start.6 = (bf16[4,256,256]{2,1,0:T(8,128)(2,1)S(1)}, bf16[4,256,256]{2,1,0:T(8,128)(2,1)}, u32[]{:S(2)}) copy-start(bf16[4,256,256]{2,1,0:T(8,128)(2,1)} %get-tuple-element.32) | copy-start | bytes 1572868
  23.9 18.6 %collective-permute-start.10 = (bf16[4,256,256]{2,1,0:T(8,128)(2,1)S(1)}, bf16[4,256,256]{2,1,0:T(8,128)(2,1)S(1)}, u32[]{:S(2)}, u32[]{:S(2)}) collective-permute-start(bf16[4,256,256]{2,1,0:T(8,128)(2,1)S(1)} %pad_add_fusion), channel_id=1, source_target_pairs={{0,24},{8,0},{16,8},{24,16},{32,56},{40,32},{48,40},{56,48},{64,88... | collective-permute-start | bytes 1572872 | tf_op jit(solution)/shard_map/ppermute | solution.py:325
  23.9 12.7 %copy-start.1 = (s32[1,2,8192]{2,1,0:T(2,128)S(1)}, s32[1,2,8192]{2,1,0:T(2,128)}, u32[]{:S(2)}) copy-start(s32[1,2,8192]{2,1,0:T(2,128)} %offsets) | copy-start | bytes 196612
  24.0 12.7 %copy-start.2 = (f32[1,2,8192]{2,1,0:T(2,128)S(1)}, f32[1,2,8192]{2,1,0:T(2,128)}, u32[]{:S(2)}) copy-start(f32[1,2,8192]{2,1,0:T(2,128)} %fractions.1) | copy-start | bytes 196612
  25.1 17.3 %collective-permute-start.8 = (bf16[4,256,256]{2,1,0:T(8,128)(2,1)S(1)}, bf16[4,256,256]{2,1,0:T(8,128)(2,1)S(1)}, u32[]{:S(2)}, u32[]{:S(2)}) collective-permute-start(bf16[4,256,256]{2,1,0:T(8,128)(2,1)S(1)} %pad_add_fusion.1), channel_id=1, source_target_pairs={{0,8},{8,16},{16,24},{24,0},{32,40},{40,48},{48,56},{56,32},{64,72... | collective-permute-start | bytes 1572872 | tf_op jit(solution)/shard_map/ppermute | solution.py:325
  28.4 7.8 %collective-permute-start = (bf16[4,128,256]{2,1,0:T(8,128)(2,1)S(1)}, bf16[4,128,256]{2,1,0:T(8,128)(2,1)S(1)}, u32[]{:S(2)}, u32[]{:S(2)}) collective-permute-start(bf16[4,128,256]{2,1,0:T(8,128)(2,1)S(1)} %copy-done.10), channel_id=1, source_target_pairs={{0,32},{8,40},{16,48},{24,56},{32,64},{40,72},{48,80},{56,88},{64,... | collective-permute-start | bytes 786440 | tf_op jit(solution)/shard_map/ppermute | solution.py:325
  30.0 17.6 %collective-permute-start.3 = (bf16[4,256,256]{2,1,0:T(8,128)(2,1)S(1)}, bf16[4,256,256]{2,1,0:T(8,128)(2,1)S(1)}, u32[]{:S(2)}, u32[]{:S(2)}) collective-permute-start(bf16[4,256,256]{2,1,0:T(8,128)(2,1)S(1)} %pad_add_fusion.2), channel_id=1, source_target_pairs={{0,96},{8,104},{16,112},{24,120},{32,0},{40,8},{48,16},{56,24},{64... | collective-permute-start | bytes 1572872 | tf_op jit(solution)/shard_map/ppermute | solution.py:325
  36.3 16.8 %collective-permute-start.1 = (bf16[4,256,256]{2,1,0:T(8,128)(2,1)S(1)}, bf16[4,256,256]{2,1,0:T(8,128)(2,1)S(1)}, u32[]{:S(2)}, u32[]{:S(2)}) collective-permute-start(bf16[4,256,256]{2,1,0:T(8,128)(2,1)S(1)} %pad_add_fusion.3), channel_id=1, source_target_pairs={{0,32},{8,40},{16,48},{24,56},{32,64},{40,72},{48,80},{56,88},{64,... | collective-permute-start | bytes 1572872 | tf_op jit(solution)/shard_map/ppermute | solution.py:325
  36.6 5.8 %copy-start.9 = (bf16[4,256,256]{2,1,0:T(8,128)(2,1)S(1)}, bf16[4,256,256]{2,1,0:T(8,128)(2,1)}, u32[]{:S(2)}) copy-start(bf16[4,256,256]{2,1,0:T(8,128)(2,1)} %get-tuple-element.36) | copy-start | bytes 1572868
  42.4 10.7 %copy-start.8 = (bf16[4,256,256]{2,1,0:T(8,128)(2,1)S(1)}, bf16[4,256,256]{2,1,0:T(8,128)(2,1)}, u32[]{:S(2)}) copy-start(bf16[4,256,256]{2,1,0:T(8,128)(2,1)} %get-tuple-element.31) | copy-start | bytes 1572868
  42.7 18.4 %copy-start.3 = (f32[1,2,8192]{2,1,0:T(2,128)S(1)}, f32[1,2,8192]{2,1,0:T(2,128)}, u32[]{:S(2)}) copy-start(f32[1,2,8192]{2,1,0:T(2,128)} %refs_10_.2) | copy-start | bytes 196612
  42.7 12.2 %collective-permute-start.13 = (bf16[1,256,256]{2,1,0:T(8,128)(2,1)S(1)}, bf16[1,256,256]{2,1,0:T(8,128)(2,1)S(1)}, u32[]{:S(2)}, u32[]{:S(2)}) collective-permute-start(bf16[1,256,256]{2,1,0:T(8,128)(2,1)S(1)} %get-tuple-element.52), channel_id=1, source_target_pairs={{0,64},{8,72},{16,80},{24,88},{32,96},{40,104},{48,112},{56,120},{... | collective-permute-start | bytes 393224 | tf_op jit(solution)/shard_map/ppermute | solution.py:325
  45.5 11.9 %collective-permute-start.12 = (bf16[1,256,256]{2,1,0:T(8,128)(2,1)S(1)}, bf16[1,256,256]{2,1,0:T(8,128)(2,1)S(1)}, u32[]{:S(2)}, u32[]{:S(2)}) collective-permute-start(bf16[1,256,256]{2,1,0:T(8,128)(2,1)S(1)} %get-tuple-element.53), channel_id=1, source_target_pairs={{0,96},{8,104},{16,112},{24,120},{32,0},{40,8},{48,16},{56,24},{64... | collective-permute-start | bytes 393224 | tf_op jit(solution)/shard_map/ppermute | solution.py:325
  47.0 10.4 %collective-permute-start.11 = (bf16[1,256,256]{2,1,0:T(8,128)(2,1)S(1)}, bf16[1,256,256]{2,1,0:T(8,128)(2,1)S(1)}, u32[]{:S(2)}, u32[]{:S(2)}) collective-permute-start(bf16[1,256,256]{2,1,0:T(8,128)(2,1)S(1)} %get-tuple-element.54), channel_id=1, source_target_pairs={{0,32},{8,40},{16,48},{24,56},{32,64},{40,72},{48,80},{56,88},{64,... | collective-permute-start | bytes 393224 | tf_op jit(solution)/shard_map/ppermute | solution.py:325
  53.3 6.7 %collective-permute-start.6 = (bf16[1,256,256]{2,1,0:T(8,128)(2,1)S(1)}, bf16[1,256,256]{2,1,0:T(8,128)(2,1)S(1)}, u32[]{:S(2)}, u32[]{:S(2)}) collective-permute-start(bf16[1,256,256]{2,1,0:T(8,128)(2,1)S(1)} %get-tuple-element.56), channel_id=1, source_target_pairs={{0,16},{8,24},{16,0},{24,8},{32,48},{40,56},{48,32},{56,40},{64,80... | collective-permute-start | bytes 393224 | tf_op jit(solution)/shard_map/ppermute | solution.py:325
  53.4 7.7 %collective-permute-start.5 = (bf16[1,256,256]{2,1,0:T(8,128)(2,1)S(1)}, bf16[1,256,256]{2,1,0:T(8,128)(2,1)S(1)}, u32[]{:S(2)}, u32[]{:S(2)}) collective-permute-start(bf16[1,256,256]{2,1,0:T(8,128)(2,1)S(1)} %get-tuple-element.57), channel_id=1, source_target_pairs={{0,24},{8,0},{16,8},{24,16},{32,56},{40,32},{48,40},{56,48},{64,88... | collective-permute-start | bytes 393224 | tf_op jit(solution)/shard_map/ppermute | solution.py:325
  54.9 6.2 %collective-permute-start.4 = (bf16[1,256,256]{2,1,0:T(8,128)(2,1)S(1)}, bf16[1,256,256]{2,1,0:T(8,128)(2,1)S(1)}, u32[]{:S(2)}, u32[]{:S(2)}) collective-permute-start(bf16[1,256,256]{2,1,0:T(8,128)(2,1)S(1)} %get-tuple-element.58), channel_id=1, source_target_pairs={{0,8},{8,16},{16,24},{24,0},{32,40},{40,48},{48,56},{56,32},{64,72... | collective-permute-start | bytes 393224 | tf_op jit(solution)/shard_map/ppermute | solution.py:325
  61.1 45.2 %copy-start.5 = (bf16[16,2,256,256]{3,2,1,0:T(8,128)(2,1)S(1)}, bf16[16,2,256,256]{3,2,1,0:T(8,128)(2,1)}, u32[]{:S(2)}) copy-start(bf16[16,2,256,256]{3,2,1,0:T(8,128)(2,1)} %constant.49.clone.right.refs_11_) | copy-start | bytes 12582916
  67.7 5.3 %collective-permute-start.23 = (bf16[1,256,256]{2,1,0:T(8,128)(2,1)S(1)}, bf16[1,256,256]{2,1,0:T(8,128)(2,1)S(1)}, u32[]{:S(2)}, u32[]{:S(2)}) collective-permute-start(bf16[1,256,256]{2,1,0:T(8,128)(2,1)S(1)} %get-tuple-element.45), channel_id=1, source_target_pairs={{0,8},{8,16},{16,24},{24,0},{32,40},{40,48},{48,56},{56,32},{64,72... | collective-permute-start | bytes 393224 | tf_op jit(solution)/shard_map/ppermute | solution.py:325
  69.6 6.6 %collective-permute-start.22 = (bf16[1,256,256]{2,1,0:T(8,128)(2,1)S(1)}, bf16[1,256,256]{2,1,0:T(8,128)(2,1)S(1)}, u32[]{:S(2)}, u32[]{:S(2)}) collective-permute-start(bf16[1,256,256]{2,1,0:T(8,128)(2,1)S(1)} %get-tuple-element.45), channel_id=1, source_target_pairs={{0,24},{8,0},{16,8},{24,16},{32,56},{40,32},{48,40},{56,48},{64,88... | collective-permute-start | bytes 393224 | tf_op jit(solution)/shard_map/ppermute | solution.py:325
  69.8 7.6 %collective-permute-start.15 = (bf16[1,256,256]{2,1,0:T(8,128)(2,1)S(1)}, bf16[1,256,256]{2,1,0:T(8,128)(2,1)S(1)}, u32[]{:S(2)}, u32[]{:S(2)}) collective-permute-start(bf16[1,256,256]{2,1,0:T(8,128)(2,1)S(1)} %get-tuple-element.44), channel_id=1, source_target_pairs={{0,32},{8,40},{16,48},{24,56},{32,64},{40,72},{48,80},{56,88},{64,... | collective-permute-start | bytes 393224 | tf_op jit(solution)/shard_map/ppermute | solution.py:325
  69.8 7.6 %collective-permute-start.14 = (bf16[1,256,256]{2,1,0:T(8,128)(2,1)S(1)}, bf16[1,256,256]{2,1,0:T(8,128)(2,1)S(1)}, u32[]{:S(2)}, u32[]{:S(2)}) collective-permute-start(bf16[1,256,256]{2,1,0:T(8,128)(2,1)S(1)} %get-tuple-element.44), channel_id=1, source_target_pairs={{0,96},{8,104},{16,112},{24,120},{32,0},{40,8},{48,16},{56,24},{64... | collective-permute-start | bytes 393224 | tf_op jit(solution)/shard_map/ppermute | solution.py:325
  73.0 7.7 %collective-permute-start.24 = (bf16[1,128,256]{2,1,0:T(8,128)(2,1)S(1)}, bf16[1,128,256]{2,1,0:T(8,128)(2,1)S(1)}, u32[]{:S(2)}, u32[]{:S(2)}) collective-permute-start(bf16[1,128,256]{2,1,0:T(8,128)(2,1)S(1)} %slice.118), channel_id=1, source_target_pairs={{0,8},{8,16},{16,24},{24,0},{32,40},{40,48},{48,56},{56,32},{64,72... | collective-permute-start | bytes 196616 | tf_op jit(solution)/shard_map/ppermute | solution.py:325
  76.1 6.3 %collective-permute-start.25 = (bf16[1,128,256]{2,1,0:T(8,128)(2,1)S(1)}, bf16[1,128,256]{2,1,0:T(8,128)(2,1)S(1)}, u32[]{:S(2)}, u32[]{:S(2)}) collective-permute-start(bf16[1,128,256]{2,1,0:T(8,128)(2,1)S(1)} %slice.119), channel_id=1, source_target_pairs={{0,24},{8,0},{16,8},{24,16},{32,56},{40,32},{48,40},{56,48},{64,88... | collective-permute-start | bytes 196616 | tf_op jit(solution)/shard_map/ppermute | solution.py:325
  77.3 8.4 %collective-permute-start.16 = (bf16[1,128,256]{2,1,0:T(8,128)(2,1)S(1)}, bf16[1,128,256]{2,1,0:T(8,128)(2,1)S(1)}, u32[]{:S(2)}, u32[]{:S(2)}) collective-permute-start(bf16[1,128,256]{2,1,0:T(8,128)(2,1)S(1)} %slice.114), channel_id=1, source_target_pairs={{0,32},{8,40},{16,48},{24,56},{32,64},{40,72},{48,80},{56,88},{64,... | collective-permute-start | bytes 196616 | tf_op jit(solution)/shard_map/ppermute | solution.py:325
  77.4 29.0 %copy-start.4 = (bf16[16,2,256,256]{3,2,1,0:T(8,128)(2,1)S(1)}, bf16[16,2,256,256]{3,2,1,0:T(8,128)(2,1)}, u32[]{:S(2)}) copy-start(bf16[16,2,256,256]{3,2,1,0:T(8,128)(2,1)} %constant.50.clone.left.refs_10_) | copy-start | bytes 12582916
  77.4 28.9 %copy-start = (s32[42]{0:T(128)S(1)}, s32[42]{0:T(128)}, u32[]{:S(2)}) copy-start(s32[42]{0:T(128)} %compare_select_fusion.3.place) | copy-start | bytes 508
  77.4 8.4 %collective-permute-start.17 = (bf16[1,128,256]{2,1,0:T(8,128)(2,1)S(1)}, bf16[1,128,256]{2,1,0:T(8,128)(2,1)S(1)}, u32[]{:S(2)}, u32[]{:S(2)}) collective-permute-start(bf16[1,128,256]{2,1,0:T(8,128)(2,1)S(1)} %slice.115), channel_id=1, source_target_pairs={{0,96},{8,104},{16,112},{24,120},{32,0},{40,8},{48,16},{56,24},{64... | collective-permute-start | bytes 196616 | tf_op jit(solution)/shard_map/ppermute | solution.py:325
  82.5 11.5 %collective-permute-start.27 = (bf16[4,256,256]{2,1,0:T(8,128)(2,1)S(1)}, bf16[4,256,256]{2,1,0:T(8,128)(2,1)S(1)}, u32[]{:S(2)}, u32[]{:S(2)}) collective-permute-start(bf16[4,256,256]{2,1,0:T(8,128)(2,1)S(1)} %maximum_maximum_fusion.1.refs_5_), channel_id=1, source_target_pairs={{0,32},{8,40},{16,48},{24,56},{32,64},{40,72},{48,80},{56,88},{64,... | collective-permute-start | bytes 1572872 | tf_op jit(solution)/shard_map/ppermute | solution.py:325
  82.6 11.5 %collective-permute-start.26 = (bf16[4,256,256]{2,1,0:T(8,128)(2,1)S(1)}, bf16[4,256,256]{2,1,0:T(8,128)(2,1)S(1)}, u32[]{:S(2)}, u32[]{:S(2)}) collective-permute-start(bf16[4,256,256]{2,1,0:T(8,128)(2,1)S(1)} %maximum_maximum_fusion.1.refs_5_), channel_id=1, source_target_pairs={{0,96},{8,104},{16,112},{24,120},{32,0},{40,8},{48,16},{56,24},{64... | collective-permute-start | bytes 1572872 | tf_op jit(solution)/shard_map/ppermute | solution.py:325
  85.8 11.5 %collective-permute-start.19 = (bf16[4,256,256]{2,1,0:T(8,128)(2,1)S(1)}, bf16[4,256,256]{2,1,0:T(8,128)(2,1)S(1)}, u32[]{:S(2)}, u32[]{:S(2)}) collective-permute-start(bf16[4,256,256]{2,1,0:T(8,128)(2,1)S(1)} %maximum_maximum_fusion.refs_0_), channel_id=1, source_target_pairs={{0,8},{8,16},{16,24},{24,0},{32,40},{40,48},{48,56},{56,32},{64,72... | collective-permute-start | bytes 1572872 | tf_op jit(solution)/shard_map/ppermute | solution.py:325
  87.3 11.4 %collective-permute-start.18 = (bf16[4,256,256]{2,1,0:T(8,128)(2,1)S(1)}, bf16[4,256,256]{2,1,0:T(8,128)(2,1)S(1)}, u32[]{:S(2)}, u32[]{:S(2)}) collective-permute-start(bf16[4,256,256]{2,1,0:T(8,128)(2,1)S(1)} %maximum_maximum_fusion.refs_0_), channel_id=1, source_target_pairs={{0,24},{8,0},{16,8},{24,16},{32,56},{40,32},{48,40},{56,48},{64,88... | collective-permute-start | bytes 1572872 | tf_op jit(solution)/shard_map/ppermute | solution.py:325
  94.0 7.7 %collective-permute-start.28 = (bf16[4,128,256]{2,1,0:T(8,128)(2,1)S(1)}, bf16[4,128,256]{2,1,0:T(8,128)(2,1)S(1)}, u32[]{:S(2)}, u32[]{:S(2)}) collective-permute-start(bf16[4,128,256]{2,1,0:T(8,128)(2,1)S(1)} %slice.120), channel_id=1, source_target_pairs={{0,32},{8,40},{16,48},{24,56},{32,64},{40,72},{48,80},{56,88},{64,... | collective-permute-start | bytes 786440 | tf_op jit(solution)/shard_map/ppermute | solution.py:325
  94.1 7.5 %collective-permute-start.29 = (bf16[4,128,256]{2,1,0:T(8,128)(2,1)S(1)}, bf16[4,128,256]{2,1,0:T(8,128)(2,1)S(1)}, u32[]{:S(2)}, u32[]{:S(2)}) collective-permute-start(bf16[4,128,256]{2,1,0:T(8,128)(2,1)S(1)} %slice.121), channel_id=1, source_target_pairs={{0,96},{8,104},{16,112},{24,120},{32,0},{40,8},{48,16},{56,24},{64... | collective-permute-start | bytes 786440 | tf_op jit(solution)/shard_map/ppermute | solution.py:325
  97.4 6.4 %collective-permute-start.20 = (bf16[4,128,256]{2,1,0:T(8,128)(2,1)S(1)}, bf16[4,128,256]{2,1,0:T(8,128)(2,1)S(1)}, u32[]{:S(2)}, u32[]{:S(2)}) collective-permute-start(bf16[4,128,256]{2,1,0:T(8,128)(2,1)S(1)} %slice.116), channel_id=1, source_target_pairs={{0,8},{8,16},{16,24},{24,0},{32,40},{40,48},{48,56},{56,32},{64,72... | collective-permute-start | bytes 786440 | tf_op jit(solution)/shard_map/ppermute | solution.py:325
  98.7 7.7 %collective-permute-start.21 = (bf16[4,128,256]{2,1,0:T(8,128)(2,1)S(1)}, bf16[4,128,256]{2,1,0:T(8,128)(2,1)S(1)}, u32[]{:S(2)}, u32[]{:S(2)}) collective-permute-start(bf16[4,128,256]{2,1,0:T(8,128)(2,1)S(1)} %slice.117), channel_id=1, source_target_pairs={{0,24},{8,0},{16,8},{24,16},{32,56},{40,32},{48,40},{56,48},{64,88... | collective-permute-start | bytes 786440 | tf_op jit(solution)/shard_map/ppermute | solution.py:325
  114.5 3.9 %collective-permute-start.30 = (bf16[4,2,152,704]{3,2,1,0:T(8,128)(2,1)S(1)}, bf16[4,2,152,704]{3,2,1,0:T(8,128)(2,1)S(1)}, u32[]{:S(2)}, u32[]{:S(2)}) collective-permute-start(bf16[4,2,152,704]{3,2,1,0:T(8,128)(2,1)S(1)} %get-tuple-element.47), channel_id=1, source_target_pairs={{0,1},{1,0},{2,3},{3,2},{4,5},{5,4},{6,7},{7,6},{8,9},{9,8},{10,11... | collective-permute-start | bytes 5136392 | tf_op jit(solution)/shard_map/ppermute | solution.py:391
  118.5 9.4 %collective-permute-start.32 = (bf16[152,704]{1,0:T(8,128)(2,1)S(1)}, bf16[152,704]{1,0:T(8,128)(2,1)S(1)}, u32[]{:S(2)}, u32[]{:S(2)}) collective-permute-start(bf16[152,704]{1,0:T(8,128)(2,1)S(1)} %get-tuple-element.60), channel_id=1, source_target_pairs={{0,6},{1,7},{2,0},{3,1},{4,2},{5,3},{6,4},{7,5},{8,14},{9,15},{10,... | collective-permute-start | bytes 642056 | tf_op jit(solution)/shard_map/ppermute | solution.py:325
  122.7 8.7 %collective-permute-start.31 = (bf16[152,704]{1,0:T(8,128)(2,1)S(1)}, bf16[152,704]{1,0:T(8,128)(2,1)S(1)}, u32[]{:S(2)}, u32[]{:S(2)}) collective-permute-start(bf16[152,704]{1,0:T(8,128)(2,1)S(1)} %get-tuple-element.61), channel_id=1, source_target_pairs={{0,2},{1,3},{2,4},{3,5},{4,6},{5,7},{6,0},{7,1},{8,10},{9,11},{10,... | collective-permute-start | bytes 642056 | tf_op jit(solution)/shard_map/ppermute | solution.py:325
  131.5 12.9 %collective-permute-start.33 = (bf16[2,152,704]{2,1,0:T(8,128)(2,1)S(1)}, bf16[2,152,704]{2,1,0:T(8,128)(2,1)S(1)}, u32[]{:S(2)}, u32[]{:S(2)}) collective-permute-start(bf16[2,152,704]{2,1,0:T(8,128)(2,1)S(1)} %get-tuple-element.50), channel_id=1, source_target_pairs={{0,2},{1,3},{2,4},{3,5},{4,6},{5,7},{6,0},{7,1},{8,10},{9,11},{10,... | collective-permute-start | bytes 1284104 | tf_op jit(solution)/shard_map/ppermute | solution.py:325
  131.6 12.8 %collective-permute-start.34 = (bf16[2,152,704]{2,1,0:T(8,128)(2,1)S(1)}, bf16[2,152,704]{2,1,0:T(8,128)(2,1)S(1)}, u32[]{:S(2)}, u32[]{:S(2)}) collective-permute-start(bf16[2,152,704]{2,1,0:T(8,128)(2,1)S(1)} %get-tuple-element.51), channel_id=1, source_target_pairs={{0,6},{1,7},{2,0},{3,1},{4,2},{5,3},{6,4},{7,5},{8,14},{9,15},{10,... | collective-permute-start | bytes 1284104 | tf_op jit(solution)/shard_map/ppermute | solution.py:325

commit v4 on v3

--- a/solution.py
+++ b/solution.py
@@ -18,21 +18,28 @@
 RING = 4
 NEAR = (0, 1, RING - 1, 2)
 MIB = 1 << 20
-VMEM_LIMIT = 58 * MIB
+FAR_LIMIT = 58 * MIB
+NEAR_LIMIT = 36 * MIB
 SMALL_LIMIT = 30 * MIB
 
 
-def phase_tables(facets):
-    sub_part = (np.arange(SUB) - SUB // 2)[:, None]
-    win_part = (np.arange(MC) - MC // 2)[None, :]
+def phase_parts(facets):
+    sub_part = np.arange(SUB) - SUB // 2
+    win_part = np.arange(MC) - MC // 2
     modulus = SUB * facets
-    tables = []
-    for offset in range(facets):
-        residue = np.mod(sub_part * win_part * facets + sub_part * offset, modulus)
-        angles = residue.astype(np.float32).astype(np.float64) * (2.0 * math.pi / modulus)
-        factor = MC ** (-0.5)
-        tables.append(np.stack([np.cos(angles) * factor, np.sin(angles) * factor]))
-    return np.stack(tables).astype(jnp.bfloat16)
+    turns = 2.0 * math.pi / modulus
+    residue = np.mod(win_part[:, None] * sub_part[None, :] * facets, modulus) * turns
+    base = np.stack([np.cos(residue), np.sin(residue)]) * MC ** (-0.5)
+    shift = np.mod(np.arange(facets)[:, None] * sub_part[None, :], modulus) * turns
+    phases = np.stack([np.cos(shift), np.sin(shift)], axis=1)
+    return base.astype(np.float32), phases.astype(np.float32)
+
+
+def transposed_table(base, phase):
+    turn_re, turn_im = phase[0, 0:1, :], phase[0, 1:2, :]
+    re = base[0] * turn_re - base[1] * turn_im
+    im = base[0] * turn_im + base[1] * turn_re
+    return re, im
 
 
 def side_by_side(*blocks):
@@ -47,26 +54,18 @@
     return jnp.dot(left, right, preferred_element_type=jnp.float32)
 
 
-def contribution_kernel(place, spec, left, right, *rest):
-    a_own, a_up, a_down, a_far_up, a_far_down = rest[:5]
-    b_own, b_up, b_down, b_far_up, b_far_down = rest[5:10]
-    windows, left_mat, right_mat = rest[10:]
-    step = pl.program_id(0)
+def transformed(targets, place, spec, base, left, right, windows, left_mat, right_mat):
     reach = windows.shape[3]
-
-    @pl.when(step == 0)
-    def _():
-        for part in range(2):
-            windows[0, part] = spec[0, part, :, :reach]
-            windows[1, part] = spec[0, part, :, STEP : STEP + reach]
-        a_re, a_im = left[0, 0], left[0, 1]
-        right_mat[...] = stacked(side_by_side(a_re, a_im), side_by_side(-a_im, a_re))
-        b_re, b_im = right[0, 0], right[0, 1]
-        left_mat[...] = stacked(side_by_side(b_re, -b_im), side_by_side(b_im, b_re))
-
+    for part in range(2):
+        windows[0, part] = spec[0, part, :, :reach]
+        windows[1, part] = spec[0, part, :, STEP : STEP + reach]
+    a_re, a_im = (x.astype(jnp.bfloat16) for x in transposed_table(base, left))
+    right_mat[...] = stacked(side_by_side(a_re, a_im), side_by_side(-a_im, a_re))
+    b_re, b_im = (x.T.astype(jnp.bfloat16) for x in transposed_table(base, right))
+    left_mat[...] = stacked(side_by_side(b_re, -b_im), side_by_side(b_im, b_re))
     views = []
-    for other in range(RING):
-        target = step * RING + other
+    for across, along in targets:
+        target = across * RING + along
         row_step = place[2 + 2 * target]
         first_col = pl.multiple_of(place[3 + 2 * target], STEP)
         odd = row_step % 2
@@ -78,63 +77,72 @@
             )
         )
     halves = f32_dot(stacked(*views), right_mat[...]).astype(jnp.bfloat16)
-    results = []
-    for other in range(RING):
-        half = halves[other * MC : (other + 1) * MC]
+    results = {}
+    for count, target in enumerate(targets):
+        half = halves[count * MC : (count + 1) * MC]
         whole = f32_dot(left_mat[...], stacked(half[:, :SUB], half[:, SUB:]))
-        results.append(whole.astype(jnp.bfloat16))
-
-    for near, out in ((0, a_own), (1, a_up), (2, a_down)):
-
-        @pl.when(step == near)
-        def _():
-            for other in range(RING):
-                out[other] = results[other][:SUB]
-
-    @pl.when(step == 3)
-    def _():
-        for other in range(RING):
-            a_far_up[other] = results[other][:HALF]
-            a_far_down[other] = results[other][HALF:SUB]
-
-    b_own[0] = results[0][SUB:]
-    b_up[0] = results[1][SUB:]
-    b_down[0] = results[2][SUB:]
-    b_far_up[0] = results[3][SUB : SUB + HALF]
-    b_far_down[0] = results[3][SUB + HALF :]
-
-
-def contributions(place, spec, tables, tables_t):
-    facets = tables.shape[0]
+        results[target] = whole.astype(jnp.bfloat16)
+    return results
+
+
+FAR = RING - 1
+FAR_TARGETS = tuple((FAR, k) for k in range(RING)) + tuple((k, FAR) for k in range(FAR))
+NEAR_TARGETS = tuple((i, k) for i in range(FAR) for k in range(FAR))
+
+
+def far_kernel(place, spec, base, left, right, *rest):
+    a_far_up, a_far_down, b_far_up, b_far_down, a_last, b_last = rest[:6]
+    results = transformed(FAR_TARGETS, place, spec, base, left, right, *rest[6:])
+    for k in range(RING):
+        a_far_up[k] = results[FAR, k][:HALF]
+        a_far_down[k] = results[FAR, k][HALF:SUB]
+        b_far_up[k] = results[k, FAR][SUB : SUB + HALF]
+        b_far_down[k] = results[k, FAR][SUB + HALF :]
+    for k in range(FAR):
+        a_last[k] = results[k, FAR][:SUB]
+        b_last[k] = results[FAR, k][SUB:]
+
+
+def near_kernel(place, spec, base, left, right, a_last, b_last, *rest):
+    a_outs, b_outs = rest[:3], rest[3:6]
+    results = transformed(NEAR_TARGETS, place, spec, base, left, right, *rest[6:])
+    for i in range(FAR):
+        for k in range(FAR):
+            a_outs[i][k] = results[i, k][:SUB]
+            b_outs[k][i] = results[i, k][SUB:]
+        a_outs[i][FAR] = a_last[i]
+        b_outs[i][FAR] = b_last[i]
+
+
+def contributions(kernel, name, limit, shapes, place, spec, base, phases, lasts=()):
     cols, rows = spec.shape[2:]
-    flops = facets * 2 * 2 * 512 * 512 * 256
-    full = jax.ShapeDtypeStruct((RING, SUB, SUB), jnp.bfloat16)
-    part = jax.ShapeDtypeStruct((RING, HALF, SUB), jnp.bfloat16)
-    shapes = (full, full, full, part, part)
-    whole = tuple(pl.BlockSpec(s.shape, lambda t, place: (0, 0, 0)) for s in shapes)
-    stepped = tuple(pl.BlockSpec((1,) + s.shape[1:], lambda t, place: (t, 0, 0)) for s in shapes)
+    whole = [pl.BlockSpec(x.shape, lambda t, place: (0, 0, 0)) for x in lasts]
     return pl.pallas_call(
-        contribution_kernel,
-        out_shape=shapes + shapes,
+        kernel,
+        out_shape=tuple(jax.ShapeDtypeStruct(s, jnp.bfloat16) for s in shapes),
         grid_spec=pltpu.PrefetchScalarGridSpec(
             num_scalar_prefetch=1,
-            grid=(RING,),
+            grid=(1,),
             in_specs=[
                 pl.BlockSpec((1, 2, cols, rows), lambda t, place: (0, 0, 0, 0)),
-                pl.BlockSpec((1, 2, MC, SUB), lambda t, place: (place[0], 0, 0, 0)),
-                pl.BlockSpec((1, 2, SUB, MC), lambda t, place: (place[1], 0, 0, 0)),
-            ],
-            out_specs=whole + stepped,
+                pl.BlockSpec((2, MC, SUB), lambda t, place: (0, 0, 0)),
+                pl.BlockSpec((1, 2, SUB), lambda t, place: (place[0], 0, 0)),
+                pl.BlockSpec((1, 2, SUB), lambda t, place: (place[1], 0, 0)),
+            ]
+            + whole,
+            out_specs=tuple(pl.BlockSpec(s, lambda t, place: (0, 0, 0)) for s in shapes),
             scratch_shapes=[
                 pltpu.VMEM((2, 2, cols, rows - STEP), jnp.bfloat16),
+                pltpu.VMEM((2 * SUB, 2 * MC), jnp.bfloat16),
                 pltpu.VMEM((2 * MC, 2 * SUB), jnp.bfloat16),
-                pltpu.VMEM((2 * SUB, 2 * MC), jnp.bfloat16),
             ],
         ),
-        compiler_params=pltpu.CompilerParams(vmem_limit_bytes=VMEM_LIMIT),
-        cost_estimate=pl.CostEstimate(flops=flops, bytes_accessed=8 * MIB, transcendentals=0),
-        name="facet_contributions",
-    )(place, spec, tables_t, tables)
+        compiler_params=pltpu.CompilerParams(vmem_limit_bytes=limit),
+        cost_estimate=pl.CostEstimate(
+            flops=8 * 2 * 2 * 512 * 512 * 256, bytes_accessed=8 * MIB, transcendentals=0
+        ),
+        name=name,
+    )(place, spec, base, phases, phases, *lasts)
 
 
 def weights_kernel(offsets, fractions, u_out, v_out):
@@ -229,7 +237,7 @@
 def adjoint_kernel(place, *refs):
     re_own, re_high, re_low, re_far_low, re_far_high = refs[:5]
     im_own, im_high, im_low, im_far_low, im_far_high = refs[5:10]
-    left, right, kept, given, plane, im_all, left_mat, right_mat = refs[10:]
+    base, left, right, kept, given, plane, im_all, left_mat, right_mat = refs[10:]
     step = pl.program_id(0)
     band_rows, cols = kept.shape[2:]
 
@@ -241,9 +249,9 @@
         im_all[2] = im_low[...]
         im_all[3, :, :HALF] = im_far_low[...]
         im_all[3, :, HALF:] = im_far_high[...]
-        a_re, a_im = left[0, 0], left[0, 1]
+        a_re, a_im = (x.astype(jnp.bfloat16) for x in transposed_table(base, left))
         left_mat[...] = stacked(side_by_side(a_re, a_im), side_by_side(-a_im, a_re))
-        b_re, b_im = right[0, 0], right[0, 1]
+        b_re, b_im = (x.T.astype(jnp.bfloat16) for x in transposed_table(base, right))
         right_mat[...] = stacked(side_by_side(b_re, -b_im), side_by_side(b_im, b_re))
 
     re_blocks = (re_own[0], re_high[0], re_low[0], stacked(re_far_low[0], re_far_high[0]))
@@ -276,8 +284,8 @@
                     out[near, part] = rows[:, :cols].astype(jnp.bfloat16)
 
 
-def adjoint_plane(place, re_parts, im_parts, tables, tables_t, bands, rows, cols):
-    facets = tables.shape[0]
+def adjoint_plane(place, re_parts, im_parts, base, phases, bands, rows, cols):
+    facets = phases.shape[0]
     flops = facets * 2 * 2 * 512 * 512 * 256
     wide = (cols + LANES - 1) // LANES * LANES
     band_shape = (RING, 2, rows // bands, cols)
@@ -292,8 +300,9 @@
             in_specs=stepped
             + whole
             + [
-                pl.BlockSpec((1, 2, MC, SUB), lambda t, place: (place[0], 0, 0, 0)),
-                pl.BlockSpec((1, 2, SUB, MC), lambda t, place: (place[1], 0, 0, 0)),
+                pl.BlockSpec((2, MC, SUB), lambda t, place: (0, 0, 0)),
+                pl.BlockSpec((1, 2, SUB), lambda t, place: (place[0], 0, 0)),
+                pl.BlockSpec((1, 2, SUB), lambda t, place: (place[1], 0, 0)),
             ],
             out_specs=(pl.BlockSpec(band_shape, lambda t, place: (0, 0, 0, 0)),) * 2,
             scratch_shapes=[
@@ -306,7 +315,7 @@
         compiler_params=pltpu.CompilerParams(vmem_limit_bytes=SMALL_LIMIT),
         cost_estimate=pl.CostEstimate(flops=flops, bytes_accessed=8 * MIB, transcendentals=0),
         name="adjoint_plane",
-    )(place, *re_parts, *im_parts, tables_t, tables)
+    )(place, *re_parts, *im_parts, base, phases, phases)
 
 
 def along_x(shift):
@@ -355,14 +364,13 @@
     return block + lax.pad(rows, jnp.zeros((), rows.dtype), space)
 
 
-def reduce_large(pieces, routes):
-    sums = []
-    for (own, up, down, far_up, far_down), route in zip(pieces, routes):
-        low, high = move(far_up, route(1)), move(far_down, route(-1))
-        up = with_rows(up, low, 0)
-        down = with_rows(down, high, HALF)
-        sums.append((own, move(up, route(1)), move(down, route(-1))))
-    return sums
+def send_far(far_up, far_down, route):
+    return move(far_up, route(1)), move(far_down, route(-1))
+
+
+def send_near(up, down, arrived, route):
+    low, high = arrived
+    return move(with_rows(up, low, 0), route(1)), move(with_rows(down, high, HALF), route(-1))
 
 
 def reduce_small(blocks, routes):
@@ -404,16 +412,25 @@
 def on_device(facet_spec, worker_of_subgrid, vis_count, bin_offsets, bin_fractions, observed):
     subs = lax.axis_size("sub")
     rows, cols = facet_spec.shape[2:]
-    table = phase_tables(lax.axis_size("facet"))
-    tables = jnp.asarray(table)
-    tables_t = jnp.asarray(np.ascontiguousarray(table.transpose(0, 1, 3, 2)))
+    base, phases = (jnp.asarray(x) for x in phase_parts(lax.axis_size("facet")))
     routes = (along_x, along_y)
     place = places(worker_of_subgrid)
-    outs = contributions(place, jnp.swapaxes(facet_spec, 2, 3), tables, tables_t)
-    first, bin_offsets = lax.optimization_barrier((outs[0], bin_offsets))
+    spec = jnp.swapaxes(facet_spec, 2, 3)
+    full, part, last = (RING, SUB, SUB), (RING, HALF, SUB), (FAR, SUB, SUB)
+    outs = contributions(
+        far_kernel, "far_parts", FAR_LIMIT, (part,) * 4 + (last,) * 2, place, spec, base, phases
+    )
+    arrived = [send_far(*outs[:2], along_x), send_far(*outs[2:4], along_y)]
+    nears = contributions(
+        near_kernel, "near_parts", NEAR_LIMIT, (full,) * 6, place, spec, base, phases, outs[4:]
+    )
+    arrived, nears, bin_offsets = lax.optimization_barrier((arrived, nears, bin_offsets))
     weights = kernel_weights(bin_offsets, bin_fractions)
-    first, weights = lax.optimization_barrier((first, weights))
-    sums = reduce_large(((first,) + tuple(outs[1:5]), outs[5:]), routes)
+    sums = [
+        (own,) + send_near(up, down, got, route)
+        for (own, up, down), got, route in zip((nears[:3], nears[3:]), arrived, routes)
+    ]
+    sums, weights = lax.optimization_barrier((sums, weights))
     wide = [sum(x.astype(jnp.float32) for x in parts) for parts in sums]
     sums = reduce_small([x.astype(jnp.bfloat16) for x in wide], routes[::-1])
     residual, re_part, im_part = residuals(
@@ -422,7 +439,7 @@
     gathered = gather_rings((re_part, im_part), routes)
     gathered = gather_rings([in_one(parts) for parts in gathered], routes[::-1])
     kept, given = adjoint_plane(
-        place, gathered[0], gathered[1], tables, tables_t, subs, rows, cols
+        place, gathered[0], gathered[1], base, phases, subs, rows, cols
     )
     update = sum_rings(kept, given)
     return (residual, update[None])

time: 146 us -> 137 us (0.938)
  starting transfers between devices: 51.5 us -> 44.9 us
  waiting for transfers between devices: 54.8 us -> 52.3 us
  other arithmetic: 5.73 us -> 3.64 us
  local copies, waits for them, and re-layouts: 0.26 us -> 2.22 us
    ppermute x34, starting transfers between devices: 51.4 us -> 44.8 us  [move(): return lax.ppermute(value, *route)]
    ppermute x34, waiting for transfers between devices: 51 us -> 48.5 us  [move(): return lax.ppermute(value, *route)]
    add x4, other arithmetic: 2.46 us -> 0.32 us  [with_rows(): return block + lax.pad(rows, jnp.zeros((), rows.dtype), space)]
    unnamed x22 -> x18, local copies, waits for them, and re-layouts: 0.05 us -> 2.02 us
    pallas_call x1 -> x2, Pallas kernels: 11.1 us -> 11.9 us  [contributions(): pl.pallas_call(kernel, out_shape=tuple((jax.ShapeDtypeStruct(s, jnp.bfloa...]
  transfers between devices with their start and end apart: 35 -> 35, of which waited for: 15 -> 18; matrix products, arithmetic and copies ran while one was open for 2% -> 0% of each run, Pallas kernels for 4% -> 7%
where the time goes in v4:
time: 137 us
  waiting for transfers between devices  52.3 us (38%)
  starting transfers between devices  44.9 us (33%)
  Pallas kernels  32.7 us (24%)
  other arithmetic  3.64 us (3%)
  local copies, waits for them, and re-layouts  2.22 us (2%)
  between operations  1.56 us (1%)
    ppermute x34, waiting for transfers between devices, move(): return lax.ppermute(value, *route)  48.5 us
    ppermute x34, starting transfers between devices, move(): return lax.ppermute(value, *route)  44.8 us
    pallas_call x2, Pallas kernels, contributions(): pl.pallas_call(kernel, out_shape=tuple((jax.ShapeDtypeStruct(s, jnp.bfloa...  11.9 us
    pallas_call x1, Pallas kernels, adjoint_plane(): pl.pallas_call(adjoint_kernel, out_shape=(jax.ShapeDtypeStruct(band_shape...  8.36 us
    pallas_call x1, Pallas kernels, residuals(): pl.pallas_call(residual_kernel, out_shape=(jax.ShapeDtypeStruct(observed....  6.61 us
    pallas_call x1, Pallas kernels, kernel_weights(): pl.pallas_call(weights_kernel, out_shape=(shape, shape), grid=(slots // B...  5.78 us
    ppermute x1, waiting for transfers between devices, sum_rings(): swapped = lax.ppermute(given, 'sub', [(i, i ^ 1) for i in range(2 * RING)])  3.82 us
  transfers between devices with their start and end apart: 35, of which 18 were waited for; matrix products, arithmetic and copies ran while one was open for 0% of the time, Pallas kernels for 7%

profile of v4, /device:TPU:24, one launch (start us, length us, event | category | flops | bytes accessed | tf_op | source)
XLA Modules:
  0.0 137.3 jit_solution(510382286486793440)
XLA Ops:
  0.7 0.8 select_reduce_fusion
  1.5 0.5 compare_select_fusion.3.place
  2.0 7.5 %far_parts.1 = (bf16[4,128,256]{2,1,0:T(8,128)(2,1)}, bf16[4,128,256]{2,1,0:T(8,128)(2,1)}, bf16[4,128,256]{2,1,0:T(8,128)(2,1)}, bf16[4,128,256]{2,1,0:T(8,128)...) custom-call(s32[42]{0:T(128)} %compare_select_fusion.3.place, bf16[1,2,704,1216]{3,2,1,0:T(8,128)(2,1)} %bitcast.23, ...), custom_call_target="tpu_custom_call" | custom-call | flops 2147483648 | bytes 8388608 | tf_op jit(solution)/shard_map/far_parts/pallas_call | solution.py:120
  9.6 1.5 %collective-permute-start = (bf16[4,128,256]{2,1,0:T(8,128)(2,1)}, bf16[4,128,256]{2,1,0:T(8,128)(2,1)S(1)}, u32[]{:S(2)}, u32[]{:S(2)}) collective-permute-start(bf16[4,128,256]{2,1,0:T(8,128)(2,1)} %get-tuple-element.42), channel_id=1, source_target_pairs={{0,32},{8,40},{16,48},{24,56},{32,64},{40,72},{48,80},{56,88},{64,... | collective-permute-start | bytes 786440 | tf_op jit(solution)/shard_map/ppermute | solution.py:334
  11.0 1.8 %collective-permute-start.1 = (bf16[4,128,256]{2,1,0:T(8,128)(2,1)}, bf16[4,128,256]{2,1,0:T(8,128)(2,1)S(1)}, u32[]{:S(2)}, u32[]{:S(2)}) collective-permute-start(bf16[4,128,256]{2,1,0:T(8,128)(2,1)} %get-tuple-element.43), channel_id=1, source_target_pairs={{0,96},{8,104},{16,112},{24,120},{32,0},{40,8},{48,16},{56,24},{64... | collective-permute-start | bytes 786440 | tf_op jit(solution)/shard_map/ppermute | solution.py:334
  12.8 0.1 collective-permute-start.2
  12.9 1.9 %collective-permute-start.3 = (bf16[4,128,256]{2,1,0:T(8,128)(2,1)}, bf16[4,128,256]{2,1,0:T(8,128)(2,1)S(1)}, u32[]{:S(2)}, u32[]{:S(2)}) collective-permute-start(bf16[4,128,256]{2,1,0:T(8,128)(2,1)} %get-tuple-element.45), channel_id=1, source_target_pairs={{0,24},{8,0},{16,8},{24,16},{32,56},{40,32},{48,40},{56,48},{64,88... | collective-permute-start | bytes 786440 | tf_op jit(solution)/shard_map/ppermute | solution.py:334
  14.9 1.0 copy-done.7
  15.8 1.0 copy-done.8
  16.8 4.4 %near_parts.1 = (bf16[4,256,256]{2,1,0:T(8,128)(2,1)S(1)}, bf16[4,256,256]{2,1,0:T(8,128)(2,1)S(1)}, bf16[4,256,256]{2,1,0:T(8,128)(2,1)S(1)}, bf16[4,256,256]{2...) custom-call(s32[42]{0:T(128)S(1)} %copy-done, ...), custom_call_target="tpu_custom_call" | custom-call | flops 2147483648 | bytes 8388608 | tf_op jit(solution)/shard_map/near_parts/pallas_call | solution.py:120
  21.3 0.5 collective-permute-done.3
  21.7 0.1 pad_add_fusion
  21.8 0.6 collective-permute-start.7
  22.4 0.1 pad_add_fusion.1
  22.5 2.8 %collective-permute-start.6 = (bf16[4,256,256]{2,1,0:T(8,128)(2,1)S(1)}, bf16[4,256,256]{2,1,0:T(8,128)(2,1)S(1)}, u32[]{:S(2)}, u32[]{:S(2)}) collective-permute-start(bf16[4,256,256]{2,1,0:T(8,128)(2,1)S(1)} %pad_add_fusion.1), channel_id=1, source_target_pairs={{0,8},{8,16},{16,24},{24,0},{32,40},{40,48},{48,56},{56,32},{64,72... | collective-permute-start | bytes 1572872 | tf_op jit(solution)/shard_map/ppermute | solution.py:334
  25.3 0.1 pad_add_fusion.2
  25.4 1.6 %collective-permute-start.5 = (bf16[4,256,256]{2,1,0:T(8,128)(2,1)S(1)}, bf16[4,256,256]{2,1,0:T(8,128)(2,1)S(1)}, u32[]{:S(2)}, u32[]{:S(2)}) collective-permute-start(bf16[4,256,256]{2,1,0:T(8,128)(2,1)S(1)} %pad_add_fusion.2), channel_id=1, source_target_pairs={{0,96},{8,104},{16,112},{24,120},{32,0},{40,8},{48,16},{56,24},{64... | collective-permute-start | bytes 1572872 | tf_op jit(solution)/shard_map/ppermute | solution.py:334
  27.0 0.1 pad_add_fusion.3
  27.1 0.5 collective-permute-start.4
  27.6 5.8 %kernel_weights.1 = (bf16[256,8192]{1,0:T(8,128)(2,1)S(1)}, bf16[256,8192]{1,0:T(8,128)(2,1)S(1)}) custom-call(s32[1,2,8192]{2,1,0:T(2,128)S(1)} %copy-done.2, f32[1,2,8192]{2,1,0:T(2,128)S(1)} %copy-done.3), custom_call_target="tpu_custom_call" | custom-call | flops 41943040 | bytes 8388608 | tf_op jit(solution)/shard_map/kernel_weights/pallas_call | solution.py:164
  33.4 1.8 %collective-permute-done.7 = bf16[4,256,256]{2,1,0:T(8,128)(2,1)S(1)} collective-permute-done((bf16[4,256,256]{2,1,0:T(8,128)(2,1)S(1)}, bf16[4,256,256]{2,1,0:T(8,128)(2,1)S(1)}, u32[]{:S(2)}, u32[]{:S(2)}) %collective-permute-start.7) | collective-permute-done | bytes 524320 | tf_op jit(solution)/shard_map/ppermute | solution.py:334
  35.2 1.8 %collective-permute-done.5 = bf16[4,256,256]{2,1,0:T(8,128)(2,1)S(1)} collective-permute-done((bf16[4,256,256]{2,1,0:T(8,128)(2,1)S(1)}, bf16[4,256,256]{2,1,0:T(8,128)(2,1)S(1)}, u32[]{:S(2)}, u32[]{:S(2)}) %collective-permute-start.5) | collective-permute-done | bytes 524320 | tf_op jit(solution)/shard_map/ppermute | solution.py:334
  37.0 2.6 %collective-permute-done.4 = bf16[4,256,256]{2,1,0:T(8,128)(2,1)S(1)} collective-permute-done((bf16[4,256,256]{2,1,0:T(8,128)(2,1)S(1)}, bf16[4,256,256]{2,1,0:T(8,128)(2,1)S(1)}, u32[]{:S(2)}, u32[]{:S(2)}) %collective-permute-start.4) | collective-permute-done | bytes 524320 | tf_op jit(solution)/shard_map/ppermute | solution.py:334
  39.6 0.4 add_convert_fusion
  40.1 0.3 collective-permute-start.13
  40.4 1.9 %collective-permute-start.12 = (bf16[1,256,256]{2,1,0:T(8,128)(2,1)S(1)}, bf16[1,256,256]{2,1,0:T(8,128)(2,1)S(1)}, u32[]{:S(2)}, u32[]{:S(2)}) collective-permute-start(bf16[1,256,256]{2,1,0:T(8,128)(2,1)S(1)} %get-tuple-element.85), channel_id=1, source_target_pairs={{0,96},{8,104},{16,112},{24,120},{32,0},{40,8},{48,16},{56,24},{64... | collective-permute-start | bytes 393224 | tf_op jit(solution)/shard_map/ppermute | solution.py:334
  42.3 0.2 collective-permute-start.11
  42.5 0.1 collective-permute-start.10
  42.6 1.3 collective-permute-start.9
  43.9 2.9 %collective-permute-done.13.refs_7_ = bf16[1,256,256]{2,1,0:T(8,128)(2,1)S(1)} collective-permute-done((bf16[1,256,256]{2,1,0:T(8,128)(2,1)S(1)}, bf16[1,256,256]{2,1,0:T(8,128)(2,1)S(1)}, u32[]{:S(2)}, u32[]{:S(2)}) %collective-permute-start.13) | collective-permute-done | bytes 131104 | tf_op jit(solution)/shard_map/ppermute | solution.py:334
  46.8 0.3 collective-permute-start.8
  47.8 0.7 collective-permute-done.11.refs_5_
  48.5 0.7 collective-permute-done.10.refs_3_
  49.2 1.1 collective-permute-done.9.refs_2_
  50.3 1.5 %collective-permute-done.8.refs_1_ = bf16[1,256,256]{2,1,0:T(8,128)(2,1)S(1)} collective-permute-done((bf16[1,256,256]{2,1,0:T(8,128)(2,1)S(1)}, bf16[1,256,256]{2,1,0:T(8,128)(2,1)S(1)}, u32[]{:S(2)}, u32[]{:S(2)}) %collective-permute-start.8) | collective-permute-done | bytes 131104 | tf_op jit(solution)/shard_map/ppermute | solution.py:334
  51.8 6.6 %residuals.1 = (f32[1,2,8192]{2,1,0:T(2,128)}, bf16[1,256,256]{2,1,0:T(8,128)(2,1)S(1)}, bf16[1,256,256]{2,1,0:T(8,128)(2,1)S(1)}) custom-call(s32[1]{0:T(128)S(6)} %copy.10.count, bf16[1,256,256]{2,1,0:T(8,128)(2,1)S(1)} %get-tuple-element.91.refs_0_, bf16[1,256,256]{2,1,0:T(8,128)(2,1)S(1)} %collective-permute-done.8.refs_1_, ...), custom_call_target="tpu_custom_call" | custom-call | flops 4294967296 | bytes 8388608 | tf_op jit(solution)/shard_map/residuals/pallas_call | solution.py:216
  58.4 1.5 %collective-permute-start.23 = (bf16[1,256,256]{2,1,0:T(8,128)(2,1)S(1)}, bf16[1,256,256]{2,1,0:T(8,128)(2,1)S(1)}, u32[]{:S(2)}, u32[]{:S(2)}) collective-permute-start(bf16[1,256,256]{2,1,0:T(8,128)(2,1)S(1)} %get-tuple-element.77), channel_id=1, source_target_pairs={{0,8},{8,16},{16,24},{24,0},{32,40},{40,48},{48,56},{56,32},{64,72... | collective-permute-start | bytes 393224 | tf_op jit(solution)/shard_map/ppermute | solution.py:334
  59.9 0.5 collective-permute-start.22
  60.5 3.2 %collective-permute-start.14 = (bf16[1,256,256]{2,1,0:T(8,128)(2,1)S(1)}, bf16[1,256,256]{2,1,0:T(8,128)(2,1)S(1)}, u32[]{:S(2)}, u32[]{:S(2)}) collective-permute-start(bf16[1,256,256]{2,1,0:T(8,128)(2,1)S(1)} %get-tuple-element.76), channel_id=1, source_target_pairs={{0,96},{8,104},{16,112},{24,120},{32,0},{40,8},{48,16},{56,24},{64... | collective-permute-start | bytes 393224 | tf_op jit(solution)/shard_map/ppermute | solution.py:334
  63.7 2.8 %collective-permute-start.24 = (bf16[1,128,256]{2,1,0:T(8,128)(2,1)S(1)}, bf16[1,128,256]{2,1,0:T(8,128)(2,1)S(1)}, u32[]{:S(2)}, u32[]{:S(2)}) collective-permute-start(bf16[1,128,256]{2,1,0:T(8,128)(2,1)S(1)} %slice.118), channel_id=1, source_target_pairs={{0,8},{8,16},{16,24},{24,0},{32,40},{40,48},{48,56},{56,32},{64,72... | collective-permute-start | bytes 196616 | tf_op jit(solution)/shard_map/ppermute | solution.py:334
  66.5 0.1 collective-permute-start.25
  66.7 3.3 %collective-permute-start.17 = (bf16[1,128,256]{2,1,0:T(8,128)(2,1)S(1)}, bf16[1,128,256]{2,1,0:T(8,128)(2,1)S(1)}, u32[]{:S(2)}, u32[]{:S(2)}) collective-permute-start(bf16[1,128,256]{2,1,0:T(8,128)(2,1)S(1)} %slice.115), channel_id=1, source_target_pairs={{0,96},{8,104},{16,112},{24,120},{32,0},{40,8},{48,16},{56,24},{64... | collective-permute-start | bytes 196616 | tf_op jit(solution)/shard_map/ppermute | solution.py:334
  70.0 2.0 %collective-permute-done.25 = bf16[1,128,256]{2,1,0:T(8,128)(2,1)S(1)} collective-permute-done((bf16[1,128,256]{2,1,0:T(8,128)(2,1)S(1)}, bf16[1,128,256]{2,1,0:T(8,128)(2,1)S(1)}, u32[]{:S(2)}, u32[]{:S(2)}) %collective-permute-start.25) | collective-permute-done | bytes 65568 | tf_op jit(solution)/shard_map/ppermute | solution.py:334
  72.1 0.3 collective-permute-start.27
  72.4 3.0 %collective-permute-start.26 = (bf16[4,256,256]{2,1,0:T(8,128)(2,1)S(1)}, bf16[4,256,256]{2,1,0:T(8,128)(2,1)S(1)}, u32[]{:S(2)}, u32[]{:S(2)}) collective-permute-start(bf16[4,256,256]{2,1,0:T(8,128)(2,1)S(1)} %maximum_maximum_fusion.1.refs_5_), channel_id=1, source_target_pairs={{0,96},{8,104},{16,112},{24,120},{32,0},{40,8},{48,16},{56,24},{64... | collective-permute-start | bytes 1572872 | tf_op jit(solution)/shard_map/ppermute | solution.py:334
  75.5 1.2 collective-permute-start.19
  76.7 0.9 collective-permute-start.18
  77.6 7.8 %collective-permute-done.27.refs_7_ = bf16[4,256,256]{2,1,0:T(8,128)(2,1)S(1)} collective-permute-done((bf16[4,256,256]{2,1,0:T(8,128)(2,1)S(1)}, bf16[4,256,256]{2,1,0:T(8,128)(2,1)S(1)}, u32[]{:S(2)}, u32[]{:S(2)}) %collective-permute-start.27) | collective-permute-done | bytes 524320 | tf_op jit(solution)/shard_map/ppermute | solution.py:334
  85.5 3.3 %collective-permute-start.29 = (bf16[4,128,256]{2,1,0:T(8,128)(2,1)S(1)}, bf16[4,128,256]{2,1,0:T(8,128)(2,1)S(1)}, u32[]{:S(2)}, u32[]{:S(2)}) collective-permute-start(bf16[4,128,256]{2,1,0:T(8,128)(2,1)S(1)} %slice.121), channel_id=1, source_target_pairs={{0,96},{8,104},{16,112},{24,120},{32,0},{40,8},{48,16},{56,24},{64... | collective-permute-start | bytes 786440 | tf_op jit(solution)/shard_map/ppermute | solution.py:334
  88.8 1.2 collective-permute-start.20
  90.1 1.1 collective-permute-start.21
  91.2 1.8 %collective-permute-done.28.refs_8_ = bf16[4,128,256]{2,1,0:T(8,128)(2,1)S(1)} collective-permute-done((bf16[4,128,256]{2,1,0:T(8,128)(2,1)S(1)}, bf16[4,128,256]{2,1,0:T(8,128)(2,1)S(1)}, u32[]{:S(2)}, u32[]{:S(2)}) %collective-permute-start.28) | collective-permute-done | bytes 262176 | tf_op jit(solution)/shard_map/ppermute | solution.py:334
  93.0 2.2 %collective-permute-done.20.refs_3_ = bf16[4,128,256]{2,1,0:T(8,128)(2,1)S(1)} collective-permute-done((bf16[4,128,256]{2,1,0:T(8,128)(2,1)S(1)}, bf16[4,128,256]{2,1,0:T(8,128)(2,1)S(1)}, u32[]{:S(2)}, u32[]{:S(2)}) %collective-permute-start.20) | collective-permute-done | bytes 262176 | tf_op jit(solution)/shard_map/ppermute | solution.py:334
  95.2 2.7 %collective-permute-done.21.refs_4_ = bf16[4,128,256]{2,1,0:T(8,128)(2,1)S(1)} collective-permute-done((bf16[4,128,256]{2,1,0:T(8,128)(2,1)S(1)}, bf16[4,128,256]{2,1,0:T(8,128)(2,1)S(1)}, u32[]{:S(2)}, u32[]{:S(2)}) %collective-permute-start.21) | collective-permute-done | bytes 262176 | tf_op jit(solution)/shard_map/ppermute | solution.py:334
  97.9 8.4 %adjoint_plane.1 = (bf16[4,2,152,704]{3,2,1,0:T(8,128)(2,1)S(1)}, bf16[4,2,152,704]{3,2,1,0:T(8,128)(2,1)S(1)}) custom-call(s32[42]{0:T(128)S(1)} %copy-done, bf16[4,256,256]{2,1,0:T(8,128)(2,1)S(1)} %maximum_maximum_fusion.refs_0_, bf16[4,256,256]{2,1,0:T(8,128)(2,1)S(1)} %collective-permute-done.18.refs_1_, ...), custom_call_target="tpu_custom_call" | custom-call | flops 4294967296 | bytes 8388608 | tf_op jit(solution)/shard_map/adjoint_plane/pallas_call | solution.py:294
  106.3 0.1 collective-permute-start.30
  106.4 3.8 %collective-permute-done.30 = bf16[4,2,152,704]{3,2,1,0:T(8,128)(2,1)S(1)} collective-permute-done((bf16[4,2,152,704]{3,2,1,0:T(8,128)(2,1)S(1)}, bf16[4,2,152,704]{3,2,1,0:T(8,128)(2,1)S(1)}, u32[]{:S(2)}, u32[]{:S(2)}) %collective-permute-start.30) | collective-permute-done | bytes 1712160 | tf_op jit(solution)/shard_map/ppermute | solution.py:399
  110.3 4.1 %collective-permute-start.32 = (bf16[152,704]{1,0:T(8,128)(2,1)S(1)}, bf16[152,704]{1,0:T(8,128)(2,1)S(1)}, u32[]{:S(2)}, u32[]{:S(2)}) collective-permute-start(bf16[152,704]{1,0:T(8,128)(2,1)S(1)} %get-tuple-element.92), channel_id=1, source_target_pairs={{0,6},{1,7},{2,0},{3,1},{4,2},{5,3},{6,4},{7,5},{8,14},{9,15},{10,... | collective-permute-start | bytes 642056 | tf_op jit(solution)/shard_map/ppermute | solution.py:334
  114.4 5.2 %collective-permute-done.32 = bf16[152,704]{1,0:T(8,128)(2,1)S(1)} collective-permute-done((bf16[152,704]{1,0:T(8,128)(2,1)S(1)}, bf16[152,704]{1,0:T(8,128)(2,1)S(1)}, u32[]{:S(2)}, u32[]{:S(2)}) %collective-permute-start.32) | collective-permute-done | bytes 214048 | tf_op jit(solution)/shard_map/ppermute | solution.py:334
  119.7 3.4 %collective-permute-done.31 = bf16[152,704]{1,0:T(8,128)(2,1)S(1)} collective-permute-done((bf16[152,704]{1,0:T(8,128)(2,1)S(1)}, bf16[152,704]{1,0:T(8,128)(2,1)S(1)}, u32[]{:S(2)}, u32[]{:S(2)}) %collective-permute-start.31) | collective-permute-done | bytes 214048 | tf_op jit(solution)/shard_map/ppermute | solution.py:334
  123.1 0.2 fusion.5
  123.3 3.2 %collective-permute-start.34 = (bf16[2,152,704]{2,1,0:T(8,128)(2,1)S(1)}, bf16[2,152,704]{2,1,0:T(8,128)(2,1)S(1)}, u32[]{:S(2)}, u32[]{:S(2)}) collective-permute-start(bf16[2,152,704]{2,1,0:T(8,128)(2,1)S(1)} %get-tuple-element.83), channel_id=1, source_target_pairs={{0,6},{1,7},{2,0},{3,1},{4,2},{5,3},{6,4},{7,5},{8,14},{9,15},{10,... | collective-permute-start | bytes 1284104 | tf_op jit(solution)/shard_map/ppermute | solution.py:334
  126.5 9.6 %collective-permute-done.33 = bf16[2,152,704]{2,1,0:T(8,128)(2,1)S(1)} collective-permute-done((bf16[2,152,704]{2,1,0:T(8,128)(2,1)S(1)}, bf16[2,152,704]{2,1,0:T(8,128)(2,1)S(1)}, u32[]{:S(2)}, u32[]{:S(2)}) %collective-permute-start.33) | collective-permute-done | bytes 428064 | tf_op jit(solution)/shard_map/ppermute | solution.py:334
  136.1 1.2 fusion.1
  (53 shorter events, 0.7 us)
Async XLA Ops:
  2.0 12.8 %copy-start = (s32[42]{0:T(128)S(1)}, s32[42]{0:T(128)}, u32[]{:S(2)}) copy-start(s32[42]{0:T(128)} %compare_select_fusion.3.place) | copy-start | bytes 508
  2.0 12.8 %copy-start.1 = (bf16[1,2,1216,704]{2,3,1,0:T(8,128)(2,1)S(1)}, bf16[1,2,1216,704]{2,3,1,0:T(8,128)(2,1)}, u32[]{:S(2)}) copy-start(bf16[1,2,1216,704]{2,3,1,0:T(8,128)(2,1)} %param.8) | copy-start | bytes 10272772
  2.0 12.8 %copy-start.5 = (f32[2,256,256]{2,1,0:T(8,128)S(1)}, f32[2,256,256]{2,1,0:T(8,128)}, u32[]{:S(2)}) copy-start(f32[2,256,256]{2,1,0:T(8,128)} %constant.49.clone.base.refs_10_) | copy-start | bytes 1572868
  2.0 12.8 %copy-start.6 = (f32[16,2,256]{2,1,0:T(2,128)S(1)}, f32[16,2,256]{2,1,0:T(2,128)}, u32[]{:S(2)}) copy-start(f32[16,2,256]{2,1,0:T(2,128)} %constant.50.clone.left.right.refs_11_.refs_12_) | copy-start | bytes 98308
  9.6 11.7 %collective-permute-start = (bf16[4,128,256]{2,1,0:T(8,128)(2,1)}, bf16[4,128,256]{2,1,0:T(8,128)(2,1)S(1)}, u32[]{:S(2)}, u32[]{:S(2)}) collective-permute-start(bf16[4,128,256]{2,1,0:T(8,128)(2,1)} %get-tuple-element.42), channel_id=1, source_target_pairs={{0,32},{8,40},{16,48},{24,56},{32,64},{40,72},{48,80},{56,88},{64,... | collective-permute-start | bytes 786440 | tf_op jit(solution)/shard_map/ppermute | solution.py:334
  11.0 10.2 %collective-permute-start.1 = (bf16[4,128,256]{2,1,0:T(8,128)(2,1)}, bf16[4,128,256]{2,1,0:T(8,128)(2,1)S(1)}, u32[]{:S(2)}, u32[]{:S(2)}) collective-permute-start(bf16[4,128,256]{2,1,0:T(8,128)(2,1)} %get-tuple-element.43), channel_id=1, source_target_pairs={{0,96},{8,104},{16,112},{24,120},{32,0},{40,8},{48,16},{56,24},{64... | collective-permute-start | bytes 786440 | tf_op jit(solution)/shard_map/ppermute | solution.py:334
  12.8 8.4 %collective-permute-start.2 = (bf16[4,128,256]{2,1,0:T(8,128)(2,1)}, bf16[4,128,256]{2,1,0:T(8,128)(2,1)S(1)}, u32[]{:S(2)}, u32[]{:S(2)}) collective-permute-start(bf16[4,128,256]{2,1,0:T(8,128)(2,1)} %get-tuple-element.44), channel_id=1, source_target_pairs={{0,8},{8,16},{16,24},{24,0},{32,40},{40,48},{48,56},{56,32},{64,72... | collective-permute-start | bytes 786440 | tf_op jit(solution)/shard_map/ppermute | solution.py:334
  12.9 8.8 %collective-permute-start.3 = (bf16[4,128,256]{2,1,0:T(8,128)(2,1)}, bf16[4,128,256]{2,1,0:T(8,128)(2,1)S(1)}, u32[]{:S(2)}, u32[]{:S(2)}) collective-permute-start(bf16[4,128,256]{2,1,0:T(8,128)(2,1)} %get-tuple-element.45), channel_id=1, source_target_pairs={{0,24},{8,0},{16,8},{24,16},{32,56},{40,32},{48,40},{56,48},{64,88... | collective-permute-start | bytes 786440 | tf_op jit(solution)/shard_map/ppermute | solution.py:334
  14.8 1.0 copy-start.7
  15.8 1.0 copy-start.8
  21.8 5.8 %copy-start.2 = (s32[1,2,8192]{2,1,0:T(2,128)S(1)}, s32[1,2,8192]{2,1,0:T(2,128)}, u32[]{:S(2)}) copy-start(s32[1,2,8192]{2,1,0:T(2,128)} %offsets) | copy-start | bytes 196612
  21.8 5.8 %copy-start.3 = (f32[1,2,8192]{2,1,0:T(2,128)S(1)}, f32[1,2,8192]{2,1,0:T(2,128)}, u32[]{:S(2)}) copy-start(f32[1,2,8192]{2,1,0:T(2,128)} %fractions.1) | copy-start | bytes 196612
  21.8 13.4 %collective-permute-start.7 = (bf16[4,256,256]{2,1,0:T(8,128)(2,1)S(1)}, bf16[4,256,256]{2,1,0:T(8,128)(2,1)S(1)}, u32[]{:S(2)}, u32[]{:S(2)}) collective-permute-start(bf16[4,256,256]{2,1,0:T(8,128)(2,1)S(1)} %pad_add_fusion), channel_id=1, source_target_pairs={{0,24},{8,0},{16,8},{24,16},{32,56},{40,32},{48,40},{56,48},{64,88... | collective-permute-start | bytes 1572872 | tf_op jit(solution)/shard_map/ppermute | solution.py:334
  22.5 12.7 %collective-permute-start.6 = (bf16[4,256,256]{2,1,0:T(8,128)(2,1)S(1)}, bf16[4,256,256]{2,1,0:T(8,128)(2,1)S(1)}, u32[]{:S(2)}, u32[]{:S(2)}) collective-permute-start(bf16[4,256,256]{2,1,0:T(8,128)(2,1)S(1)} %pad_add_fusion.1), channel_id=1, source_target_pairs={{0,8},{8,16},{16,24},{24,0},{32,40},{40,48},{48,56},{56,32},{64,72... | collective-permute-start | bytes 1572872 | tf_op jit(solution)/shard_map/ppermute | solution.py:334
  25.4 11.6 %collective-permute-start.5 = (bf16[4,256,256]{2,1,0:T(8,128)(2,1)S(1)}, bf16[4,256,256]{2,1,0:T(8,128)(2,1)S(1)}, u32[]{:S(2)}, u32[]{:S(2)}) collective-permute-start(bf16[4,256,256]{2,1,0:T(8,128)(2,1)S(1)} %pad_add_fusion.2), channel_id=1, source_target_pairs={{0,96},{8,104},{16,112},{24,120},{32,0},{40,8},{48,16},{56,24},{64... | collective-permute-start | bytes 1572872 | tf_op jit(solution)/shard_map/ppermute | solution.py:334
  27.1 12.5 %collective-permute-start.4 = (bf16[4,256,256]{2,1,0:T(8,128)(2,1)S(1)}, bf16[4,256,256]{2,1,0:T(8,128)(2,1)S(1)}, u32[]{:S(2)}, u32[]{:S(2)}) collective-permute-start(bf16[4,256,256]{2,1,0:T(8,128)(2,1)S(1)} %pad_add_fusion.3), channel_id=1, source_target_pairs={{0,32},{8,40},{16,48},{24,56},{32,64},{40,72},{48,80},{56,88},{64,... | collective-permute-start | bytes 1572872 | tf_op jit(solution)/shard_map/ppermute | solution.py:334
  40.0 11.8 %copy-start.4 = (f32[1,2,8192]{2,1,0:T(2,128)S(1)}, f32[1,2,8192]{2,1,0:T(2,128)}, u32[]{:S(2)}) copy-start(f32[1,2,8192]{2,1,0:T(2,128)} %refs_10_.2) | copy-start | bytes 196612
  40.1 6.7 %collective-permute-start.13 = (bf16[1,256,256]{2,1,0:T(8,128)(2,1)S(1)}, bf16[1,256,256]{2,1,0:T(8,128)(2,1)S(1)}, u32[]{:S(2)}, u32[]{:S(2)}) collective-permute-start(bf16[1,256,256]{2,1,0:T(8,128)(2,1)S(1)} %get-tuple-element.84), channel_id=1, source_target_pairs={{0,64},{8,72},{16,80},{24,88},{32,96},{40,104},{48,112},{56,120},{... | collective-permute-start | bytes 393224 | tf_op jit(solution)/shard_map/ppermute | solution.py:334
  40.4 7.4 %collective-permute-start.12 = (bf16[1,256,256]{2,1,0:T(8,128)(2,1)S(1)}, bf16[1,256,256]{2,1,0:T(8,128)(2,1)S(1)}, u32[]{:S(2)}, u32[]{:S(2)}) collective-permute-start(bf16[1,256,256]{2,1,0:T(8,128)(2,1)S(1)} %get-tuple-element.85), channel_id=1, source_target_pairs={{0,96},{8,104},{16,112},{24,120},{32,0},{40,8},{48,16},{56,24},{64... | collective-permute-start | bytes 393224 | tf_op jit(solution)/shard_map/ppermute | solution.py:334
  42.3 6.2 %collective-permute-start.11 = (bf16[1,256,256]{2,1,0:T(8,128)(2,1)S(1)}, bf16[1,256,256]{2,1,0:T(8,128)(2,1)S(1)}, u32[]{:S(2)}, u32[]{:S(2)}) collective-permute-start(bf16[1,256,256]{2,1,0:T(8,128)(2,1)S(1)} %get-tuple-element.86), channel_id=1, source_target_pairs={{0,32},{8,40},{16,48},{24,56},{32,64},{40,72},{48,80},{56,88},{64,... | collective-permute-start | bytes 393224 | tf_op jit(solution)/shard_map/ppermute | solution.py:334
  42.5 6.7 %collective-permute-start.10 = (bf16[1,256,256]{2,1,0:T(8,128)(2,1)S(1)}, bf16[1,256,256]{2,1,0:T(8,128)(2,1)S(1)}, u32[]{:S(2)}, u32[]{:S(2)}) collective-permute-start(bf16[1,256,256]{2,1,0:T(8,128)(2,1)S(1)} %get-tuple-element.88), channel_id=1, source_target_pairs={{0,16},{8,24},{16,0},{24,8},{32,48},{40,56},{48,32},{56,40},{64,80... | collective-permute-start | bytes 393224 | tf_op jit(solution)/shard_map/ppermute | solution.py:334
  42.6 7.6 %collective-permute-start.9 = (bf16[1,256,256]{2,1,0:T(8,128)(2,1)S(1)}, bf16[1,256,256]{2,1,0:T(8,128)(2,1)S(1)}, u32[]{:S(2)}, u32[]{:S(2)}) collective-permute-start(bf16[1,256,256]{2,1,0:T(8,128)(2,1)S(1)} %get-tuple-element.89), channel_id=1, source_target_pairs={{0,24},{8,0},{16,8},{24,16},{32,56},{40,32},{48,40},{56,48},{64,88... | collective-permute-start | bytes 393224 | tf_op jit(solution)/shard_map/ppermute | solution.py:334
  46.8 5.0 %collective-permute-start.8 = (bf16[1,256,256]{2,1,0:T(8,128)(2,1)S(1)}, bf16[1,256,256]{2,1,0:T(8,128)(2,1)S(1)}, u32[]{:S(2)}, u32[]{:S(2)}) collective-permute-start(bf16[1,256,256]{2,1,0:T(8,128)(2,1)S(1)} %get-tuple-element.90), channel_id=1, source_target_pairs={{0,8},{8,16},{16,24},{24,0},{32,40},{40,48},{48,56},{56,32},{64,72... | collective-permute-start | bytes 393224 | tf_op jit(solution)/shard_map/ppermute | solution.py:334
  58.4 5.3 %collective-permute-start.23 = (bf16[1,256,256]{2,1,0:T(8,128)(2,1)S(1)}, bf16[1,256,256]{2,1,0:T(8,128)(2,1)S(1)}, u32[]{:S(2)}, u32[]{:S(2)}) collective-permute-start(bf16[1,256,256]{2,1,0:T(8,128)(2,1)S(1)} %get-tuple-element.77), channel_id=1, source_target_pairs={{0,8},{8,16},{16,24},{24,0},{32,40},{40,48},{48,56},{56,32},{64,72... | collective-permute-start | bytes 393224 | tf_op jit(solution)/shard_map/ppermute | solution.py:334
  59.9 6.6 %collective-permute-start.22 = (bf16[1,256,256]{2,1,0:T(8,128)(2,1)S(1)}, bf16[1,256,256]{2,1,0:T(8,128)(2,1)S(1)}, u32[]{:S(2)}, u32[]{:S(2)}) collective-permute-start(bf16[1,256,256]{2,1,0:T(8,128)(2,1)S(1)} %get-tuple-element.77), channel_id=1, source_target_pairs={{0,24},{8,0},{16,8},{24,16},{32,56},{40,32},{48,40},{56,48},{64,88... | collective-permute-start | bytes 393224 | tf_op jit(solution)/shard_map/ppermute | solution.py:334
  60.4 6.2 %collective-permute-start.15 = (bf16[1,256,256]{2,1,0:T(8,128)(2,1)S(1)}, bf16[1,256,256]{2,1,0:T(8,128)(2,1)S(1)}, u32[]{:S(2)}, u32[]{:S(2)}) collective-permute-start(bf16[1,256,256]{2,1,0:T(8,128)(2,1)S(1)} %get-tuple-element.76), channel_id=1, source_target_pairs={{0,32},{8,40},{16,48},{24,56},{32,64},{40,72},{48,80},{56,88},{64,... | collective-permute-start | bytes 393224 | tf_op jit(solution)/shard_map/ppermute | solution.py:334
  60.5 6.2 %collective-permute-start.14 = (bf16[1,256,256]{2,1,0:T(8,128)(2,1)S(1)}, bf16[1,256,256]{2,1,0:T(8,128)(2,1)S(1)}, u32[]{:S(2)}, u32[]{:S(2)}) collective-permute-start(bf16[1,256,256]{2,1,0:T(8,128)(2,1)S(1)} %get-tuple-element.76), channel_id=1, source_target_pairs={{0,96},{8,104},{16,112},{24,120},{32,0},{40,8},{48,16},{56,24},{64... | collective-permute-start | bytes 393224 | tf_op jit(solution)/shard_map/ppermute | solution.py:334
  63.7 6.3 %collective-permute-start.24 = (bf16[1,128,256]{2,1,0:T(8,128)(2,1)S(1)}, bf16[1,128,256]{2,1,0:T(8,128)(2,1)S(1)}, u32[]{:S(2)}, u32[]{:S(2)}) collective-permute-start(bf16[1,128,256]{2,1,0:T(8,128)(2,1)S(1)} %slice.118), channel_id=1, source_target_pairs={{0,8},{8,16},{16,24},{24,0},{32,40},{40,48},{48,56},{56,32},{64,72... | collective-permute-start | bytes 196616 | tf_op jit(solution)/shard_map/ppermute | solution.py:334
  66.5 5.5 %collective-permute-start.25 = (bf16[1,128,256]{2,1,0:T(8,128)(2,1)S(1)}, bf16[1,128,256]{2,1,0:T(8,128)(2,1)S(1)}, u32[]{:S(2)}, u32[]{:S(2)}) collective-permute-start(bf16[1,128,256]{2,1,0:T(8,128)(2,1)S(1)} %slice.119), channel_id=1, source_target_pairs={{0,24},{8,0},{16,8},{24,16},{32,56},{40,32},{48,40},{56,48},{64,88... | collective-permute-start | bytes 196616 | tf_op jit(solution)/shard_map/ppermute | solution.py:334
  66.6 8.8 %collective-permute-start.16 = (bf16[1,128,256]{2,1,0:T(8,128)(2,1)S(1)}, bf16[1,128,256]{2,1,0:T(8,128)(2,1)S(1)}, u32[]{:S(2)}, u32[]{:S(2)}) collective-permute-start(bf16[1,128,256]{2,1,0:T(8,128)(2,1)S(1)} %slice.114), channel_id=1, source_target_pairs={{0,32},{8,40},{16,48},{24,56},{32,64},{40,72},{48,80},{56,88},{64,... | collective-permute-start | bytes 196616 | tf_op jit(solution)/shard_map/ppermute | solution.py:334
  66.7 8.7 %collective-permute-start.17 = (bf16[1,128,256]{2,1,0:T(8,128)(2,1)S(1)}, bf16[1,128,256]{2,1,0:T(8,128)(2,1)S(1)}, u32[]{:S(2)}, u32[]{:S(2)}) collective-permute-start(bf16[1,128,256]{2,1,0:T(8,128)(2,1)S(1)} %slice.115), channel_id=1, source_target_pairs={{0,96},{8,104},{16,112},{24,120},{32,0},{40,8},{48,16},{56,24},{64... | collective-permute-start | bytes 196616 | tf_op jit(solution)/shard_map/ppermute | solution.py:334
  72.1 13.3 %collective-permute-start.27 = (bf16[4,256,256]{2,1,0:T(8,128)(2,1)S(1)}, bf16[4,256,256]{2,1,0:T(8,128)(2,1)S(1)}, u32[]{:S(2)}, u32[]{:S(2)}) collective-permute-start(bf16[4,256,256]{2,1,0:T(8,128)(2,1)S(1)} %maximum_maximum_fusion.1.refs_5_), channel_id=1, source_target_pairs={{0,32},{8,40},{16,48},{24,56},{32,64},{40,72},{48,80},{56,88},{64,... | collective-permute-start | bytes 1572872 | tf_op jit(solution)/shard_map/ppermute | solution.py:334
  72.4 13.0 %collective-permute-start.26 = (bf16[4,256,256]{2,1,0:T(8,128)(2,1)S(1)}, bf16[4,256,256]{2,1,0:T(8,128)(2,1)S(1)}, u32[]{:S(2)}, u32[]{:S(2)}) collective-permute-start(bf16[4,256,256]{2,1,0:T(8,128)(2,1)S(1)} %maximum_maximum_fusion.1.refs_5_), channel_id=1, source_target_pairs={{0,96},{8,104},{16,112},{24,120},{32,0},{40,8},{48,16},{56,24},{64... | collective-permute-start | bytes 1572872 | tf_op jit(solution)/shard_map/ppermute | solution.py:334
  75.5 13.3 %collective-permute-start.19 = (bf16[4,256,256]{2,1,0:T(8,128)(2,1)S(1)}, bf16[4,256,256]{2,1,0:T(8,128)(2,1)S(1)}, u32[]{:S(2)}, u32[]{:S(2)}) collective-permute-start(bf16[4,256,256]{2,1,0:T(8,128)(2,1)S(1)} %maximum_maximum_fusion.refs_0_), channel_id=1, source_target_pairs={{0,8},{8,16},{16,24},{24,0},{32,40},{40,48},{48,56},{56,32},{64,72... | collective-permute-start | bytes 1572872 | tf_op jit(solution)/shard_map/ppermute | solution.py:334
  76.7 13.4 %collective-permute-start.18 = (bf16[4,256,256]{2,1,0:T(8,128)(2,1)S(1)}, bf16[4,256,256]{2,1,0:T(8,128)(2,1)S(1)}, u32[]{:S(2)}, u32[]{:S(2)}) collective-permute-start(bf16[4,256,256]{2,1,0:T(8,128)(2,1)S(1)} %maximum_maximum_fusion.refs_0_), channel_id=1, source_target_pairs={{0,24},{8,0},{16,8},{24,16},{32,56},{40,32},{48,40},{56,48},{64,88... | collective-permute-start | bytes 1572872 | tf_op jit(solution)/shard_map/ppermute | solution.py:334
  85.4 7.7 %collective-permute-start.28 = (bf16[4,128,256]{2,1,0:T(8,128)(2,1)S(1)}, bf16[4,128,256]{2,1,0:T(8,128)(2,1)S(1)}, u32[]{:S(2)}, u32[]{:S(2)}) collective-permute-start(bf16[4,128,256]{2,1,0:T(8,128)(2,1)S(1)} %slice.120), channel_id=1, source_target_pairs={{0,32},{8,40},{16,48},{24,56},{32,64},{40,72},{48,80},{56,88},{64,... | collective-permute-start | bytes 786440 | tf_op jit(solution)/shard_map/ppermute | solution.py:334
  85.5 7.5 %collective-permute-start.29 = (bf16[4,128,256]{2,1,0:T(8,128)(2,1)S(1)}, bf16[4,128,256]{2,1,0:T(8,128)(2,1)S(1)}, u32[]{:S(2)}, u32[]{:S(2)}) collective-permute-start(bf16[4,128,256]{2,1,0:T(8,128)(2,1)S(1)} %slice.121), channel_id=1, source_target_pairs={{0,96},{8,104},{16,112},{24,120},{32,0},{40,8},{48,16},{56,24},{64... | collective-permute-start | bytes 786440 | tf_op jit(solution)/shard_map/ppermute | solution.py:334
  88.8 6.4 %collective-permute-start.20 = (bf16[4,128,256]{2,1,0:T(8,128)(2,1)S(1)}, bf16[4,128,256]{2,1,0:T(8,128)(2,1)S(1)}, u32[]{:S(2)}, u32[]{:S(2)}) collective-permute-start(bf16[4,128,256]{2,1,0:T(8,128)(2,1)S(1)} %slice.116), channel_id=1, source_target_pairs={{0,8},{8,16},{16,24},{24,0},{32,40},{40,48},{48,56},{56,32},{64,72... | collective-permute-start | bytes 786440 | tf_op jit(solution)/shard_map/ppermute | solution.py:334
  90.1 7.9 %collective-permute-start.21 = (bf16[4,128,256]{2,1,0:T(8,128)(2,1)S(1)}, bf16[4,128,256]{2,1,0:T(8,128)(2,1)S(1)}, u32[]{:S(2)}, u32[]{:S(2)}) collective-permute-start(bf16[4,128,256]{2,1,0:T(8,128)(2,1)S(1)} %slice.117), channel_id=1, source_target_pairs={{0,24},{8,0},{16,8},{24,16},{32,56},{40,32},{48,40},{56,48},{64,88... | collective-permute-start | bytes 786440 | tf_op jit(solution)/shard_map/ppermute | solution.py:334
  106.3 3.9 %collective-permute-start.30 = (bf16[4,2,152,704]{3,2,1,0:T(8,128)(2,1)S(1)}, bf16[4,2,152,704]{3,2,1,0:T(8,128)(2,1)S(1)}, u32[]{:S(2)}, u32[]{:S(2)}) collective-permute-start(bf16[4,2,152,704]{3,2,1,0:T(8,128)(2,1)S(1)} %get-tuple-element.79), channel_id=1, source_target_pairs={{0,1},{1,0},{2,3},{3,2},{4,5},{5,4},{6,7},{7,6},{8,9},{9,8},{10,11... | collective-permute-start | bytes 5136392 | tf_op jit(solution)/shard_map/ppermute | solution.py:399
  110.3 9.3 %collective-permute-start.32 = (bf16[152,704]{1,0:T(8,128)(2,1)S(1)}, bf16[152,704]{1,0:T(8,128)(2,1)S(1)}, u32[]{:S(2)}, u32[]{:S(2)}) collective-permute-start(bf16[152,704]{1,0:T(8,128)(2,1)S(1)} %get-tuple-element.92), channel_id=1, source_target_pairs={{0,6},{1,7},{2,0},{3,1},{4,2},{5,3},{6,4},{7,5},{8,14},{9,15},{10,... | collective-permute-start | bytes 642056 | tf_op jit(solution)/shard_map/ppermute | solution.py:334
  114.4 8.7 %collective-permute-start.31 = (bf16[152,704]{1,0:T(8,128)(2,1)S(1)}, bf16[152,704]{1,0:T(8,128)(2,1)S(1)}, u32[]{:S(2)}, u32[]{:S(2)}) collective-permute-start(bf16[152,704]{1,0:T(8,128)(2,1)S(1)} %get-tuple-element.93), channel_id=1, source_target_pairs={{0,2},{1,3},{2,4},{3,5},{4,6},{5,7},{6,0},{7,1},{8,10},{9,11},{10,... | collective-permute-start | bytes 642056 | tf_op jit(solution)/shard_map/ppermute | solution.py:334
  123.2 12.9 %collective-permute-start.33 = (bf16[2,152,704]{2,1,0:T(8,128)(2,1)S(1)}, bf16[2,152,704]{2,1,0:T(8,128)(2,1)S(1)}, u32[]{:S(2)}, u32[]{:S(2)}) collective-permute-start(bf16[2,152,704]{2,1,0:T(8,128)(2,1)S(1)} %get-tuple-element.82), channel_id=1, source_target_pairs={{0,2},{1,3},{2,4},{3,5},{4,6},{5,7},{6,0},{7,1},{8,10},{9,11},{10,... | collective-permute-start | bytes 1284104 | tf_op jit(solution)/shard_map/ppermute | solution.py:334
  123.3 12.8 %collective-permute-start.34 = (bf16[2,152,704]{2,1,0:T(8,128)(2,1)S(1)}, bf16[2,152,704]{2,1,0:T(8,128)(2,1)S(1)}, u32[]{:S(2)}, u32[]{:S(2)}) collective-permute-start(bf16[2,152,704]{2,1,0:T(8,128)(2,1)S(1)} %get-tuple-element.83), channel_id=1, source_target_pairs={{0,6},{1,7},{2,0},{3,1},{4,2},{5,3},{6,4},{7,5},{8,14},{9,15},{10,... | collective-permute-start | bytes 1284104 | tf_op jit(solution)/shard_map/ppermute | solution.py:334

commit v5 on v4

--- a/solution.py
+++ b/solution.py
@@ -54,11 +54,9 @@
     return jnp.dot(left, right, preferred_element_type=jnp.float32)
 
 
-def transformed(targets, place, spec, base, left, right, windows, left_mat, right_mat):
-    reach = windows.shape[3]
+def transformed(targets, place, spec, base, left, right, shifted, left_mat, right_mat):
     for part in range(2):
-        windows[0, part] = spec[0, part, :, :reach]
-        windows[1, part] = spec[0, part, :, STEP : STEP + reach]
+        shifted[part] = spec[0, part, :, STEP : STEP + shifted.shape[2]]
     a_re, a_im = (x.astype(jnp.bfloat16) for x in transposed_table(base, left))
     right_mat[...] = stacked(side_by_side(a_re, a_im), side_by_side(-a_im, a_re))
     b_re, b_im = (x.T.astype(jnp.bfloat16) for x in transposed_table(base, right))
@@ -68,14 +66,14 @@
         target = across * RING + along
         row_step = place[2 + 2 * target]
         first_col = pl.multiple_of(place[3 + 2 * target], STEP)
-        odd = row_step % 2
+        odd = row_step % 2 == 1
         first_row = pl.multiple_of(row_step // 2 * LANES, LANES)
-        views.append(
-            side_by_side(
-                windows[odd, 0, pl.ds(first_col, MC), pl.ds(first_row, MC)],
-                windows[odd, 1, pl.ds(first_col, MC), pl.ds(first_row, MC)],
-            )
-        )
+        parts = []
+        for part in range(2):
+            at_even = spec[0, part, pl.ds(first_col, MC), pl.ds(first_row, MC)]
+            at_odd = shifted[part, pl.ds(first_col, MC), pl.ds(first_row, MC)]
+            parts.append(jnp.where(odd, at_odd, at_even))
+        views.append(side_by_side(*parts))
     halves = f32_dot(stacked(*views), right_mat[...]).astype(jnp.bfloat16)
     results = {}
     for count, target in enumerate(targets):
@@ -103,20 +101,17 @@
         b_last[k] = results[FAR, k][SUB:]
 
 
-def near_kernel(place, spec, base, left, right, a_last, b_last, *rest):
+def near_kernel(place, spec, base, left, right, *rest):
     a_outs, b_outs = rest[:3], rest[3:6]
     results = transformed(NEAR_TARGETS, place, spec, base, left, right, *rest[6:])
     for i in range(FAR):
         for k in range(FAR):
             a_outs[i][k] = results[i, k][:SUB]
             b_outs[k][i] = results[i, k][SUB:]
-        a_outs[i][FAR] = a_last[i]
-        b_outs[i][FAR] = b_last[i]
-
-
-def contributions(kernel, name, limit, shapes, place, spec, base, phases, lasts=()):
+
+
+def contributions(kernel, name, limit, shapes, place, spec, base, phases):
     cols, rows = spec.shape[2:]
-    whole = [pl.BlockSpec(x.shape, lambda t, place: (0, 0, 0)) for x in lasts]
     return pl.pallas_call(
         kernel,
         out_shape=tuple(jax.ShapeDtypeStruct(s, jnp.bfloat16) for s in shapes),
@@ -128,11 +123,10 @@
                 pl.BlockSpec((2, MC, SUB), lambda t, place: (0, 0, 0)),
                 pl.BlockSpec((1, 2, SUB), lambda t, place: (place[0], 0, 0)),
                 pl.BlockSpec((1, 2, SUB), lambda t, place: (place[1], 0, 0)),
-            ]
-            + whole,
+            ],
             out_specs=tuple(pl.BlockSpec(s, lambda t, place: (0, 0, 0)) for s in shapes),
             scratch_shapes=[
-                pltpu.VMEM((2, 2, cols, rows - STEP), jnp.bfloat16),
+                pltpu.VMEM((2, cols, rows - STEP), jnp.bfloat16),
                 pltpu.VMEM((2 * SUB, 2 * MC), jnp.bfloat16),
                 pltpu.VMEM((2 * MC, 2 * SUB), jnp.bfloat16),
             ],
@@ -142,7 +136,7 @@
             flops=8 * 2 * 2 * 512 * 512 * 256, bytes_accessed=8 * MIB, transcendentals=0
         ),
         name=name,
-    )(place, spec, base, phases, phases, *lasts)
+    )(place, spec, base, phases, phases)
 
 
 def weights_kernel(offsets, fractions, u_out, v_out):
@@ -416,21 +410,25 @@
     routes = (along_x, along_y)
     place = places(worker_of_subgrid)
     spec = jnp.swapaxes(facet_spec, 2, 3)
-    full, part, last = (RING, SUB, SUB), (RING, HALF, SUB), (FAR, SUB, SUB)
+    part, most = (RING, HALF, SUB), (FAR, SUB, SUB)
     outs = contributions(
-        far_kernel, "far_parts", FAR_LIMIT, (part,) * 4 + (last,) * 2, place, spec, base, phases
+        far_kernel, "far_parts", FAR_LIMIT, (part,) * 4 + (most,) * 2, place, spec, base, phases
     )
     arrived = [send_far(*outs[:2], along_x), send_far(*outs[2:4], along_y)]
     nears = contributions(
-        near_kernel, "near_parts", NEAR_LIMIT, (full,) * 6, place, spec, base, phases, outs[4:]
+        near_kernel, "near_parts", NEAR_LIMIT, (most,) * 6, place, spec, base, phases
     )
     arrived, nears, bin_offsets = lax.optimization_barrier((arrived, nears, bin_offsets))
+    nears = [
+        jnp.concatenate([block, outs[4 + k // 3][k % 3][None]]) for k, block in enumerate(nears)
+    ]
     weights = kernel_weights(bin_offsets, bin_fractions)
     sums = [
         (own,) + send_near(up, down, got, route)
         for (own, up, down), got, route in zip((nears[:3], nears[3:]), arrived, routes)
     ]
-    sums, weights = lax.optimization_barrier((sums, weights))
+    (own, weights) = lax.optimization_barrier((sums[0][0], weights))
+    sums[0] = (own,) + sums[0][1:]
     wide = [sum(x.astype(jnp.float32) for x in parts) for parts in sums]
     sums = reduce_small([x.astype(jnp.bfloat16) for x in wide], routes[::-1])
     residual, re_part, im_part = residuals(

time: 137 us -> 137 us (level)
  starting transfers between devices: 44.9 us -> 48.4 us
  local copies, waits for them, and re-layouts: 2.22 us -> 0.3 us
  waiting for transfers between devices: 52.3 us -> 50.9 us
    ppermute x34, starting transfers between devices: 44.8 us -> 48.3 us  [move(): return lax.ppermute(value, *route)]
    unnamed x18, local copies, waits for them, and re-layouts: 2.02 us -> 0.04 us
    ppermute x34, waiting for transfers between devices: 48.5 us -> 47.1 us  [move(): return lax.ppermute(value, *route)]
  transfers between devices with their start and end apart: 35 -> 35, of which waited for: 18 -> 16; matrix products, arithmetic and copies ran while one was open for 0% -> 1% of each run, Pallas kernels for 7% -> 7%
where the time goes in v5:
time: 137 us
  waiting for transfers between devices  50.9 us (37%)
  starting transfers between devices  48.4 us (35%)
  Pallas kernels  32.4 us (24%)
  other arithmetic  3.66 us (3%)
  between operations  1.62 us (1%)
    ppermute x34, starting transfers between devices, move(): return lax.ppermute(value, *route)  48.3 us
    ppermute x34, waiting for transfers between devices, move(): return lax.ppermute(value, *route)  47.1 us
    pallas_call x2, Pallas kernels, contributions(): pl.pallas_call(kernel, out_shape=tuple((jax.ShapeDtypeStruct(s, jnp.bfloa...  11.6 us
    pallas_call x1, Pallas kernels, adjoint_plane(): pl.pallas_call(adjoint_kernel, out_shape=(jax.ShapeDtypeStruct(band_shape...  8.39 us
    pallas_call x1, Pallas kernels, residuals(): pl.pallas_call(residual_kernel, out_shape=(jax.ShapeDtypeStruct(observed....  6.6 us
    pallas_call x1, Pallas kernels, kernel_weights(): pl.pallas_call(weights_kernel, out_shape=(shape, shape), grid=(slots // B...  5.81 us
    ppermute x1, waiting for transfers between devices, sum_rings(): swapped = lax.ppermute(given, 'sub', [(i, i ^ 1) for i in range(2 * RING)])  3.82 us
  transfers between devices with their start and end apart: 35, of which 16 were waited for; matrix products, arithmetic and copies ran while one was open for 1% of the time, Pallas kernels for 7%

profile of v5, /device:TPU:24, one launch (start us, length us, event | category | flops | bytes accessed | tf_op | source)
XLA Modules:
  0.0 137.2 jit_solution(7331538513800716503)
XLA Ops:
  0.7 0.8 select_reduce_fusion
  1.5 0.5 compare_select_fusion.3.place
  2.0 7.3 %far_parts.1 = (bf16[4,128,256]{2,1,0:T(8,128)(2,1)}, bf16[4,128,256]{2,1,0:T(8,128)(2,1)}, bf16[4,128,256]{2,1,0:T(8,128)(2,1)}, bf16[4,128,256]{2,1,0:T(8,128)...) custom-call(s32[42]{0:T(128)} %compare_select_fusion.3.place, bf16[1,2,704,1216]{3,2,1,0:T(8,128)(2,1)} %bitcast.23, ...), custom_call_target="tpu_custom_call" | custom-call | flops 2147483648 | bytes 8388608 | tf_op jit(solution)/shard_map/far_parts/pallas_call | solution.py:115
  9.4 1.5 %collective-permute-start = (bf16[4,128,256]{2,1,0:T(8,128)(2,1)}, bf16[4,128,256]{2,1,0:T(8,128)(2,1)S(1)}, u32[]{:S(2)}, u32[]{:S(2)}) collective-permute-start(bf16[4,128,256]{2,1,0:T(8,128)(2,1)} %get-tuple-element.37), channel_id=1, source_target_pairs={{0,32},{8,40},{16,48},{24,56},{32,64},{40,72},{48,80},{56,88},{64,... | collective-permute-start | bytes 786440 | tf_op jit(solution)/shard_map/ppermute | solution.py:328
  10.9 1.7 %collective-permute-start.1 = (bf16[4,128,256]{2,1,0:T(8,128)(2,1)}, bf16[4,128,256]{2,1,0:T(8,128)(2,1)S(1)}, u32[]{:S(2)}, u32[]{:S(2)}) collective-permute-start(bf16[4,128,256]{2,1,0:T(8,128)(2,1)} %get-tuple-element.38), channel_id=1, source_target_pairs={{0,96},{8,104},{16,112},{24,120},{32,0},{40,8},{48,16},{56,24},{64... | collective-permute-start | bytes 786440 | tf_op jit(solution)/shard_map/ppermute | solution.py:328
  12.6 0.2 collective-permute-start.2
  12.8 1.9 %collective-permute-start.3 = (bf16[4,128,256]{2,1,0:T(8,128)(2,1)}, bf16[4,128,256]{2,1,0:T(8,128)(2,1)S(1)}, u32[]{:S(2)}, u32[]{:S(2)}) collective-permute-start(bf16[4,128,256]{2,1,0:T(8,128)(2,1)} %get-tuple-element.40), channel_id=1, source_target_pairs={{0,24},{8,0},{16,8},{24,16},{32,56},{40,32},{48,40},{56,48},{64,88... | collective-permute-start | bytes 786440 | tf_op jit(solution)/shard_map/ppermute | solution.py:328
  14.7 4.2 %near_parts.1 = (bf16[3,256,256]{2,1,0:T(8,128)(2,1)S(1)}, bf16[3,256,256]{2,1,0:T(8,128)(2,1)S(1)}, bf16[3,256,256]{2,1,0:T(8,128)(2,1)S(1)}, bf16[3,256,256]{2...) custom-call(s32[42]{0:T(128)S(1)} %copy-done, ...), custom_call_target="tpu_custom_call" | custom-call | flops 2147483648 | bytes 8388608 | tf_op jit(solution)/shard_map/near_parts/pallas_call | solution.py:115
  19.0 1.4 collective-permute-done.2
  20.3 1.2 collective-permute-done.3
  21.6 0.1 maximum_add_fusion.3
  21.7 0.6 collective-permute-start.10
  22.3 0.1 maximum_add_fusion.2
  22.4 2.8 %collective-permute-start.9 = (bf16[4,256,256]{2,1,0:T(8,128)(2,1)S(1)}, bf16[4,256,256]{2,1,0:T(8,128)(2,1)S(1)}, u32[]{:S(2)}, u32[]{:S(2)}) collective-permute-start(bf16[4,256,256]{2,1,0:T(8,128)(2,1)S(1)} %maximum_add_fusion.2), channel_id=1, source_target_pairs={{0,8},{8,16},{16,24},{24,0},{32,40},{40,48},{48,56},{56,32},{64,72... | collective-permute-start | bytes 1572872 | tf_op jit(solution)/shard_map/ppermute | solution.py:328
  25.1 0.1 maximum_add_fusion.1
  25.2 1.6 %collective-permute-start.5 = (bf16[4,256,256]{2,1,0:T(8,128)(2,1)S(1)}, bf16[4,256,256]{2,1,0:T(8,128)(2,1)S(1)}, u32[]{:S(2)}, u32[]{:S(2)}) collective-permute-start(bf16[4,256,256]{2,1,0:T(8,128)(2,1)S(1)} %maximum_add_fusion.1), channel_id=1, source_target_pairs={{0,96},{8,104},{16,112},{24,120},{32,0},{40,8},{48,16},{56,24},{64... | collective-permute-start | bytes 1572872 | tf_op jit(solution)/shard_map/ppermute | solution.py:328
  26.8 0.1 maximum_add_fusion
  26.9 0.6 collective-permute-start.4
  27.5 5.8 %kernel_weights.1 = (bf16[256,8192]{1,0:T(8,128)(2,1)S(1)}, bf16[256,8192]{1,0:T(8,128)(2,1)S(1)}) custom-call(s32[1,2,8192]{2,1,0:T(2,128)S(1)} %copy-done.2, f32[1,2,8192]{2,1,0:T(2,128)S(1)} %copy-done.3), custom_call_target="tpu_custom_call" | custom-call | flops 41943040 | bytes 8388608 | tf_op jit(solution)/shard_map/kernel_weights/pallas_call | solution.py:158
  33.3 1.6 %collective-permute-done.10 = bf16[4,256,256]{2,1,0:T(8,128)(2,1)S(1)} collective-permute-done((bf16[4,256,256]{2,1,0:T(8,128)(2,1)S(1)}, bf16[4,256,256]{2,1,0:T(8,128)(2,1)S(1)}, u32[]{:S(2)}, u32[]{:S(2)}) %collective-permute-start.10) | collective-permute-done | bytes 524320 | tf_op jit(solution)/shard_map/ppermute | solution.py:328
  35.0 0.2 add_convert_fusion
  35.3 1.8 %collective-permute-start.13 = (bf16[1,256,256]{2,1,0:T(8,128)(2,1)S(1)}, bf16[1,256,256]{2,1,0:T(8,128)(2,1)S(1)}, u32[]{:S(2)}, u32[]{:S(2)}) collective-permute-start(bf16[1,256,256]{2,1,0:T(8,128)(2,1)S(1)} %get-tuple-element.74), channel_id=1, source_target_pairs={{0,64},{8,72},{16,80},{24,88},{32,96},{40,104},{48,112},{56,120},{... | collective-permute-start | bytes 393224 | tf_op jit(solution)/shard_map/ppermute | solution.py:328
  37.1 1.1 collective-permute-start.12
  38.2 0.9 collective-permute-start.11
  39.1 4.4 %collective-permute-done.4 = bf16[4,256,256]{2,1,0:T(8,128)(2,1)S(1)} collective-permute-done((bf16[4,256,256]{2,1,0:T(8,128)(2,1)S(1)}, bf16[4,256,256]{2,1,0:T(8,128)(2,1)S(1)}, u32[]{:S(2)}, u32[]{:S(2)}) %collective-permute-start.4) | collective-permute-done | bytes 524320 | tf_op jit(solution)/shard_map/ppermute | solution.py:328
  43.5 0.2 add_convert_fusion.1
  43.8 0.1 collective-permute-start.8
  43.9 0.1 collective-permute-start.7
  44.0 3.2 %collective-permute-start.6 = (bf16[1,256,256]{2,1,0:T(8,128)(2,1)S(1)}, bf16[1,256,256]{2,1,0:T(8,128)(2,1)S(1)}, u32[]{:S(2)}, u32[]{:S(2)}) collective-permute-start(bf16[1,256,256]{2,1,0:T(8,128)(2,1)S(1)} %get-tuple-element.80), channel_id=1, source_target_pairs={{0,8},{8,16},{16,24},{24,0},{32,40},{40,48},{48,56},{56,32},{64,72... | collective-permute-start | bytes 393224 | tf_op jit(solution)/shard_map/ppermute | solution.py:328
  47.9 2.6 %collective-permute-done.8.refs_3_ = bf16[1,256,256]{2,1,0:T(8,128)(2,1)S(1)} collective-permute-done((bf16[1,256,256]{2,1,0:T(8,128)(2,1)S(1)}, bf16[1,256,256]{2,1,0:T(8,128)(2,1)S(1)}, u32[]{:S(2)}, u32[]{:S(2)}) %collective-permute-start.8) | collective-permute-done | bytes 131104 | tf_op jit(solution)/shard_map/ppermute | solution.py:328
  50.4 1.1 collective-permute-done.7.refs_2_
  51.5 6.6 %residuals.1 = (f32[1,2,8192]{2,1,0:T(2,128)}, bf16[1,256,256]{2,1,0:T(8,128)(2,1)S(1)}, bf16[1,256,256]{2,1,0:T(8,128)(2,1)S(1)}) custom-call(s32[1]{0:T(128)S(6)} %copy.10.count, bf16[1,256,256]{2,1,0:T(8,128)(2,1)S(1)} %get-tuple-element.81.refs_0_, bf16[1,256,256]{2,1,0:T(8,128)(2,1)S(1)} %collective-permute-done.6.refs_1_, ...), custom_call_target="tpu_custom_call" | custom-call | flops 4294967296 | bytes 8388608 | tf_op jit(solution)/shard_map/residuals/pallas_call | solution.py:210
  58.1 1.8 %collective-permute-start.23 = (bf16[1,256,256]{2,1,0:T(8,128)(2,1)S(1)}, bf16[1,256,256]{2,1,0:T(8,128)(2,1)S(1)}, u32[]{:S(2)}, u32[]{:S(2)}) collective-permute-start(bf16[1,256,256]{2,1,0:T(8,128)(2,1)S(1)} %get-tuple-element.67), channel_id=1, source_target_pairs={{0,8},{8,16},{16,24},{24,0},{32,40},{40,48},{48,56},{56,32},{64,72... | collective-permute-start | bytes 393224 | tf_op jit(solution)/shard_map/ppermute | solution.py:328
  60.0 0.2 collective-permute-start.22
  60.2 3.2 %collective-permute-start.14 = (bf16[1,256,256]{2,1,0:T(8,128)(2,1)S(1)}, bf16[1,256,256]{2,1,0:T(8,128)(2,1)S(1)}, u32[]{:S(2)}, u32[]{:S(2)}) collective-permute-start(bf16[1,256,256]{2,1,0:T(8,128)(2,1)S(1)} %get-tuple-element.66), channel_id=1, source_target_pairs={{0,96},{8,104},{16,112},{24,120},{32,0},{40,8},{48,16},{56,24},{64... | collective-permute-start | bytes 393224 | tf_op jit(solution)/shard_map/ppermute | solution.py:328
  63.4 3.1 %collective-permute-start.24 = (bf16[1,128,256]{2,1,0:T(8,128)(2,1)S(1)}, bf16[1,128,256]{2,1,0:T(8,128)(2,1)S(1)}, u32[]{:S(2)}, u32[]{:S(2)}) collective-permute-start(bf16[1,128,256]{2,1,0:T(8,128)(2,1)S(1)} %slice.142), channel_id=1, source_target_pairs={{0,8},{8,16},{16,24},{24,0},{32,40},{40,48},{48,56},{56,32},{64,72... | collective-permute-start | bytes 196616 | tf_op jit(solution)/shard_map/ppermute | solution.py:328
  66.6 0.1 collective-permute-start.25
  66.6 0.1 collective-permute-done.15
  66.8 3.5 %collective-permute-start.17 = (bf16[1,128,256]{2,1,0:T(8,128)(2,1)S(1)}, bf16[1,128,256]{2,1,0:T(8,128)(2,1)S(1)}, u32[]{:S(2)}, u32[]{:S(2)}) collective-permute-start(bf16[1,128,256]{2,1,0:T(8,128)(2,1)S(1)} %slice.139), channel_id=1, source_target_pairs={{0,96},{8,104},{16,112},{24,120},{32,0},{40,8},{48,16},{56,24},{64... | collective-permute-start | bytes 196616 | tf_op jit(solution)/shard_map/ppermute | solution.py:328
  70.3 2.6 %collective-permute-done.25 = bf16[1,128,256]{2,1,0:T(8,128)(2,1)S(1)} collective-permute-done((bf16[1,128,256]{2,1,0:T(8,128)(2,1)S(1)}, bf16[1,128,256]{2,1,0:T(8,128)(2,1)S(1)}, u32[]{:S(2)}, u32[]{:S(2)}) %collective-permute-start.25) | collective-permute-done | bytes 65568 | tf_op jit(solution)/shard_map/ppermute | solution.py:328
  72.9 0.1 collective-permute-start.27
  73.0 3.2 %collective-permute-start.26 = (bf16[4,256,256]{2,1,0:T(8,128)(2,1)S(1)}, bf16[4,256,256]{2,1,0:T(8,128)(2,1)S(1)}, u32[]{:S(2)}, u32[]{:S(2)}) collective-permute-start(bf16[4,256,256]{2,1,0:T(8,128)(2,1)S(1)} %maximum_maximum_fusion.1.refs_5_), channel_id=1, source_target_pairs={{0,96},{8,104},{16,112},{24,120},{32,0},{40,8},{48,16},{56,24},{64... | collective-permute-start | bytes 1572872 | tf_op jit(solution)/shard_map/ppermute | solution.py:328
  76.3 1.3 collective-permute-start.19
  77.6 0.8 collective-permute-start.18
  78.4 6.4 %collective-permute-done.27.refs_7_ = bf16[4,256,256]{2,1,0:T(8,128)(2,1)S(1)} collective-permute-done((bf16[4,256,256]{2,1,0:T(8,128)(2,1)S(1)}, bf16[4,256,256]{2,1,0:T(8,128)(2,1)S(1)}, u32[]{:S(2)}, u32[]{:S(2)}) %collective-permute-start.27) | collective-permute-done | bytes 524320 | tf_op jit(solution)/shard_map/ppermute | solution.py:328
  84.8 0.1 collective-permute-start.28
  84.9 3.3 %collective-permute-start.29 = (bf16[4,128,256]{2,1,0:T(8,128)(2,1)S(1)}, bf16[4,128,256]{2,1,0:T(8,128)(2,1)S(1)}, u32[]{:S(2)}, u32[]{:S(2)}) collective-permute-start(bf16[4,128,256]{2,1,0:T(8,128)(2,1)S(1)} %slice.145), channel_id=1, source_target_pairs={{0,96},{8,104},{16,112},{24,120},{32,0},{40,8},{48,16},{56,24},{64... | collective-permute-start | bytes 786440 | tf_op jit(solution)/shard_map/ppermute | solution.py:328
  88.2 1.9 %collective-permute-start.20 = (bf16[4,128,256]{2,1,0:T(8,128)(2,1)S(1)}, bf16[4,128,256]{2,1,0:T(8,128)(2,1)S(1)}, u32[]{:S(2)}, u32[]{:S(2)}) collective-permute-start(bf16[4,128,256]{2,1,0:T(8,128)(2,1)S(1)} %slice.140), channel_id=1, source_target_pairs={{0,8},{8,16},{16,24},{24,0},{32,40},{40,48},{48,56},{56,32},{64,72... | collective-permute-start | bytes 786440 | tf_op jit(solution)/shard_map/ppermute | solution.py:328
  90.2 0.5 collective-permute-start.21
  90.6 1.8 %collective-permute-done.28.refs_8_ = bf16[4,128,256]{2,1,0:T(8,128)(2,1)S(1)} collective-permute-done((bf16[4,128,256]{2,1,0:T(8,128)(2,1)S(1)}, bf16[4,128,256]{2,1,0:T(8,128)(2,1)S(1)}, u32[]{:S(2)}, u32[]{:S(2)}) %collective-permute-start.28) | collective-permute-done | bytes 262176 | tf_op jit(solution)/shard_map/ppermute | solution.py:328
  92.5 2.2 %collective-permute-done.20.refs_3_ = bf16[4,128,256]{2,1,0:T(8,128)(2,1)S(1)} collective-permute-done((bf16[4,128,256]{2,1,0:T(8,128)(2,1)S(1)}, bf16[4,128,256]{2,1,0:T(8,128)(2,1)S(1)}, u32[]{:S(2)}, u32[]{:S(2)}) %collective-permute-start.20) | collective-permute-done | bytes 262176 | tf_op jit(solution)/shard_map/ppermute | solution.py:328
  94.7 3.4 %collective-permute-done.21.refs_4_ = bf16[4,128,256]{2,1,0:T(8,128)(2,1)S(1)} collective-permute-done((bf16[4,128,256]{2,1,0:T(8,128)(2,1)S(1)}, bf16[4,128,256]{2,1,0:T(8,128)(2,1)S(1)}, u32[]{:S(2)}, u32[]{:S(2)}) %collective-permute-start.21) | collective-permute-done | bytes 262176 | tf_op jit(solution)/shard_map/ppermute | solution.py:328
  98.0 8.4 %adjoint_plane.1 = (bf16[4,2,152,704]{3,2,1,0:T(8,128)(2,1)S(1)}, bf16[4,2,152,704]{3,2,1,0:T(8,128)(2,1)S(1)}) custom-call(s32[42]{0:T(128)S(1)} %copy-done, bf16[4,256,256]{2,1,0:T(8,128)(2,1)S(1)} %maximum_maximum_fusion.refs_0_, bf16[4,256,256]{2,1,0:T(8,128)(2,1)S(1)} %collective-permute-done.18.refs_1_, ...), custom_call_target="tpu_custom_call" | custom-call | flops 4294967296 | bytes 8388608 | tf_op jit(solution)/shard_map/adjoint_plane/pallas_call | solution.py:288
  106.4 0.1 collective-permute-start.30
  106.5 3.8 %collective-permute-done.30 = bf16[4,2,152,704]{3,2,1,0:T(8,128)(2,1)S(1)} collective-permute-done((bf16[4,2,152,704]{3,2,1,0:T(8,128)(2,1)S(1)}, bf16[4,2,152,704]{3,2,1,0:T(8,128)(2,1)S(1)}, u32[]{:S(2)}, u32[]{:S(2)}) %collective-permute-start.30) | collective-permute-done | bytes 1712160 | tf_op jit(solution)/shard_map/ppermute | solution.py:393
  110.3 0.1 slice_add_fusion.1
  110.5 3.9 %collective-permute-start.32 = (bf16[152,704]{1,0:T(8,128)(2,1)S(1)}, bf16[152,704]{1,0:T(8,128)(2,1)S(1)}, u32[]{:S(2)}, u32[]{:S(2)}) collective-permute-start(bf16[152,704]{1,0:T(8,128)(2,1)S(1)} %get-tuple-element.82), channel_id=1, source_target_pairs={{0,6},{1,7},{2,0},{3,1},{4,2},{5,3},{6,4},{7,5},{8,14},{9,15},{10,... | collective-permute-start | bytes 642056 | tf_op jit(solution)/shard_map/ppermute | solution.py:328
  114.3 5.2 %collective-permute-done.32 = bf16[152,704]{1,0:T(8,128)(2,1)S(1)} collective-permute-done((bf16[152,704]{1,0:T(8,128)(2,1)S(1)}, bf16[152,704]{1,0:T(8,128)(2,1)S(1)}, u32[]{:S(2)}, u32[]{:S(2)}) %collective-permute-start.32) | collective-permute-done | bytes 214048 | tf_op jit(solution)/shard_map/ppermute | solution.py:328
  119.6 3.4 %collective-permute-done.31 = bf16[152,704]{1,0:T(8,128)(2,1)S(1)} collective-permute-done((bf16[152,704]{1,0:T(8,128)(2,1)S(1)}, bf16[152,704]{1,0:T(8,128)(2,1)S(1)}, u32[]{:S(2)}, u32[]{:S(2)}) %collective-permute-start.31) | collective-permute-done | bytes 214048 | tf_op jit(solution)/shard_map/ppermute | solution.py:328
  123.0 0.2 fusion.5
  123.2 0.1 collective-permute-start.33
  123.2 3.2 %collective-permute-start.34 = (bf16[2,152,704]{2,1,0:T(8,128)(2,1)S(1)}, bf16[2,152,704]{2,1,0:T(8,128)(2,1)S(1)}, u32[]{:S(2)}, u32[]{:S(2)}) collective-permute-start(bf16[2,152,704]{2,1,0:T(8,128)(2,1)S(1)} %get-tuple-element.73), channel_id=1, source_target_pairs={{0,6},{1,7},{2,0},{3,1},{4,2},{5,3},{6,4},{7,5},{8,14},{9,15},{10,... | collective-permute-start | bytes 1284104 | tf_op jit(solution)/shard_map/ppermute | solution.py:328
  126.5 9.6 %collective-permute-done.33 = bf16[2,152,704]{2,1,0:T(8,128)(2,1)S(1)} collective-permute-done((bf16[2,152,704]{2,1,0:T(8,128)(2,1)S(1)}, bf16[2,152,704]{2,1,0:T(8,128)(2,1)S(1)}, u32[]{:S(2)}, u32[]{:S(2)}) %collective-permute-start.33) | collective-permute-done | bytes 428064 | tf_op jit(solution)/shard_map/ppermute | solution.py:328
  136.0 1.2 fusion.1
  (56 shorter events, 0.5 us)
Async XLA Ops:
  2.0 12.6 %copy-start = (s32[42]{0:T(128)S(1)}, s32[42]{0:T(128)}, u32[]{:S(2)}) copy-start(s32[42]{0:T(128)} %compare_select_fusion.3.place) | copy-start | bytes 508
  2.0 12.6 %copy-start.1 = (bf16[1,2,1216,704]{2,3,1,0:T(8,128)(2,1)S(1)}, bf16[1,2,1216,704]{2,3,1,0:T(8,128)(2,1)}, u32[]{:S(2)}) copy-start(bf16[1,2,1216,704]{2,3,1,0:T(8,128)(2,1)} %param.8) | copy-start | bytes 10272772
  2.0 12.6 %copy-start.5 = (f32[2,256,256]{2,1,0:T(8,128)S(1)}, f32[2,256,256]{2,1,0:T(8,128)}, u32[]{:S(2)}) copy-start(f32[2,256,256]{2,1,0:T(8,128)} %constant.49.clone.base.refs_10_) | copy-start | bytes 1572868
  2.0 12.6 %copy-start.6 = (f32[16,2,256]{2,1,0:T(2,128)S(1)}, f32[16,2,256]{2,1,0:T(2,128)}, u32[]{:S(2)}) copy-start(f32[16,2,256]{2,1,0:T(2,128)} %constant.50.clone.left.right.refs_11_.refs_12_) | copy-start | bytes 98308
  9.4 9.6 %collective-permute-start = (bf16[4,128,256]{2,1,0:T(8,128)(2,1)}, bf16[4,128,256]{2,1,0:T(8,128)(2,1)S(1)}, u32[]{:S(2)}, u32[]{:S(2)}) collective-permute-start(bf16[4,128,256]{2,1,0:T(8,128)(2,1)} %get-tuple-element.37), channel_id=1, source_target_pairs={{0,32},{8,40},{16,48},{24,56},{32,64},{40,72},{48,80},{56,88},{64,... | collective-permute-start | bytes 786440 | tf_op jit(solution)/shard_map/ppermute | solution.py:328
  10.9 8.1 %collective-permute-start.1 = (bf16[4,128,256]{2,1,0:T(8,128)(2,1)}, bf16[4,128,256]{2,1,0:T(8,128)(2,1)S(1)}, u32[]{:S(2)}, u32[]{:S(2)}) collective-permute-start(bf16[4,128,256]{2,1,0:T(8,128)(2,1)} %get-tuple-element.38), channel_id=1, source_target_pairs={{0,96},{8,104},{16,112},{24,120},{32,0},{40,8},{48,16},{56,24},{64... | collective-permute-start | bytes 786440 | tf_op jit(solution)/shard_map/ppermute | solution.py:328
  12.6 7.7 %collective-permute-start.2 = (bf16[4,128,256]{2,1,0:T(8,128)(2,1)}, bf16[4,128,256]{2,1,0:T(8,128)(2,1)S(1)}, u32[]{:S(2)}, u32[]{:S(2)}) collective-permute-start(bf16[4,128,256]{2,1,0:T(8,128)(2,1)} %get-tuple-element.39), channel_id=1, source_target_pairs={{0,8},{8,16},{16,24},{24,0},{32,40},{40,48},{48,56},{56,32},{64,72... | collective-permute-start | bytes 786440 | tf_op jit(solution)/shard_map/ppermute | solution.py:328
  12.8 6.1 %copy-start.7 = (bf16[3,256,256]{2,1,0:T(8,128)(2,1)S(1)}, bf16[3,256,256]{2,1,0:T(8,128)(2,1)}, u32[]{:S(2)}) copy-start(bf16[3,256,256]{2,1,0:T(8,128)(2,1)} %get-tuple-element.48) | copy-start | bytes 1179652
  12.8 6.1 %copy-start.8 = (bf16[3,256,256]{2,1,0:T(8,128)(2,1)S(1)}, bf16[3,256,256]{2,1,0:T(8,128)(2,1)}, u32[]{:S(2)}) copy-start(bf16[3,256,256]{2,1,0:T(8,128)(2,1)} %get-tuple-element.58) | copy-start | bytes 1179652
  12.8 8.8 %collective-permute-start.3 = (bf16[4,128,256]{2,1,0:T(8,128)(2,1)}, bf16[4,128,256]{2,1,0:T(8,128)(2,1)S(1)}, u32[]{:S(2)}, u32[]{:S(2)}) collective-permute-start(bf16[4,128,256]{2,1,0:T(8,128)(2,1)} %get-tuple-element.40), channel_id=1, source_target_pairs={{0,24},{8,0},{16,8},{24,16},{32,56},{40,32},{48,40},{56,48},{64,88... | collective-permute-start | bytes 786440 | tf_op jit(solution)/shard_map/ppermute | solution.py:328
  21.7 13.3 %collective-permute-start.10 = (bf16[4,256,256]{2,1,0:T(8,128)(2,1)S(1)}, bf16[4,256,256]{2,1,0:T(8,128)(2,1)S(1)}, u32[]{:S(2)}, u32[]{:S(2)}) collective-permute-start(bf16[4,256,256]{2,1,0:T(8,128)(2,1)S(1)} %maximum_add_fusion.3), channel_id=1, source_target_pairs={{0,24},{8,0},{16,8},{24,16},{32,56},{40,32},{48,40},{56,48},{64,88... | collective-permute-start | bytes 1572872 | tf_op jit(solution)/shard_map/ppermute | solution.py:328
  22.3 5.2 %copy-start.2 = (s32[1,2,8192]{2,1,0:T(2,128)S(1)}, s32[1,2,8192]{2,1,0:T(2,128)}, u32[]{:S(2)}) copy-start(s32[1,2,8192]{2,1,0:T(2,128)} %offsets) | copy-start | bytes 196612
  22.3 5.2 %copy-start.3 = (f32[1,2,8192]{2,1,0:T(2,128)S(1)}, f32[1,2,8192]{2,1,0:T(2,128)}, u32[]{:S(2)}) copy-start(f32[1,2,8192]{2,1,0:T(2,128)} %fractions.1) | copy-start | bytes 196612
  22.4 12.6 %collective-permute-start.9 = (bf16[4,256,256]{2,1,0:T(8,128)(2,1)S(1)}, bf16[4,256,256]{2,1,0:T(8,128)(2,1)S(1)}, u32[]{:S(2)}, u32[]{:S(2)}) collective-permute-start(bf16[4,256,256]{2,1,0:T(8,128)(2,1)S(1)} %maximum_add_fusion.2), channel_id=1, source_target_pairs={{0,8},{8,16},{16,24},{24,0},{32,40},{40,48},{48,56},{56,32},{64,72... | collective-permute-start | bytes 1572872 | tf_op jit(solution)/shard_map/ppermute | solution.py:328
  25.2 13.9 %collective-permute-start.5 = (bf16[4,256,256]{2,1,0:T(8,128)(2,1)S(1)}, bf16[4,256,256]{2,1,0:T(8,128)(2,1)S(1)}, u32[]{:S(2)}, u32[]{:S(2)}) collective-permute-start(bf16[4,256,256]{2,1,0:T(8,128)(2,1)S(1)} %maximum_add_fusion.1), channel_id=1, source_target_pairs={{0,96},{8,104},{16,112},{24,120},{32,0},{40,8},{48,16},{56,24},{64... | collective-permute-start | bytes 1572872 | tf_op jit(solution)/shard_map/ppermute | solution.py:328
  26.9 16.6 %collective-permute-start.4 = (bf16[4,256,256]{2,1,0:T(8,128)(2,1)S(1)}, bf16[4,256,256]{2,1,0:T(8,128)(2,1)S(1)}, u32[]{:S(2)}, u32[]{:S(2)}) collective-permute-start(bf16[4,256,256]{2,1,0:T(8,128)(2,1)S(1)} %maximum_add_fusion), channel_id=1, source_target_pairs={{0,32},{8,40},{16,48},{24,56},{32,64},{40,72},{48,80},{56,88},{64,... | collective-permute-start | bytes 1572872 | tf_op jit(solution)/shard_map/ppermute | solution.py:328
  35.2 16.3 %copy-start.4 = (f32[1,2,8192]{2,1,0:T(2,128)S(1)}, f32[1,2,8192]{2,1,0:T(2,128)}, u32[]{:S(2)}) copy-start(f32[1,2,8192]{2,1,0:T(2,128)} %refs_10_.2) | copy-start | bytes 196612
  35.3 8.7 %collective-permute-start.13 = (bf16[1,256,256]{2,1,0:T(8,128)(2,1)S(1)}, bf16[1,256,256]{2,1,0:T(8,128)(2,1)S(1)}, u32[]{:S(2)}, u32[]{:S(2)}) collective-permute-start(bf16[1,256,256]{2,1,0:T(8,128)(2,1)S(1)} %get-tuple-element.74), channel_id=1, source_target_pairs={{0,64},{8,72},{16,80},{24,88},{32,96},{40,104},{48,112},{56,120},{... | collective-permute-start | bytes 393224 | tf_op jit(solution)/shard_map/ppermute | solution.py:328
  37.1 10.8 %collective-permute-start.12 = (bf16[1,256,256]{2,1,0:T(8,128)(2,1)S(1)}, bf16[1,256,256]{2,1,0:T(8,128)(2,1)S(1)}, u32[]{:S(2)}, u32[]{:S(2)}) collective-permute-start(bf16[1,256,256]{2,1,0:T(8,128)(2,1)S(1)} %get-tuple-element.75), channel_id=1, source_target_pairs={{0,96},{8,104},{16,112},{24,120},{32,0},{40,8},{48,16},{56,24},{64... | collective-permute-start | bytes 393224 | tf_op jit(solution)/shard_map/ppermute | solution.py:328
  38.2 9.7 %collective-permute-start.11 = (bf16[1,256,256]{2,1,0:T(8,128)(2,1)S(1)}, bf16[1,256,256]{2,1,0:T(8,128)(2,1)S(1)}, u32[]{:S(2)}, u32[]{:S(2)}) collective-permute-start(bf16[1,256,256]{2,1,0:T(8,128)(2,1)S(1)} %get-tuple-element.76), channel_id=1, source_target_pairs={{0,32},{8,40},{16,48},{24,56},{32,64},{40,72},{48,80},{56,88},{64,... | collective-permute-start | bytes 393224 | tf_op jit(solution)/shard_map/ppermute | solution.py:328
  43.8 6.7 %collective-permute-start.8 = (bf16[1,256,256]{2,1,0:T(8,128)(2,1)S(1)}, bf16[1,256,256]{2,1,0:T(8,128)(2,1)S(1)}, u32[]{:S(2)}, u32[]{:S(2)}) collective-permute-start(bf16[1,256,256]{2,1,0:T(8,128)(2,1)S(1)} %get-tuple-element.78), channel_id=1, source_target_pairs={{0,16},{8,24},{16,0},{24,8},{32,48},{40,56},{48,32},{56,40},{64,80... | collective-permute-start | bytes 393224 | tf_op jit(solution)/shard_map/ppermute | solution.py:328
  43.9 7.7 %collective-permute-start.7 = (bf16[1,256,256]{2,1,0:T(8,128)(2,1)S(1)}, bf16[1,256,256]{2,1,0:T(8,128)(2,1)S(1)}, u32[]{:S(2)}, u32[]{:S(2)}) collective-permute-start(bf16[1,256,256]{2,1,0:T(8,128)(2,1)S(1)} %get-tuple-element.79), channel_id=1, source_target_pairs={{0,24},{8,0},{16,8},{24,16},{32,56},{40,32},{48,40},{56,48},{64,88... | collective-permute-start | bytes 393224 | tf_op jit(solution)/shard_map/ppermute | solution.py:328
  44.0 7.6 %collective-permute-start.6 = (bf16[1,256,256]{2,1,0:T(8,128)(2,1)S(1)}, bf16[1,256,256]{2,1,0:T(8,128)(2,1)S(1)}, u32[]{:S(2)}, u32[]{:S(2)}) collective-permute-start(bf16[1,256,256]{2,1,0:T(8,128)(2,1)S(1)} %get-tuple-element.80), channel_id=1, source_target_pairs={{0,8},{8,16},{16,24},{24,0},{32,40},{40,48},{48,56},{56,32},{64,72... | collective-permute-start | bytes 393224 | tf_op jit(solution)/shard_map/ppermute | solution.py:328
  58.1 5.3 %collective-permute-start.23 = (bf16[1,256,256]{2,1,0:T(8,128)(2,1)S(1)}, bf16[1,256,256]{2,1,0:T(8,128)(2,1)S(1)}, u32[]{:S(2)}, u32[]{:S(2)}) collective-permute-start(bf16[1,256,256]{2,1,0:T(8,128)(2,1)S(1)} %get-tuple-element.67), channel_id=1, source_target_pairs={{0,8},{8,16},{16,24},{24,0},{32,40},{40,48},{48,56},{56,32},{64,72... | collective-permute-start | bytes 393224 | tf_op jit(solution)/shard_map/ppermute | solution.py:328
  60.0 6.6 %collective-permute-start.22 = (bf16[1,256,256]{2,1,0:T(8,128)(2,1)S(1)}, bf16[1,256,256]{2,1,0:T(8,128)(2,1)S(1)}, u32[]{:S(2)}, u32[]{:S(2)}) collective-permute-start(bf16[1,256,256]{2,1,0:T(8,128)(2,1)S(1)} %get-tuple-element.67), channel_id=1, source_target_pairs={{0,24},{8,0},{16,8},{24,16},{32,56},{40,32},{48,40},{56,48},{64,88... | collective-permute-start | bytes 393224 | tf_op jit(solution)/shard_map/ppermute | solution.py:328
  60.2 6.6 %collective-permute-start.15 = (bf16[1,256,256]{2,1,0:T(8,128)(2,1)S(1)}, bf16[1,256,256]{2,1,0:T(8,128)(2,1)S(1)}, u32[]{:S(2)}, u32[]{:S(2)}) collective-permute-start(bf16[1,256,256]{2,1,0:T(8,128)(2,1)S(1)} %get-tuple-element.66), channel_id=1, source_target_pairs={{0,32},{8,40},{16,48},{24,56},{32,64},{40,72},{48,80},{56,88},{64,... | collective-permute-start | bytes 393224 | tf_op jit(solution)/shard_map/ppermute | solution.py:328
  60.2 6.6 %collective-permute-start.14 = (bf16[1,256,256]{2,1,0:T(8,128)(2,1)S(1)}, bf16[1,256,256]{2,1,0:T(8,128)(2,1)S(1)}, u32[]{:S(2)}, u32[]{:S(2)}) collective-permute-start(bf16[1,256,256]{2,1,0:T(8,128)(2,1)S(1)} %get-tuple-element.66), channel_id=1, source_target_pairs={{0,96},{8,104},{16,112},{24,120},{32,0},{40,8},{48,16},{56,24},{64... | collective-permute-start | bytes 393224 | tf_op jit(solution)/shard_map/ppermute | solution.py:328
  63.4 6.9 %collective-permute-start.24 = (bf16[1,128,256]{2,1,0:T(8,128)(2,1)S(1)}, bf16[1,128,256]{2,1,0:T(8,128)(2,1)S(1)}, u32[]{:S(2)}, u32[]{:S(2)}) collective-permute-start(bf16[1,128,256]{2,1,0:T(8,128)(2,1)S(1)} %slice.142), channel_id=1, source_target_pairs={{0,8},{8,16},{16,24},{24,0},{32,40},{40,48},{48,56},{56,32},{64,72... | collective-permute-start | bytes 196616 | tf_op jit(solution)/shard_map/ppermute | solution.py:328
  66.6 6.3 %collective-permute-start.25 = (bf16[1,128,256]{2,1,0:T(8,128)(2,1)S(1)}, bf16[1,128,256]{2,1,0:T(8,128)(2,1)S(1)}, u32[]{:S(2)}, u32[]{:S(2)}) collective-permute-start(bf16[1,128,256]{2,1,0:T(8,128)(2,1)S(1)} %slice.143), channel_id=1, source_target_pairs={{0,24},{8,0},{16,8},{24,16},{32,56},{40,32},{48,40},{56,48},{64,88... | collective-permute-start | bytes 196616 | tf_op jit(solution)/shard_map/ppermute | solution.py:328
  66.7 9.5 %collective-permute-start.16 = (bf16[1,128,256]{2,1,0:T(8,128)(2,1)S(1)}, bf16[1,128,256]{2,1,0:T(8,128)(2,1)S(1)}, u32[]{:S(2)}, u32[]{:S(2)}) collective-permute-start(bf16[1,128,256]{2,1,0:T(8,128)(2,1)S(1)} %slice.138), channel_id=1, source_target_pairs={{0,32},{8,40},{16,48},{24,56},{32,64},{40,72},{48,80},{56,88},{64,... | collective-permute-start | bytes 196616 | tf_op jit(solution)/shard_map/ppermute | solution.py:328
  66.8 9.4 %collective-permute-start.17 = (bf16[1,128,256]{2,1,0:T(8,128)(2,1)S(1)}, bf16[1,128,256]{2,1,0:T(8,128)(2,1)S(1)}, u32[]{:S(2)}, u32[]{:S(2)}) collective-permute-start(bf16[1,128,256]{2,1,0:T(8,128)(2,1)S(1)} %slice.139), channel_id=1, source_target_pairs={{0,96},{8,104},{16,112},{24,120},{32,0},{40,8},{48,16},{56,24},{64... | collective-permute-start | bytes 196616 | tf_op jit(solution)/shard_map/ppermute | solution.py:328
  72.9 11.9 %collective-permute-start.27 = (bf16[4,256,256]{2,1,0:T(8,128)(2,1)S(1)}, bf16[4,256,256]{2,1,0:T(8,128)(2,1)S(1)}, u32[]{:S(2)}, u32[]{:S(2)}) collective-permute-start(bf16[4,256,256]{2,1,0:T(8,128)(2,1)S(1)} %maximum_maximum_fusion.1.refs_5_), channel_id=1, source_target_pairs={{0,32},{8,40},{16,48},{24,56},{32,64},{40,72},{48,80},{56,88},{64,... | collective-permute-start | bytes 1572872 | tf_op jit(solution)/shard_map/ppermute | solution.py:328
  73.0 11.9 %collective-permute-start.26 = (bf16[4,256,256]{2,1,0:T(8,128)(2,1)S(1)}, bf16[4,256,256]{2,1,0:T(8,128)(2,1)S(1)}, u32[]{:S(2)}, u32[]{:S(2)}) collective-permute-start(bf16[4,256,256]{2,1,0:T(8,128)(2,1)S(1)} %maximum_maximum_fusion.1.refs_5_), channel_id=1, source_target_pairs={{0,96},{8,104},{16,112},{24,120},{32,0},{40,8},{48,16},{56,24},{64... | collective-permute-start | bytes 1572872 | tf_op jit(solution)/shard_map/ppermute | solution.py:328
  76.3 11.9 %collective-permute-start.19 = (bf16[4,256,256]{2,1,0:T(8,128)(2,1)S(1)}, bf16[4,256,256]{2,1,0:T(8,128)(2,1)S(1)}, u32[]{:S(2)}, u32[]{:S(2)}) collective-permute-start(bf16[4,256,256]{2,1,0:T(8,128)(2,1)S(1)} %maximum_maximum_fusion.refs_0_), channel_id=1, source_target_pairs={{0,8},{8,16},{16,24},{24,0},{32,40},{40,48},{48,56},{56,32},{64,72... | collective-permute-start | bytes 1572872 | tf_op jit(solution)/shard_map/ppermute | solution.py:328
  77.6 12.6 %collective-permute-start.18 = (bf16[4,256,256]{2,1,0:T(8,128)(2,1)S(1)}, bf16[4,256,256]{2,1,0:T(8,128)(2,1)S(1)}, u32[]{:S(2)}, u32[]{:S(2)}) collective-permute-start(bf16[4,256,256]{2,1,0:T(8,128)(2,1)S(1)} %maximum_maximum_fusion.refs_0_), channel_id=1, source_target_pairs={{0,24},{8,0},{16,8},{24,16},{32,56},{40,32},{48,40},{56,48},{64,88... | collective-permute-start | bytes 1572872 | tf_op jit(solution)/shard_map/ppermute | solution.py:328
  84.8 7.7 %collective-permute-start.28 = (bf16[4,128,256]{2,1,0:T(8,128)(2,1)S(1)}, bf16[4,128,256]{2,1,0:T(8,128)(2,1)S(1)}, u32[]{:S(2)}, u32[]{:S(2)}) collective-permute-start(bf16[4,128,256]{2,1,0:T(8,128)(2,1)S(1)} %slice.144), channel_id=1, source_target_pairs={{0,32},{8,40},{16,48},{24,56},{32,64},{40,72},{48,80},{56,88},{64,... | collective-permute-start | bytes 786440 | tf_op jit(solution)/shard_map/ppermute | solution.py:328
  84.9 7.5 %collective-permute-start.29 = (bf16[4,128,256]{2,1,0:T(8,128)(2,1)S(1)}, bf16[4,128,256]{2,1,0:T(8,128)(2,1)S(1)}, u32[]{:S(2)}, u32[]{:S(2)}) collective-permute-start(bf16[4,128,256]{2,1,0:T(8,128)(2,1)S(1)} %slice.145), channel_id=1, source_target_pairs={{0,96},{8,104},{16,112},{24,120},{32,0},{40,8},{48,16},{56,24},{64... | collective-permute-start | bytes 786440 | tf_op jit(solution)/shard_map/ppermute | solution.py:328
  88.2 6.4 %collective-permute-start.20 = (bf16[4,128,256]{2,1,0:T(8,128)(2,1)S(1)}, bf16[4,128,256]{2,1,0:T(8,128)(2,1)S(1)}, u32[]{:S(2)}, u32[]{:S(2)}) collective-permute-start(bf16[4,128,256]{2,1,0:T(8,128)(2,1)S(1)} %slice.140), channel_id=1, source_target_pairs={{0,8},{8,16},{16,24},{24,0},{32,40},{40,48},{48,56},{56,32},{64,72... | collective-permute-start | bytes 786440 | tf_op jit(solution)/shard_map/ppermute | solution.py:328
  90.2 7.9 %collective-permute-start.21 = (bf16[4,128,256]{2,1,0:T(8,128)(2,1)S(1)}, bf16[4,128,256]{2,1,0:T(8,128)(2,1)S(1)}, u32[]{:S(2)}, u32[]{:S(2)}) collective-permute-start(bf16[4,128,256]{2,1,0:T(8,128)(2,1)S(1)} %slice.141), channel_id=1, source_target_pairs={{0,24},{8,0},{16,8},{24,16},{32,56},{40,32},{48,40},{56,48},{64,88... | collective-permute-start | bytes 786440 | tf_op jit(solution)/shard_map/ppermute | solution.py:328
  106.4 3.9 %collective-permute-start.30 = (bf16[4,2,152,704]{3,2,1,0:T(8,128)(2,1)S(1)}, bf16[4,2,152,704]{3,2,1,0:T(8,128)(2,1)S(1)}, u32[]{:S(2)}, u32[]{:S(2)}) collective-permute-start(bf16[4,2,152,704]{3,2,1,0:T(8,128)(2,1)S(1)} %get-tuple-element.69), channel_id=1, source_target_pairs={{0,1},{1,0},{2,3},{3,2},{4,5},{5,4},{6,7},{7,6},{8,9},{9,8},{10,11... | collective-permute-start | bytes 5136392 | tf_op jit(solution)/shard_map/ppermute | solution.py:393
  110.5 9.1 %collective-permute-start.32 = (bf16[152,704]{1,0:T(8,128)(2,1)S(1)}, bf16[152,704]{1,0:T(8,128)(2,1)S(1)}, u32[]{:S(2)}, u32[]{:S(2)}) collective-permute-start(bf16[152,704]{1,0:T(8,128)(2,1)S(1)} %get-tuple-element.82), channel_id=1, source_target_pairs={{0,6},{1,7},{2,0},{3,1},{4,2},{5,3},{6,4},{7,5},{8,14},{9,15},{10,... | collective-permute-start | bytes 642056 | tf_op jit(solution)/shard_map/ppermute | solution.py:328
  114.3 8.7 %collective-permute-start.31 = (bf16[152,704]{1,0:T(8,128)(2,1)S(1)}, bf16[152,704]{1,0:T(8,128)(2,1)S(1)}, u32[]{:S(2)}, u32[]{:S(2)}) collective-permute-start(bf16[152,704]{1,0:T(8,128)(2,1)S(1)} %get-tuple-element.83), channel_id=1, source_target_pairs={{0,2},{1,3},{2,4},{3,5},{4,6},{5,7},{6,0},{7,1},{8,10},{9,11},{10,... | collective-permute-start | bytes 642056 | tf_op jit(solution)/shard_map/ppermute | solution.py:328
  123.2 12.9 %collective-permute-start.33 = (bf16[2,152,704]{2,1,0:T(8,128)(2,1)S(1)}, bf16[2,152,704]{2,1,0:T(8,128)(2,1)S(1)}, u32[]{:S(2)}, u32[]{:S(2)}) collective-permute-start(bf16[2,152,704]{2,1,0:T(8,128)(2,1)S(1)} %get-tuple-element.72), channel_id=1, source_target_pairs={{0,2},{1,3},{2,4},{3,5},{4,6},{5,7},{6,0},{7,1},{8,10},{9,11},{10,... | collective-permute-start | bytes 1284104 | tf_op jit(solution)/shard_map/ppermute | solution.py:328
  123.2 12.8 %collective-permute-start.34 = (bf16[2,152,704]{2,1,0:T(8,128)(2,1)S(1)}, bf16[2,152,704]{2,1,0:T(8,128)(2,1)S(1)}, u32[]{:S(2)}, u32[]{:S(2)}) collective-permute-start(bf16[2,152,704]{2,1,0:T(8,128)(2,1)S(1)} %get-tuple-element.73), channel_id=1, source_target_pairs={{0,6},{1,7},{2,0},{3,1},{4,2},{5,3},{6,4},{7,5},{8,14},{9,15},{10,... | collective-permute-start | bytes 1284104 | tf_op jit(solution)/shard_map/ppermute | solution.py:328

commit v6 on v5

--- a/solution.py
+++ b/solution.py
@@ -54,13 +54,16 @@
     return jnp.dot(left, right, preferred_element_type=jnp.float32)
 
 
-def transformed(targets, place, spec, base, left, right, shifted, left_mat, right_mat):
-    for part in range(2):
-        shifted[part] = spec[0, part, :, STEP : STEP + shifted.shape[2]]
+def set_tables(base, left, right, left_mat, right_mat):
     a_re, a_im = (x.astype(jnp.bfloat16) for x in transposed_table(base, left))
     right_mat[...] = stacked(side_by_side(a_re, a_im), side_by_side(-a_im, a_re))
     b_re, b_im = (x.T.astype(jnp.bfloat16) for x in transposed_table(base, right))
     left_mat[...] = stacked(side_by_side(b_re, -b_im), side_by_side(b_im, b_re))
+
+
+def transformed(targets, place, spec, shifted, left_mat, right_mat):
+    for part in range(2):
+        shifted[part] = spec[0, part, :, STEP : STEP + shifted.shape[2]]
     views = []
     for across, along in targets:
         target = across * RING + along
@@ -88,9 +91,43 @@
 NEAR_TARGETS = tuple((i, k) for i in range(FAR) for k in range(FAR))
 
 
-def far_kernel(place, spec, base, left, right, *rest):
-    a_far_up, a_far_down, b_far_up, b_far_down, a_last, b_last = rest[:6]
-    results = transformed(FAR_TARGETS, place, spec, base, left, right, *rest[6:])
+def set_places(worker, place, held):
+    facet = lax.axis_index("facet")
+    sub = lax.axis_index("sub")
+    facets, subs = RING * RING, 2 * RING
+
+    def look(subgrid, carry):
+        row = worker[subgrid]
+        held[jnp.where(row & (subs - 1) == sub, row >> 3, facets)] = subgrid
+        return carry
+
+    lax.fori_loop(0, facets * subs, look, 0, unroll=8)
+    place[0] = facet
+    place[1] = (5 * facet + 3) & (facets - 1)
+    for across in range(RING):
+        for along in range(RING):
+            x_at = ((facet >> 2) + NEAR[across]) & (RING - 1)
+            y_at = (facet + NEAR[along]) & (RING - 1)
+            subgrid = held[x_at * RING + y_at]
+            entry = 2 + 2 * (across * RING + along)
+            place[entry] = subgrid >> 3
+            place[entry + 1] = (subgrid & (subs - 1)) * STEP
+    for group in range(2):
+        for near in range(RING):
+            z_at = ((sub >> 1) + NEAR[near]) & (RING - 1)
+            place[2 + 2 * facets + RING * group + near] = z_at * 2 + ((sub & 1) ^ group)
+
+
+def far_kernel(worker, spec, base, phases, *rest):
+    a_far_up, a_far_down, b_far_up, b_far_down, a_last, b_last, place = rest[:7]
+    held, spec_copy, arrival, shifted, left_mat, right_mat = rest[7:]
+    load = pltpu.make_async_copy(spec, spec_copy, arrival)
+    load.start()
+    set_places(worker, place, held)
+    left, right = phases[pl.ds(place[0], 1)], phases[pl.ds(place[1], 1)]
+    set_tables(base, left, right, left_mat, right_mat)
+    load.wait()
+    results = transformed(FAR_TARGETS, place, spec_copy, shifted, left_mat, right_mat)
     for k in range(RING):
         a_far_up[k] = results[FAR, k][:HALF]
         a_far_down[k] = results[FAR, k][HALF:SUB]
@@ -103,39 +140,82 @@
 
 def near_kernel(place, spec, base, left, right, *rest):
     a_outs, b_outs = rest[:3], rest[3:6]
-    results = transformed(NEAR_TARGETS, place, spec, base, left, right, *rest[6:])
+    shifted, left_mat, right_mat = rest[6:]
+    set_tables(base, left, right, left_mat, right_mat)
+    results = transformed(NEAR_TARGETS, place, spec, shifted, left_mat, right_mat)
     for i in range(FAR):
         for k in range(FAR):
             a_outs[i][k] = results[i, k][:SUB]
             b_outs[k][i] = results[i, k][SUB:]
 
 
-def contributions(kernel, name, limit, shapes, place, spec, base, phases):
+def cut_scratch(cols, rows):
+    return [
+        pltpu.VMEM((2, cols, rows - STEP), jnp.bfloat16),
+        pltpu.VMEM((2 * SUB, 2 * MC), jnp.bfloat16),
+        pltpu.VMEM((2 * MC, 2 * SUB), jnp.bfloat16),
+    ]
+
+
+CUT_COST = pl.CostEstimate(
+    flops=8 * 2 * 2 * 512 * 512 * 256, bytes_accessed=8 * MIB, transcendentals=0
+)
+
+
+def whole_block(shape):
+    return pl.BlockSpec(shape, lambda t, scalars: (0,) * len(shape))
+
+
+def far_parts(worker, spec, base, phases, shapes):
+    cols, rows = spec.shape[2:]
+    entries = 2 + 2 * RING * RING + 2 * RING
+    return pl.pallas_call(
+        far_kernel,
+        out_shape=tuple(jax.ShapeDtypeStruct(s, jnp.bfloat16) for s in shapes)
+        + (jax.ShapeDtypeStruct((entries,), jnp.int32),),
+        grid_spec=pltpu.PrefetchScalarGridSpec(
+            num_scalar_prefetch=1,
+            grid=(1,),
+            in_specs=[
+                pl.BlockSpec(memory_space=pl.ANY),
+                whole_block(base.shape),
+                whole_block(phases.shape),
+            ],
+            out_specs=tuple(whole_block(s) for s in shapes)
+            + (pl.BlockSpec(memory_space=pltpu.SMEM),),
+            scratch_shapes=[
+                pltpu.SMEM((2 * RING * RING,), jnp.int32),
+                pltpu.VMEM((1, 2, cols, rows), jnp.bfloat16),
+                pltpu.SemaphoreType.DMA,
+            ]
+            + cut_scratch(cols, rows),
+        ),
+        compiler_params=pltpu.CompilerParams(vmem_limit_bytes=FAR_LIMIT),
+        cost_estimate=CUT_COST,
+        name="far_parts",
+    )(worker, spec, base, phases)
+
+
+def near_parts(place, spec, base, phases, shapes):
     cols, rows = spec.shape[2:]
     return pl.pallas_call(
-        kernel,
+        near_kernel,
         out_shape=tuple(jax.ShapeDtypeStruct(s, jnp.bfloat16) for s in shapes),
         grid_spec=pltpu.PrefetchScalarGridSpec(
             num_scalar_prefetch=1,
             grid=(1,),
             in_specs=[
-                pl.BlockSpec((1, 2, cols, rows), lambda t, place: (0, 0, 0, 0)),
-                pl.BlockSpec((2, MC, SUB), lambda t, place: (0, 0, 0)),
+                whole_block(spec.shape),
+                whole_block(base.shape),
                 pl.BlockSpec((1, 2, SUB), lambda t, place: (place[0], 0, 0)),
                 pl.BlockSpec((1, 2, SUB), lambda t, place: (place[1], 0, 0)),
             ],
-            out_specs=tuple(pl.BlockSpec(s, lambda t, place: (0, 0, 0)) for s in shapes),
-            scratch_shapes=[
-                pltpu.VMEM((2, cols, rows - STEP), jnp.bfloat16),
-                pltpu.VMEM((2 * SUB, 2 * MC), jnp.bfloat16),
-                pltpu.VMEM((2 * MC, 2 * SUB), jnp.bfloat16),
-            ],
+            out_specs=tuple(whole_block(s) for s in shapes),
+            scratch_shapes=cut_scratch(cols, rows),
         ),
-        compiler_params=pltpu.CompilerParams(vmem_limit_bytes=limit),
-        cost_estimate=pl.CostEstimate(
-            flops=8 * 2 * 2 * 512 * 512 * 256, bytes_accessed=8 * MIB, transcendentals=0
-        ),
-        name=name,
+        compiler_params=pltpu.CompilerParams(vmem_limit_bytes=NEAR_LIMIT),
+        cost_estimate=CUT_COST,
+        name="near_parts",
     )(place, spec, base, phases, phases)
 
 
@@ -328,30 +408,6 @@
     return lax.ppermute(value, *route)
 
 
-def near_shift(index):
-    return index ^ (index >> 1)
-
-
-def places(worker):
-    facet = lax.axis_index("facet")
-    sub = lax.axis_index("sub")
-    subs = lax.axis_size("sub")
-    facets = RING * RING
-    entry = jnp.arange(2 + 2 * facets + 2 * RING, dtype=jnp.int32)
-    target = ((entry - 2) >> 1) & (facets - 1)
-    x_at = ((facet >> 2) + near_shift(target >> 2)) & (RING - 1)
-    y_at = (facet + near_shift(target & (RING - 1))) & (RING - 1)
-    row = (x_at * RING + y_at) * subs + sub
-    ids = jnp.arange(worker.shape[0], dtype=jnp.int32)
-    held = jnp.sum(jnp.where(worker[None, :] == row[:, None], ids[None, :], 0), axis=1)
-    corner = jnp.where(entry & 1 == 0, held >> 3, (held & (subs - 1)) * STEP)
-    table = jnp.where(entry == 0, facet, (5 * facet + 3) & (facets - 1))
-    band = entry - 2 - 2 * facets
-    z_at = ((sub >> 1) + near_shift(band & (RING - 1))) & (RING - 1)
-    band = z_at * 2 + ((sub & 1) ^ (band >> 2 & 1))
-    return jnp.where(entry < 2, table, jnp.where(entry < 2 + 2 * facets, corner, band)).astype(jnp.int32)
-
-
 def with_rows(block, rows, first):
     space = [(0, 0, 0)] * block.ndim
     space[-2] = (first, block.shape[-2] - rows.shape[-2] - first, 0)
@@ -391,16 +447,17 @@
 
 def sum_rings(kept, given):
     swapped = lax.ppermute(given, "sub", [(i, i ^ 1) for i in range(2 * RING)])
-    far = (kept[3] + swapped[3])
-    low = move(far[0], along_z(1))
-    high = move(far[1], along_z(-1))
-    low, high = lax.optimization_barrier((low, high))
-    nothing = jnp.zeros_like(low)
-    up = kept[1] + swapped[1] + jnp.stack([low, nothing])
-    down = kept[2] + swapped[2] + jnp.stack([nothing, high])
-    low, high = move(up, along_z(1)), move(down, along_z(-1))
-    wide = [x.astype(jnp.float32) for x in (kept[0], swapped[0], low, high)]
-    return wide[0] + wide[1] + wide[2] + wide[3]
+    chip = kept + swapped
+    low = move(chip[3, 0], along_z(1))
+    high = move(chip[3, 1], along_z(-1))
+    up_im = move(chip[1, 1], along_z(1))
+    down_re = move(chip[2, 0], along_z(-1))
+    up_re = move(chip[1, 0] + low, along_z(1))
+    down_im = move(chip[2, 1] + high, along_z(-1))
+    own = kept[0].astype(jnp.float32) + swapped[0].astype(jnp.float32)
+    re = own[0] + up_re.astype(jnp.float32) + down_re.astype(jnp.float32)
+    im = own[1] + up_im.astype(jnp.float32) + down_im.astype(jnp.float32)
+    return jnp.stack([re, im])
 
 
 def on_device(facet_spec, worker_of_subgrid, vis_count, bin_offsets, bin_fractions, observed):
@@ -408,16 +465,11 @@
     rows, cols = facet_spec.shape[2:]
     base, phases = (jnp.asarray(x) for x in phase_parts(lax.axis_size("facet")))
     routes = (along_x, along_y)
-    place = places(worker_of_subgrid)
     spec = jnp.swapaxes(facet_spec, 2, 3)
     part, most = (RING, HALF, SUB), (FAR, SUB, SUB)
-    outs = contributions(
-        far_kernel, "far_parts", FAR_LIMIT, (part,) * 4 + (most,) * 2, place, spec, base, phases
-    )
+    *outs, place = far_parts(worker_of_subgrid, spec, base, phases, (part,) * 4 + (most,) * 2)
     arrived = [send_far(*outs[:2], along_x), send_far(*outs[2:4], along_y)]
-    nears = contributions(
-        near_kernel, "near_parts", NEAR_LIMIT, (most,) * 6, place, spec, base, phases
-    )
+    nears = near_parts(place, spec, base, phases, (most,) * 6)
     arrived, nears, bin_offsets = lax.optimization_barrier((arrived, nears, bin_offsets))
     nears = [
         jnp.concatenate([block, outs[4 + k // 3][k % 3][None]]) for k, block in enumerate(nears)

time: 137 us -> 132 us (0.964)
  waiting for transfers between devices: 50.9 us -> 40.9 us
  starting transfers between devices: 48.4 us -> 52.2 us
    ppermute x34 -> x36, waiting for transfers between devices: 47.1 us -> 37.1 us  [move(): return lax.ppermute(value, *route)]
    ppermute x34 -> x36, starting transfers between devices: 48.3 us -> 52.1 us  [move(): return lax.ppermute(value, *route)]
  transfers between devices with their start and end apart: 35 -> 37, of which waited for: 16 -> 16; matrix products, arithmetic and copies ran while one was open for 1% -> 1% of each run, Pallas kernels for 7% -> 8%
where the time goes in v6:
time: 132 us
  starting transfers between devices  52.2 us (40%)
  waiting for transfers between devices  40.9 us (31%)
  Pallas kernels  33.2 us (25%)
  other arithmetic  2.77 us (2%)
  between operations  1.65 us (1%)
    ppermute x36, starting transfers between devices, move(): return lax.ppermute(value, *route)  52.1 us
    ppermute x36, waiting for transfers between devices, move(): return lax.ppermute(value, *route)  37.1 us
    pallas_call x1, Pallas kernels, adjoint_plane(): pl.pallas_call(adjoint_kernel, out_shape=(jax.ShapeDtypeStruct(band_shape...  8.35 us
    pallas_call x1, Pallas kernels, far_parts(): pl.pallas_call(far_kernel, out_shape=tuple((jax.ShapeDtypeStruct(s, jnp.b...  8.24 us
    pallas_call x1, Pallas kernels, residuals(): pl.pallas_call(residual_kernel, out_shape=(jax.ShapeDtypeStruct(observed....  6.62 us
    pallas_call x1, Pallas kernels, kernel_weights(): pl.pallas_call(weights_kernel, out_shape=(shape, shape), grid=(slots // B...  5.81 us
    pallas_call x1, Pallas kernels, near_parts(): pl.pallas_call(near_kernel, out_shape=tuple((jax.ShapeDtypeStruct(s, jnp....  4.19 us
    ppermute x1, waiting for transfers between devices, sum_rings(): swapped = lax.ppermute(given, 'sub', [(i, i ^ 1) for i in range(2 * RING)])  3.82 us
  transfers between devices with their start and end apart: 37, of which 16 were waited for; matrix products, arithmetic and copies ran while one was open for 1% of the time, Pallas kernels for 8%

profile of v6, /device:TPU:24, one launch (start us, length us, event | category | flops | bytes accessed | tf_op | source)
XLA Modules:
  0.0 131.7 jit_solution(6097258426664399600)
XLA Ops:
  0.7 8.2 %far_parts.1 = (bf16[4,128,256]{2,1,0:T(8,128)(2,1)}, bf16[4,128,256]{2,1,0:T(8,128)(2,1)}, bf16[4,128,256]{2,1,0:T(8,128)(2,1)}, bf16[4,128,256]{2,1,0:T(8,128)...) custom-call(s32[128]{0:T(128)} %worker.1, bf16[1,2,704,1216]{3,2,1,0:T(8,128)(2,1)} %bitcast.39, ...), custom_call_target="tpu_custom_call" | custom-call | flops 2147483648 | bytes 8388608 | tf_op jit(solution)/shard_map/far_parts/pallas_call | solution.py:172
  8.9 1.6 %collective-permute-start = (bf16[4,128,256]{2,1,0:T(8,128)(2,1)}, bf16[4,128,256]{2,1,0:T(8,128)(2,1)S(1)}, u32[]{:S(2)}, u32[]{:S(2)}) collective-permute-start(bf16[4,128,256]{2,1,0:T(8,128)(2,1)} %get-tuple-element.36), channel_id=1, source_target_pairs={{0,32},{8,40},{16,48},{24,56},{32,64},{40,72},{48,80},{56,88},{64,... | collective-permute-start | bytes 786440 | tf_op jit(solution)/shard_map/ppermute | solution.py:408
  10.5 1.8 %collective-permute-start.1 = (bf16[4,128,256]{2,1,0:T(8,128)(2,1)}, bf16[4,128,256]{2,1,0:T(8,128)(2,1)S(1)}, u32[]{:S(2)}, u32[]{:S(2)}) collective-permute-start(bf16[4,128,256]{2,1,0:T(8,128)(2,1)} %get-tuple-element.37), channel_id=1, source_target_pairs={{0,96},{8,104},{16,112},{24,120},{32,0},{40,8},{48,16},{56,24},{64... | collective-permute-start | bytes 786440 | tf_op jit(solution)/shard_map/ppermute | solution.py:408
  12.2 0.1 collective-permute-start.2
  12.4 1.9 %collective-permute-start.3 = (bf16[4,128,256]{2,1,0:T(8,128)(2,1)}, bf16[4,128,256]{2,1,0:T(8,128)(2,1)S(1)}, u32[]{:S(2)}, u32[]{:S(2)}) collective-permute-start(bf16[4,128,256]{2,1,0:T(8,128)(2,1)} %get-tuple-element.39), channel_id=1, source_target_pairs={{0,24},{8,0},{16,8},{24,16},{32,56},{40,32},{48,40},{56,48},{64,88... | collective-permute-start | bytes 786440 | tf_op jit(solution)/shard_map/ppermute | solution.py:408
  14.3 0.7 copy-done.6
  14.9 4.2 %near_parts.1 = (bf16[3,256,256]{2,1,0:T(8,128)(2,1)S(1)}, bf16[3,256,256]{2,1,0:T(8,128)(2,1)S(1)}, bf16[3,256,256]{2,1,0:T(8,128)(2,1)S(1)}, bf16[3,256,256]{2...) custom-call(s32[42]{0:T(128)S(1)} %copy-done.6, ...), custom_call_target="tpu_custom_call" | custom-call | flops 2147483648 | bytes 8388608 | tf_op jit(solution)/shard_map/near_parts/pallas_call | solution.py:201
  19.2 0.7 collective-permute-done.2
  19.9 1.2 collective-permute-done.3
  21.1 0.1 maximum_add_fusion.3
  21.2 0.6 collective-permute-start.10
  21.8 0.1 maximum_add_fusion.2
  21.9 2.8 %collective-permute-start.9 = (bf16[4,256,256]{2,1,0:T(8,128)(2,1)S(1)}, bf16[4,256,256]{2,1,0:T(8,128)(2,1)S(1)}, u32[]{:S(2)}, u32[]{:S(2)}) collective-permute-start(bf16[4,256,256]{2,1,0:T(8,128)(2,1)S(1)} %maximum_add_fusion.2), channel_id=1, source_target_pairs={{0,8},{8,16},{16,24},{24,0},{32,40},{40,48},{48,56},{56,32},{64,72... | collective-permute-start | bytes 1572872 | tf_op jit(solution)/shard_map/ppermute | solution.py:408
  24.7 0.1 maximum_add_fusion.1
  24.8 1.6 %collective-permute-start.5 = (bf16[4,256,256]{2,1,0:T(8,128)(2,1)S(1)}, bf16[4,256,256]{2,1,0:T(8,128)(2,1)S(1)}, u32[]{:S(2)}, u32[]{:S(2)}) collective-permute-start(bf16[4,256,256]{2,1,0:T(8,128)(2,1)S(1)} %maximum_add_fusion.1), channel_id=1, source_target_pairs={{0,96},{8,104},{16,112},{24,120},{32,0},{40,8},{48,16},{56,24},{64... | collective-permute-start | bytes 1572872 | tf_op jit(solution)/shard_map/ppermute | solution.py:408
  26.4 0.1 maximum_add_fusion
  26.5 0.6 collective-permute-start.4
  27.1 5.8 %kernel_weights.1 = (bf16[256,8192]{1,0:T(8,128)(2,1)S(1)}, bf16[256,8192]{1,0:T(8,128)(2,1)S(1)}) custom-call(s32[1,2,8192]{2,1,0:T(2,128)S(1)} %copy-done.1, f32[1,2,8192]{2,1,0:T(2,128)S(1)} %copy-done.2), custom_call_target="tpu_custom_call" | custom-call | flops 41943040 | bytes 8388608 | tf_op jit(solution)/shard_map/kernel_weights/pallas_call | solution.py:238
  32.9 1.6 %collective-permute-done.10 = bf16[4,256,256]{2,1,0:T(8,128)(2,1)S(1)} collective-permute-done((bf16[4,256,256]{2,1,0:T(8,128)(2,1)S(1)}, bf16[4,256,256]{2,1,0:T(8,128)(2,1)S(1)}, u32[]{:S(2)}, u32[]{:S(2)}) %collective-permute-start.10) | collective-permute-done | bytes 524320 | tf_op jit(solution)/shard_map/ppermute | solution.py:408
  34.5 0.2 add_convert_fusion
  34.8 1.8 %collective-permute-start.13 = (bf16[1,256,256]{2,1,0:T(8,128)(2,1)S(1)}, bf16[1,256,256]{2,1,0:T(8,128)(2,1)S(1)}, u32[]{:S(2)}, u32[]{:S(2)}) collective-permute-start(bf16[1,256,256]{2,1,0:T(8,128)(2,1)S(1)} %get-tuple-element.78), channel_id=1, source_target_pairs={{0,64},{8,72},{16,80},{24,88},{32,96},{40,104},{48,112},{56,120},{... | collective-permute-start | bytes 393224 | tf_op jit(solution)/shard_map/ppermute | solution.py:408
  36.6 1.1 collective-permute-start.12
  37.7 0.9 collective-permute-start.11
  38.7 4.4 %collective-permute-done.4 = bf16[4,256,256]{2,1,0:T(8,128)(2,1)S(1)} collective-permute-done((bf16[4,256,256]{2,1,0:T(8,128)(2,1)S(1)}, bf16[4,256,256]{2,1,0:T(8,128)(2,1)S(1)}, u32[]{:S(2)}, u32[]{:S(2)}) %collective-permute-start.4) | collective-permute-done | bytes 524320 | tf_op jit(solution)/shard_map/ppermute | solution.py:408
  43.1 0.2 add_convert_fusion.1
  43.3 0.1 collective-permute-start.8
  43.4 0.1 collective-permute-start.7
  43.5 3.2 %collective-permute-start.6 = (bf16[1,256,256]{2,1,0:T(8,128)(2,1)S(1)}, bf16[1,256,256]{2,1,0:T(8,128)(2,1)S(1)}, u32[]{:S(2)}, u32[]{:S(2)}) collective-permute-start(bf16[1,256,256]{2,1,0:T(8,128)(2,1)S(1)} %get-tuple-element.84), channel_id=1, source_target_pairs={{0,8},{8,16},{16,24},{24,0},{32,40},{40,48},{48,56},{56,32},{64,72... | collective-permute-start | bytes 393224 | tf_op jit(solution)/shard_map/ppermute | solution.py:408
  47.4 2.6 %collective-permute-done.8.refs_3_ = bf16[1,256,256]{2,1,0:T(8,128)(2,1)S(1)} collective-permute-done((bf16[1,256,256]{2,1,0:T(8,128)(2,1)S(1)}, bf16[1,256,256]{2,1,0:T(8,128)(2,1)S(1)}, u32[]{:S(2)}, u32[]{:S(2)}) %collective-permute-start.8) | collective-permute-done | bytes 131104 | tf_op jit(solution)/shard_map/ppermute | solution.py:408
  50.0 1.1 collective-permute-done.7.refs_2_
  51.1 6.6 %residuals.1 = (f32[1,2,8192]{2,1,0:T(2,128)}, bf16[1,256,256]{2,1,0:T(8,128)(2,1)S(1)}, bf16[1,256,256]{2,1,0:T(8,128)(2,1)S(1)}) custom-call(s32[1]{0:T(128)S(6)} %copy.10.count, bf16[1,256,256]{2,1,0:T(8,128)(2,1)S(1)} %get-tuple-element.85.refs_0_, bf16[1,256,256]{2,1,0:T(8,128)(2,1)S(1)} %collective-permute-done.6.refs_1_, ...), custom_call_target="tpu_custom_call" | custom-call | flops 4294967296 | bytes 8388608 | tf_op jit(solution)/shard_map/residuals/pallas_call | solution.py:290
  57.7 1.8 %collective-permute-start.23 = (bf16[1,256,256]{2,1,0:T(8,128)(2,1)S(1)}, bf16[1,256,256]{2,1,0:T(8,128)(2,1)S(1)}, u32[]{:S(2)}, u32[]{:S(2)}) collective-permute-start(bf16[1,256,256]{2,1,0:T(8,128)(2,1)S(1)} %get-tuple-element.67), channel_id=1, source_target_pairs={{0,8},{8,16},{16,24},{24,0},{32,40},{40,48},{48,56},{56,32},{64,72... | collective-permute-start | bytes 393224 | tf_op jit(solution)/shard_map/ppermute | solution.py:408
  59.5 0.2 collective-permute-start.22
  59.7 3.2 %collective-permute-start.14 = (bf16[1,256,256]{2,1,0:T(8,128)(2,1)S(1)}, bf16[1,256,256]{2,1,0:T(8,128)(2,1)S(1)}, u32[]{:S(2)}, u32[]{:S(2)}) collective-permute-start(bf16[1,256,256]{2,1,0:T(8,128)(2,1)S(1)} %get-tuple-element.66), channel_id=1, source_target_pairs={{0,96},{8,104},{16,112},{24,120},{32,0},{40,8},{48,16},{56,24},{64... | collective-permute-start | bytes 393224 | tf_op jit(solution)/shard_map/ppermute | solution.py:408
  63.0 3.1 %collective-permute-start.24 = (bf16[1,128,256]{2,1,0:T(8,128)(2,1)S(1)}, bf16[1,128,256]{2,1,0:T(8,128)(2,1)S(1)}, u32[]{:S(2)}, u32[]{:S(2)}) collective-permute-start(bf16[1,128,256]{2,1,0:T(8,128)(2,1)S(1)} %slice.142), channel_id=1, source_target_pairs={{0,8},{8,16},{16,24},{24,0},{32,40},{40,48},{48,56},{56,32},{64,72... | collective-permute-start | bytes 196616 | tf_op jit(solution)/shard_map/ppermute | solution.py:408
  66.2 0.1 collective-permute-done.15
  66.3 3.6 %collective-permute-start.17 = (bf16[1,128,256]{2,1,0:T(8,128)(2,1)S(1)}, bf16[1,128,256]{2,1,0:T(8,128)(2,1)S(1)}, u32[]{:S(2)}, u32[]{:S(2)}) collective-permute-start(bf16[1,128,256]{2,1,0:T(8,128)(2,1)S(1)} %slice.139), channel_id=1, source_target_pairs={{0,96},{8,104},{16,112},{24,120},{32,0},{40,8},{48,16},{56,24},{64... | collective-permute-start | bytes 196616 | tf_op jit(solution)/shard_map/ppermute | solution.py:408
  69.9 2.5 %collective-permute-done.25 = bf16[1,128,256]{2,1,0:T(8,128)(2,1)S(1)} collective-permute-done((bf16[1,128,256]{2,1,0:T(8,128)(2,1)S(1)}, bf16[1,128,256]{2,1,0:T(8,128)(2,1)S(1)}, u32[]{:S(2)}, u32[]{:S(2)}) %collective-permute-start.25) | collective-permute-done | bytes 65568 | tf_op jit(solution)/shard_map/ppermute | solution.py:408
  72.5 3.2 %collective-permute-start.26 = (bf16[4,256,256]{2,1,0:T(8,128)(2,1)S(1)}, bf16[4,256,256]{2,1,0:T(8,128)(2,1)S(1)}, u32[]{:S(2)}, u32[]{:S(2)}) collective-permute-start(bf16[4,256,256]{2,1,0:T(8,128)(2,1)S(1)} %maximum_maximum_fusion.1.refs_5_), channel_id=1, source_target_pairs={{0,96},{8,104},{16,112},{24,120},{32,0},{40,8},{48,16},{56,24},{64... | collective-permute-start | bytes 1572872 | tf_op jit(solution)/shard_map/ppermute | solution.py:408
  75.8 1.3 %collective-permute-start.19 = (bf16[4,256,256]{2,1,0:T(8,128)(2,1)S(1)}, bf16[4,256,256]{2,1,0:T(8,128)(2,1)S(1)}, u32[]{:S(2)}, u32[]{:S(2)}) collective-permute-start(bf16[4,256,256]{2,1,0:T(8,128)(2,1)S(1)} %maximum_maximum_fusion.refs_0_), channel_id=1, source_target_pairs={{0,8},{8,16},{16,24},{24,0},{32,40},{40,48},{48,56},{56,32},{64,72... | collective-permute-start | bytes 1572872 | tf_op jit(solution)/shard_map/ppermute | solution.py:408
  77.1 0.8 collective-permute-start.18
  77.9 6.4 %collective-permute-done.27.refs_7_ = bf16[4,256,256]{2,1,0:T(8,128)(2,1)S(1)} collective-permute-done((bf16[4,256,256]{2,1,0:T(8,128)(2,1)S(1)}, bf16[4,256,256]{2,1,0:T(8,128)(2,1)S(1)}, u32[]{:S(2)}, u32[]{:S(2)}) %collective-permute-start.27) | collective-permute-done | bytes 524320 | tf_op jit(solution)/shard_map/ppermute | solution.py:408
  84.5 3.3 %collective-permute-start.29 = (bf16[4,128,256]{2,1,0:T(8,128)(2,1)S(1)}, bf16[4,128,256]{2,1,0:T(8,128)(2,1)S(1)}, u32[]{:S(2)}, u32[]{:S(2)}) collective-permute-start(bf16[4,128,256]{2,1,0:T(8,128)(2,1)S(1)} %slice.145), channel_id=1, source_target_pairs={{0,96},{8,104},{16,112},{24,120},{32,0},{40,8},{48,16},{56,24},{64... | collective-permute-start | bytes 786440 | tf_op jit(solution)/shard_map/ppermute | solution.py:408
  87.8 1.9 %collective-permute-start.20 = (bf16[4,128,256]{2,1,0:T(8,128)(2,1)S(1)}, bf16[4,128,256]{2,1,0:T(8,128)(2,1)S(1)}, u32[]{:S(2)}, u32[]{:S(2)}) collective-permute-start(bf16[4,128,256]{2,1,0:T(8,128)(2,1)S(1)} %slice.140), channel_id=1, source_target_pairs={{0,8},{8,16},{16,24},{24,0},{32,40},{40,48},{48,56},{56,32},{64,72... | collective-permute-start | bytes 786440 | tf_op jit(solution)/shard_map/ppermute | solution.py:408
  89.7 0.5 collective-permute-start.21
  90.2 1.8 %collective-permute-done.28.refs_8_ = bf16[4,128,256]{2,1,0:T(8,128)(2,1)S(1)} collective-permute-done((bf16[4,128,256]{2,1,0:T(8,128)(2,1)S(1)}, bf16[4,128,256]{2,1,0:T(8,128)(2,1)S(1)}, u32[]{:S(2)}, u32[]{:S(2)}) %collective-permute-start.28) | collective-permute-done | bytes 262176 | tf_op jit(solution)/shard_map/ppermute | solution.py:408
  92.0 2.2 %collective-permute-done.20.refs_3_ = bf16[4,128,256]{2,1,0:T(8,128)(2,1)S(1)} collective-permute-done((bf16[4,128,256]{2,1,0:T(8,128)(2,1)S(1)}, bf16[4,128,256]{2,1,0:T(8,128)(2,1)S(1)}, u32[]{:S(2)}, u32[]{:S(2)}) %collective-permute-start.20) | collective-permute-done | bytes 262176 | tf_op jit(solution)/shard_map/ppermute | solution.py:408
  94.2 3.4 %collective-permute-done.21.refs_4_ = bf16[4,128,256]{2,1,0:T(8,128)(2,1)S(1)} collective-permute-done((bf16[4,128,256]{2,1,0:T(8,128)(2,1)S(1)}, bf16[4,128,256]{2,1,0:T(8,128)(2,1)S(1)}, u32[]{:S(2)}, u32[]{:S(2)}) %collective-permute-start.21) | collective-permute-done | bytes 262176 | tf_op jit(solution)/shard_map/ppermute | solution.py:408
  97.6 8.3 %adjoint_plane.1 = (bf16[4,2,152,704]{3,2,1,0:T(8,128)(2,1)S(1)}, bf16[4,2,152,704]{3,2,1,0:T(8,128)(2,1)S(1)}) custom-call(s32[42]{0:T(128)S(1)} %copy-done.7, bf16[4,256,256]{2,1,0:T(8,128)(2,1)S(1)} %maximum_maximum_fusion.refs_0_, bf16[4,256,256]{2,1,0:T(8,128)(2,1)S(1)} %collective-permute-done.18.refs_1_, ...), custom_call_target="tpu_custom_call" | custom-call | flops 4294967296 | bytes 8388608 | tf_op jit(solution)/shard_map/adjoint_plane/pallas_call | solution.py:368
  105.9 0.1 collective-permute-start.30
  106.0 3.8 %collective-permute-done.30 = bf16[4,2,152,704]{3,2,1,0:T(8,128)(2,1)S(1)} collective-permute-done((bf16[4,2,152,704]{3,2,1,0:T(8,128)(2,1)S(1)}, bf16[4,2,152,704]{3,2,1,0:T(8,128)(2,1)S(1)}, u32[]{:S(2)}, u32[]{:S(2)}) %collective-permute-start.30) | collective-permute-done | bytes 1712160 | tf_op jit(solution)/shard_map/ppermute | solution.py:449
  109.9 0.5 add.66
  110.5 1.9 %collective-permute-start.31 = (bf16[152,704]{1,0:T(8,128)(2,1)S(1)}, bf16[152,704]{1,0:T(8,128)(2,1)S(1)}, u32[]{:S(2)}, u32[]{:S(2)}) collective-permute-start(bf16[152,704]{1,0:T(8,128)(2,1)S(1)} %get-tuple-element.72), channel_id=1, source_target_pairs={{0,2},{1,3},{2,4},{3,5},{4,6},{5,7},{6,0},{7,1},{8,10},{9,11},{10,... | collective-permute-start | bytes 642056 | tf_op jit(solution)/shard_map/ppermute | solution.py:408
  112.4 2.2 %collective-permute-start.35 = (bf16[152,704]{1,0:T(8,128)(2,1)S(1)}, bf16[152,704]{1,0:T(8,128)(2,1)S(1)}, u32[]{:S(2)}, u32[]{:S(2)}) collective-permute-start(bf16[152,704]{1,0:T(8,128)(2,1)S(1)} %get-tuple-element.73), channel_id=1, source_target_pairs={{0,6},{1,7},{2,0},{3,1},{4,2},{5,3},{6,4},{7,5},{8,14},{9,15},{10,... | collective-permute-start | bytes 642056 | tf_op jit(solution)/shard_map/ppermute | solution.py:408
  114.6 3.2 %collective-permute-start.33 = (bf16[152,704]{1,0:T(8,128)(2,1)S(1)}, bf16[152,704]{1,0:T(8,128)(2,1)S(1)}, u32[]{:S(2)}, u32[]{:S(2)}) collective-permute-start(bf16[152,704]{1,0:T(8,128)(2,1)S(1)} %get-tuple-element.75), channel_id=1, source_target_pairs={{0,6},{1,7},{2,0},{3,1},{4,2},{5,3},{6,4},{7,5},{8,14},{9,15},{10,... | collective-permute-start | bytes 642056 | tf_op jit(solution)/shard_map/ppermute | solution.py:408
  117.8 3.2 %collective-permute-done.31 = bf16[152,704]{1,0:T(8,128)(2,1)S(1)} collective-permute-done((bf16[152,704]{1,0:T(8,128)(2,1)S(1)}, bf16[152,704]{1,0:T(8,128)(2,1)S(1)}, u32[]{:S(2)}, u32[]{:S(2)}) %collective-permute-start.31) | collective-permute-done | bytes 214048 | tf_op jit(solution)/shard_map/ppermute | solution.py:408
  121.0 0.1 fusion.7
  121.0 2.0 %collective-permute-start.32 = (bf16[152,704]{1,0:T(8,128)(2,1)S(1)}, bf16[152,704]{1,0:T(8,128)(2,1)S(1)}, u32[]{:S(2)}, u32[]{:S(2)}) collective-permute-start(bf16[152,704]{1,0:T(8,128)(2,1)S(1)} %get-tuple-element.70), channel_id=1, source_target_pairs={{0,2},{1,3},{2,4},{3,5},{4,6},{5,7},{6,0},{7,1},{8,10},{9,11},{10,... | collective-permute-start | bytes 642056 | tf_op jit(solution)/shard_map/ppermute | solution.py:408
  123.0 1.5 %collective-permute-start.36 = (bf16[152,704]{1,0:T(8,128)(2,1)S(1)}, bf16[152,704]{1,0:T(8,128)(2,1)S(1)}, u32[]{:S(2)}, u32[]{:S(2)}) collective-permute-start(bf16[152,704]{1,0:T(8,128)(2,1)S(1)} %get-tuple-element.71), channel_id=1, source_target_pairs={{0,6},{1,7},{2,0},{3,1},{4,2},{5,3},{6,4},{7,5},{8,14},{9,15},{10,... | collective-permute-start | bytes 642056 | tf_op jit(solution)/shard_map/ppermute | solution.py:408
  124.5 0.1 convert_add_fusion
  124.6 1.3 %collective-permute-done.34 = bf16[152,704]{1,0:T(8,128)(2,1)S(1)} collective-permute-done((bf16[152,704]{1,0:T(8,128)(2,1)S(1)}, bf16[152,704]{1,0:T(8,128)(2,1)S(1)}, u32[]{:S(2)}, u32[]{:S(2)}) %collective-permute-start.34) | collective-permute-done | bytes 214048 | tf_op jit(solution)/shard_map/ppermute | solution.py:408
  126.0 4.5 %collective-permute-done.32 = bf16[152,704]{1,0:T(8,128)(2,1)S(1)} collective-permute-done((bf16[152,704]{1,0:T(8,128)(2,1)S(1)}, bf16[152,704]{1,0:T(8,128)(2,1)S(1)}, u32[]{:S(2)}, u32[]{:S(2)}) %collective-permute-start.32) | collective-permute-done | bytes 214048 | tf_op jit(solution)/shard_map/ppermute | solution.py:408
  130.5 0.2 fusion.5
  130.6 1.0 maximum_bitcast_fusion
  (61 shorter events, 0.8 us)
Async XLA Ops:
  0.6 13.6 %copy-start = (bf16[1,2,1216,704]{2,3,1,0:T(8,128)(2,1)S(1)}, bf16[1,2,1216,704]{2,3,1,0:T(8,128)(2,1)}, u32[]{:S(2)}) copy-start(bf16[1,2,1216,704]{2,3,1,0:T(8,128)(2,1)} %param.8) | copy-start | bytes 10272772
  0.6 13.6 %copy-start.4 = (f32[2,256,256]{2,1,0:T(8,128)S(1)}, f32[2,256,256]{2,1,0:T(8,128)}, u32[]{:S(2)}) copy-start(f32[2,256,256]{2,1,0:T(8,128)} %constant.6.clone.base.refs_10_) | copy-start | bytes 1572868
  0.7 13.6 %copy-start.5 = (f32[16,2,256]{2,1,0:T(2,128)S(1)}, f32[16,2,256]{2,1,0:T(2,128)}, u32[]{:S(2)}) copy-start(f32[16,2,256]{2,1,0:T(2,128)} %constant.7.clone.phases.left.right.refs_11_.refs_12_) | copy-start | bytes 98308
  8.9 10.3 %collective-permute-start = (bf16[4,128,256]{2,1,0:T(8,128)(2,1)}, bf16[4,128,256]{2,1,0:T(8,128)(2,1)S(1)}, u32[]{:S(2)}, u32[]{:S(2)}) collective-permute-start(bf16[4,128,256]{2,1,0:T(8,128)(2,1)} %get-tuple-element.36), channel_id=1, source_target_pairs={{0,32},{8,40},{16,48},{24,56},{32,64},{40,72},{48,80},{56,88},{64,... | collective-permute-start | bytes 786440 | tf_op jit(solution)/shard_map/ppermute | solution.py:408
  10.5 8.8 %collective-permute-start.1 = (bf16[4,128,256]{2,1,0:T(8,128)(2,1)}, bf16[4,128,256]{2,1,0:T(8,128)(2,1)S(1)}, u32[]{:S(2)}, u32[]{:S(2)}) collective-permute-start(bf16[4,128,256]{2,1,0:T(8,128)(2,1)} %get-tuple-element.37), channel_id=1, source_target_pairs={{0,96},{8,104},{16,112},{24,120},{32,0},{40,8},{48,16},{56,24},{64... | collective-permute-start | bytes 786440 | tf_op jit(solution)/shard_map/ppermute | solution.py:408
  12.2 7.7 %collective-permute-start.2 = (bf16[4,128,256]{2,1,0:T(8,128)(2,1)}, bf16[4,128,256]{2,1,0:T(8,128)(2,1)S(1)}, u32[]{:S(2)}, u32[]{:S(2)}) collective-permute-start(bf16[4,128,256]{2,1,0:T(8,128)(2,1)} %get-tuple-element.38), channel_id=1, source_target_pairs={{0,8},{8,16},{16,24},{24,0},{32,40},{40,48},{48,56},{56,32},{64,72... | collective-permute-start | bytes 786440 | tf_op jit(solution)/shard_map/ppermute | solution.py:408
  12.4 8.8 %collective-permute-start.3 = (bf16[4,128,256]{2,1,0:T(8,128)(2,1)}, bf16[4,128,256]{2,1,0:T(8,128)(2,1)S(1)}, u32[]{:S(2)}, u32[]{:S(2)}) collective-permute-start(bf16[4,128,256]{2,1,0:T(8,128)(2,1)} %get-tuple-element.39), channel_id=1, source_target_pairs={{0,24},{8,0},{16,8},{24,16},{32,56},{40,32},{48,40},{56,48},{64,88... | collective-permute-start | bytes 786440 | tf_op jit(solution)/shard_map/ppermute | solution.py:408
  14.3 0.7 copy-start.6
  14.9 4.2 %copy-start.8 = (bf16[3,256,256]{2,1,0:T(8,128)(2,1)S(1)}, bf16[3,256,256]{2,1,0:T(8,128)(2,1)}, u32[]{:S(2)}) copy-start(bf16[3,256,256]{2,1,0:T(8,128)(2,1)} %get-tuple-element.48) | copy-start | bytes 1179652
  14.9 4.2 %copy-start.9 = (bf16[3,256,256]{2,1,0:T(8,128)(2,1)S(1)}, bf16[3,256,256]{2,1,0:T(8,128)(2,1)}, u32[]{:S(2)}) copy-start(bf16[3,256,256]{2,1,0:T(8,128)(2,1)} %get-tuple-element.58) | copy-start | bytes 1179652
  21.2 13.3 %collective-permute-start.10 = (bf16[4,256,256]{2,1,0:T(8,128)(2,1)S(1)}, bf16[4,256,256]{2,1,0:T(8,128)(2,1)S(1)}, u32[]{:S(2)}, u32[]{:S(2)}) collective-permute-start(bf16[4,256,256]{2,1,0:T(8,128)(2,1)S(1)} %maximum_add_fusion.3), channel_id=1, source_target_pairs={{0,24},{8,0},{16,8},{24,16},{32,56},{40,32},{48,40},{56,48},{64,88... | collective-permute-start | bytes 1572872 | tf_op jit(solution)/shard_map/ppermute | solution.py:408
  21.9 5.2 %copy-start.1 = (s32[1,2,8192]{2,1,0:T(2,128)S(1)}, s32[1,2,8192]{2,1,0:T(2,128)}, u32[]{:S(2)}) copy-start(s32[1,2,8192]{2,1,0:T(2,128)} %offsets) | copy-start | bytes 196612
  21.9 5.2 %copy-start.2 = (f32[1,2,8192]{2,1,0:T(2,128)S(1)}, f32[1,2,8192]{2,1,0:T(2,128)}, u32[]{:S(2)}) copy-start(f32[1,2,8192]{2,1,0:T(2,128)} %fractions.1) | copy-start | bytes 196612
  21.9 12.6 %collective-permute-start.9 = (bf16[4,256,256]{2,1,0:T(8,128)(2,1)S(1)}, bf16[4,256,256]{2,1,0:T(8,128)(2,1)S(1)}, u32[]{:S(2)}, u32[]{:S(2)}) collective-permute-start(bf16[4,256,256]{2,1,0:T(8,128)(2,1)S(1)} %maximum_add_fusion.2), channel_id=1, source_target_pairs={{0,8},{8,16},{16,24},{24,0},{32,40},{40,48},{48,56},{56,32},{64,72... | collective-permute-start | bytes 1572872 | tf_op jit(solution)/shard_map/ppermute | solution.py:408
  24.8 13.9 %collective-permute-start.5 = (bf16[4,256,256]{2,1,0:T(8,128)(2,1)S(1)}, bf16[4,256,256]{2,1,0:T(8,128)(2,1)S(1)}, u32[]{:S(2)}, u32[]{:S(2)}) collective-permute-start(bf16[4,256,256]{2,1,0:T(8,128)(2,1)S(1)} %maximum_add_fusion.1), channel_id=1, source_target_pairs={{0,96},{8,104},{16,112},{24,120},{32,0},{40,8},{48,16},{56,24},{64... | collective-permute-start | bytes 1572872 | tf_op jit(solution)/shard_map/ppermute | solution.py:408
  26.5 16.6 %collective-permute-start.4 = (bf16[4,256,256]{2,1,0:T(8,128)(2,1)S(1)}, bf16[4,256,256]{2,1,0:T(8,128)(2,1)S(1)}, u32[]{:S(2)}, u32[]{:S(2)}) collective-permute-start(bf16[4,256,256]{2,1,0:T(8,128)(2,1)S(1)} %maximum_add_fusion), channel_id=1, source_target_pairs={{0,32},{8,40},{16,48},{24,56},{32,64},{40,72},{48,80},{56,88},{64,... | collective-permute-start | bytes 1572872 | tf_op jit(solution)/shard_map/ppermute | solution.py:408
  34.7 16.3 %copy-start.3 = (f32[1,2,8192]{2,1,0:T(2,128)S(1)}, f32[1,2,8192]{2,1,0:T(2,128)}, u32[]{:S(2)}) copy-start(f32[1,2,8192]{2,1,0:T(2,128)} %refs_10_.2) | copy-start | bytes 196612
  34.8 8.7 %collective-permute-start.13 = (bf16[1,256,256]{2,1,0:T(8,128)(2,1)S(1)}, bf16[1,256,256]{2,1,0:T(8,128)(2,1)S(1)}, u32[]{:S(2)}, u32[]{:S(2)}) collective-permute-start(bf16[1,256,256]{2,1,0:T(8,128)(2,1)S(1)} %get-tuple-element.78), channel_id=1, source_target_pairs={{0,64},{8,72},{16,80},{24,88},{32,96},{40,104},{48,112},{56,120},{... | collective-permute-start | bytes 393224 | tf_op jit(solution)/shard_map/ppermute | solution.py:408
  36.6 10.8 %collective-permute-start.12 = (bf16[1,256,256]{2,1,0:T(8,128)(2,1)S(1)}, bf16[1,256,256]{2,1,0:T(8,128)(2,1)S(1)}, u32[]{:S(2)}, u32[]{:S(2)}) collective-permute-start(bf16[1,256,256]{2,1,0:T(8,128)(2,1)S(1)} %get-tuple-element.79), channel_id=1, source_target_pairs={{0,96},{8,104},{16,112},{24,120},{32,0},{40,8},{48,16},{56,24},{64... | collective-permute-start | bytes 393224 | tf_op jit(solution)/shard_map/ppermute | solution.py:408
  37.7 9.6 %collective-permute-start.11 = (bf16[1,256,256]{2,1,0:T(8,128)(2,1)S(1)}, bf16[1,256,256]{2,1,0:T(8,128)(2,1)S(1)}, u32[]{:S(2)}, u32[]{:S(2)}) collective-permute-start(bf16[1,256,256]{2,1,0:T(8,128)(2,1)S(1)} %get-tuple-element.80), channel_id=1, source_target_pairs={{0,32},{8,40},{16,48},{24,56},{32,64},{40,72},{48,80},{56,88},{64,... | collective-permute-start | bytes 393224 | tf_op jit(solution)/shard_map/ppermute | solution.py:408
  43.3 6.7 %collective-permute-start.8 = (bf16[1,256,256]{2,1,0:T(8,128)(2,1)S(1)}, bf16[1,256,256]{2,1,0:T(8,128)(2,1)S(1)}, u32[]{:S(2)}, u32[]{:S(2)}) collective-permute-start(bf16[1,256,256]{2,1,0:T(8,128)(2,1)S(1)} %get-tuple-element.82), channel_id=1, source_target_pairs={{0,16},{8,24},{16,0},{24,8},{32,48},{40,56},{48,32},{56,40},{64,80... | collective-permute-start | bytes 393224 | tf_op jit(solution)/shard_map/ppermute | solution.py:408
  43.4 7.7 %collective-permute-start.7 = (bf16[1,256,256]{2,1,0:T(8,128)(2,1)S(1)}, bf16[1,256,256]{2,1,0:T(8,128)(2,1)S(1)}, u32[]{:S(2)}, u32[]{:S(2)}) collective-permute-start(bf16[1,256,256]{2,1,0:T(8,128)(2,1)S(1)} %get-tuple-element.83), channel_id=1, source_target_pairs={{0,24},{8,0},{16,8},{24,16},{32,56},{40,32},{48,40},{56,48},{64,88... | collective-permute-start | bytes 393224 | tf_op jit(solution)/shard_map/ppermute | solution.py:408
  43.5 7.6 %collective-permute-start.6 = (bf16[1,256,256]{2,1,0:T(8,128)(2,1)S(1)}, bf16[1,256,256]{2,1,0:T(8,128)(2,1)S(1)}, u32[]{:S(2)}, u32[]{:S(2)}) collective-permute-start(bf16[1,256,256]{2,1,0:T(8,128)(2,1)S(1)} %get-tuple-element.84), channel_id=1, source_target_pairs={{0,8},{8,16},{16,24},{24,0},{32,40},{40,48},{48,56},{56,32},{64,72... | collective-permute-start | bytes 393224 | tf_op jit(solution)/shard_map/ppermute | solution.py:408
  57.7 5.3 %collective-permute-start.23 = (bf16[1,256,256]{2,1,0:T(8,128)(2,1)S(1)}, bf16[1,256,256]{2,1,0:T(8,128)(2,1)S(1)}, u32[]{:S(2)}, u32[]{:S(2)}) collective-permute-start(bf16[1,256,256]{2,1,0:T(8,128)(2,1)S(1)} %get-tuple-element.67), channel_id=1, source_target_pairs={{0,8},{8,16},{16,24},{24,0},{32,40},{40,48},{48,56},{56,32},{64,72... | collective-permute-start | bytes 393224 | tf_op jit(solution)/shard_map/ppermute | solution.py:408
  59.5 6.6 %collective-permute-start.22 = (bf16[1,256,256]{2,1,0:T(8,128)(2,1)S(1)}, bf16[1,256,256]{2,1,0:T(8,128)(2,1)S(1)}, u32[]{:S(2)}, u32[]{:S(2)}) collective-permute-start(bf16[1,256,256]{2,1,0:T(8,128)(2,1)S(1)} %get-tuple-element.67), channel_id=1, source_target_pairs={{0,24},{8,0},{16,8},{24,16},{32,56},{40,32},{48,40},{56,48},{64,88... | collective-permute-start | bytes 393224 | tf_op jit(solution)/shard_map/ppermute | solution.py:408
  59.7 6.6 %collective-permute-start.15 = (bf16[1,256,256]{2,1,0:T(8,128)(2,1)S(1)}, bf16[1,256,256]{2,1,0:T(8,128)(2,1)S(1)}, u32[]{:S(2)}, u32[]{:S(2)}) collective-permute-start(bf16[1,256,256]{2,1,0:T(8,128)(2,1)S(1)} %get-tuple-element.66), channel_id=1, source_target_pairs={{0,32},{8,40},{16,48},{24,56},{32,64},{40,72},{48,80},{56,88},{64,... | collective-permute-start | bytes 393224 | tf_op jit(solution)/shard_map/ppermute | solution.py:408
  59.7 6.6 %collective-permute-start.14 = (bf16[1,256,256]{2,1,0:T(8,128)(2,1)S(1)}, bf16[1,256,256]{2,1,0:T(8,128)(2,1)S(1)}, u32[]{:S(2)}, u32[]{:S(2)}) collective-permute-start(bf16[1,256,256]{2,1,0:T(8,128)(2,1)S(1)} %get-tuple-element.66), channel_id=1, source_target_pairs={{0,96},{8,104},{16,112},{24,120},{32,0},{40,8},{48,16},{56,24},{64... | collective-permute-start | bytes 393224 | tf_op jit(solution)/shard_map/ppermute | solution.py:408
  63.0 6.9 %collective-permute-start.24 = (bf16[1,128,256]{2,1,0:T(8,128)(2,1)S(1)}, bf16[1,128,256]{2,1,0:T(8,128)(2,1)S(1)}, u32[]{:S(2)}, u32[]{:S(2)}) collective-permute-start(bf16[1,128,256]{2,1,0:T(8,128)(2,1)S(1)} %slice.142), channel_id=1, source_target_pairs={{0,8},{8,16},{16,24},{24,0},{32,40},{40,48},{48,56},{56,32},{64,72... | collective-permute-start | bytes 196616 | tf_op jit(solution)/shard_map/ppermute | solution.py:408
  66.1 6.3 %collective-permute-start.25 = (bf16[1,128,256]{2,1,0:T(8,128)(2,1)S(1)}, bf16[1,128,256]{2,1,0:T(8,128)(2,1)S(1)}, u32[]{:S(2)}, u32[]{:S(2)}) collective-permute-start(bf16[1,128,256]{2,1,0:T(8,128)(2,1)S(1)} %slice.143), channel_id=1, source_target_pairs={{0,24},{8,0},{16,8},{24,16},{32,56},{40,32},{48,40},{56,48},{64,88... | collective-permute-start | bytes 196616 | tf_op jit(solution)/shard_map/ppermute | solution.py:408
  66.3 9.5 %collective-permute-start.16 = (bf16[1,128,256]{2,1,0:T(8,128)(2,1)S(1)}, bf16[1,128,256]{2,1,0:T(8,128)(2,1)S(1)}, u32[]{:S(2)}, u32[]{:S(2)}) collective-permute-start(bf16[1,128,256]{2,1,0:T(8,128)(2,1)S(1)} %slice.138), channel_id=1, source_target_pairs={{0,32},{8,40},{16,48},{24,56},{32,64},{40,72},{48,80},{56,88},{64,... | collective-permute-start | bytes 196616 | tf_op jit(solution)/shard_map/ppermute | solution.py:408
  66.3 31.3 %copy-start.7 = (s32[42]{0:T(128)S(1)}, s32[42]{0:T(128)}, u32[]{:S(2)}) copy-start(s32[42]{0:T(128)} %get-tuple-element.40.place) | copy-start | bytes 508
  66.3 9.4 %collective-permute-start.17 = (bf16[1,128,256]{2,1,0:T(8,128)(2,1)S(1)}, bf16[1,128,256]{2,1,0:T(8,128)(2,1)S(1)}, u32[]{:S(2)}, u32[]{:S(2)}) collective-permute-start(bf16[1,128,256]{2,1,0:T(8,128)(2,1)S(1)} %slice.139), channel_id=1, source_target_pairs={{0,96},{8,104},{16,112},{24,120},{32,0},{40,8},{48,16},{56,24},{64... | collective-permute-start | bytes 196616 | tf_op jit(solution)/shard_map/ppermute | solution.py:408
  72.4 11.9 %collective-permute-start.27 = (bf16[4,256,256]{2,1,0:T(8,128)(2,1)S(1)}, bf16[4,256,256]{2,1,0:T(8,128)(2,1)S(1)}, u32[]{:S(2)}, u32[]{:S(2)}) collective-permute-start(bf16[4,256,256]{2,1,0:T(8,128)(2,1)S(1)} %maximum_maximum_fusion.1.refs_5_), channel_id=1, source_target_pairs={{0,32},{8,40},{16,48},{24,56},{32,64},{40,72},{48,80},{56,88},{64,... | collective-permute-start | bytes 1572872 | tf_op jit(solution)/shard_map/ppermute | solution.py:408
  72.5 11.9 %collective-permute-start.26 = (bf16[4,256,256]{2,1,0:T(8,128)(2,1)S(1)}, bf16[4,256,256]{2,1,0:T(8,128)(2,1)S(1)}, u32[]{:S(2)}, u32[]{:S(2)}) collective-permute-start(bf16[4,256,256]{2,1,0:T(8,128)(2,1)S(1)} %maximum_maximum_fusion.1.refs_5_), channel_id=1, source_target_pairs={{0,96},{8,104},{16,112},{24,120},{32,0},{40,8},{48,16},{56,24},{64... | collective-permute-start | bytes 1572872 | tf_op jit(solution)/shard_map/ppermute | solution.py:408
  75.8 12.0 %collective-permute-start.19 = (bf16[4,256,256]{2,1,0:T(8,128)(2,1)S(1)}, bf16[4,256,256]{2,1,0:T(8,128)(2,1)S(1)}, u32[]{:S(2)}, u32[]{:S(2)}) collective-permute-start(bf16[4,256,256]{2,1,0:T(8,128)(2,1)S(1)} %maximum_maximum_fusion.refs_0_), channel_id=1, source_target_pairs={{0,8},{8,16},{16,24},{24,0},{32,40},{40,48},{48,56},{56,32},{64,72... | collective-permute-start | bytes 1572872 | tf_op jit(solution)/shard_map/ppermute | solution.py:408
  77.1 12.6 %collective-permute-start.18 = (bf16[4,256,256]{2,1,0:T(8,128)(2,1)S(1)}, bf16[4,256,256]{2,1,0:T(8,128)(2,1)S(1)}, u32[]{:S(2)}, u32[]{:S(2)}) collective-permute-start(bf16[4,256,256]{2,1,0:T(8,128)(2,1)S(1)} %maximum_maximum_fusion.refs_0_), channel_id=1, source_target_pairs={{0,24},{8,0},{16,8},{24,16},{32,56},{40,32},{48,40},{56,48},{64,88... | collective-permute-start | bytes 1572872 | tf_op jit(solution)/shard_map/ppermute | solution.py:408
  84.4 7.7 %collective-permute-start.28 = (bf16[4,128,256]{2,1,0:T(8,128)(2,1)S(1)}, bf16[4,128,256]{2,1,0:T(8,128)(2,1)S(1)}, u32[]{:S(2)}, u32[]{:S(2)}) collective-permute-start(bf16[4,128,256]{2,1,0:T(8,128)(2,1)S(1)} %slice.144), channel_id=1, source_target_pairs={{0,32},{8,40},{16,48},{24,56},{32,64},{40,72},{48,80},{56,88},{64,... | collective-permute-start | bytes 786440 | tf_op jit(solution)/shard_map/ppermute | solution.py:408
  84.5 7.5 %collective-permute-start.29 = (bf16[4,128,256]{2,1,0:T(8,128)(2,1)S(1)}, bf16[4,128,256]{2,1,0:T(8,128)(2,1)S(1)}, u32[]{:S(2)}, u32[]{:S(2)}) collective-permute-start(bf16[4,128,256]{2,1,0:T(8,128)(2,1)S(1)} %slice.145), channel_id=1, source_target_pairs={{0,96},{8,104},{16,112},{24,120},{32,0},{40,8},{48,16},{56,24},{64... | collective-permute-start | bytes 786440 | tf_op jit(solution)/shard_map/ppermute | solution.py:408
  87.8 6.4 %collective-permute-start.20 = (bf16[4,128,256]{2,1,0:T(8,128)(2,1)S(1)}, bf16[4,128,256]{2,1,0:T(8,128)(2,1)S(1)}, u32[]{:S(2)}, u32[]{:S(2)}) collective-permute-start(bf16[4,128,256]{2,1,0:T(8,128)(2,1)S(1)} %slice.140), channel_id=1, source_target_pairs={{0,8},{8,16},{16,24},{24,0},{32,40},{40,48},{48,56},{56,32},{64,72... | collective-permute-start | bytes 786440 | tf_op jit(solution)/shard_map/ppermute | solution.py:408
  89.7 7.9 %collective-permute-start.21 = (bf16[4,128,256]{2,1,0:T(8,128)(2,1)S(1)}, bf16[4,128,256]{2,1,0:T(8,128)(2,1)S(1)}, u32[]{:S(2)}, u32[]{:S(2)}) collective-permute-start(bf16[4,128,256]{2,1,0:T(8,128)(2,1)S(1)} %slice.141), channel_id=1, source_target_pairs={{0,24},{8,0},{16,8},{24,16},{32,56},{40,32},{48,40},{56,48},{64,88... | collective-permute-start | bytes 786440 | tf_op jit(solution)/shard_map/ppermute | solution.py:408
  105.9 3.9 %collective-permute-start.30 = (bf16[4,2,152,704]{3,2,1,0:T(8,128)(2,1)S(1)}, bf16[4,2,152,704]{3,2,1,0:T(8,128)(2,1)S(1)}, u32[]{:S(2)}, u32[]{:S(2)}) collective-permute-start(bf16[4,2,152,704]{3,2,1,0:T(8,128)(2,1)S(1)} %get-tuple-element.69), channel_id=1, source_target_pairs={{0,1},{1,0},{2,3},{3,2},{4,5},{5,4},{6,7},{7,6},{8,9},{9,8},{10,11... | collective-permute-start | bytes 5136392 | tf_op jit(solution)/shard_map/ppermute | solution.py:449
  110.5 10.5 %collective-permute-start.31 = (bf16[152,704]{1,0:T(8,128)(2,1)S(1)}, bf16[152,704]{1,0:T(8,128)(2,1)S(1)}, u32[]{:S(2)}, u32[]{:S(2)}) collective-permute-start(bf16[152,704]{1,0:T(8,128)(2,1)S(1)} %get-tuple-element.72), channel_id=1, source_target_pairs={{0,2},{1,3},{2,4},{3,5},{4,6},{5,7},{6,0},{7,1},{8,10},{9,11},{10,... | collective-permute-start | bytes 642056 | tf_op jit(solution)/shard_map/ppermute | solution.py:408
  112.4 8.6 %collective-permute-start.35 = (bf16[152,704]{1,0:T(8,128)(2,1)S(1)}, bf16[152,704]{1,0:T(8,128)(2,1)S(1)}, u32[]{:S(2)}, u32[]{:S(2)}) collective-permute-start(bf16[152,704]{1,0:T(8,128)(2,1)S(1)} %get-tuple-element.73), channel_id=1, source_target_pairs={{0,6},{1,7},{2,0},{3,1},{4,2},{5,3},{6,4},{7,5},{8,14},{9,15},{10,... | collective-permute-start | bytes 642056 | tf_op jit(solution)/shard_map/ppermute | solution.py:408
  114.6 11.4 %collective-permute-start.34 = (bf16[152,704]{1,0:T(8,128)(2,1)S(1)}, bf16[152,704]{1,0:T(8,128)(2,1)S(1)}, u32[]{:S(2)}, u32[]{:S(2)}) collective-permute-start(bf16[152,704]{1,0:T(8,128)(2,1)S(1)} %get-tuple-element.74), channel_id=1, source_target_pairs={{0,2},{1,3},{2,4},{3,5},{4,6},{5,7},{6,0},{7,1},{8,10},{9,11},{10,... | collective-permute-start | bytes 642056 | tf_op jit(solution)/shard_map/ppermute | solution.py:408
  114.6 11.4 %collective-permute-start.33 = (bf16[152,704]{1,0:T(8,128)(2,1)S(1)}, bf16[152,704]{1,0:T(8,128)(2,1)S(1)}, u32[]{:S(2)}, u32[]{:S(2)}) collective-permute-start(bf16[152,704]{1,0:T(8,128)(2,1)S(1)} %get-tuple-element.75), channel_id=1, source_target_pairs={{0,6},{1,7},{2,0},{3,1},{4,2},{5,3},{6,4},{7,5},{8,14},{9,15},{10,... | collective-permute-start | bytes 642056 | tf_op jit(solution)/shard_map/ppermute | solution.py:408
  121.0 9.4 %collective-permute-start.32 = (bf16[152,704]{1,0:T(8,128)(2,1)S(1)}, bf16[152,704]{1,0:T(8,128)(2,1)S(1)}, u32[]{:S(2)}, u32[]{:S(2)}) collective-permute-start(bf16[152,704]{1,0:T(8,128)(2,1)S(1)} %get-tuple-element.70), channel_id=1, source_target_pairs={{0,2},{1,3},{2,4},{3,5},{4,6},{5,7},{6,0},{7,1},{8,10},{9,11},{10,... | collective-permute-start | bytes 642056 | tf_op jit(solution)/shard_map/ppermute | solution.py:408
  123.0 7.5 %collective-permute-start.36 = (bf16[152,704]{1,0:T(8,128)(2,1)S(1)}, bf16[152,704]{1,0:T(8,128)(2,1)S(1)}, u32[]{:S(2)}, u32[]{:S(2)}) collective-permute-start(bf16[152,704]{1,0:T(8,128)(2,1)S(1)} %get-tuple-element.71), channel_id=1, source_target_pairs={{0,6},{1,7},{2,0},{3,1},{4,2},{5,3},{6,4},{7,5},{8,14},{9,15},{10,... | collective-permute-start | bytes 642056 | tf_op jit(solution)/shard_map/ppermute | solution.py:408

commit v7 on v6

--- a/solution.py
+++ b/solution.py
@@ -12,7 +12,7 @@
 MC = 256
 STEP = 64
 KS = 8
-BLOCK = 2048
+BLOCK = 4096
 LANES = 128
 HALF = SUB // 2
 RING = 4

time: 132 us -> 131 us (level)
  transfers between devices with their start and end apart: 37 -> 37, of which waited for: 16 -> 15; matrix products, arithmetic and copies ran while one was open for 1% -> 1% of each run, Pallas kernels for 8% -> 8%
where the time goes in v7:
time: 131 us
  starting transfers between devices  51.7 us (39%)
  waiting for transfers between devices  41.2 us (31%)
  Pallas kernels  32.7 us (25%)
  other arithmetic  2.77 us (2%)
  between operations  1.66 us (1%)
    ppermute x36, starting transfers between devices, move(): return lax.ppermute(value, *route)  51.6 us
    ppermute x36, waiting for transfers between devices, move(): return lax.ppermute(value, *route)  37.4 us
    pallas_call x1, Pallas kernels, adjoint_plane(): pl.pallas_call(adjoint_kernel, out_shape=(jax.ShapeDtypeStruct(band_shape...  8.36 us
    pallas_call x1, Pallas kernels, far_parts(): pl.pallas_call(far_kernel, out_shape=tuple((jax.ShapeDtypeStruct(s, jnp.b...  8.24 us
    pallas_call x1, Pallas kernels, residuals(): pl.pallas_call(residual_kernel, out_shape=(jax.ShapeDtypeStruct(observed....  6.16 us
    pallas_call x1, Pallas kernels, kernel_weights(): pl.pallas_call(weights_kernel, out_shape=(shape, shape), grid=(slots // B...  5.77 us
    pallas_call x1, Pallas kernels, near_parts(): pl.pallas_call(near_kernel, out_shape=tuple((jax.ShapeDtypeStruct(s, jnp....  4.19 us
    ppermute x1, waiting for transfers between devices, sum_rings(): swapped = lax.ppermute(given, 'sub', [(i, i ^ 1) for i in range(2 * RING)])  3.82 us
  transfers between devices with their start and end apart: 37, of which 15 were waited for; matrix products, arithmetic and copies ran while one was open for 1% of the time, Pallas kernels for 8%

profile of v7, /device:TPU:24, one launch (start us, length us, event | category | flops | bytes accessed | tf_op | source)
XLA Modules:
  0.0 131.0 jit_solution(5218213745351382400)
XLA Ops:
  0.7 8.2 %far_parts.1 = (bf16[4,128,256]{2,1,0:T(8,128)(2,1)}, bf16[4,128,256]{2,1,0:T(8,128)(2,1)}, bf16[4,128,256]{2,1,0:T(8,128)(2,1)}, bf16[4,128,256]{2,1,0:T(8,128)...) custom-call(s32[128]{0:T(128)} %worker.1, bf16[1,2,704,1216]{3,2,1,0:T(8,128)(2,1)} %bitcast.39, ...), custom_call_target="tpu_custom_call" | custom-call | flops 2147483648 | bytes 8388608 | tf_op jit(solution)/shard_map/far_parts/pallas_call | solution.py:172
  8.9 1.6 %collective-permute-start = (bf16[4,128,256]{2,1,0:T(8,128)(2,1)}, bf16[4,128,256]{2,1,0:T(8,128)(2,1)S(1)}, u32[]{:S(2)}, u32[]{:S(2)}) collective-permute-start(bf16[4,128,256]{2,1,0:T(8,128)(2,1)} %get-tuple-element.36), channel_id=1, source_target_pairs={{0,32},{8,40},{16,48},{24,56},{32,64},{40,72},{48,80},{56,88},{64,... | collective-permute-start | bytes 786440 | tf_op jit(solution)/shard_map/ppermute | solution.py:408
  10.5 1.7 %collective-permute-start.1 = (bf16[4,128,256]{2,1,0:T(8,128)(2,1)}, bf16[4,128,256]{2,1,0:T(8,128)(2,1)S(1)}, u32[]{:S(2)}, u32[]{:S(2)}) collective-permute-start(bf16[4,128,256]{2,1,0:T(8,128)(2,1)} %get-tuple-element.37), channel_id=1, source_target_pairs={{0,96},{8,104},{16,112},{24,120},{32,0},{40,8},{48,16},{56,24},{64... | collective-permute-start | bytes 786440 | tf_op jit(solution)/shard_map/ppermute | solution.py:408
  12.2 0.1 collective-permute-start.2
  12.4 1.9 %collective-permute-start.3 = (bf16[4,128,256]{2,1,0:T(8,128)(2,1)}, bf16[4,128,256]{2,1,0:T(8,128)(2,1)S(1)}, u32[]{:S(2)}, u32[]{:S(2)}) collective-permute-start(bf16[4,128,256]{2,1,0:T(8,128)(2,1)} %get-tuple-element.39), channel_id=1, source_target_pairs={{0,24},{8,0},{16,8},{24,16},{32,56},{40,32},{48,40},{56,48},{64,88... | collective-permute-start | bytes 786440 | tf_op jit(solution)/shard_map/ppermute | solution.py:408
  14.3 0.7 copy-done.6
  14.9 4.2 %near_parts.1 = (bf16[3,256,256]{2,1,0:T(8,128)(2,1)S(1)}, bf16[3,256,256]{2,1,0:T(8,128)(2,1)S(1)}, bf16[3,256,256]{2,1,0:T(8,128)(2,1)S(1)}, bf16[3,256,256]{2...) custom-call(s32[42]{0:T(128)S(1)} %copy-done.6, ...), custom_call_target="tpu_custom_call" | custom-call | flops 2147483648 | bytes 8388608 | tf_op jit(solution)/shard_map/near_parts/pallas_call | solution.py:201
  19.2 0.7 collective-permute-done.2
  19.9 1.2 collective-permute-done.3
  21.1 0.1 maximum_add_fusion.3
  21.2 0.6 collective-permute-start.10
  21.8 0.1 maximum_add_fusion.2
  21.9 2.8 %collective-permute-start.9 = (bf16[4,256,256]{2,1,0:T(8,128)(2,1)S(1)}, bf16[4,256,256]{2,1,0:T(8,128)(2,1)S(1)}, u32[]{:S(2)}, u32[]{:S(2)}) collective-permute-start(bf16[4,256,256]{2,1,0:T(8,128)(2,1)S(1)} %maximum_add_fusion.2), channel_id=1, source_target_pairs={{0,8},{8,16},{16,24},{24,0},{32,40},{40,48},{48,56},{56,32},{64,72... | collective-permute-start | bytes 1572872 | tf_op jit(solution)/shard_map/ppermute | solution.py:408
  24.7 0.1 maximum_add_fusion.1
  24.8 1.6 %collective-permute-start.5 = (bf16[4,256,256]{2,1,0:T(8,128)(2,1)S(1)}, bf16[4,256,256]{2,1,0:T(8,128)(2,1)S(1)}, u32[]{:S(2)}, u32[]{:S(2)}) collective-permute-start(bf16[4,256,256]{2,1,0:T(8,128)(2,1)S(1)} %maximum_add_fusion.1), channel_id=1, source_target_pairs={{0,96},{8,104},{16,112},{24,120},{32,0},{40,8},{48,16},{56,24},{64... | collective-permute-start | bytes 1572872 | tf_op jit(solution)/shard_map/ppermute | solution.py:408
  26.4 0.1 maximum_add_fusion
  26.5 0.7 collective-permute-start.4
  27.3 5.8 %kernel_weights.1 = (bf16[256,8192]{1,0:T(8,128)(2,1)S(1)}, bf16[256,8192]{1,0:T(8,128)(2,1)S(1)}) custom-call(s32[1,2,8192]{2,1,0:T(2,128)S(1)} %copy-done.1, f32[1,2,8192]{2,1,0:T(2,128)S(1)} %copy-done.2), custom_call_target="tpu_custom_call" | custom-call | flops 41943040 | bytes 8388608 | tf_op jit(solution)/shard_map/kernel_weights/pallas_call | solution.py:238
  33.0 1.5 %collective-permute-done.10 = bf16[4,256,256]{2,1,0:T(8,128)(2,1)S(1)} collective-permute-done((bf16[4,256,256]{2,1,0:T(8,128)(2,1)S(1)}, bf16[4,256,256]{2,1,0:T(8,128)(2,1)S(1)}, u32[]{:S(2)}, u32[]{:S(2)}) %collective-permute-start.10) | collective-permute-done | bytes 524320 | tf_op jit(solution)/shard_map/ppermute | solution.py:408
  34.5 0.2 add_convert_fusion
  34.8 1.8 %collective-permute-start.13 = (bf16[1,256,256]{2,1,0:T(8,128)(2,1)S(1)}, bf16[1,256,256]{2,1,0:T(8,128)(2,1)S(1)}, u32[]{:S(2)}, u32[]{:S(2)}) collective-permute-start(bf16[1,256,256]{2,1,0:T(8,128)(2,1)S(1)} %get-tuple-element.78), channel_id=1, source_target_pairs={{0,64},{8,72},{16,80},{24,88},{32,96},{40,104},{48,112},{56,120},{... | collective-permute-start | bytes 393224 | tf_op jit(solution)/shard_map/ppermute | solution.py:408
  36.6 1.1 collective-permute-start.12
  37.7 0.9 collective-permute-start.11
  38.6 4.6 %collective-permute-done.4 = bf16[4,256,256]{2,1,0:T(8,128)(2,1)S(1)} collective-permute-done((bf16[4,256,256]{2,1,0:T(8,128)(2,1)S(1)}, bf16[4,256,256]{2,1,0:T(8,128)(2,1)S(1)}, u32[]{:S(2)}, u32[]{:S(2)}) %collective-permute-start.4) | collective-permute-done | bytes 524320 | tf_op jit(solution)/shard_map/ppermute | solution.py:408
  43.3 0.2 add_convert_fusion.1
  43.5 0.1 collective-permute-start.8
  43.6 0.1 collective-permute-start.7
  43.7 3.2 %collective-permute-start.6 = (bf16[1,256,256]{2,1,0:T(8,128)(2,1)S(1)}, bf16[1,256,256]{2,1,0:T(8,128)(2,1)S(1)}, u32[]{:S(2)}, u32[]{:S(2)}) collective-permute-start(bf16[1,256,256]{2,1,0:T(8,128)(2,1)S(1)} %get-tuple-element.84), channel_id=1, source_target_pairs={{0,8},{8,16},{16,24},{24,0},{32,40},{40,48},{48,56},{56,32},{64,72... | collective-permute-start | bytes 393224 | tf_op jit(solution)/shard_map/ppermute | solution.py:408
  47.6 2.6 %collective-permute-done.8.refs_3_ = bf16[1,256,256]{2,1,0:T(8,128)(2,1)S(1)} collective-permute-done((bf16[1,256,256]{2,1,0:T(8,128)(2,1)S(1)}, bf16[1,256,256]{2,1,0:T(8,128)(2,1)S(1)}, u32[]{:S(2)}, u32[]{:S(2)}) %collective-permute-start.8) | collective-permute-done | bytes 131104 | tf_op jit(solution)/shard_map/ppermute | solution.py:408
  50.2 1.1 collective-permute-done.7.refs_2_
  51.3 6.2 %residuals.1 = (f32[1,2,8192]{2,1,0:T(2,128)}, bf16[1,256,256]{2,1,0:T(8,128)(2,1)S(1)}, bf16[1,256,256]{2,1,0:T(8,128)(2,1)S(1)}) custom-call(s32[1]{0:T(128)S(6)} %copy.10.count, bf16[1,256,256]{2,1,0:T(8,128)(2,1)S(1)} %get-tuple-element.85.refs_0_, bf16[1,256,256]{2,1,0:T(8,128)(2,1)S(1)} %collective-permute-done.6.refs_1_, ...), custom_call_target="tpu_custom_call" | custom-call | flops 4294967296 | bytes 8388608 | tf_op jit(solution)/shard_map/residuals/pallas_call | solution.py:290
  57.4 1.8 %collective-permute-start.23 = (bf16[1,256,256]{2,1,0:T(8,128)(2,1)S(1)}, bf16[1,256,256]{2,1,0:T(8,128)(2,1)S(1)}, u32[]{:S(2)}, u32[]{:S(2)}) collective-permute-start(bf16[1,256,256]{2,1,0:T(8,128)(2,1)S(1)} %get-tuple-element.67), channel_id=1, source_target_pairs={{0,8},{8,16},{16,24},{24,0},{32,40},{40,48},{48,56},{56,32},{64,72... | collective-permute-start | bytes 393224 | tf_op jit(solution)/shard_map/ppermute | solution.py:408
  59.2 0.2 collective-permute-start.22
  59.4 3.2 %collective-permute-start.14 = (bf16[1,256,256]{2,1,0:T(8,128)(2,1)S(1)}, bf16[1,256,256]{2,1,0:T(8,128)(2,1)S(1)}, u32[]{:S(2)}, u32[]{:S(2)}) collective-permute-start(bf16[1,256,256]{2,1,0:T(8,128)(2,1)S(1)} %get-tuple-element.66), channel_id=1, source_target_pairs={{0,96},{8,104},{16,112},{24,120},{32,0},{40,8},{48,16},{56,24},{64... | collective-permute-start | bytes 393224 | tf_op jit(solution)/shard_map/ppermute | solution.py:408
  62.7 3.1 %collective-permute-start.24 = (bf16[1,128,256]{2,1,0:T(8,128)(2,1)S(1)}, bf16[1,128,256]{2,1,0:T(8,128)(2,1)S(1)}, u32[]{:S(2)}, u32[]{:S(2)}) collective-permute-start(bf16[1,128,256]{2,1,0:T(8,128)(2,1)S(1)} %slice.142), channel_id=1, source_target_pairs={{0,8},{8,16},{16,24},{24,0},{32,40},{40,48},{48,56},{56,32},{64,72... | collective-permute-start | bytes 196616 | tf_op jit(solution)/shard_map/ppermute | solution.py:408
  65.8 0.1 collective-permute-start.25
  66.0 3.4 %collective-permute-start.17 = (bf16[1,128,256]{2,1,0:T(8,128)(2,1)S(1)}, bf16[1,128,256]{2,1,0:T(8,128)(2,1)S(1)}, u32[]{:S(2)}, u32[]{:S(2)}) collective-permute-start(bf16[1,128,256]{2,1,0:T(8,128)(2,1)S(1)} %slice.139), channel_id=1, source_target_pairs={{0,96},{8,104},{16,112},{24,120},{32,0},{40,8},{48,16},{56,24},{64... | collective-permute-start | bytes 196616 | tf_op jit(solution)/shard_map/ppermute | solution.py:408
  69.4 2.6 %collective-permute-done.25 = bf16[1,128,256]{2,1,0:T(8,128)(2,1)S(1)} collective-permute-done((bf16[1,128,256]{2,1,0:T(8,128)(2,1)S(1)}, bf16[1,128,256]{2,1,0:T(8,128)(2,1)S(1)}, u32[]{:S(2)}, u32[]{:S(2)}) %collective-permute-start.25) | collective-permute-done | bytes 65568 | tf_op jit(solution)/shard_map/ppermute | solution.py:408
  72.2 3.2 %collective-permute-start.26 = (bf16[4,256,256]{2,1,0:T(8,128)(2,1)S(1)}, bf16[4,256,256]{2,1,0:T(8,128)(2,1)S(1)}, u32[]{:S(2)}, u32[]{:S(2)}) collective-permute-start(bf16[4,256,256]{2,1,0:T(8,128)(2,1)S(1)} %maximum_maximum_fusion.1.refs_5_), channel_id=1, source_target_pairs={{0,96},{8,104},{16,112},{24,120},{32,0},{40,8},{48,16},{56,24},{64... | collective-permute-start | bytes 1572872 | tf_op jit(solution)/shard_map/ppermute | solution.py:408
  75.5 1.3 %collective-permute-start.19 = (bf16[4,256,256]{2,1,0:T(8,128)(2,1)S(1)}, bf16[4,256,256]{2,1,0:T(8,128)(2,1)S(1)}, u32[]{:S(2)}, u32[]{:S(2)}) collective-permute-start(bf16[4,256,256]{2,1,0:T(8,128)(2,1)S(1)} %maximum_maximum_fusion.refs_0_), channel_id=1, source_target_pairs={{0,8},{8,16},{16,24},{24,0},{32,40},{40,48},{48,56},{56,32},{64,72... | collective-permute-start | bytes 1572872 | tf_op jit(solution)/shard_map/ppermute | solution.py:408
  76.8 0.8 collective-permute-start.18
  77.6 6.5 %collective-permute-done.27.refs_7_ = bf16[4,256,256]{2,1,0:T(8,128)(2,1)S(1)} collective-permute-done((bf16[4,256,256]{2,1,0:T(8,128)(2,1)S(1)}, bf16[4,256,256]{2,1,0:T(8,128)(2,1)S(1)}, u32[]{:S(2)}, u32[]{:S(2)}) %collective-permute-start.27) | collective-permute-done | bytes 524320 | tf_op jit(solution)/shard_map/ppermute | solution.py:408
  84.2 3.3 %collective-permute-start.29 = (bf16[4,128,256]{2,1,0:T(8,128)(2,1)S(1)}, bf16[4,128,256]{2,1,0:T(8,128)(2,1)S(1)}, u32[]{:S(2)}, u32[]{:S(2)}) collective-permute-start(bf16[4,128,256]{2,1,0:T(8,128)(2,1)S(1)} %slice.145), channel_id=1, source_target_pairs={{0,96},{8,104},{16,112},{24,120},{32,0},{40,8},{48,16},{56,24},{64... | collective-permute-start | bytes 786440 | tf_op jit(solution)/shard_map/ppermute | solution.py:408
  87.5 2.0 %collective-permute-start.20 = (bf16[4,128,256]{2,1,0:T(8,128)(2,1)S(1)}, bf16[4,128,256]{2,1,0:T(8,128)(2,1)S(1)}, u32[]{:S(2)}, u32[]{:S(2)}) collective-permute-start(bf16[4,128,256]{2,1,0:T(8,128)(2,1)S(1)} %slice.140), channel_id=1, source_target_pairs={{0,8},{8,16},{16,24},{24,0},{32,40},{40,48},{48,56},{56,32},{64,72... | collective-permute-start | bytes 786440 | tf_op jit(solution)/shard_map/ppermute | solution.py:408
  89.6 0.1 collective-permute-start.21
  89.7 2.0 %collective-permute-done.28.refs_8_ = bf16[4,128,256]{2,1,0:T(8,128)(2,1)S(1)} collective-permute-done((bf16[4,128,256]{2,1,0:T(8,128)(2,1)S(1)}, bf16[4,128,256]{2,1,0:T(8,128)(2,1)S(1)}, u32[]{:S(2)}, u32[]{:S(2)}) %collective-permute-start.28) | collective-permute-done | bytes 262176 | tf_op jit(solution)/shard_map/ppermute | solution.py:408
  91.8 2.2 %collective-permute-done.20.refs_3_ = bf16[4,128,256]{2,1,0:T(8,128)(2,1)S(1)} collective-permute-done((bf16[4,128,256]{2,1,0:T(8,128)(2,1)S(1)}, bf16[4,128,256]{2,1,0:T(8,128)(2,1)S(1)}, u32[]{:S(2)}, u32[]{:S(2)}) %collective-permute-start.20) | collective-permute-done | bytes 262176 | tf_op jit(solution)/shard_map/ppermute | solution.py:408
  94.0 3.3 %collective-permute-done.21.refs_4_ = bf16[4,128,256]{2,1,0:T(8,128)(2,1)S(1)} collective-permute-done((bf16[4,128,256]{2,1,0:T(8,128)(2,1)S(1)}, bf16[4,128,256]{2,1,0:T(8,128)(2,1)S(1)}, u32[]{:S(2)}, u32[]{:S(2)}) %collective-permute-start.21) | collective-permute-done | bytes 262176 | tf_op jit(solution)/shard_map/ppermute | solution.py:408
  97.3 8.4 %adjoint_plane.1 = (bf16[4,2,152,704]{3,2,1,0:T(8,128)(2,1)S(1)}, bf16[4,2,152,704]{3,2,1,0:T(8,128)(2,1)S(1)}) custom-call(s32[42]{0:T(128)S(1)} %copy-done.7, bf16[4,256,256]{2,1,0:T(8,128)(2,1)S(1)} %maximum_maximum_fusion.refs_0_, bf16[4,256,256]{2,1,0:T(8,128)(2,1)S(1)} %collective-permute-done.18.refs_1_, ...), custom_call_target="tpu_custom_call" | custom-call | flops 4294967296 | bytes 8388608 | tf_op jit(solution)/shard_map/adjoint_plane/pallas_call | solution.py:368
  105.6 0.1 collective-permute-start.30
  105.7 3.8 %collective-permute-done.30 = bf16[4,2,152,704]{3,2,1,0:T(8,128)(2,1)S(1)} collective-permute-done((bf16[4,2,152,704]{3,2,1,0:T(8,128)(2,1)S(1)}, bf16[4,2,152,704]{3,2,1,0:T(8,128)(2,1)S(1)}, u32[]{:S(2)}, u32[]{:S(2)}) %collective-permute-start.30) | collective-permute-done | bytes 1712160 | tf_op jit(solution)/shard_map/ppermute | solution.py:449
  109.5 0.5 add.66
  110.1 1.5 %collective-permute-start.31 = (bf16[152,704]{1,0:T(8,128)(2,1)S(1)}, bf16[152,704]{1,0:T(8,128)(2,1)S(1)}, u32[]{:S(2)}, u32[]{:S(2)}) collective-permute-start(bf16[152,704]{1,0:T(8,128)(2,1)S(1)} %get-tuple-element.72), channel_id=1, source_target_pairs={{0,2},{1,3},{2,4},{3,5},{4,6},{5,7},{6,0},{7,1},{8,10},{9,11},{10,... | collective-permute-start | bytes 642056 | tf_op jit(solution)/shard_map/ppermute | solution.py:408
  111.7 2.2 %collective-permute-start.35 = (bf16[152,704]{1,0:T(8,128)(2,1)S(1)}, bf16[152,704]{1,0:T(8,128)(2,1)S(1)}, u32[]{:S(2)}, u32[]{:S(2)}) collective-permute-start(bf16[152,704]{1,0:T(8,128)(2,1)S(1)} %get-tuple-element.73), channel_id=1, source_target_pairs={{0,6},{1,7},{2,0},{3,1},{4,2},{5,3},{6,4},{7,5},{8,14},{9,15},{10,... | collective-permute-start | bytes 642056 | tf_op jit(solution)/shard_map/ppermute | solution.py:408
  113.9 3.2 %collective-permute-start.33 = (bf16[152,704]{1,0:T(8,128)(2,1)S(1)}, bf16[152,704]{1,0:T(8,128)(2,1)S(1)}, u32[]{:S(2)}, u32[]{:S(2)}) collective-permute-start(bf16[152,704]{1,0:T(8,128)(2,1)S(1)} %get-tuple-element.75), channel_id=1, source_target_pairs={{0,6},{1,7},{2,0},{3,1},{4,2},{5,3},{6,4},{7,5},{8,14},{9,15},{10,... | collective-permute-start | bytes 642056 | tf_op jit(solution)/shard_map/ppermute | solution.py:408
  117.1 3.2 %collective-permute-done.31 = bf16[152,704]{1,0:T(8,128)(2,1)S(1)} collective-permute-done((bf16[152,704]{1,0:T(8,128)(2,1)S(1)}, bf16[152,704]{1,0:T(8,128)(2,1)S(1)}, u32[]{:S(2)}, u32[]{:S(2)}) %collective-permute-start.31) | collective-permute-done | bytes 214048 | tf_op jit(solution)/shard_map/ppermute | solution.py:408
  120.3 0.1 fusion.7
  120.3 2.0 %collective-permute-start.32 = (bf16[152,704]{1,0:T(8,128)(2,1)S(1)}, bf16[152,704]{1,0:T(8,128)(2,1)S(1)}, u32[]{:S(2)}, u32[]{:S(2)}) collective-permute-start(bf16[152,704]{1,0:T(8,128)(2,1)S(1)} %get-tuple-element.70), channel_id=1, source_target_pairs={{0,2},{1,3},{2,4},{3,5},{4,6},{5,7},{6,0},{7,1},{8,10},{9,11},{10,... | collective-permute-start | bytes 642056 | tf_op jit(solution)/shard_map/ppermute | solution.py:408
  122.3 1.5 %collective-permute-start.36 = (bf16[152,704]{1,0:T(8,128)(2,1)S(1)}, bf16[152,704]{1,0:T(8,128)(2,1)S(1)}, u32[]{:S(2)}, u32[]{:S(2)}) collective-permute-start(bf16[152,704]{1,0:T(8,128)(2,1)S(1)} %get-tuple-element.71), channel_id=1, source_target_pairs={{0,6},{1,7},{2,0},{3,1},{4,2},{5,3},{6,4},{7,5},{8,14},{9,15},{10,... | collective-permute-start | bytes 642056 | tf_op jit(solution)/shard_map/ppermute | solution.py:408
  123.8 0.1 convert_add_fusion
  123.9 1.3 %collective-permute-done.34 = bf16[152,704]{1,0:T(8,128)(2,1)S(1)} collective-permute-done((bf16[152,704]{1,0:T(8,128)(2,1)S(1)}, bf16[152,704]{1,0:T(8,128)(2,1)S(1)}, u32[]{:S(2)}, u32[]{:S(2)}) %collective-permute-start.34) | collective-permute-done | bytes 214048 | tf_op jit(solution)/shard_map/ppermute | solution.py:408
  125.3 4.5 %collective-permute-done.32 = bf16[152,704]{1,0:T(8,128)(2,1)S(1)} collective-permute-done((bf16[152,704]{1,0:T(8,128)(2,1)S(1)}, bf16[152,704]{1,0:T(8,128)(2,1)S(1)}, u32[]{:S(2)}, u32[]{:S(2)}) %collective-permute-start.32) | collective-permute-done | bytes 214048 | tf_op jit(solution)/shard_map/ppermute | solution.py:408
  129.8 0.2 fusion.5
  129.9 1.0 maximum_bitcast_fusion
  (61 shorter events, 0.8 us)
Async XLA Ops:
  0.6 13.6 %copy-start = (bf16[1,2,1216,704]{2,3,1,0:T(8,128)(2,1)S(1)}, bf16[1,2,1216,704]{2,3,1,0:T(8,128)(2,1)}, u32[]{:S(2)}) copy-start(bf16[1,2,1216,704]{2,3,1,0:T(8,128)(2,1)} %param.8) | copy-start | bytes 10272772
  0.6 13.6 %copy-start.4 = (f32[2,256,256]{2,1,0:T(8,128)S(1)}, f32[2,256,256]{2,1,0:T(8,128)}, u32[]{:S(2)}) copy-start(f32[2,256,256]{2,1,0:T(8,128)} %constant.6.clone.base.refs_10_) | copy-start | bytes 1572868
  0.7 13.6 %copy-start.5 = (f32[16,2,256]{2,1,0:T(2,128)S(1)}, f32[16,2,256]{2,1,0:T(2,128)}, u32[]{:S(2)}) copy-start(f32[16,2,256]{2,1,0:T(2,128)} %constant.7.clone.phases.left.right.refs_11_.refs_12_) | copy-start | bytes 98308
  8.9 10.3 %collective-permute-start = (bf16[4,128,256]{2,1,0:T(8,128)(2,1)}, bf16[4,128,256]{2,1,0:T(8,128)(2,1)S(1)}, u32[]{:S(2)}, u32[]{:S(2)}) collective-permute-start(bf16[4,128,256]{2,1,0:T(8,128)(2,1)} %get-tuple-element.36), channel_id=1, source_target_pairs={{0,32},{8,40},{16,48},{24,56},{32,64},{40,72},{48,80},{56,88},{64,... | collective-permute-start | bytes 786440 | tf_op jit(solution)/shard_map/ppermute | solution.py:408
  10.5 8.8 %collective-permute-start.1 = (bf16[4,128,256]{2,1,0:T(8,128)(2,1)}, bf16[4,128,256]{2,1,0:T(8,128)(2,1)S(1)}, u32[]{:S(2)}, u32[]{:S(2)}) collective-permute-start(bf16[4,128,256]{2,1,0:T(8,128)(2,1)} %get-tuple-element.37), channel_id=1, source_target_pairs={{0,96},{8,104},{16,112},{24,120},{32,0},{40,8},{48,16},{56,24},{64... | collective-permute-start | bytes 786440 | tf_op jit(solution)/shard_map/ppermute | solution.py:408
  12.2 7.7 %collective-permute-start.2 = (bf16[4,128,256]{2,1,0:T(8,128)(2,1)}, bf16[4,128,256]{2,1,0:T(8,128)(2,1)S(1)}, u32[]{:S(2)}, u32[]{:S(2)}) collective-permute-start(bf16[4,128,256]{2,1,0:T(8,128)(2,1)} %get-tuple-element.38), channel_id=1, source_target_pairs={{0,8},{8,16},{16,24},{24,0},{32,40},{40,48},{48,56},{56,32},{64,72... | collective-permute-start | bytes 786440 | tf_op jit(solution)/shard_map/ppermute | solution.py:408
  12.4 8.8 %collective-permute-start.3 = (bf16[4,128,256]{2,1,0:T(8,128)(2,1)}, bf16[4,128,256]{2,1,0:T(8,128)(2,1)S(1)}, u32[]{:S(2)}, u32[]{:S(2)}) collective-permute-start(bf16[4,128,256]{2,1,0:T(8,128)(2,1)} %get-tuple-element.39), channel_id=1, source_target_pairs={{0,24},{8,0},{16,8},{24,16},{32,56},{40,32},{48,40},{56,48},{64,88... | collective-permute-start | bytes 786440 | tf_op jit(solution)/shard_map/ppermute | solution.py:408
  14.2 0.7 copy-start.6
  14.9 4.2 %copy-start.8 = (bf16[3,256,256]{2,1,0:T(8,128)(2,1)S(1)}, bf16[3,256,256]{2,1,0:T(8,128)(2,1)}, u32[]{:S(2)}) copy-start(bf16[3,256,256]{2,1,0:T(8,128)(2,1)} %get-tuple-element.48) | copy-start | bytes 1179652
  14.9 4.2 %copy-start.9 = (bf16[3,256,256]{2,1,0:T(8,128)(2,1)S(1)}, bf16[3,256,256]{2,1,0:T(8,128)(2,1)}, u32[]{:S(2)}) copy-start(bf16[3,256,256]{2,1,0:T(8,128)(2,1)} %get-tuple-element.58) | copy-start | bytes 1179652
  21.2 13.3 %collective-permute-start.10 = (bf16[4,256,256]{2,1,0:T(8,128)(2,1)S(1)}, bf16[4,256,256]{2,1,0:T(8,128)(2,1)S(1)}, u32[]{:S(2)}, u32[]{:S(2)}) collective-permute-start(bf16[4,256,256]{2,1,0:T(8,128)(2,1)S(1)} %maximum_add_fusion.3), channel_id=1, source_target_pairs={{0,24},{8,0},{16,8},{24,16},{32,56},{40,32},{48,40},{56,48},{64,88... | collective-permute-start | bytes 1572872 | tf_op jit(solution)/shard_map/ppermute | solution.py:408
  21.9 5.4 %copy-start.1 = (s32[1,2,8192]{2,1,0:T(2,128)S(1)}, s32[1,2,8192]{2,1,0:T(2,128)}, u32[]{:S(2)}) copy-start(s32[1,2,8192]{2,1,0:T(2,128)} %offsets) | copy-start | bytes 196612
  21.9 5.4 %copy-start.2 = (f32[1,2,8192]{2,1,0:T(2,128)S(1)}, f32[1,2,8192]{2,1,0:T(2,128)}, u32[]{:S(2)}) copy-start(f32[1,2,8192]{2,1,0:T(2,128)} %fractions.1) | copy-start | bytes 196612
  21.9 12.6 %collective-permute-start.9 = (bf16[4,256,256]{2,1,0:T(8,128)(2,1)S(1)}, bf16[4,256,256]{2,1,0:T(8,128)(2,1)S(1)}, u32[]{:S(2)}, u32[]{:S(2)}) collective-permute-start(bf16[4,256,256]{2,1,0:T(8,128)(2,1)S(1)} %maximum_add_fusion.2), channel_id=1, source_target_pairs={{0,8},{8,16},{16,24},{24,0},{32,40},{40,48},{48,56},{56,32},{64,72... | collective-permute-start | bytes 1572872 | tf_op jit(solution)/shard_map/ppermute | solution.py:408
  24.8 13.9 %collective-permute-start.5 = (bf16[4,256,256]{2,1,0:T(8,128)(2,1)S(1)}, bf16[4,256,256]{2,1,0:T(8,128)(2,1)S(1)}, u32[]{:S(2)}, u32[]{:S(2)}) collective-permute-start(bf16[4,256,256]{2,1,0:T(8,128)(2,1)S(1)} %maximum_add_fusion.1), channel_id=1, source_target_pairs={{0,96},{8,104},{16,112},{24,120},{32,0},{40,8},{48,16},{56,24},{64... | collective-permute-start | bytes 1572872 | tf_op jit(solution)/shard_map/ppermute | solution.py:408
  26.5 16.8 %collective-permute-start.4 = (bf16[4,256,256]{2,1,0:T(8,128)(2,1)S(1)}, bf16[4,256,256]{2,1,0:T(8,128)(2,1)S(1)}, u32[]{:S(2)}, u32[]{:S(2)}) collective-permute-start(bf16[4,256,256]{2,1,0:T(8,128)(2,1)S(1)} %maximum_add_fusion), channel_id=1, source_target_pairs={{0,32},{8,40},{16,48},{24,56},{32,64},{40,72},{48,80},{56,88},{64,... | collective-permute-start | bytes 1572872 | tf_op jit(solution)/shard_map/ppermute | solution.py:408
  34.7 16.5 %copy-start.3 = (f32[1,2,8192]{2,1,0:T(2,128)S(1)}, f32[1,2,8192]{2,1,0:T(2,128)}, u32[]{:S(2)}) copy-start(f32[1,2,8192]{2,1,0:T(2,128)} %refs_10_.2) | copy-start | bytes 196612
  34.8 8.9 %collective-permute-start.13 = (bf16[1,256,256]{2,1,0:T(8,128)(2,1)S(1)}, bf16[1,256,256]{2,1,0:T(8,128)(2,1)S(1)}, u32[]{:S(2)}, u32[]{:S(2)}) collective-permute-start(bf16[1,256,256]{2,1,0:T(8,128)(2,1)S(1)} %get-tuple-element.78), channel_id=1, source_target_pairs={{0,64},{8,72},{16,80},{24,88},{32,96},{40,104},{48,112},{56,120},{... | collective-permute-start | bytes 393224 | tf_op jit(solution)/shard_map/ppermute | solution.py:408
  36.6 10.9 %collective-permute-start.12 = (bf16[1,256,256]{2,1,0:T(8,128)(2,1)S(1)}, bf16[1,256,256]{2,1,0:T(8,128)(2,1)S(1)}, u32[]{:S(2)}, u32[]{:S(2)}) collective-permute-start(bf16[1,256,256]{2,1,0:T(8,128)(2,1)S(1)} %get-tuple-element.79), channel_id=1, source_target_pairs={{0,96},{8,104},{16,112},{24,120},{32,0},{40,8},{48,16},{56,24},{64... | collective-permute-start | bytes 393224 | tf_op jit(solution)/shard_map/ppermute | solution.py:408
  37.7 9.8 %collective-permute-start.11 = (bf16[1,256,256]{2,1,0:T(8,128)(2,1)S(1)}, bf16[1,256,256]{2,1,0:T(8,128)(2,1)S(1)}, u32[]{:S(2)}, u32[]{:S(2)}) collective-permute-start(bf16[1,256,256]{2,1,0:T(8,128)(2,1)S(1)} %get-tuple-element.80), channel_id=1, source_target_pairs={{0,32},{8,40},{16,48},{24,56},{32,64},{40,72},{48,80},{56,88},{64,... | collective-permute-start | bytes 393224 | tf_op jit(solution)/shard_map/ppermute | solution.py:408
  43.5 6.7 %collective-permute-start.8 = (bf16[1,256,256]{2,1,0:T(8,128)(2,1)S(1)}, bf16[1,256,256]{2,1,0:T(8,128)(2,1)S(1)}, u32[]{:S(2)}, u32[]{:S(2)}) collective-permute-start(bf16[1,256,256]{2,1,0:T(8,128)(2,1)S(1)} %get-tuple-element.82), channel_id=1, source_target_pairs={{0,16},{8,24},{16,0},{24,8},{32,48},{40,56},{48,32},{56,40},{64,80... | collective-permute-start | bytes 393224 | tf_op jit(solution)/shard_map/ppermute | solution.py:408
  43.6 7.7 %collective-permute-start.7 = (bf16[1,256,256]{2,1,0:T(8,128)(2,1)S(1)}, bf16[1,256,256]{2,1,0:T(8,128)(2,1)S(1)}, u32[]{:S(2)}, u32[]{:S(2)}) collective-permute-start(bf16[1,256,256]{2,1,0:T(8,128)(2,1)S(1)} %get-tuple-element.83), channel_id=1, source_target_pairs={{0,24},{8,0},{16,8},{24,16},{32,56},{40,32},{48,40},{56,48},{64,88... | collective-permute-start | bytes 393224 | tf_op jit(solution)/shard_map/ppermute | solution.py:408
  43.7 7.6 %collective-permute-start.6 = (bf16[1,256,256]{2,1,0:T(8,128)(2,1)S(1)}, bf16[1,256,256]{2,1,0:T(8,128)(2,1)S(1)}, u32[]{:S(2)}, u32[]{:S(2)}) collective-permute-start(bf16[1,256,256]{2,1,0:T(8,128)(2,1)S(1)} %get-tuple-element.84), channel_id=1, source_target_pairs={{0,8},{8,16},{16,24},{24,0},{32,40},{40,48},{48,56},{56,32},{64,72... | collective-permute-start | bytes 393224 | tf_op jit(solution)/shard_map/ppermute | solution.py:408
  57.4 5.3 %collective-permute-start.23 = (bf16[1,256,256]{2,1,0:T(8,128)(2,1)S(1)}, bf16[1,256,256]{2,1,0:T(8,128)(2,1)S(1)}, u32[]{:S(2)}, u32[]{:S(2)}) collective-permute-start(bf16[1,256,256]{2,1,0:T(8,128)(2,1)S(1)} %get-tuple-element.67), channel_id=1, source_target_pairs={{0,8},{8,16},{16,24},{24,0},{32,40},{40,48},{48,56},{56,32},{64,72... | collective-permute-start | bytes 393224 | tf_op jit(solution)/shard_map/ppermute | solution.py:408
  59.2 6.6 %collective-permute-start.22 = (bf16[1,256,256]{2,1,0:T(8,128)(2,1)S(1)}, bf16[1,256,256]{2,1,0:T(8,128)(2,1)S(1)}, u32[]{:S(2)}, u32[]{:S(2)}) collective-permute-start(bf16[1,256,256]{2,1,0:T(8,128)(2,1)S(1)} %get-tuple-element.67), channel_id=1, source_target_pairs={{0,24},{8,0},{16,8},{24,16},{32,56},{40,32},{48,40},{56,48},{64,88... | collective-permute-start | bytes 393224 | tf_op jit(solution)/shard_map/ppermute | solution.py:408
  59.4 6.5 %collective-permute-start.15 = (bf16[1,256,256]{2,1,0:T(8,128)(2,1)S(1)}, bf16[1,256,256]{2,1,0:T(8,128)(2,1)S(1)}, u32[]{:S(2)}, u32[]{:S(2)}) collective-permute-start(bf16[1,256,256]{2,1,0:T(8,128)(2,1)S(1)} %get-tuple-element.66), channel_id=1, source_target_pairs={{0,32},{8,40},{16,48},{24,56},{32,64},{40,72},{48,80},{56,88},{64,... | collective-permute-start | bytes 393224 | tf_op jit(solution)/shard_map/ppermute | solution.py:408
  59.4 6.6 %collective-permute-start.14 = (bf16[1,256,256]{2,1,0:T(8,128)(2,1)S(1)}, bf16[1,256,256]{2,1,0:T(8,128)(2,1)S(1)}, u32[]{:S(2)}, u32[]{:S(2)}) collective-permute-start(bf16[1,256,256]{2,1,0:T(8,128)(2,1)S(1)} %get-tuple-element.66), channel_id=1, source_target_pairs={{0,96},{8,104},{16,112},{24,120},{32,0},{40,8},{48,16},{56,24},{64... | collective-permute-start | bytes 393224 | tf_op jit(solution)/shard_map/ppermute | solution.py:408
  62.7 6.8 %collective-permute-start.24 = (bf16[1,128,256]{2,1,0:T(8,128)(2,1)S(1)}, bf16[1,128,256]{2,1,0:T(8,128)(2,1)S(1)}, u32[]{:S(2)}, u32[]{:S(2)}) collective-permute-start(bf16[1,128,256]{2,1,0:T(8,128)(2,1)S(1)} %slice.142), channel_id=1, source_target_pairs={{0,8},{8,16},{16,24},{24,0},{32,40},{40,48},{48,56},{56,32},{64,72... | collective-permute-start | bytes 196616 | tf_op jit(solution)/shard_map/ppermute | solution.py:408
  65.8 6.3 %collective-permute-start.25 = (bf16[1,128,256]{2,1,0:T(8,128)(2,1)S(1)}, bf16[1,128,256]{2,1,0:T(8,128)(2,1)S(1)}, u32[]{:S(2)}, u32[]{:S(2)}) collective-permute-start(bf16[1,128,256]{2,1,0:T(8,128)(2,1)S(1)} %slice.143), channel_id=1, source_target_pairs={{0,24},{8,0},{16,8},{24,16},{32,56},{40,32},{48,40},{56,48},{64,88... | collective-permute-start | bytes 196616 | tf_op jit(solution)/shard_map/ppermute | solution.py:408
  65.9 9.5 %collective-permute-start.16 = (bf16[1,128,256]{2,1,0:T(8,128)(2,1)S(1)}, bf16[1,128,256]{2,1,0:T(8,128)(2,1)S(1)}, u32[]{:S(2)}, u32[]{:S(2)}) collective-permute-start(bf16[1,128,256]{2,1,0:T(8,128)(2,1)S(1)} %slice.138), channel_id=1, source_target_pairs={{0,32},{8,40},{16,48},{24,56},{32,64},{40,72},{48,80},{56,88},{64,... | collective-permute-start | bytes 196616 | tf_op jit(solution)/shard_map/ppermute | solution.py:408
  66.0 31.2 %copy-start.7 = (s32[42]{0:T(128)S(1)}, s32[42]{0:T(128)}, u32[]{:S(2)}) copy-start(s32[42]{0:T(128)} %get-tuple-element.40.place) | copy-start | bytes 508
  66.0 9.4 %collective-permute-start.17 = (bf16[1,128,256]{2,1,0:T(8,128)(2,1)S(1)}, bf16[1,128,256]{2,1,0:T(8,128)(2,1)S(1)}, u32[]{:S(2)}, u32[]{:S(2)}) collective-permute-start(bf16[1,128,256]{2,1,0:T(8,128)(2,1)S(1)} %slice.139), channel_id=1, source_target_pairs={{0,96},{8,104},{16,112},{24,120},{32,0},{40,8},{48,16},{56,24},{64... | collective-permute-start | bytes 196616 | tf_op jit(solution)/shard_map/ppermute | solution.py:408
  72.1 11.9 %collective-permute-start.27 = (bf16[4,256,256]{2,1,0:T(8,128)(2,1)S(1)}, bf16[4,256,256]{2,1,0:T(8,128)(2,1)S(1)}, u32[]{:S(2)}, u32[]{:S(2)}) collective-permute-start(bf16[4,256,256]{2,1,0:T(8,128)(2,1)S(1)} %maximum_maximum_fusion.1.refs_5_), channel_id=1, source_target_pairs={{0,32},{8,40},{16,48},{24,56},{32,64},{40,72},{48,80},{56,88},{64,... | collective-permute-start | bytes 1572872 | tf_op jit(solution)/shard_map/ppermute | solution.py:408
  72.2 12.0 %collective-permute-start.26 = (bf16[4,256,256]{2,1,0:T(8,128)(2,1)S(1)}, bf16[4,256,256]{2,1,0:T(8,128)(2,1)S(1)}, u32[]{:S(2)}, u32[]{:S(2)}) collective-permute-start(bf16[4,256,256]{2,1,0:T(8,128)(2,1)S(1)} %maximum_maximum_fusion.1.refs_5_), channel_id=1, source_target_pairs={{0,96},{8,104},{16,112},{24,120},{32,0},{40,8},{48,16},{56,24},{64... | collective-permute-start | bytes 1572872 | tf_op jit(solution)/shard_map/ppermute | solution.py:408
  75.5 12.0 %collective-permute-start.19 = (bf16[4,256,256]{2,1,0:T(8,128)(2,1)S(1)}, bf16[4,256,256]{2,1,0:T(8,128)(2,1)S(1)}, u32[]{:S(2)}, u32[]{:S(2)}) collective-permute-start(bf16[4,256,256]{2,1,0:T(8,128)(2,1)S(1)} %maximum_maximum_fusion.refs_0_), channel_id=1, source_target_pairs={{0,8},{8,16},{16,24},{24,0},{32,40},{40,48},{48,56},{56,32},{64,72... | collective-permute-start | bytes 1572872 | tf_op jit(solution)/shard_map/ppermute | solution.py:408
  76.8 12.7 %collective-permute-start.18 = (bf16[4,256,256]{2,1,0:T(8,128)(2,1)S(1)}, bf16[4,256,256]{2,1,0:T(8,128)(2,1)S(1)}, u32[]{:S(2)}, u32[]{:S(2)}) collective-permute-start(bf16[4,256,256]{2,1,0:T(8,128)(2,1)S(1)} %maximum_maximum_fusion.refs_0_), channel_id=1, source_target_pairs={{0,24},{8,0},{16,8},{24,16},{32,56},{40,32},{48,40},{56,48},{64,88... | collective-permute-start | bytes 1572872 | tf_op jit(solution)/shard_map/ppermute | solution.py:408
  84.1 7.7 %collective-permute-start.28 = (bf16[4,128,256]{2,1,0:T(8,128)(2,1)S(1)}, bf16[4,128,256]{2,1,0:T(8,128)(2,1)S(1)}, u32[]{:S(2)}, u32[]{:S(2)}) collective-permute-start(bf16[4,128,256]{2,1,0:T(8,128)(2,1)S(1)} %slice.144), channel_id=1, source_target_pairs={{0,32},{8,40},{16,48},{24,56},{32,64},{40,72},{48,80},{56,88},{64,... | collective-permute-start | bytes 786440 | tf_op jit(solution)/shard_map/ppermute | solution.py:408
  84.2 7.5 %collective-permute-start.29 = (bf16[4,128,256]{2,1,0:T(8,128)(2,1)S(1)}, bf16[4,128,256]{2,1,0:T(8,128)(2,1)S(1)}, u32[]{:S(2)}, u32[]{:S(2)}) collective-permute-start(bf16[4,128,256]{2,1,0:T(8,128)(2,1)S(1)} %slice.145), channel_id=1, source_target_pairs={{0,96},{8,104},{16,112},{24,120},{32,0},{40,8},{48,16},{56,24},{64... | collective-permute-start | bytes 786440 | tf_op jit(solution)/shard_map/ppermute | solution.py:408
  87.5 6.4 %collective-permute-start.20 = (bf16[4,128,256]{2,1,0:T(8,128)(2,1)S(1)}, bf16[4,128,256]{2,1,0:T(8,128)(2,1)S(1)}, u32[]{:S(2)}, u32[]{:S(2)}) collective-permute-start(bf16[4,128,256]{2,1,0:T(8,128)(2,1)S(1)} %slice.140), channel_id=1, source_target_pairs={{0,8},{8,16},{16,24},{24,0},{32,40},{40,48},{48,56},{56,32},{64,72... | collective-permute-start | bytes 786440 | tf_op jit(solution)/shard_map/ppermute | solution.py:408
  89.6 7.7 %collective-permute-start.21 = (bf16[4,128,256]{2,1,0:T(8,128)(2,1)S(1)}, bf16[4,128,256]{2,1,0:T(8,128)(2,1)S(1)}, u32[]{:S(2)}, u32[]{:S(2)}) collective-permute-start(bf16[4,128,256]{2,1,0:T(8,128)(2,1)S(1)} %slice.141), channel_id=1, source_target_pairs={{0,24},{8,0},{16,8},{24,16},{32,56},{40,32},{48,40},{56,48},{64,88... | collective-permute-start | bytes 786440 | tf_op jit(solution)/shard_map/ppermute | solution.py:408
  105.6 3.9 %collective-permute-start.30 = (bf16[4,2,152,704]{3,2,1,0:T(8,128)(2,1)S(1)}, bf16[4,2,152,704]{3,2,1,0:T(8,128)(2,1)S(1)}, u32[]{:S(2)}, u32[]{:S(2)}) collective-permute-start(bf16[4,2,152,704]{3,2,1,0:T(8,128)(2,1)S(1)} %get-tuple-element.69), channel_id=1, source_target_pairs={{0,1},{1,0},{2,3},{3,2},{4,5},{5,4},{6,7},{7,6},{8,9},{9,8},{10,11... | collective-permute-start | bytes 5136392 | tf_op jit(solution)/shard_map/ppermute | solution.py:449
  110.1 10.1 %collective-permute-start.31 = (bf16[152,704]{1,0:T(8,128)(2,1)S(1)}, bf16[152,704]{1,0:T(8,128)(2,1)S(1)}, u32[]{:S(2)}, u32[]{:S(2)}) collective-permute-start(bf16[152,704]{1,0:T(8,128)(2,1)S(1)} %get-tuple-element.72), channel_id=1, source_target_pairs={{0,2},{1,3},{2,4},{3,5},{4,6},{5,7},{6,0},{7,1},{8,10},{9,11},{10,... | collective-permute-start | bytes 642056 | tf_op jit(solution)/shard_map/ppermute | solution.py:408
  111.7 8.6 %collective-permute-start.35 = (bf16[152,704]{1,0:T(8,128)(2,1)S(1)}, bf16[152,704]{1,0:T(8,128)(2,1)S(1)}, u32[]{:S(2)}, u32[]{:S(2)}) collective-permute-start(bf16[152,704]{1,0:T(8,128)(2,1)S(1)} %get-tuple-element.73), channel_id=1, source_target_pairs={{0,6},{1,7},{2,0},{3,1},{4,2},{5,3},{6,4},{7,5},{8,14},{9,15},{10,... | collective-permute-start | bytes 642056 | tf_op jit(solution)/shard_map/ppermute | solution.py:408
  113.9 11.4 %collective-permute-start.34 = (bf16[152,704]{1,0:T(8,128)(2,1)S(1)}, bf16[152,704]{1,0:T(8,128)(2,1)S(1)}, u32[]{:S(2)}, u32[]{:S(2)}) collective-permute-start(bf16[152,704]{1,0:T(8,128)(2,1)S(1)} %get-tuple-element.74), channel_id=1, source_target_pairs={{0,2},{1,3},{2,4},{3,5},{4,6},{5,7},{6,0},{7,1},{8,10},{9,11},{10,... | collective-permute-start | bytes 642056 | tf_op jit(solution)/shard_map/ppermute | solution.py:408
  113.9 11.4 %collective-permute-start.33 = (bf16[152,704]{1,0:T(8,128)(2,1)S(1)}, bf16[152,704]{1,0:T(8,128)(2,1)S(1)}, u32[]{:S(2)}, u32[]{:S(2)}) collective-permute-start(bf16[152,704]{1,0:T(8,128)(2,1)S(1)} %get-tuple-element.75), channel_id=1, source_target_pairs={{0,6},{1,7},{2,0},{3,1},{4,2},{5,3},{6,4},{7,5},{8,14},{9,15},{10,... | collective-permute-start | bytes 642056 | tf_op jit(solution)/shard_map/ppermute | solution.py:408
  120.3 9.4 %collective-permute-start.32 = (bf16[152,704]{1,0:T(8,128)(2,1)S(1)}, bf16[152,704]{1,0:T(8,128)(2,1)S(1)}, u32[]{:S(2)}, u32[]{:S(2)}) collective-permute-start(bf16[152,704]{1,0:T(8,128)(2,1)S(1)} %get-tuple-element.70), channel_id=1, source_target_pairs={{0,2},{1,3},{2,4},{3,5},{4,6},{5,7},{6,0},{7,1},{8,10},{9,11},{10,... | collective-permute-start | bytes 642056 | tf_op jit(solution)/shard_map/ppermute | solution.py:408
  122.3 7.4 %collective-permute-start.36 = (bf16[152,704]{1,0:T(8,128)(2,1)S(1)}, bf16[152,704]{1,0:T(8,128)(2,1)S(1)}, u32[]{:S(2)}, u32[]{:S(2)}) collective-permute-start(bf16[152,704]{1,0:T(8,128)(2,1)S(1)} %get-tuple-element.71), channel_id=1, source_target_pairs={{0,6},{1,7},{2,0},{3,1},{4,2},{5,3},{6,4},{7,5},{8,14},{9,15},{10,... | collective-permute-start | bytes 642056 | tf_op jit(solution)/shard_map/ppermute | solution.py:408
